TPU v7x, 32 devices: a whole 2x2x4 slice. The times are simulated.
32 devices in a mesh: dp: 8 (over z, x), tensor: 4 (over y, core).
Axes of the slice: x: 2, y: 2, z: 4, core: 2. Of those that a mesh axis runs over, the one named last changes fastest.
Arguments:
- inputs: bfloat16 [8, 1024, 512], P('dp'), may hold values from -6 to 6
- memory: bfloat16 [8, 512, 512], P('dp'), may hold values from -6 to 6
- counts: int32 [8], P('dp'), may hold values from 341 to 1024, as said below
- attn_gain: float32 [512], replicated, may hold values from 0.5 to 1.5
- attn_shift: float32 [512], replicated, may hold values from -2 to 2
- w_query: bfloat16 [512, 512], P(None, 'tensor'), may hold values from -0.25 to 0.25
- w_key: bfloat16 [512, 512], P(None, 'tensor'), may hold values from -0.25 to 0.25
- w_value: bfloat16 [512, 512], P(None, 'tensor'), may hold values from -0.25 to 0.25
- w_pos: bfloat16 [512, 512], P(None, 'tensor'), may hold values from -0.25 to 0.25
- bias_u: float32 [8, 64], P('tensor'), may hold values from -4 to 4
- bias_v: float32 [8, 64], P('tensor'), may hold values from -4 to 4
- w_out: bfloat16 [512, 512], P('tensor'), may hold values from -1 to 1
- ffn_gain: float32 [512], replicated, may hold values from 0.5 to 1.5
- ffn_shift: float32 [512], replicated, may hold values from -2 to 2
- w_up: bfloat16 [512, 2048], P(None, 'tensor'), may hold values from -0.25 to 0.25
- up_bias: float32 [2048], P('tensor'), may hold values from -2 to 2
- w_down: bfloat16 [2048, 512], P('tensor'), may hold values from -0.125 to 0.125
- down_bias: float32 [512], replicated, may hold values from -2 to 2
- out_grad: bfloat16 [8, 1024, 512], P('dp'), may hold values from -6 to 6
Outputs:
- output: bfloat16 [8, 1024, 512], P('dp')
- input_grad: bfloat16 [8, 1024, 512], P('dp')
- grad_attn_gain: float32 [512], replicated
- grad_attn_shift: float32 [512], replicated
- grad_w_query: float32 [512, 512], P(None, 'tensor')
- grad_w_key: float32 [512, 512], P(None, 'tensor')
- grad_w_value: float32 [512, 512], P(None, 'tensor')
- grad_w_pos: float32 [512, 512], P(None, 'tensor')
- grad_bias_u: float32 [8, 64], P('tensor')
- grad_bias_v: float32 [8, 64], P('tensor')
- grad_w_out: float32 [512, 512], P('tensor')
- grad_ffn_gain: float32 [512], replicated
- grad_ffn_shift: float32 [512], replicated
- grad_w_up: float32 [512, 2048], P(None, 'tensor')
- grad_up_bias: float32 [2048], P('tensor')
- grad_w_down: float32 [2048, 512], P('tensor')
- grad_down_bias: float32 [512], replicated
Inputs may be any that keep to these rules, and one draw needn't show every extreme that they name: Each entry counts the live leading rows of its sequence; one sequence in every draw has all 1024 rows live.
All inputs are finite; a program needn't handle non-finite values.
Results may differ from a plain program's by a relative error of at most 0.024.
Values may be sent and summed in bfloat16 or wider, within the bound.
No kernel may reach another device: no remote copies, remote signals or barrier semaphores. Data moves between devices by JAX's collectives and lax.ppermute only.
A program may use at most 192 MiB of HBM per device.

v0:
```python
import functools

import jax
import jax.numpy as jnp
import numpy as np
from jax import lax
from jax.experimental import pallas as pl
from jax.experimental.pallas import tpu as pltpu
from jax.sharding import PartitionSpec as P

HEAD = 64
BF = jnp.bfloat16
FL = jnp.float32
eps_norm = 1e-05
neg_fill = -1e30
VMEM_LIMIT = 24 * 1024 * 1024
small = 16


def mm(left, right):
    return lax.dot_general(left, right, (((1,), (0,)), ((), ())), preferred_element_type=FL)


def mm_t(left, right):
    return lax.dot_general(left, right, (((1,), (1,)), ((), ())), preferred_element_type=FL)


def t_mm(left, right):
    return lax.dot_general(left, right, (((0,), (0,)), ((), ())), preferred_element_type=FL)


def norm_parts(rows):
    center = rows - jnp.mean(rows, axis=-1, keepdims=True)
    spread = jnp.mean(center * center, axis=-1, keepdims=True)
    inv = lax.rsqrt(spread + eps_norm)
    return center * inv, inv


def norm_back(scaled, unit, inv):
    flat = jnp.mean(scaled, axis=-1, keepdims=True)
    along = jnp.mean(scaled * unit, axis=-1, keepdims=True)
    return inv * (scaled - flat - unit * along)


def head_lanes(wide, h):
    lane = lax.broadcasted_iota(jnp.int32, (1, wide), 1)
    return (lane >= h * HEAD) & (lane < (h + 1) * HEAD)


def col_sum(rows):
    return jnp.sum(rows, axis=0, keepdims=True)


def loop(count, body):
    def step(i, carry):
        body(i)
        return carry

    lax.fori_loop(0, count, step, 0)


def rows_of(i, size):
    return pl.ds(pl.multiple_of(i * size, size), size)


def by_core(core, part, keep_ref, send_ref, rows, at):
    @pl.when(core == part)
    def _():
        keep_ref[at, :] = rows

    @pl.when(core != part)
    def _():
        send_ref[at, :] = rows


def added(left, right):
    return (left.astype(FL) + right.astype(FL)).astype(BF)


def make_queries(normed, spots, at, refs, heads):
    w_ref, wpos_ref, bu, bv, sin_ref, cos_ref, qb_ref, qv_ref = refs
    wide = heads * HEAD
    scale = HEAD ** (-0.5)
    query = mm(normed, w_ref[:, :wide]).astype(BF).astype(FL)
    query_u = (query + bu).astype(BF).astype(FL) * scale
    query_v = (query + bv).astype(BF).astype(FL) * scale
    qv_ref[at, :] = query_v.astype(BF)
    sin = sin_ref[spots, :]
    cos = cos_ref[spots, :]
    half = sin.shape[1]
    for h in range(heads):
        lanes = head_lanes(wide, h)
        qb_ref[h, at, :wide] = jnp.where(lanes, query_u, 0.0).astype(BF)
        coef = mm_t(jnp.where(lanes, query_v, 0.0).astype(BF), wpos_ref[...])
        on_sin, on_cos = coef[:, :half], coef[:, half:]
        qb_ref[h, at, wide : wide + half] = (on_sin * sin + on_cos * cos).astype(BF)
        qb_ref[h, at, wide + half :] = (on_cos * sin - on_sin * cos).astype(BF)


def attend(first, block, mem_len, heads, count, qb_ref, kt_ref, v_ref, probs_ref, ctx_ref, ctx_scr):
    wide = heads * HEAD
    rows = qb_ref.shape[1]
    for part in range(rows // block):
        at = slice(part * block, (part + 1) * block)
        start = first + part * block
        seen = mem_len + start + block

        def one_head(h):
            scores = mm_t(qb_ref[h, at, :], kt_ref[:seen, :])
            query_pos = start + lax.broadcasted_iota(jnp.int32, (block, 1), 0)
            limit = jnp.minimum(query_pos, count - 1)
            key_pos = lax.broadcasted_iota(jnp.int32, (block, seen - mem_len), 1)
            scores = jnp.concatenate(
                [scores[:, :mem_len], jnp.where(key_pos <= limit, scores[:, mem_len:], neg_fill)], axis=1
            )
            expo = jnp.exp(scores - jnp.max(scores, axis=-1, keepdims=True))
            probs = (expo * (1.0 / jnp.sum(expo, axis=-1, keepdims=True))).astype(BF)
            probs_ref[h, at, :seen] = probs
            found = mm(probs, v_ref[:seen, :])
            ctx_scr[...] = jnp.where(head_lanes(wide, h), found, ctx_scr[...])

        loop(heads, one_head)
        ctx_ref[at, :] = ctx_scr[...].astype(BF)


def front_kernel(
    first, block, heads,
    place_ref, count_ref, x_in, mem_in, g_in, wq_in, wk_in, wv_in, wpos_in, wup_in, wdown_in, wout_in,
    shift_in, gain_in, fgain_in, fshift_in, upb_in, downb_in, bu_in, bv_in, table_in, sin_in, cos_in,
    x_ref, mem_ref, g_ref, w_ref, wpos_ref, wup_ref, wdown_ref, wout_ref, gain_ref, fgain_ref, fshift_ref, upb_ref,
    downb_ref, sin_ref, cos_ref, bias_ref, normed_ref, kt_ref, v_ref, qb_ref, qv_ref, probs_ref, ctx_ref,
    shift_ref, bu_ref, bv_ref, ctx_scr, sems,
):
    wide = heads * HEAD
    mem_len = mem_in.shape[0]
    seq_len = x_in.shape[0]
    todo = [
        (mem_in, mem_ref), (gain_in, gain_ref), (shift_in, shift_ref), (wk_in, w_ref.at[:, wide : 2 * wide]),
        (wv_in, w_ref.at[:, 2 * wide :]), (x_in, x_ref), (wq_in, w_ref.at[:, :wide]), (bu_in, bu_ref), (bv_in, bv_ref),
        (wpos_in, wpos_ref), (sin_in, sin_ref), (cos_in, cos_ref), (table_in, kt_ref.at[:, wide:]),
        (wout_in, wout_ref), (wup_in, wup_ref), (wdown_in, wdown_ref), (g_in, g_ref), (fgain_in, fgain_ref),
        (fshift_in, fshift_ref), (upb_in, upb_ref), (downb_in, downb_ref),
    ]
    copies = [pltpu.make_async_copy(src, dst, sems.at[i]) for i, (src, dst) in enumerate(todo)]
    for copy in copies:
        copy.start()
    for copy in copies[:5]:
        copy.wait()

    def project(rows_ref, at, to):
        unit, _ = norm_parts(rows_ref[at, :].astype(FL))
        normed = (unit * gain_ref[...] + shift_ref[...]).astype(BF)
        normed_ref[to, :] = normed
        pair = mm(normed, w_ref[:, wide:]).astype(BF)
        kt_ref[to, :wide] = pair[:, :wide]
        v_ref[to, :] = pair[:, wide:]

    def some_memory(i):
        project(mem_ref, rows_of(i, block), rows_of(i, block))

    def some_rows(i):
        project(x_ref, rows_of(i, block), rows_of(i + mem_len // block, block))

    loop(mem_len // block, some_memory)
    for copy in copies[5:7]:
        copy.wait()
    loop(seq_len // block, some_rows)
    for copy in copies[7:13]:
        copy.wait()
    bias_ref[0:1, :] = jnp.concatenate([bu_ref[h : h + 1, :] for h in range(heads)], axis=1)
    bias_ref[1:2, :] = jnp.concatenate([bv_ref[h : h + 1, :] for h in range(heads)], axis=1)

    def some_queries(i):
        at = rows_of(i, block)
        spots = rows_of(i + first // block, block)
        make_queries(
            normed_ref[rows_of(i + (mem_len + first) // block, block), :], spots, at,
            (w_ref, wpos_ref, bias_ref[0:1, :], bias_ref[1:2, :], sin_ref, cos_ref, qb_ref, qv_ref), heads,
        )

    loop((seq_len - first) // block, some_queries)
    attend(first, block, mem_len, heads, count_ref[0], qb_ref, kt_ref, v_ref, probs_ref, ctx_ref, ctx_scr)
    for copy in copies[13:]:
        copy.wait()


def second_kernel(
    first, block, heads, mem_len,
    count_ref, normed_ref, kt_ref, v_ref, w_ref, wpos_ref, bias_ref, sin_ref, cos_ref,
    qb_ref, qv_ref, probs_ref, ctx_ref, ctx_scr,
):
    def some_queries(i):
        at = rows_of(i, block)
        spots = rows_of(i + first // block, block)
        make_queries(
            normed_ref[rows_of(i + (mem_len + first) // block, block), :], spots, at,
            (w_ref, wpos_ref, bias_ref[0:1, :], bias_ref[1:2, :], sin_ref, cos_ref, qb_ref, qv_ref), heads,
        )

    loop(qb_ref.shape[1] // block, some_queries)
    attend(first, block, mem_len, heads, count_ref[0], qb_ref, kt_ref, v_ref, probs_ref, ctx_ref, ctx_scr)


def ffn_rows_kernel(
    first, block,
    place_ref, x_ref, c0_ref, c1_ref, c2_ref, c3_ref, o0_ref, o1_ref, o2_ref, o3_ref, gain_ref, shift_ref, up_ref,
    upb_ref, down_ref, g_ref,
    hidden_ref, normed_ref, activ_ref, gpre_ref, keep_ref, send_ref, vec_ref, upb_out,
):
    core = place_ref[0]
    vec_ref[...] = jnp.zeros(vec_ref.shape, FL)
    upb_out[...] = jnp.zeros(upb_out.shape, FL)

    def one(i):
        at = rows_of(i, block)
        spots = rows_of(i + first // block, block)
        attended = mm(c0_ref[at, :], o0_ref[...]) + mm(c1_ref[at, :], o1_ref[...])
        attended = attended + (mm(c2_ref[at, :], o2_ref[...]) + mm(c3_ref[at, :], o3_ref[...]))
        hidden = x_ref[spots, :].astype(FL) + attended
        hidden_ref[at, :] = hidden
        unit, _ = norm_parts(hidden)
        normed = (unit * gain_ref[...] + shift_ref[...]).astype(BF)
        normed_ref[at, :] = normed
        pre = mm(normed, up_ref[...]) + upb_ref[...]
        cdf = 0.5 + 0.5 * lax.erf(pre * np.float32(0.5**0.5))
        activ_ref[at, :] = (pre * cdf).astype(BF)
        slope = cdf + pre * jnp.exp(-0.5 * pre * pre) * np.float32((2 * np.pi) ** -0.5)
        grads = g_ref[spots, :]
        grad_pre = (mm_t(grads, down_ref[...]) * slope).astype(BF)
        gpre_ref[at, :] = grad_pre
        back = mm_t(grad_pre, up_ref[...])
        by_core(core, i, keep_ref, send_ref, back.astype(BF), slice(0, block))
        vec_ref[0:1, :] += col_sum(back * unit)
        vec_ref[1:2, :] += col_sum(back)
        vec_ref[2:3, :] += col_sum(grads.astype(FL))
        upb_out[...] += col_sum(grad_pre.astype(FL))

    loop(2, one)


def ffn_late_kernel(
    first, place_ref, activ_ref, gpre_ref, normed_ref, down_ref, g_ref, ctx_in, share_ref, up_out, down_out, ctx_out
):
    ctx_out[...] = ctx_in[...]
    size = activ_ref.shape[0]
    activ = activ_ref[...]
    share_ref[...] = mm(activ, down_ref[...]).astype(BF)
    down_out[...] = t_mm(activ, g_ref[first : first + size, :])
    up_out[...] = t_mm(normed_ref[...], gpre_ref[...])


def ffn_early_kernel(
    first,
    place_ref, activ_ref, gpre_ref, normed_ref, down_ref, g_ref, late_ref, up_in, down_in,
    share_ref, f_keep, f_send,
):
    size = activ_ref.shape[0]
    activ = activ_ref[...]
    up = up_in[...] + t_mm(normed_ref[...], gpre_ref[...])
    by_core(place_ref[1] & 1, 0, f_keep, f_send, up.astype(BF), slice(None))
    down = down_in[...] + t_mm(activ, g_ref[first : first + size, :])
    by_core(place_ref[1] & 1, 1, f_keep, f_send, down.astype(BF), slice(None))
    share_ref[:size, :] = mm(activ, down_ref[...]).astype(BF)
    share_ref[size:, :] = late_ref[...]


def back_rows(
    first, block, heads, mem_len, place_ref, hidden_ref, mine_ref, other_ref, g_ref, fgain_ref, wout_ref, ctx_ref,
    probs_ref, qb_ref, qv_ref, kt_ref, v_ref, wpos_ref, sin_ref, cos_ref,
    gh_ref, dk_ref, dv_ref, dpos_ref, dout_ref, dq_ref, bias_ref, grad_u, grad_v,
):
    core = place_ref[0]
    wide = heads * HEAD
    half = sin_ref.shape[1]
    scale = HEAD ** (-0.5)
    for part in range(2):
        at = slice(part * block, (part + 1) * block)
        spots = slice(first + part * block, first + (part + 1) * block)
        seen = mem_len + first + (part + 1) * block
        unit, inv = norm_parts(hidden_ref[at, :])
        summed = jnp.where(core == part, mine_ref[...].astype(FL), other_ref[...].astype(FL))
        grad_hidden = g_ref[spots, :].astype(FL) + norm_back(summed * fgain_ref[...], unit, inv)
        gh_ref[at, :] = grad_hidden
        gh = grad_hidden.astype(BF)
        context = ctx_ref[at, :]
        grad_context = mm_t(gh, wout_ref[...]).astype(BF).astype(FL)
        dout_ref[...] += t_mm(context, gh)
        along_context = grad_context * context.astype(FL)

        def one_head(h):
            lanes = head_lanes(wide, h)
            delta = jnp.sum(jnp.where(lanes, along_context, 0.0), axis=-1, keepdims=True)
            own = jnp.where(lanes, grad_context, 0.0).astype(BF)
            probs = probs_ref[h, at, :seen]
            grad_score = (probs.astype(FL) * (mm_t(own, v_ref[:seen, :]) - delta)).astype(BF)
            dv_ref[:, :seen] += t_mm(own, probs)
            dk_ref[:, :seen] += t_mm(qb_ref[h, at, :wide], grad_score)
            spread = mm(grad_score, kt_ref[:seen, :])
            grad_u[...] = jnp.where(lanes, spread[:, :wide], grad_u[...])
            sin = sin_ref[spots, :]
            cos = cos_ref[spots, :]
            on_cos, on_sin = spread[:, wide : wide + half], spread[:, wide + half :]
            turned = jnp.concatenate(
                [(on_cos * sin - on_sin * cos).astype(BF), (on_cos * cos + on_sin * sin).astype(BF)], axis=1
            )
            grad_v[...] = jnp.where(lanes, mm(turned, wpos_ref[...]), grad_v[...])
            query_v = jnp.where(lanes, qv_ref[at, :].astype(FL), 0.0).astype(BF)
            dpos_ref[...] += t_mm(query_v, turned)

        loop(heads, one_head)
        bias_ref[0:1, :] += col_sum(grad_u[...]) * scale
        bias_ref[1:2, :] += col_sum(grad_v[...]) * scale
        dq_ref[at, :] = ((grad_u[...] + grad_v[...]) * scale).astype(BF)


def back_share(cols, dq_rows, unit, dk_ref, dv_ref, weights):
    pair = [dk_ref[:, cols].T.astype(BF), dv_ref[:, cols].T.astype(BF)]
    back = mm_t(jnp.concatenate(dq_rows + pair, axis=1), weights)
    return back, col_sum(back * unit), col_sum(back)


def back_late_kernel(
    first, block, heads, mem_len,
    place_ref, hidden_ref, mine_ref, other_ref, g_ref, fgain_ref, wout_ref, ctx_ref, probs_ref, qb_ref, qv_ref, kt_ref,
    v_ref, wpos_ref, sin_ref, cos_ref, x_ref, w_ref,
    gh_ref, dk_ref, dv_ref, dpos_ref, dout_ref, dq_ref, bias_ref, share_ref, vec_ref, grad_u, grad_v,
):
    for ref in (dk_ref, dv_ref, dpos_ref, dout_ref, bias_ref):
        ref[...] = jnp.zeros(ref.shape, FL)
    back_rows(
        first, block, heads, mem_len, place_ref, hidden_ref, mine_ref, other_ref, g_ref, fgain_ref, wout_ref, ctx_ref,
        probs_ref, qb_ref, qv_ref, kt_ref, v_ref, wpos_ref, sin_ref, cos_ref,
        gh_ref, dk_ref, dv_ref, dpos_ref, dout_ref, dq_ref, bias_ref, grad_u, grad_v,
    )
    vec_ref[...] = jnp.zeros(vec_ref.shape, FL)
    for part in range(2):
        at = slice(part * block, (part + 1) * block)
        spots = slice(first + part * block, first + (part + 1) * block)
        cols = slice(mem_len + first + part * block, mem_len + first + (part + 1) * block)
        unit, _ = norm_parts(x_ref[spots, :].astype(FL))
        back, gain_sum, shift_sum = back_share(cols, [dq_ref[at, :]], unit, dk_ref, dv_ref, w_ref[...])
        share_ref[at, :] = back.astype(BF)
        vec_ref[0:1, :] += gain_sum
        vec_ref[1:2, :] += shift_sum


def back_early_kernel(
    first, block, heads, mem_len, n_tensor, size,
    place_ref, hidden_ref, mine_ref, other_ref, g_ref, fgain_ref, wout_ref, ctx_ref, probs_ref, qb_ref, qv_ref, kt_ref,
    v_ref, wpos_ref, sin_ref, cos_ref, x_ref, w_ref, mem_ref, normed_ref, dk_in, dv_in, dpos_in, dout_in, dq_in,
    bias_in, late_ref, vec_in, vec_l, vec_e, upb_l, upb_e, ffn_ref,
    gh_ref, keep_ref, send_ref, a_keep, a_send,
    dk_ref, dv_ref, dpos_ref, dout_ref, dq_ref, vec_ref, bias_ref, grad_u, grad_v,
):
    wide = heads * HEAD
    core = place_ref[0]
    for part in range(2):
        at = slice(part * block, (part + 1) * block)
        by_core(core, part, keep_ref, send_ref, late_ref[at, :], slice(block, 2 * block))
        by_core(core, part, keep_ref, send_ref, ffn_ref[at, :], slice(2 * block, 3 * block))
        at = slice((part + 2) * block, (part + 3) * block)
        by_core(core, part, keep_ref, send_ref, ffn_ref[at, :], slice(3 * block, 4 * block))
    for ref, old in ((dk_ref, dk_in), (dv_ref, dv_in), (dpos_ref, dpos_in), (dout_ref, dout_in), (bias_ref, bias_in)):
        ref[...] = old[...]
    back_rows(
        first, block, heads, mem_len, place_ref, hidden_ref, mine_ref, other_ref, g_ref, fgain_ref, wout_ref, ctx_ref,
        probs_ref, qb_ref, qv_ref, kt_ref, v_ref, wpos_ref, sin_ref, cos_ref,
        gh_ref, dk_ref, dv_ref, dpos_ref, dout_ref, dq_ref, bias_ref, grad_u, grad_v,
    )
    normed = normed_ref[...]
    dq_all = jnp.concatenate([dq_ref[...], dq_in[...]], axis=0)
    grads = [
        t_mm(dq_all, normed[mem_len:]),
        mm(dk_ref[...].astype(BF), normed),
        mm(dv_ref[...].astype(BF), normed),
        dpos_ref[...],
        dout_ref[...],
    ]
    grads = jnp.concatenate(grads, axis=0)
    vec_ref[...] = vec_in[...]
    for part in range(2):
        at = slice(part * block, (part + 1) * block)
        spots = slice(first + part * block, first + (part + 1) * block)
        cols = slice(mem_len + first + part * block, mem_len + first + (part + 1) * block)
        unit, _ = norm_parts(x_ref[spots, :].astype(FL))
        back, gain_sum, shift_sum = back_share(cols, [dq_ref[at, :]], unit, dk_ref, dv_ref, w_ref[...])
        by_core(core, part, keep_ref, send_ref, back.astype(BF), slice(0, block))
        vec_ref[0:1, :] += gain_sum
        vec_ref[1:2, :] += shift_sum
    for at in range(0, mem_len, block):
        cols = slice(at, at + block)
        unit, _ = norm_parts(mem_ref[cols, :].astype(FL))
        _, gain_sum, shift_sum = back_share(cols, [], unit, dk_ref, dv_ref, w_ref[:, wide:])
        vec_ref[0:1, :] += gain_sum
        vec_ref[1:2, :] += shift_sum
    width = vec_ref.shape[1]
    wider = jnp.zeros((1, width - wide), FL)
    rows = [vec_ref[...], vec_l[0:2, :] + vec_e[0:2, :], (vec_l[2:3, :] + vec_e[2:3, :]) * (1.0 / n_tensor)]
    rows += [jnp.concatenate([bias_ref[i : i + 1, :], wider], axis=1) for i in range(2)]
    for i in range(upb_l.shape[1] // width):
        cols = slice(i * width, (i + 1) * width)
        rows.append(upb_l[:, cols] + upb_e[:, cols])
    rows.append(jnp.zeros((small - 7 - upb_l.shape[1] // width, width), FL))
    rows = jnp.concatenate(rows, axis=0).astype(BF)
    step = size + small
    for d in range(2 * a_keep.shape[0] // step):
        here = max(0, min(size, 5 * wide - d * size))
        piece = [grads[d * size : d * size + here].astype(BF)] if here else []
        piece += [jnp.zeros((size - here, width), BF)] if here < size else []
        piece = jnp.concatenate([*piece, rows], axis=0)
        per_half = a_keep.shape[0] // step
        at = slice(d % per_half * step, (d % per_half + 1) * step)
        by_core(place_ref[1] & 1, d // per_half, a_keep, a_send, piece, at)


def weights_kernel(wide, bit, place_ref, mine_ref, got_ref, *refs):
    outs, rows_ref = refs[:5], refs[5]
    join(place_ref, bit, mine_ref, got_ref, rows_ref)
    for i in range(4):
        outs[i][...] = rows_ref[i * wide : (i + 1) * wide, :].T
    outs[4][...] = rows_ref[4 * wide : 5 * wide, :]


def small_kernel(heads, n_tensor, *refs):
    mine, outs = refs[0], refs[n_tensor:]
    total = mine[...]
    for other in refs[1:n_tensor]:
        total = total + other[...]
    for i in range(5):
        outs[i][...] = total[i : i + 1, :]
    for k in range(2):
        for h in range(heads):
            outs[5 + k][h : h + 1, :] = mine[5 + k : 6 + k, h * HEAD : (h + 1) * HEAD]
    width = mine.shape[1]
    for i in range(outs[7].shape[1] // width):
        outs[7][:, i * width : (i + 1) * width] = mine[7 + i : 8 + i, :]


def ffn_grads_kernel(place_ref, mine_ref, got_ref, up_ref, down_ref):
    own = (place_ref[1] & 1) == 0
    mine, got = mine_ref[...].astype(FL), got_ref[...].astype(FL)
    up_ref[...] = jnp.where(own, mine, got)
    down_ref[...] = jnp.where(own, got, mine)


def finish_kernel(
    block, place_ref, x_ref, gain_ref, gh_e, gh_l, hidden_e, hidden_l, mine_ref, other_ref, bias_ref, out_ref, grad_ref
):
    core = place_ref[0]

    def some_rows(gh_ref, hidden_ref, first):
        def body(i):
            at = rows_of(i, block)
            spots = rows_of(i + 2 * first, block)

            def summed(group):
                rows = slice(group * block, (group + 1) * block)
                return jnp.where(core == i, mine_ref[rows, :].astype(FL), other_ref[rows, :].astype(FL))

            unit, inv = norm_parts(x_ref[spots, :].astype(FL))
            grad_ref[spots, :] = (gh_ref[at, :] + norm_back(summed(first) * gain_ref[...], unit, inv)).astype(BF)
            out_ref[spots, :] = (hidden_ref[at, :] + summed(first + 2) + bias_ref[...]).astype(BF)

        return body

    loop(2, some_rows(gh_e, hidden_e, 0))
    loop(2, some_rows(gh_l, hidden_l, 1))


def halve(place_ref, bit, total, keep_ref, send_ref):
    size = total.shape[0] // 2
    high = (place_ref[1] >> bit) & 1
    by_core(high, 0, keep_ref, send_ref, total[:size], slice(None))
    by_core(high, 1, keep_ref, send_ref, total[size:], slice(None))


def join(place_ref, bit, mine_ref, got_ref, out_ref):
    size = mine_ref.shape[0]
    high = ((place_ref[1] >> bit) & 1) == 1
    mine, got = mine_ref[...].astype(FL), got_ref[...].astype(FL)
    out_ref[:size, :] = jnp.where(high, got, mine).astype(out_ref.dtype)
    out_ref[size:, :] = jnp.where(high, mine, got).astype(out_ref.dtype)


SMEM = pl.BlockSpec(memory_space=pltpu.SMEM)
SPECS = {s: pl.BlockSpec(memory_space=s) for s in (pltpu.VMEM, pltpu.HBM)}


def call(kernel, outs, args, name, flops, scratch=(), space=pltpu.VMEM, after=(), out_space=None):
    count, extra = len(args), len(after)

    def body(*refs):
        kernel(*refs[:count], *refs[count + extra :])

    specs = [SMEM if a.dtype == jnp.int32 else SPECS[space] for a in args]
    specs += [pl.BlockSpec(memory_space=pl.ANY)] * extra
    if space is pltpu.HBM:
        args = [a if a.dtype == jnp.int32 else pltpu.with_memory_space_constraint(a, space) for a in args]
    return pl.pallas_call(
        body,
        out_shape=[out_space(s, d) if out_space else jax.ShapeDtypeStruct(s, d) for s, d in outs],
        in_specs=specs,
        out_specs=[SPECS[pltpu.VMEM]] * len(outs),
        scratch_shapes=scratch,
        compiler_params=pltpu.CompilerParams(vmem_limit_bytes=VMEM_LIMIT),
        cost_estimate=pl.CostEstimate(flops=1, bytes_accessed=1, transcendentals=0),
        name=name,
    )(*args, *after)


def swap(rows, axis, size, bit):
    return lax.ppermute(rows, axis, [(i, i ^ bit) for i in range(size)])


def work_kernel(jobs, place_ref, *refs):
    ins, outs = refs[: 2 * len(jobs)], list(refs[2 * len(jobs) :])
    for i, (kind, bit) in enumerate(jobs):
        mine, got = ins[2 * i : 2 * i + 2]
        if kind == "halve":
            halve(place_ref, bit, added(mine[...], got[...]), outs.pop(0), outs.pop(0))
        elif kind == "join":
            join(place_ref, bit, mine, got, outs.pop(0))
        elif kind == "sum":
            outs.pop(0)[...] = added(mine[...], got[...])
        else:
            total = mine[...].astype(FL) + got[...].astype(FL)
            size = outs[0].shape[0]
            outs.pop(0)[...] = total[:size].astype(BF)
            outs.pop(0)[...] = total[size:]


def work(place, jobs, name, after=()):
    outs = []
    for kind, _, mine, _ in jobs:
        size, width = mine.shape
        outs += {
            "halve": [((size // 2, width), BF)] * 2,
            "join": [((2 * size, width), BF)],
            "sum": [((size, width), BF)],
            "split": [((size - small, width), BF), ((small, width), FL)],
        }[kind]
    args = [a for job in jobs for a in job[2:]]
    return list(
        call(functools.partial(work_kernel, [job[:2] for job in jobs]), outs, (place, *args), name, 1e6, after=after)
    )


class Chain:
    def __init__(self, keep, send, n_dp):
        self.rows, self.send, self.n_dp, self.done = keep, send, n_dp, 0
        self.steps = (n_dp - 1).bit_length()
        self.start()

    def bit(self):
        return min(self.done, 2 * self.steps - 1 - self.done)

    def start(self):
        self.got = swap(self.send, "dp", self.n_dp, 1 << self.bit())

    def last(self):
        return self.done == 2 * self.steps - 1

    def job(self, end="sum"):
        if self.done < self.steps - 1:
            kind, bit = "halve", self.done + 1
        else:
            kind, bit = (end, 0) if self.done == self.steps - 1 else ("join", self.bit())
        return kind, bit, self.rows, self.got

    def take(self, results):
        kind = self.job()[0]
        self.rows = self.send = results.pop(0)
        if kind == "halve":
            self.send = results.pop(0)
        self.done += 1
        self.start()


def cores(rows, n_tensor):
    return swap(rows, "tensor", n_tensor, 1)


def chips(rows, n_tensor):
    return rows, swap(rows, "tensor", n_tensor, 2)


def copy_kernel(in_ref, out_ref):
    out_ref[...] = in_ref[...]


def per_device(n_dp, n_tensor, *args):
    (inputs, memory, counts, attn_gain, attn_shift, w_query, w_key, w_value, w_pos, bias_u, bias_v, w_out,
     ffn_gain, ffn_shift, w_up, up_bias, w_down, down_bias, out_grad) = args
    _, seq_len, width = inputs.shape
    mem_len = memory.shape[1]
    total = mem_len + seq_len
    wide = w_query.shape[1]
    heads = wide // HEAD
    ff = w_up.shape[1]
    chunk = seq_len // 2
    block = chunk // 2
    late = chunk
    place = jnp.stack([lax.axis_index("tensor") & 1, lax.axis_index("dp")]).astype(jnp.int32)
    x, mem, g = inputs[0], memory[0], out_grad[0]
    row = lambda v: v.reshape(1, -1)

    freq = 1.0 / 10000.0 ** (np.arange(0, width, 2, dtype=np.float64) / width)
    key_phase = np.arange(total)[:, None] * freq[None, :]
    table = jnp.asarray(np.concatenate([np.cos(key_phase), np.sin(key_phase)], axis=1).astype(BF))
    row_phase = (np.arange(seq_len) + mem_len)[:, None] * freq[None, :]
    sin = jnp.asarray(np.sin(row_phase).astype(np.float32))
    cos = jnp.asarray(np.cos(row_phase).astype(np.float32))

    outs_of = [w_out] + [swap(w_out, "tensor", n_tensor, k) for k in range(1, n_tensor)]

    def attend_outs(seen):
        return [((heads, chunk, wide + width), BF), ((chunk, wide), BF), ((heads, chunk, seen), BF), ((chunk, wide), BF)]

    ctx_scr = pltpu.VMEM((block, wide), FL)
    vectors = [row(v) for v in (attn_shift, attn_gain, ffn_gain, ffn_shift, up_bias, down_bias)]
    copied = [
        *[(a.shape, BF) for a in (x, mem, g)], ((width, 3 * wide), BF), *[(a.shape, BF) for a in (w_pos, w_up, w_down, w_out)],
        *[(a.shape, FL) for a in (*vectors[1:], sin, cos)], ((2, wide), FL),
    ]
    found = call(
        functools.partial(front_kernel, late, block, heads),
        [*copied, ((total, width), BF), ((total, wide + width), BF), ((total, wide), BF), *attend_outs(total)],
        (place, counts, x, mem, g, w_query, w_key, w_value, w_pos, w_up, w_down, w_out, *vectors, bias_u, bias_v, table, sin,
         cos), "front", 6e9,
        [pltpu.VMEM((1, width), FL)] + [pltpu.VMEM(bias_u.shape, FL)] * 2 + [ctx_scr, pltpu.SemaphoreType.DMA((21,))],
        pltpu.HBM,
    )
    x, mem, g, weights, w_pos, w_up, w_down, w_out = found[:8]
    attn_gain, ffn_gain, ffn_shift, up_bias, down_bias, sin, cos, biases, normed, keys, values, *saved_l = found[8:]
    ctx_l = [saved_l[-1], cores(saved_l[-1], n_tensor), swap(saved_l[-1], "tensor", n_tensor, 2)]
    saved_e = call(
        functools.partial(second_kernel, 0, block, heads, mem_len),
        attend_outs(mem_len + chunk),
        (counts, normed, keys, values, weights, w_pos, biases, sin, cos), "second", 4e9, [ctx_scr],
    )
    ctx_e = [saved_e[-1], cores(saved_e[-1], n_tensor), swap(saved_e[-1], "tensor", n_tensor, 2)]
    (relay,) = call(copy_kernel, [(ctx_l[2].shape, BF)], (ctx_l[2],), "relay_late", 1e6, after=saved_e[-1:])
    ctx_l.append(cores(relay, n_tensor))

    def ffn_rows(first, ctx, name, after):
        return call(
            functools.partial(ffn_rows_kernel, first, block),
            [((chunk, width), FL), ((chunk, width), BF), ((chunk, ff), BF), ((chunk, ff), BF), ((block, width), BF),
             ((block, width), BF), ((3, width), FL), ((1, ff), FL)],
            (place, x, *ctx, *outs_of, ffn_gain, ffn_shift, w_up, up_bias, w_down, g), name, 2e9, after=after,
        )

    hidden_l, normed_l, activ, gpre, keep_l, send, vec_l, upb_l = ffn_rows(late, ctx_l, "ffn_rows_late", saved_e[-1:])
    gnt_l = cores(send, n_tensor)
    share, up_l, down_l, relay = call(
        functools.partial(ffn_late_kernel, late),
        [((chunk, width), BF), ((width, ff), FL), ((ff, width), FL), ((chunk, wide), BF)],
        (place, activ, gpre, normed_l, w_down, g, ctx_e[2]), "ffn_late", 1e9,
    )
    ctx_e.append(cores(relay, n_tensor))
    (gnt_l,) = work(place, [("sum", 0, keep_l, gnt_l)], "add_late", (share,))
    gnt_l = chips(gnt_l, n_tensor)
    hidden_e, normed_e, activ, gpre, keep_e, send, vec_e, upb_e = ffn_rows(0, ctx_e, "ffn_rows_early", gnt_l[:1])
    gnt_e = cores(send, n_tensor)
    share, f_keep, f_send = call(
        functools.partial(ffn_early_kernel, 0),
        [(x.shape, BF)] + [((chunk, width), BF)] * 2,
        (place, activ, gpre, normed_e, w_down, g, share, up_l, down_l), "ffn_early", 1e9,
    )
    ffn = Chain(f_keep, f_send, n_dp)
    gnt_l, gnt_e = work(place, [("sum", 0, *gnt_l), ("sum", 0, keep_e, gnt_e)], "add_early", (f_keep,))
    gnt_l = (gnt_l, cores(gnt_l, n_tensor))
    gnt_e = chips(gnt_e, n_tensor)

    sums = [((wide, total), FL), ((wide, total), FL), ((wide, width), FL), ((wide, width), FL), ((chunk, wide), BF)]
    turn_scr = [ctx_scr, ctx_scr]

    def back_args(hidden, gnt, saved):
        qb, qv, probs, ctx = saved
        return (place, hidden, *gnt, g, ffn_gain, w_out, ctx, probs, qb, qv, keys, values, w_pos, sin, cos, x, weights)

    gh_l, dk, dv, dpos, dout, dq, bias, part, vec = call(
        functools.partial(back_late_kernel, late, block, heads, mem_len),
        [((chunk, width), FL), *sums, ((2, wide), FL), ((chunk, width), BF), ((2, width), FL)],
        back_args(hidden_l, gnt_l, saved_l), "back_late", 8e9, turn_scr,
    )
    gnt_e, *results = work(place, [("sum", 0, *gnt_e), ffn.job()], "add_middle", (vec,))
    ffn.take(results)
    gnt_e = (gnt_e, cores(gnt_e, n_tensor))
    size = max(16, -(-5 * wide // n_dp // 16) * 16)
    gh_e, keep, send, a_keep, a_send = call(
        functools.partial(back_early_kernel, 0, block, heads, mem_len, n_tensor, size),
        [((chunk, width), FL), *[((seq_len, width), BF)] * 2, *[((n_dp // 2 * (size + small), width), BF)] * 2],
        (*back_args(hidden_e, gnt_e, saved_e), mem, normed, dk, dv, dpos, dout, dq, bias, part, vec, vec_l, vec_e, upb_l,
         upb_e, share),
        "back_early", 6e9, [pltpu.VMEM(s, d) for s, d in (*sums, ((2, width), FL), ((2, wide), FL))] + turn_scr,
    )
    attn = Chain(a_keep, a_send, n_dp)
    send = cores(send, n_tensor)
    rows, *results = work(place, [("sum", 0, keep, send), ffn.job()], "step_ffn")
    ffn.take(results)
    rows = chips(rows, n_tensor)
    count = 0
    while not attn.last():
        chains = [attn] + [c for c in (ffn,) if not c.last()]
        jobs = [attn.job("split")] + [c.job() for c in chains[1:]]
        if attn.done == attn.steps:
            jobs.append(("sum", 0, *rows))
        results = work(place, jobs, f"step_{count}")
        if attn.done == attn.steps:
            rows = results.pop()
            rows = (rows, cores(rows, n_tensor))
        if attn.done == attn.steps - 1:
            totals = results.pop(1)
            totals = [totals] + [swap(totals, "tensor", n_tensor, k) for k in range(1, n_tensor)]
        for c in chains:
            c.take(results)
        count += 1
    vecs = call(
        functools.partial(small_kernel, heads, n_tensor),
        [((1, width), FL)] * 5 + [((heads, HEAD), FL)] * 2 + [((1, ff), FL)], totals, "small", 1e6,
    )
    g_up, g_down = call(
        ffn_grads_kernel, [((width, ff), FL), ((ff, width), FL)], (place, ffn.rows, ffn.got), "ffn_grads", 1e6,
        after=vecs[:1], out_space=pltpu.HBM,
    )
    g_up_there = pltpu.with_memory_space_constraint(g_up, pltpu.HBM)
    output, input_grad = call(
        functools.partial(finish_kernel, block), [(x.shape, BF)] * 2,
        (place, x, attn_gain, gh_e, gh_l, hidden_e, hidden_l, *rows, down_bias), "finish", 1e8, after=(g_up_there,),
        out_space=pltpu.HBM,
    )
    output_there = pltpu.with_memory_space_constraint(output, pltpu.HBM)
    g_query, g_key, g_value, g_pos, g_out = call(
        functools.partial(weights_kernel, wide, attn.bit()),
        [((width, wide), FL)] * 4 + [((wide, width), FL)], (place, attn.rows, attn.got), "weights", 1e6,
        [pltpu.VMEM((n_dp * size, width), FL)], after=(output_there,), out_space=pltpu.HBM,
    )
    return (
        output[None],
        input_grad[None],
        vecs[0].reshape(-1),
        vecs[1].reshape(-1),
        g_query,
        g_key,
        g_value,
        g_pos,
        vecs[5],
        vecs[6],
        g_out,
        vecs[2].reshape(-1),
        vecs[3].reshape(-1),
        g_up,
        vecs[7].reshape(-1),
        g_down,
        vecs[4].reshape(-1),
    )


def solution(mesh):
    split, whole = P(None, "tensor"), P()
    return jax.shard_map(
        functools.partial(per_device, mesh.shape["dp"], mesh.shape["tensor"]),
        mesh=mesh,
        in_specs=(
            P("dp", None, None), P("dp", None, None), P("dp"), whole, whole, split, split, split, split,
            P("tensor", None), P("tensor", None), P("tensor", None), whole, whole, split, P("tensor"),
            P("tensor", None), whole, P("dp", None, None),
        ),
        out_specs=(
            P("dp", None, None), P("dp", None, None), whole, whole, split, split, split, split,
            P("tensor", None), P("tensor", None), P("tensor", None), whole, whole, split, P("tensor"),
            P("tensor", None), whole,
        ),
        check_vma=False,
    )
```

profile of v0, /device:TPU:0, one launch (start us, length us, event | category | flops | bytes accessed | tf_op | source)
XLA Modules:
  0.0 135.3 jit_solution(14758934004225627458)
XLA Ops:
  1.4 11.4 %front.1 = (bf16[1024,512]{1,0:T(8,128)(2,1)S(1)}, bf16[512,512]{1,0:T(8,128)(2,1)S(1)}, bf16[1024,512]{1,0:T(8,128)(2,1)S(1)}, bf16[512,384]{1,0:T(8,128)(2,1)S...) custom-call(s32[2]{0:T(128)S(1)} %pad_add_fusion.refs_0_, ...), custom_call_target="tpu_custom_call" | custom-call | flops 1 | bytes 1 | tf_op jit(solution)/shard_map/front/pallas_call | solution.py:499
  12.8 3.0 %collective-permute-start.3 = (bf16[512,128]{1,0:T(8,128)(2,1)S(1)}, bf16[512,128]{1,0:T(8,128)(2,1)S(1)}, u32[]{:S(2)}, u32[]{:S(2)}) collective-permute-start(bf16[512,128]{1,0:T(8,128)(2,1)S(1)} %get-tuple-element.128.refs_2_.refs_7_), channel_id=1, source_target_pairs={{0,2},{1,3},{2,0},{3,1},{4,6},{5,7},{6,4},{7,5},{8,10},{9,11},{10,... | collective-permute-start | bytes 393224 | tf_op jit(solution)/shard_map/ppermute | solution.py:512
  15.9 0.5 collective-permute-start.5
  16.4 1.3 collective-permute-start.7
  17.7 5.3 %second.1 = (bf16[2,512,640]{2,1,0:T(8,128)(2,1)S(1)}, bf16[512,128]{1,0:T(8,128)(2,1)S(1)}, bf16[2,512,1024]{2,1,0:T(8,128)(2,1)S(1)}, bf16[512,128]{1,0:T(8,128)(2,1)S(1)}) custom-call(s32[1]{0:T(128)S(6)} %copy.39.refs_1_.refs_0_, bf16[1536,512]{1,0:T(8,128)(2,1)S(1)} %get-tuple-element.119.refs_1_.refs_19_, ...), custom_call_target="tpu_custom_call" | custom-call | flops 1 | bytes 1 | tf_op jit(solution)/shard_map/second/pallas_call | solution.py:499
  23.0 0.8 collective-permute-start.4
  24.0 0.4 collective-permute-done.7.refs_9_
  24.4 0.5 collective-permute-done.4.refs_5_
  24.9 3.6 %ffn_rows_late.1 = (f32[512,512]{1,0:T(8,128)S(1)}, bf16[512,512]{1,0:T(8,128)(2,1)S(1)}, bf16[512,512]{1,0:T(8,128)(2,1)S(1)}, bf16[512,512]{1,0:T(8,128)(2,1)S...) custom-call(s32[2]{0:T(128)S(1)} %pad_add_fusion.refs_0_, ...), custom_call_target="tpu_custom_call" | custom-call | flops 1 | bytes 1 | tf_op jit(solution)/shard_map/ffn_rows_late/pallas_call | solution.py:499
  28.5 0.4 collective-permute-start.9
  29.0 0.3 collective-permute-done.1.refs_6_.refs_4_
  29.4 1.5 %ffn_late.1 = (bf16[512,512]{1,0:T(8,128)(2,1)S(1)}, f32[512,512]{1,0:T(8,128)S(1)}, f32[512,512]{1,0:T(8,128)S(1)}, bf16[512,128]{1,0:T(8,128)(2,1)S(1)}) custom-call(s32[2]{0:T(128)S(1)} %pad_add_fusion.refs_0_, bf16[512,512]{1,0:T(8,128)(2,1)S(1)} %get-tuple-element.135.refs_1_, bf16[512,512]{1,0:T(8,128)(2,1)S(1)} %get-tuple-element.136.refs_2_, ...), custom_call_target="tpu_custom_call" | custom-call | flops 1 | bytes 1 | tf_op jit(solution)/shard_map/ffn_late/pallas_call | solution.py:499
  31.0 0.6 add_late.1.refs_16_.refs_1_
  31.6 0.7 collective-permute-done.8.refs_5_
  32.3 3.6 %ffn_rows_early.1 = (f32[512,512]{1,0:T(8,128)S(1)}, bf16[512,512]{1,0:T(8,128)(2,1)S(1)}, bf16[512,512]{1,0:T(8,128)(2,1)S(1)}, bf16[512,512]{1,0:T(8,128)(2,1)...) custom-call(s32[2]{0:T(128)S(1)} %pad_add_fusion.refs_0_, ...), custom_call_target="tpu_custom_call" | custom-call | flops 1 | bytes 1 | tf_op jit(solution)/shard_map/ffn_rows_early/pallas_call | solution.py:499
  35.9 0.2 collective-permute-start.11
  36.2 1.2 collective-permute-start.10
  37.4 2.2 %ffn_early.1 = (bf16[1024,512]{1,0:T(8,128)(2,1)S(1)}, bf16[512,512]{1,0:T(8,128)(2,1)S(1)}, bf16[512,512]{1,0:T(8,128)(2,1)S(1)}) custom-call(s32[2]{0:T(128)S(1)} %pad_add_fusion.refs_0_, bf16[512,512]{1,0:T(8,128)(2,1)S(1)} %get-tuple-element.145.refs_1_, bf16[512,512]{1,0:T(8,128)(2,1)S(1)} %get-tuple-element.146.refs_2_, ...), custom_call_target="tpu_custom_call" | custom-call | flops 1 | bytes 1 | tf_op jit(solution)/shard_map/ffn_early/pallas_call | solution.py:499
  39.6 1.6 %collective-permute-start.13 = (bf16[512,512]{1,0:T(8,128)(2,1)S(1)}, bf16[512,512]{1,0:T(8,128)(2,1)S(1)}, u32[]{:S(2)}, u32[]{:S(2)}) collective-permute-start(bf16[512,512]{1,0:T(8,128)(2,1)S(1)} %get-tuple-element.152), channel_id=1, source_target_pairs={{0,4},{4,0},{8,12},{12,8},{16,20},{20,16},{24,28},{28,24},{1,5},{5... | collective-permute-start | bytes 1572872 | tf_op jit(solution)/shard_map/ppermute | solution.py:512
  41.1 3.6 %collective-permute-done.10.refs_2_ = bf16[256,512]{1,0:T(8,128)(2,1)S(1)} collective-permute-done((bf16[256,512]{1,0:T(8,128)(2,1)S(1)}, bf16[256,512]{1,0:T(8,128)(2,1)S(1)}, u32[]{:S(2)}, u32[]{:S(2)}) %collective-permute-start.10) | collective-permute-done | bytes 262176 | tf_op jit(solution)/shard_map/ppermute | solution.py:512
  44.7 0.7 add_early.1
  45.5 1.1 collective-permute-start.12
  46.5 0.5 collective-permute-done.14.refs_3_
  47.0 7.8 %back_late.1 = (f32[512,512]{1,0:T(8,128)S(1)}, f32[128,1536]{1,0:T(8,128)S(1)}, f32[128,1536]{1,0:T(8,128)S(1)}, f32[128,512]{1,0:T(8,128)S(1)}, f32[128,512]{1...) custom-call(s32[2]{0:T(128)S(1)} %pad_add_fusion.refs_0_, ...), custom_call_target="tpu_custom_call" | custom-call | flops 1 | bytes 1 | tf_op jit(solution)/shard_map/back_late/pallas_call | solution.py:499
  54.9 0.9 add_middle.1
  55.7 0.2 collective-permute-start.15
  55.9 1.4 %collective-permute-done.15.refs_3_ = bf16[256,512]{1,0:T(8,128)(2,1)S(1)} collective-permute-done((bf16[256,512]{1,0:T(8,128)(2,1)S(1)}, bf16[256,512]{1,0:T(8,128)(2,1)S(1)}, u32[]{:S(2)}, u32[]{:S(2)}) %collective-permute-start.15) | collective-permute-done | bytes 262176 | tf_op jit(solution)/shard_map/ppermute | solution.py:512
  57.3 8.3 %back_early.1 = (f32[512,512]{1,0:T(8,128)S(1)}, bf16[1024,512]{1,0:T(8,128)(2,1)S(1)}, bf16[1024,512]{1,0:T(8,128)(2,1)S(1)}, bf16[384,512]{1,0:T(8,128)(2,1)S(1)}, bf16[384,512]{1,0:T(8,128)(2,1)S(1)}) custom-call(s32[2]{0:T(128)S(1)} %pad_add_fusion.refs_0_, f32[512,512]{1,0:T(8,128)S(1)} %get-tuple-element.142.refs_1_.refs_5_, ...), custom_call_target="tpu_custom_call" | custom-call | flops 1 | bytes 1 | tf_op jit(solution)/shard_map/back_early/pallas_call | solution.py:499
  65.7 0.2 collective-permute-start.17
  65.9 1.6 %collective-permute-start.18 = (bf16[256,512]{1,0:T(8,128)(2,1)S(1)}, bf16[256,512]{1,0:T(8,128)(2,1)S(1)}, u32[]{:S(2)}, u32[]{:S(2)}) collective-permute-start(bf16[256,512]{1,0:T(8,128)(2,1)S(1)} %get-tuple-element.184), channel_id=1, source_target_pairs={{0,8},{4,12},{8,0},{12,4},{16,24},{20,28},{24,16},{28,20},{1,9},{5... | collective-permute-start | bytes 786440 | tf_op jit(solution)/shard_map/ppermute | solution.py:512
  67.4 7.0 %collective-permute-done.18.refs_4_ = bf16[256,512]{1,0:T(8,128)(2,1)S(1)} collective-permute-done((bf16[256,512]{1,0:T(8,128)(2,1)S(1)}, bf16[256,512]{1,0:T(8,128)(2,1)S(1)}, u32[]{:S(2)}, u32[]{:S(2)}) %collective-permute-start.18) | collective-permute-done | bytes 262176 | tf_op jit(solution)/shard_map/ppermute | solution.py:512
  74.4 0.9 step_ffn.1
  75.4 1.1 collective-permute-start.25
  76.4 1.5 %collective-permute-start.16 = (bf16[384,512]{1,0:T(8,128)(2,1)S(1)}, bf16[384,512]{1,0:T(8,128)(2,1)S(1)}, u32[]{:S(2)}, u32[]{:S(2)}) collective-permute-start(bf16[384,512]{1,0:T(8,128)(2,1)S(1)} %get-tuple-element.180), channel_id=1, source_target_pairs={{0,4},{4,0},{8,12},{12,8},{16,20},{20,16},{24,28},{28,24},{1,5},{5... | collective-permute-start | bytes 1179656 | tf_op jit(solution)/shard_map/ppermute | solution.py:512
  77.9 2.6 %collective-permute-start.19 = (bf16[128,512]{1,0:T(8,128)(2,1)S(1)}, bf16[128,512]{1,0:T(8,128)(2,1)S(1)}, u32[]{:S(2)}, u32[]{:S(2)}) collective-permute-start(bf16[128,512]{1,0:T(8,128)(2,1)S(1)} %get-tuple-element.186), channel_id=1, source_target_pairs={{0,16},{4,20},{8,24},{12,28},{16,0},{20,4},{24,8},{28,12},{1,17},{... | collective-permute-start | bytes 393224 | tf_op jit(solution)/shard_map/ppermute | solution.py:512
  80.5 6.2 %collective-permute-done.16.refs_2_ = bf16[384,512]{1,0:T(8,128)(2,1)S(1)} collective-permute-done((bf16[384,512]{1,0:T(8,128)(2,1)S(1)}, bf16[384,512]{1,0:T(8,128)(2,1)S(1)}, u32[]{:S(2)}, u32[]{:S(2)}) %collective-permute-start.16) | collective-permute-done | bytes 393248 | tf_op jit(solution)/shard_map/ppermute | solution.py:512
  86.7 0.8 step_0.1
  87.5 1.6 %collective-permute-start.20 = (bf16[192,512]{1,0:T(8,128)(2,1)S(1)}, bf16[192,512]{1,0:T(8,128)(2,1)S(1)}, u32[]{:S(2)}, u32[]{:S(2)}) collective-permute-start(bf16[192,512]{1,0:T(8,128)(2,1)S(1)} %get-tuple-element.188), channel_id=1, source_target_pairs={{0,8},{4,12},{8,0},{12,4},{16,24},{20,28},{24,16},{28,20},{1,9},{5... | collective-permute-start | bytes 589832 | tf_op jit(solution)/shard_map/ppermute | solution.py:512
  89.1 2.6 %collective-permute-start.21 = (bf16[128,512]{1,0:T(8,128)(2,1)S(1)}, bf16[128,512]{1,0:T(8,128)(2,1)S(1)}, u32[]{:S(2)}, u32[]{:S(2)}) collective-permute-start(bf16[128,512]{1,0:T(8,128)(2,1)S(1)} %get-tuple-element.189.refs_3_), channel_id=1, source_target_pairs={{0,16},{4,20},{8,24},{12,28},{16,0},{20,4},{24,8},{28,12},{1,17},{... | collective-permute-start | bytes 393224 | tf_op jit(solution)/shard_map/ppermute | solution.py:512
  91.7 4.1 %collective-permute-done.21.refs_4_ = bf16[128,512]{1,0:T(8,128)(2,1)S(1)} collective-permute-done((bf16[128,512]{1,0:T(8,128)(2,1)S(1)}, bf16[128,512]{1,0:T(8,128)(2,1)S(1)}, u32[]{:S(2)}, u32[]{:S(2)}) %collective-permute-start.21) | collective-permute-done | bytes 131104 | tf_op jit(solution)/shard_map/ppermute | solution.py:512
  95.8 0.9 step_1.1
  96.7 2.5 %collective-permute-start.23 = (bf16[256,512]{1,0:T(8,128)(2,1)S(1)}, bf16[256,512]{1,0:T(8,128)(2,1)S(1)}, u32[]{:S(2)}, u32[]{:S(2)}) collective-permute-start(bf16[256,512]{1,0:T(8,128)(2,1)S(1)} %get-tuple-element.192.refs_3_), channel_id=1, source_target_pairs={{0,8},{4,12},{8,0},{12,4},{16,24},{20,28},{24,16},{28,20},{1,9},{5... | collective-permute-start | bytes 786440 | tf_op jit(solution)/shard_map/ppermute | solution.py:512
  99.2 1.7 %collective-permute-start.22 = (bf16[96,512]{1,0:T(8,128)(2,1)S(1)}, bf16[96,512]{1,0:T(8,128)(2,1)S(1)}, u32[]{:S(2)}, u32[]{:S(2)}) collective-permute-start(bf16[96,512]{1,0:T(8,128)(2,1)S(1)} %get-tuple-element.191), channel_id=1, source_target_pairs={{0,16},{4,20},{8,24},{12,28},{16,0},{20,4},{24,8},{28,12},{1,17},{... | collective-permute-start | bytes 294920 | tf_op jit(solution)/shard_map/ppermute | solution.py:512
  100.9 3.9 %collective-permute-done.22.refs_2_ = bf16[96,512]{1,0:T(8,128)(2,1)S(1)} collective-permute-done((bf16[96,512]{1,0:T(8,128)(2,1)S(1)}, bf16[96,512]{1,0:T(8,128)(2,1)S(1)}, u32[]{:S(2)}, u32[]{:S(2)}) %collective-permute-start.22) | collective-permute-done | bytes 98336 | tf_op jit(solution)/shard_map/ppermute | solution.py:512
  104.8 0.1 collective-permute-done.23.refs_4_
  104.9 0.7 step_2.1
  105.6 2.7 %collective-permute-start.24 = (bf16[80,512]{1,0:T(8,128)(2,1)S(1)}, bf16[80,512]{1,0:T(8,128)(2,1)S(1)}, u32[]{:S(2)}, u32[]{:S(2)}) collective-permute-start(bf16[80,512]{1,0:T(8,128)(2,1)S(1)} %get-tuple-element.193.refs_1_), channel_id=1, source_target_pairs={{0,16},{4,20},{8,24},{12,28},{16,0},{20,4},{24,8},{28,12},{1,17},{... | collective-permute-start | bytes 245768 | tf_op jit(solution)/shard_map/ppermute | solution.py:512
  108.3 2.7 %collective-permute-done.24.refs_2_ = bf16[80,512]{1,0:T(8,128)(2,1)S(1)} collective-permute-done((bf16[80,512]{1,0:T(8,128)(2,1)S(1)}, bf16[80,512]{1,0:T(8,128)(2,1)S(1)}, u32[]{:S(2)}, u32[]{:S(2)}) %collective-permute-start.24) | collective-permute-done | bytes 81952 | tf_op jit(solution)/shard_map/ppermute | solution.py:512
  111.0 0.8 step_3.1
  111.9 1.5 %collective-permute-start.27 = (bf16[512,512]{1,0:T(8,128)(2,1)S(1)}, bf16[512,512]{1,0:T(8,128)(2,1)S(1)}, u32[]{:S(2)}, u32[]{:S(2)}) collective-permute-start(bf16[512,512]{1,0:T(8,128)(2,1)S(1)} %get-tuple-element.197.refs_1_), channel_id=1, source_target_pairs={{0,4},{4,0},{8,12},{12,8},{16,20},{20,16},{24,28},{28,24},{1,5},{5... | collective-permute-start | bytes 1572872 | tf_op jit(solution)/shard_map/ppermute | solution.py:512
  113.4 2.2 %collective-permute-start.31 = (bf16[160,512]{1,0:T(8,128)(2,1)S(1)}, bf16[160,512]{1,0:T(8,128)(2,1)S(1)}, u32[]{:S(2)}, u32[]{:S(2)}) collective-permute-start(bf16[160,512]{1,0:T(8,128)(2,1)S(1)} %get-tuple-element.204.refs_1_), channel_id=1, source_target_pairs={{0,8},{4,12},{8,0},{12,4},{16,24},{20,28},{24,16},{28,20},{1,9},{5... | collective-permute-start | bytes 491528 | tf_op jit(solution)/shard_map/ppermute | solution.py:512
  115.6 4.5 %collective-permute-done.31.refs_2_ = bf16[160,512]{1,0:T(8,128)(2,1)S(1)} collective-permute-done((bf16[160,512]{1,0:T(8,128)(2,1)S(1)}, bf16[160,512]{1,0:T(8,128)(2,1)S(1)}, u32[]{:S(2)}, u32[]{:S(2)}) %collective-permute-start.31) | collective-permute-done | bytes 163872 | tf_op jit(solution)/shard_map/ppermute | solution.py:512
  120.1 0.6 step_4.1.refs_1_
  120.7 1.2 collective-permute-start.32
  121.9 1.0 collective-permute-start.29
  122.9 0.2 collective-permute-done.28.refs_1_
  123.1 0.8 collective-permute-start.30
  123.9 1.9 %collective-permute-done.29.refs_2_ = f32[16,512]{1,0:T(8,128)S(1)} collective-permute-done((f32[16,512]{1,0:T(8,128)S(1)}, f32[16,512]{1,0:T(8,128)S(1)}, u32[]{:S(2)}, u32[]{:S(2)}) %collective-permute-start.29) | collective-permute-done | bytes 32800 | tf_op jit(solution)/shard_map/ppermute | solution.py:512
  125.8 0.6 collective-permute-done.30.refs_3_
  126.4 0.6 small.1
  127.1 0.7 copy-done.1
  127.8 2.1 %ffn_grads.1 = (f32[512,512]{1,0:T(8,128)}, f32[512,512]{1,0:T(8,128)}) custom-call(s32[2]{0:T(128)S(1)} %pad_add_fusion.refs_0_, bf16[512,512]{1,0:T(8,128)(2,1)S(1)} %get-tuple-element.197.refs_1_, bf16[512,512]{1,0:T(8,128)(2,1)S(1)} %collective-permute-done.27.refs_2_, f32[1,512]{1,0:T(1,128)S(1)} %copy-done.1), custom_call_target="tpu_custom_call" | custom-call | flops 1 | bytes 1 | tf_op jit(solution)/shard_map/ffn_grads/pallas_call | solution.py:499
  129.8 3.8 %finish.1 = (bf16[1024,512]{1,0:T(8,128)(2,1)}, bf16[1024,512]{1,0:T(8,128)(2,1)}) custom-call(s32[2]{0:T(128)S(1)} %pad_add_fusion.refs_0_, bf16[1024,512]{1,0:T(8,128)(2,1)S(1)} %get-tuple-element.117.refs_1_.refs_16_, f32[1,512]{1,0:T(1,128)S(1)} %get-tuple-element.118.refs_2_, f32[512,512]{1,0:T(8,128)S(1)} %get-tuple-element.177.refs_3_, ...), custom_call_target="tpu_custom_call" | custom-call | flops 1 | bytes 1 | tf_op jit(solution)/shard_map/finish/pallas_call | solution.py:499
  133.6 1.7 %weights.1 = (f32[512,128]{1,0:T(8,128)}, f32[512,128]{1,0:T(8,128)}, f32[512,128]{1,0:T(8,128)}, f32[512,128]{1,0:T(8,128)}, f32[128,512]{1,0:T(8,128)}) custom-call(s32[2]{0:T(128)S(1)} %pad_add_fusion.refs_0_, bf16[320,512]{1,0:T(8,128)(2,1)S(1)} %step_4.1.refs_1_, bf16[320,512]{1,0:T(8,128)(2,1)S(1)} %collective-permute-done.32.refs_2_, ...), custom_call_target="tpu_custom_call" | custom-call | flops 1 | bytes 1 | tf_op jit(solution)/shard_map/weights/pallas_call | solution.py:499
  (29 shorter events, 0.7 us)
Async XLA Ops:
  1.4 14.5 %copy-start = (bf16[128,512]{1,0:T(8,128)(2,1)S(1)}, bf16[128,512]{1,0:T(8,128)(2,1)}, u32[]{:S(2)}) copy-start(bf16[128,512]{1,0:T(8,128)(2,1)} %refs_6_.5) | copy-start | bytes 393220
  12.8 10.2 %collective-permute-start.3 = (bf16[512,128]{1,0:T(8,128)(2,1)S(1)}, bf16[512,128]{1,0:T(8,128)(2,1)S(1)}, u32[]{:S(2)}, u32[]{:S(2)}) collective-permute-start(bf16[512,128]{1,0:T(8,128)(2,1)S(1)} %get-tuple-element.128.refs_2_.refs_7_), channel_id=1, source_target_pairs={{0,2},{1,3},{2,0},{3,1},{4,6},{5,7},{6,4},{7,5},{8,10},{9,11},{10,... | collective-permute-start | bytes 393224 | tf_op jit(solution)/shard_map/ppermute | solution.py:512
  15.8 8.0 %collective-permute-start.2 = (bf16[512,128]{1,0:T(8,128)(2,1)S(1)}, bf16[512,128]{1,0:T(8,128)(2,1)S(1)}, u32[]{:S(2)}, u32[]{:S(2)}) collective-permute-start(bf16[512,128]{1,0:T(8,128)(2,1)S(1)} %get-tuple-element.128.refs_2_.refs_7_), channel_id=1, source_target_pairs={{0,1},{1,0},{2,3},{3,2},{4,5},{5,4},{6,7},{7,6},{8,9},{9,8},{10,11... | collective-permute-start | bytes 393224 | tf_op jit(solution)/shard_map/ppermute | solution.py:512
  15.9 8.1 %collective-permute-start.5 = (bf16[128,512]{1,0:T(8,128)(2,1)S(1)}, bf16[128,512]{1,0:T(8,128)(2,1)S(1)}, u32[]{:S(2)}, u32[]{:S(2)}) collective-permute-start(bf16[128,512]{1,0:T(8,128)(2,1)S(1)} %copy-done), channel_id=1, source_target_pairs={{0,1},{1,0},{2,3},{3,2},{4,5},{5,4},{6,7},{7,6},{8,9},{9,8},{10,11... | collective-permute-start | bytes 393224 | tf_op jit(solution)/shard_map/ppermute | solution.py:512
  16.4 7.6 %collective-permute-start.6 = (bf16[128,512]{1,0:T(8,128)(2,1)S(1)}, bf16[128,512]{1,0:T(8,128)(2,1)S(1)}, u32[]{:S(2)}, u32[]{:S(2)}) collective-permute-start(bf16[128,512]{1,0:T(8,128)(2,1)S(1)} %copy-done), channel_id=1, source_target_pairs={{0,2},{1,3},{2,0},{3,1},{4,6},{5,7},{6,4},{7,5},{8,10},{9,11},{10,... | collective-permute-start | bytes 393224 | tf_op jit(solution)/shard_map/ppermute | solution.py:512
  16.4 7.9 %collective-permute-start.7 = (bf16[128,512]{1,0:T(8,128)(2,1)S(1)}, bf16[128,512]{1,0:T(8,128)(2,1)S(1)}, u32[]{:S(2)}, u32[]{:S(2)}) collective-permute-start(bf16[128,512]{1,0:T(8,128)(2,1)S(1)} %copy-done), channel_id=1, source_target_pairs={{0,3},{1,2},{2,1},{3,0},{4,7},{5,6},{6,5},{7,4},{8,11},{9,10},{10,... | collective-permute-start | bytes 393224 | tf_op jit(solution)/shard_map/ppermute | solution.py:512
  23.0 1.8 %collective-permute-start.4 = (bf16[512,128]{1,0:T(8,128)(2,1)S(1)}, bf16[512,128]{1,0:T(8,128)(2,1)S(1)}, u32[]{:S(2)}, u32[]{:S(2)}) collective-permute-start(bf16[512,128]{1,0:T(8,128)(2,1)S(1)} %relay_late.1), channel_id=1, source_target_pairs={{0,1},{1,0},{2,3},{3,2},{4,5},{5,4},{6,7},{7,6},{8,9},{9,8},{10,11... | collective-permute-start | bytes 393224 | tf_op jit(solution)/shard_map/ppermute | solution.py:512
  23.9 5.5 %collective-permute-start.1 = (bf16[512,128]{1,0:T(8,128)(2,1)S(1)}, bf16[512,128]{1,0:T(8,128)(2,1)S(1)}, u32[]{:S(2)}, u32[]{:S(2)}) collective-permute-start(bf16[512,128]{1,0:T(8,128)(2,1)S(1)} %get-tuple-element.127.refs_1_.refs_16_.refs_2_.refs_7_), channel_id=1, source_target_pairs={{0,2},{1,3},{2,0},{3,1},{4,6},{5,7},{6,4},{7,5},{8,10},{9,11},{10,... | collective-permute-start | bytes 393224 | tf_op jit(solution)/shard_map/ppermute | solution.py:512
  28.5 2.6 %collective-permute-start.9 = (bf16[256,512]{1,0:T(8,128)(2,1)S(1)}, bf16[256,512]{1,0:T(8,128)(2,1)S(1)}, u32[]{:S(2)}, u32[]{:S(2)}) collective-permute-start(bf16[256,512]{1,0:T(8,128)(2,1)S(1)} %get-tuple-element.140), channel_id=1, source_target_pairs={{0,1},{1,0},{2,3},{3,2},{4,5},{5,4},{6,7},{7,6},{8,9},{9,8},{10,11... | collective-permute-start | bytes 786440 | tf_op jit(solution)/shard_map/ppermute | solution.py:512
  28.9 2.7 %collective-permute-start = (bf16[512,128]{1,0:T(8,128)(2,1)S(1)}, bf16[512,128]{1,0:T(8,128)(2,1)S(1)}, u32[]{:S(2)}, u32[]{:S(2)}) collective-permute-start(bf16[512,128]{1,0:T(8,128)(2,1)S(1)} %get-tuple-element.127.refs_1_.refs_16_.refs_2_.refs_7_), channel_id=1, source_target_pairs={{0,1},{1,0},{2,3},{3,2},{4,5},{5,4},{6,7},{7,6},{8,9},{9,8},{10,11... | collective-permute-start | bytes 393224 | tf_op jit(solution)/shard_map/ppermute | solution.py:512
  30.9 1.4 %collective-permute-start.8 = (bf16[512,128]{1,0:T(8,128)(2,1)S(1)}, bf16[512,128]{1,0:T(8,128)(2,1)S(1)}, u32[]{:S(2)}, u32[]{:S(2)}) collective-permute-start(bf16[512,128]{1,0:T(8,128)(2,1)S(1)} %get-tuple-element.138), channel_id=1, source_target_pairs={{0,1},{1,0},{2,3},{3,2},{4,5},{5,4},{6,7},{7,6},{8,9},{9,8},{10,11... | collective-permute-start | bytes 393224 | tf_op jit(solution)/shard_map/ppermute | solution.py:512
  35.9 5.2 %collective-permute-start.11 = (bf16[256,512]{1,0:T(8,128)(2,1)S(1)}, bf16[256,512]{1,0:T(8,128)(2,1)S(1)}, u32[]{:S(2)}, u32[]{:S(2)}) collective-permute-start(bf16[256,512]{1,0:T(8,128)(2,1)S(1)} %get-tuple-element.144), channel_id=1, source_target_pairs={{0,1},{1,0},{2,3},{3,2},{4,5},{5,4},{6,7},{7,6},{8,9},{9,8},{10,11... | collective-permute-start | bytes 786440 | tf_op jit(solution)/shard_map/ppermute | solution.py:512
  36.2 8.6 %collective-permute-start.10 = (bf16[256,512]{1,0:T(8,128)(2,1)S(1)}, bf16[256,512]{1,0:T(8,128)(2,1)S(1)}, u32[]{:S(2)}, u32[]{:S(2)}) collective-permute-start(bf16[256,512]{1,0:T(8,128)(2,1)S(1)} %add_late.1.refs_16_.refs_1_), channel_id=1, source_target_pairs={{0,2},{1,3},{2,0},{3,1},{4,6},{5,7},{6,4},{7,5},{8,10},{9,11},{10,... | collective-permute-start | bytes 786440 | tf_op jit(solution)/shard_map/ppermute | solution.py:512
  39.6 15.3 %collective-permute-start.13 = (bf16[512,512]{1,0:T(8,128)(2,1)S(1)}, bf16[512,512]{1,0:T(8,128)(2,1)S(1)}, u32[]{:S(2)}, u32[]{:S(2)}) collective-permute-start(bf16[512,512]{1,0:T(8,128)(2,1)S(1)} %get-tuple-element.152), channel_id=1, source_target_pairs={{0,4},{4,0},{8,12},{12,8},{16,20},{20,16},{24,28},{28,24},{1,5},{5... | collective-permute-start | bytes 1572872 | tf_op jit(solution)/shard_map/ppermute | solution.py:512
  45.4 1.6 %collective-permute-start.14 = (bf16[256,512]{1,0:T(8,128)(2,1)S(1)}, bf16[256,512]{1,0:T(8,128)(2,1)S(1)}, u32[]{:S(2)}, u32[]{:S(2)}) collective-permute-start(bf16[256,512]{1,0:T(8,128)(2,1)S(1)} %get-tuple-element.154.refs_2_), channel_id=1, source_target_pairs={{0,1},{1,0},{2,3},{3,2},{4,5},{5,4},{6,7},{7,6},{8,9},{9,8},{10,11... | collective-permute-start | bytes 786440 | tf_op jit(solution)/shard_map/ppermute | solution.py:512
  45.5 9.4 %collective-permute-start.12 = (bf16[256,512]{1,0:T(8,128)(2,1)S(1)}, bf16[256,512]{1,0:T(8,128)(2,1)S(1)}, u32[]{:S(2)}, u32[]{:S(2)}) collective-permute-start(bf16[256,512]{1,0:T(8,128)(2,1)S(1)} %get-tuple-element.151.refs_1_), channel_id=1, source_target_pairs={{0,2},{1,3},{2,0},{3,1},{4,6},{5,7},{6,4},{7,5},{8,10},{9,11},{10,... | collective-permute-start | bytes 786440 | tf_op jit(solution)/shard_map/ppermute | solution.py:512
  55.7 1.6 %collective-permute-start.15 = (bf16[256,512]{1,0:T(8,128)(2,1)S(1)}, bf16[256,512]{1,0:T(8,128)(2,1)S(1)}, u32[]{:S(2)}, u32[]{:S(2)}) collective-permute-start(bf16[256,512]{1,0:T(8,128)(2,1)S(1)} %get-tuple-element.160.refs_2_), channel_id=1, source_target_pairs={{0,1},{1,0},{2,3},{3,2},{4,5},{5,4},{6,7},{7,6},{8,9},{9,8},{10,11... | collective-permute-start | bytes 786440 | tf_op jit(solution)/shard_map/ppermute | solution.py:512
  65.7 8.8 %collective-permute-start.17 = (bf16[1024,512]{1,0:T(8,128)(2,1)S(1)}, bf16[1024,512]{1,0:T(8,128)(2,1)S(1)}, u32[]{:S(2)}, u32[]{:S(2)}) collective-permute-start(bf16[1024,512]{1,0:T(8,128)(2,1)S(1)} %get-tuple-element.182), channel_id=1, source_target_pairs={{0,1},{1,0},{2,3},{3,2},{4,5},{5,4},{6,7},{7,6},{8,9},{9,8},{10,11... | collective-permute-start | bytes 3145736 | tf_op jit(solution)/shard_map/ppermute | solution.py:512
  65.9 8.6 %collective-permute-start.18 = (bf16[256,512]{1,0:T(8,128)(2,1)S(1)}, bf16[256,512]{1,0:T(8,128)(2,1)S(1)}, u32[]{:S(2)}, u32[]{:S(2)}) collective-permute-start(bf16[256,512]{1,0:T(8,128)(2,1)S(1)} %get-tuple-element.184), channel_id=1, source_target_pairs={{0,8},{4,12},{8,0},{12,4},{16,24},{20,28},{24,16},{28,20},{1,9},{5... | collective-permute-start | bytes 786440 | tf_op jit(solution)/shard_map/ppermute | solution.py:512
  75.4 35.7 %collective-permute-start.25 = (bf16[1024,512]{1,0:T(8,128)(2,1)S(1)}, bf16[1024,512]{1,0:T(8,128)(2,1)S(1)}, u32[]{:S(2)}, u32[]{:S(2)}) collective-permute-start(bf16[1024,512]{1,0:T(8,128)(2,1)S(1)} %get-tuple-element.194.refs_3_), channel_id=1, source_target_pairs={{0,2},{1,3},{2,0},{3,1},{4,6},{5,7},{6,4},{7,5},{8,10},{9,11},{10,... | collective-permute-start | bytes 3145736 | tf_op jit(solution)/shard_map/ppermute | solution.py:512
  76.4 10.3 %collective-permute-start.16 = (bf16[384,512]{1,0:T(8,128)(2,1)S(1)}, bf16[384,512]{1,0:T(8,128)(2,1)S(1)}, u32[]{:S(2)}, u32[]{:S(2)}) collective-permute-start(bf16[384,512]{1,0:T(8,128)(2,1)S(1)} %get-tuple-element.180), channel_id=1, source_target_pairs={{0,4},{4,0},{8,12},{12,8},{16,20},{20,16},{24,28},{28,24},{1,5},{5... | collective-permute-start | bytes 1179656 | tf_op jit(solution)/shard_map/ppermute | solution.py:512
  77.9 8.8 %collective-permute-start.19 = (bf16[128,512]{1,0:T(8,128)(2,1)S(1)}, bf16[128,512]{1,0:T(8,128)(2,1)S(1)}, u32[]{:S(2)}, u32[]{:S(2)}) collective-permute-start(bf16[128,512]{1,0:T(8,128)(2,1)S(1)} %get-tuple-element.186), channel_id=1, source_target_pairs={{0,16},{4,20},{8,24},{12,28},{16,0},{20,4},{24,8},{28,12},{1,17},{... | collective-permute-start | bytes 393224 | tf_op jit(solution)/shard_map/ppermute | solution.py:512
  87.5 8.3 %collective-permute-start.20 = (bf16[192,512]{1,0:T(8,128)(2,1)S(1)}, bf16[192,512]{1,0:T(8,128)(2,1)S(1)}, u32[]{:S(2)}, u32[]{:S(2)}) collective-permute-start(bf16[192,512]{1,0:T(8,128)(2,1)S(1)} %get-tuple-element.188), channel_id=1, source_target_pairs={{0,8},{4,12},{8,0},{12,4},{16,24},{20,28},{24,16},{28,20},{1,9},{5... | collective-permute-start | bytes 589832 | tf_op jit(solution)/shard_map/ppermute | solution.py:512
  89.1 6.7 %collective-permute-start.21 = (bf16[128,512]{1,0:T(8,128)(2,1)S(1)}, bf16[128,512]{1,0:T(8,128)(2,1)S(1)}, u32[]{:S(2)}, u32[]{:S(2)}) collective-permute-start(bf16[128,512]{1,0:T(8,128)(2,1)S(1)} %get-tuple-element.189.refs_3_), channel_id=1, source_target_pairs={{0,16},{4,20},{8,24},{12,28},{16,0},{20,4},{24,8},{28,12},{1,17},{... | collective-permute-start | bytes 393224 | tf_op jit(solution)/shard_map/ppermute | solution.py:512
  96.7 8.2 %collective-permute-start.23 = (bf16[256,512]{1,0:T(8,128)(2,1)S(1)}, bf16[256,512]{1,0:T(8,128)(2,1)S(1)}, u32[]{:S(2)}, u32[]{:S(2)}) collective-permute-start(bf16[256,512]{1,0:T(8,128)(2,1)S(1)} %get-tuple-element.192.refs_3_), channel_id=1, source_target_pairs={{0,8},{4,12},{8,0},{12,4},{16,24},{20,28},{24,16},{28,20},{1,9},{5... | collective-permute-start | bytes 786440 | tf_op jit(solution)/shard_map/ppermute | solution.py:512
  99.2 5.6 %collective-permute-start.22 = (bf16[96,512]{1,0:T(8,128)(2,1)S(1)}, bf16[96,512]{1,0:T(8,128)(2,1)S(1)}, u32[]{:S(2)}, u32[]{:S(2)}) collective-permute-start(bf16[96,512]{1,0:T(8,128)(2,1)S(1)} %get-tuple-element.191), channel_id=1, source_target_pairs={{0,16},{4,20},{8,24},{12,28},{16,0},{20,4},{24,8},{28,12},{1,17},{... | collective-permute-start | bytes 294920 | tf_op jit(solution)/shard_map/ppermute | solution.py:512
  105.6 5.4 %collective-permute-start.24 = (bf16[80,512]{1,0:T(8,128)(2,1)S(1)}, bf16[80,512]{1,0:T(8,128)(2,1)S(1)}, u32[]{:S(2)}, u32[]{:S(2)}) collective-permute-start(bf16[80,512]{1,0:T(8,128)(2,1)S(1)} %get-tuple-element.193.refs_1_), channel_id=1, source_target_pairs={{0,16},{4,20},{8,24},{12,28},{16,0},{20,4},{24,8},{28,12},{1,17},{... | collective-permute-start | bytes 245768 | tf_op jit(solution)/shard_map/ppermute | solution.py:512
  111.9 18.0 %collective-permute-start.26 = (bf16[1024,512]{1,0:T(8,128)(2,1)S(1)}, bf16[1024,512]{1,0:T(8,128)(2,1)S(1)}, u32[]{:S(2)}, u32[]{:S(2)}) collective-permute-start(bf16[1024,512]{1,0:T(8,128)(2,1)S(1)} %get-tuple-element.195.refs_7_), channel_id=1, source_target_pairs={{0,1},{1,0},{2,3},{3,2},{4,5},{5,4},{6,7},{7,6},{8,9},{9,8},{10,11... | collective-permute-start | bytes 3145736 | tf_op jit(solution)/shard_map/ppermute | solution.py:512
  111.9 15.1 %collective-permute-start.27 = (bf16[512,512]{1,0:T(8,128)(2,1)S(1)}, bf16[512,512]{1,0:T(8,128)(2,1)S(1)}, u32[]{:S(2)}, u32[]{:S(2)}) collective-permute-start(bf16[512,512]{1,0:T(8,128)(2,1)S(1)} %get-tuple-element.197.refs_1_), channel_id=1, source_target_pairs={{0,4},{4,0},{8,12},{12,8},{16,20},{20,16},{24,28},{28,24},{1,5},{5... | collective-permute-start | bytes 1572872 | tf_op jit(solution)/shard_map/ppermute | solution.py:512
  113.4 6.7 %collective-permute-start.31 = (bf16[160,512]{1,0:T(8,128)(2,1)S(1)}, bf16[160,512]{1,0:T(8,128)(2,1)S(1)}, u32[]{:S(2)}, u32[]{:S(2)}) collective-permute-start(bf16[160,512]{1,0:T(8,128)(2,1)S(1)} %get-tuple-element.204.refs_1_), channel_id=1, source_target_pairs={{0,8},{4,12},{8,0},{12,4},{16,24},{20,28},{24,16},{28,20},{1,9},{5... | collective-permute-start | bytes 491528 | tf_op jit(solution)/shard_map/ppermute | solution.py:512
  120.7 12.9 %collective-permute-start.32 = (bf16[320,512]{1,0:T(8,128)(2,1)S(1)}, bf16[320,512]{1,0:T(8,128)(2,1)S(1)}, u32[]{:S(2)}, u32[]{:S(2)}) collective-permute-start(bf16[320,512]{1,0:T(8,128)(2,1)S(1)} %step_4.1.refs_1_), channel_id=1, source_target_pairs={{0,4},{4,0},{8,12},{12,8},{16,20},{20,16},{24,28},{28,24},{1,5},{5... | collective-permute-start | bytes 983048 | tf_op jit(solution)/shard_map/ppermute | solution.py:512
  121.9 1.2 collective-permute-start.28
  121.9 3.9 %collective-permute-start.29 = (f32[16,512]{1,0:T(8,128)S(1)}, f32[16,512]{1,0:T(8,128)S(1)}, u32[]{:S(2)}, u32[]{:S(2)}) collective-permute-start(f32[16,512]{1,0:T(8,128)S(1)} %get-tuple-element.198.refs_0_), channel_id=1, source_target_pairs={{0,2},{1,3},{2,0},{3,1},{4,6},{5,7},{6,4},{7,5},{8,10},{9,11},{10,... | collective-permute-start | bytes 98312 | tf_op jit(solution)/shard_map/ppermute | solution.py:512
  123.1 3.3 %collective-permute-start.30 = (f32[16,512]{1,0:T(8,128)S(1)}, f32[16,512]{1,0:T(8,128)S(1)}, u32[]{:S(2)}, u32[]{:S(2)}) collective-permute-start(f32[16,512]{1,0:T(8,128)S(1)} %get-tuple-element.198.refs_0_), channel_id=1, source_target_pairs={{0,3},{1,2},{2,1},{3,0},{4,7},{5,6},{6,5},{7,4},{8,11},{9,10},{10,... | collective-permute-start | bytes 98312 | tf_op jit(solution)/shard_map/ppermute | solution.py:512
  127.1 0.7 copy-start.1
where the time goes:
time: 135 us
  Pallas kernels  58.8 us (44%)
  waiting for transfers between devices  38.6 us (29%)
  starting transfers between devices  35.6 us (26%)
  between operations  1.51 us (1%)
    pallas_call x22, Pallas kernels, call(): pl.pallas_call(body, out_shape=[out_space(s, d) if out_space else jax.Sha...  58.8 us
    ppermute x33, waiting for transfers between devices, swap(): return lax.ppermute(rows, axis, [(i, i ^ bit) for i in range(size)])  38.6 us
    ppermute x33, starting transfers between devices, swap(): return lax.ppermute(rows, axis, [(i, i ^ bit) for i in range(size)])  35.6 us
  transfers between devices with their start and end apart: 33, of which 17 were waited for; matrix products, arithmetic and copies ran while one was open for 0% of the time, Pallas kernels for 23%

commit v1 on v0

--- a/solution.py
+++ b/solution.py
@@ -15,6 +15,7 @@
 neg_fill = -1e30
 VMEM_LIMIT = 24 * 1024 * 1024
 small = 16
+UNROLL = [2, 2, 2]
 
 
 def mm(left, right):
@@ -51,12 +52,12 @@
     return jnp.sum(rows, axis=0, keepdims=True)
 
 
-def loop(count, body):
+def loop(count, body, unroll=1):
     def step(i, carry):
         body(i)
         return carry
 
-    lax.fori_loop(0, count, step, 0)
+    lax.fori_loop(0, count, step, 0, unroll=unroll)
 
 
 def rows_of(i, size):
@@ -119,7 +120,7 @@
             found = mm(probs, v_ref[:seen, :])
             ctx_scr[...] = jnp.where(head_lanes(wide, h), found, ctx_scr[...])
 
-        loop(heads, one_head)
+        loop(heads, one_head, UNROLL[2])
         ctx_ref[at, :] = ctx_scr[...].astype(BF)
 
 
@@ -161,10 +162,10 @@
     def some_rows(i):
         project(x_ref, rows_of(i, block), rows_of(i + mem_len // block, block))
 
-    loop(mem_len // block, some_memory)
+    loop(mem_len // block, some_memory, UNROLL[0])
     for copy in copies[5:7]:
         copy.wait()
-    loop(seq_len // block, some_rows)
+    loop(seq_len // block, some_rows, UNROLL[0])
     for copy in copies[7:13]:
         copy.wait()
     bias_ref[0:1, :] = jnp.concatenate([bu_ref[h : h + 1, :] for h in range(heads)], axis=1)
@@ -178,7 +179,7 @@
             (w_ref, wpos_ref, bias_ref[0:1, :], bias_ref[1:2, :], sin_ref, cos_ref, qb_ref, qv_ref), heads,
         )
 
-    loop((seq_len - first) // block, some_queries)
+    loop((seq_len - first) // block, some_queries, UNROLL[1])
     attend(first, block, mem_len, heads, count_ref[0], qb_ref, kt_ref, v_ref, probs_ref, ctx_ref, ctx_scr)
     for copy in copies[13:]:
         copy.wait()
@@ -197,7 +198,7 @@
             (w_ref, wpos_ref, bias_ref[0:1, :], bias_ref[1:2, :], sin_ref, cos_ref, qb_ref, qv_ref), heads,
         )
 
-    loop(qb_ref.shape[1] // block, some_queries)
+    loop(qb_ref.shape[1] // block, some_queries, UNROLL[1])
     attend(first, block, mem_len, heads, count_ref[0], qb_ref, kt_ref, v_ref, probs_ref, ctx_ref, ctx_scr)
 
 
@@ -205,10 +206,8 @@
     first, block,
     place_ref, x_ref, c0_ref, c1_ref, c2_ref, c3_ref, o0_ref, o1_ref, o2_ref, o3_ref, gain_ref, shift_ref, up_ref,
     upb_ref, down_ref, g_ref,
-    hidden_ref, normed_ref, activ_ref, gpre_ref, keep_ref, send_ref, vec_ref, upb_out,
-):
-    core = place_ref[0]
-    vec_ref[...] = jnp.zeros(vec_ref.shape, FL)
+    hidden_ref, normed_ref, activ_ref, gpre_ref, upb_out,
+):
     upb_out[...] = jnp.zeros(upb_out.shape, FL)
 
     def one(i):
@@ -228,40 +227,61 @@
         grads = g_ref[spots, :]
         grad_pre = (mm_t(grads, down_ref[...]) * slope).astype(BF)
         gpre_ref[at, :] = grad_pre
-        back = mm_t(grad_pre, up_ref[...])
+        upb_out[...] += col_sum(grad_pre.astype(FL))
+
+    loop(2, one, 2)
+
+
+def ffn_back_kernel(block, place_ref, gpre_ref, up_ref, ctx_in, keep_ref, send_ref, back_ref, ctx_out):
+    ctx_out[...] = ctx_in[...]
+    core = place_ref[0]
+
+    def one(i):
+        at = rows_of(i, block)
+        back = mm_t(gpre_ref[at, :], up_ref[...])
+        back_ref[at, :] = back
         by_core(core, i, keep_ref, send_ref, back.astype(BF), slice(0, block))
-        vec_ref[0:1, :] += col_sum(back * unit)
-        vec_ref[1:2, :] += col_sum(back)
-        vec_ref[2:3, :] += col_sum(grads.astype(FL))
-        upb_out[...] += col_sum(grad_pre.astype(FL))
-
-    loop(2, one)
+
+    loop(2, one, 2)
+
+
+def ffn_sums(first, back_ref, hidden_ref, g_ref, vec_ref):
+    size = back_ref.shape[0]
+    back = back_ref[...]
+    unit, _ = norm_parts(hidden_ref[...])
+    vec_ref[0:1, :] = col_sum(back * unit)
+    vec_ref[1:2, :] = col_sum(back)
+    vec_ref[2:3, :] = col_sum(g_ref[first : first + size, :].astype(FL))
 
 
 def ffn_late_kernel(
-    first, place_ref, activ_ref, gpre_ref, normed_ref, down_ref, g_ref, ctx_in, share_ref, up_out, down_out, ctx_out
-):
-    ctx_out[...] = ctx_in[...]
+    first, place_ref, activ_ref, gpre_ref, normed_ref, down_ref, g_ref, back_ref, hidden_ref,
+    share_ref, up_out, down_out, vec_ref,
+):
     size = activ_ref.shape[0]
     activ = activ_ref[...]
     share_ref[...] = mm(activ, down_ref[...]).astype(BF)
     down_out[...] = t_mm(activ, g_ref[first : first + size, :])
     up_out[...] = t_mm(normed_ref[...], gpre_ref[...])
+    ffn_sums(first, back_ref, hidden_ref, g_ref, vec_ref)
 
 
 def ffn_early_kernel(
     first,
-    place_ref, activ_ref, gpre_ref, normed_ref, down_ref, g_ref, late_ref, up_in, down_in,
-    share_ref, f_keep, f_send,
-):
+    place_ref, activ_ref, gpre_ref, normed_ref, down_ref, g_ref, back_ref, hidden_ref, late_ref, up_in, down_in, sum_ref,
+    got_ref,
+    share_ref, up_keep, up_send, down_keep, down_send, sum_out, vec_ref,
+):
+    sum_out[...] = added(sum_ref[...], got_ref[...])
     size = activ_ref.shape[0]
     activ = activ_ref[...]
     up = up_in[...] + t_mm(normed_ref[...], gpre_ref[...])
-    by_core(place_ref[1] & 1, 0, f_keep, f_send, up.astype(BF), slice(None))
+    halve(place_ref, 0, up.astype(BF), up_keep, up_send)
     down = down_in[...] + t_mm(activ, g_ref[first : first + size, :])
-    by_core(place_ref[1] & 1, 1, f_keep, f_send, down.astype(BF), slice(None))
+    halve(place_ref, 1, down.astype(BF), down_keep, down_send)
     share_ref[:size, :] = mm(activ, down_ref[...]).astype(BF)
     share_ref[size:, :] = late_ref[...]
+    ffn_sums(first, back_ref, hidden_ref, g_ref, vec_ref)
 
 
 def back_rows(
@@ -307,7 +327,7 @@
             query_v = jnp.where(lanes, qv_ref[at, :].astype(FL), 0.0).astype(BF)
             dpos_ref[...] += t_mm(query_v, turned)
 
-        loop(heads, one_head)
+        loop(heads, one_head, 2)
         bias_ref[0:1, :] += col_sum(grad_u[...]) * scale
         bias_ref[1:2, :] += col_sum(grad_v[...]) * scale
         dq_ref[at, :] = ((grad_u[...] + grad_v[...]) * scale).astype(BF)
@@ -345,13 +365,30 @@
 
 
 def back_early_kernel(
+    first, block, heads, mem_len,
+    place_ref, hidden_ref, mine_ref, other_ref, g_ref, fgain_ref, wout_ref, ctx_ref, probs_ref, qb_ref, qv_ref, kt_ref,
+    v_ref, wpos_ref, sin_ref, cos_ref, dk_in, dv_in, dpos_in, dout_in, bias_in,
+    gh_ref, dk_ref, dv_ref, dpos_ref, dout_ref, dq_ref, bias_ref, grad_u, grad_v,
+):
+    for ref, old in ((dk_ref, dk_in), (dv_ref, dv_in), (dpos_ref, dpos_in), (dout_ref, dout_in), (bias_ref, bias_in)):
+        ref[...] = old[...]
+    back_rows(
+        first, block, heads, mem_len, place_ref, hidden_ref, mine_ref, other_ref, g_ref, fgain_ref, wout_ref, ctx_ref,
+        probs_ref, qb_ref, qv_ref, kt_ref, v_ref, wpos_ref, sin_ref, cos_ref,
+        gh_ref, dk_ref, dv_ref, dpos_ref, dout_ref, dq_ref, bias_ref, grad_u, grad_v,
+    )
+
+
+def back_end_kernel(
     first, block, heads, mem_len, n_tensor, size,
-    place_ref, hidden_ref, mine_ref, other_ref, g_ref, fgain_ref, wout_ref, ctx_ref, probs_ref, qb_ref, qv_ref, kt_ref,
-    v_ref, wpos_ref, sin_ref, cos_ref, x_ref, w_ref, mem_ref, normed_ref, dk_in, dv_in, dpos_in, dout_in, dq_in,
-    bias_in, late_ref, vec_in, vec_l, vec_e, upb_l, upb_e, ffn_ref,
-    gh_ref, keep_ref, send_ref, a_keep, a_send,
-    dk_ref, dv_ref, dpos_ref, dout_ref, dq_ref, vec_ref, bias_ref, grad_u, grad_v,
-):
+    place_ref, x_ref, w_ref, mem_ref, normed_ref, dk_ref, dv_ref, dpos_ref, dout_ref, dq_ref, bias_ref, dq_in, late_ref,
+    vec_in, vec_l, vec_e, upb_l, upb_e, ffn_ref, up_keep,
+    up_got, down_keep, down_got,
+    keep_ref, send_ref, a_keep, a_send, f_ref, vec_ref,
+):
+    half = up_keep.shape[0]
+    f_ref[:half, :] = added(up_keep[...], up_got[...])
+    f_ref[half:, :] = added(down_keep[...], down_got[...])
     wide = heads * HEAD
     core = place_ref[0]
     for part in range(2):
@@ -360,13 +397,6 @@
         by_core(core, part, keep_ref, send_ref, ffn_ref[at, :], slice(2 * block, 3 * block))
         at = slice((part + 2) * block, (part + 3) * block)
         by_core(core, part, keep_ref, send_ref, ffn_ref[at, :], slice(3 * block, 4 * block))
-    for ref, old in ((dk_ref, dk_in), (dv_ref, dv_in), (dpos_ref, dpos_in), (dout_ref, dout_in), (bias_ref, bias_in)):
-        ref[...] = old[...]
-    back_rows(
-        first, block, heads, mem_len, place_ref, hidden_ref, mine_ref, other_ref, g_ref, fgain_ref, wout_ref, ctx_ref,
-        probs_ref, qb_ref, qv_ref, kt_ref, v_ref, wpos_ref, sin_ref, cos_ref,
-        gh_ref, dk_ref, dv_ref, dpos_ref, dout_ref, dq_ref, bias_ref, grad_u, grad_v,
-    )
     normed = normed_ref[...]
     dq_all = jnp.concatenate([dq_ref[...], dq_in[...]], axis=0)
     grads = [
@@ -436,11 +466,9 @@
         outs[7][:, i * width : (i + 1) * width] = mine[7 + i : 8 + i, :]
 
 
-def ffn_grads_kernel(place_ref, mine_ref, got_ref, up_ref, down_ref):
-    own = (place_ref[1] & 1) == 0
-    mine, got = mine_ref[...].astype(FL), got_ref[...].astype(FL)
-    up_ref[...] = jnp.where(own, mine, got)
-    down_ref[...] = jnp.where(own, got, mine)
+def ffn_grads_kernel(up_rows, down_rows, up_ref, down_ref):
+    up_ref[...] = up_rows[...].astype(FL)
+    down_ref[...] = down_rows[...].astype(FL)
 
 
 def finish_kernel(
@@ -525,8 +553,9 @@
         else:
             total = mine[...].astype(FL) + got[...].astype(FL)
             size = outs[0].shape[0]
-            outs.pop(0)[...] = total[:size].astype(BF)
-            outs.pop(0)[...] = total[size:]
+            for part in (total[:size], total[size:]):
+                out = outs.pop(0)
+                out[...] = part.astype(out.dtype)
 
 
 def work(place, jobs, name, after=()):
@@ -535,6 +564,7 @@
         size, width = mine.shape
         outs += {
             "halve": [((size // 2, width), BF)] * 2,
+            "two": [((size // 2, width), BF)] * 2,
             "join": [((2 * size, width), BF)],
             "sum": [((size, width), BF)],
             "split": [((size - small, width), BF), ((small, width), FL)],
@@ -546,25 +576,27 @@
 
 
 class Chain:
-    def __init__(self, keep, send, n_dp):
-        self.rows, self.send, self.n_dp, self.done = keep, send, n_dp, 0
-        self.steps = (n_dp - 1).bit_length()
+    def __init__(self, rows, send, bits, n_dp, end="sum"):
+        self.rows, self.send, self.bits, self.n_dp, self.end, self.done = rows, send, bits, n_dp, end, 0
         self.start()
 
     def bit(self):
-        return min(self.done, 2 * self.steps - 1 - self.done)
+        return self.bits[min(self.done, 2 * len(self.bits) - 2 - self.done)]
 
     def start(self):
         self.got = swap(self.send, "dp", self.n_dp, 1 << self.bit())
 
-    def last(self):
-        return self.done == 2 * self.steps - 1
-
-    def job(self, end="sum"):
-        if self.done < self.steps - 1:
-            kind, bit = "halve", self.done + 1
+    def left(self):
+        return 2 * len(self.bits) - 2 - self.done
+
+    def job(self):
+        last = len(self.bits) - 1
+        if self.done < last - 1:
+            kind, bit = "halve", self.bits[self.done + 1]
+        elif self.done <= last:
+            kind, bit = (self.end if self.done == last else "sum"), 0
         else:
-            kind, bit = (end, 0) if self.done == self.steps - 1 else ("join", self.bit())
+            kind, bit = "join", self.bit()
         return kind, bit, self.rows, self.got
 
     def take(self, results):
@@ -573,15 +605,20 @@
         if kind == "halve":
             self.send = results.pop(0)
         self.done += 1
-        self.start()
+        if self.left() >= 0:
+            self.start()
 
 
 def cores(rows, n_tensor):
     return swap(rows, "tensor", n_tensor, 1)
 
 
+def other_chips(rows, n_tensor):
+    return swap(rows, "tensor", n_tensor, 2)
+
+
 def chips(rows, n_tensor):
-    return rows, swap(rows, "tensor", n_tensor, 2)
+    return rows, other_chips(rows, n_tensor)
 
 
 def copy_kernel(in_ref, out_ref):
@@ -645,31 +682,40 @@
     def ffn_rows(first, ctx, name, after):
         return call(
             functools.partial(ffn_rows_kernel, first, block),
-            [((chunk, width), FL), ((chunk, width), BF), ((chunk, ff), BF), ((chunk, ff), BF), ((block, width), BF),
-             ((block, width), BF), ((3, width), FL), ((1, ff), FL)],
+            [((chunk, width), FL), ((chunk, width), BF), ((chunk, ff), BF), ((chunk, ff), BF), ((1, ff), FL)],
             (place, x, *ctx, *outs_of, ffn_gain, ffn_shift, w_up, up_bias, w_down, g), name, 2e9, after=after,
         )
 
-    hidden_l, normed_l, activ, gpre, keep_l, send, vec_l, upb_l = ffn_rows(late, ctx_l, "ffn_rows_late", saved_e[-1:])
+    def ffn_back(gpre, relayed, name):
+        return call(
+            functools.partial(ffn_back_kernel, block),
+            [((block, width), BF)] * 2 + [((chunk, width), FL), ((chunk, wide), BF)], (place, gpre, w_up, relayed), name, 1e9,
+        )
+
+    hidden_l, normed_l, activ, gpre, upb_l = ffn_rows(late, ctx_l, "ffn_rows_late", saved_e[-1:])
+    keep_l, send, back, relay = ffn_back(gpre, ctx_e[2], "ffn_back_late")
     gnt_l = cores(send, n_tensor)
-    share, up_l, down_l, relay = call(
+    ctx_e.append(cores(relay, n_tensor))
+    share, up_l, down_l, vec_l = call(
         functools.partial(ffn_late_kernel, late),
-        [((chunk, width), BF), ((width, ff), FL), ((ff, width), FL), ((chunk, wide), BF)],
-        (place, activ, gpre, normed_l, w_down, g, ctx_e[2]), "ffn_late", 1e9,
-    )
-    ctx_e.append(cores(relay, n_tensor))
+        [((chunk, width), BF), ((width, ff), FL), ((ff, width), FL), ((3, width), FL)],
+        (place, activ, gpre, normed_l, w_down, g, back, hidden_l), "ffn_late", 1e9,
+    )
     (gnt_l,) = work(place, [("sum", 0, keep_l, gnt_l)], "add_late", (share,))
     gnt_l = chips(gnt_l, n_tensor)
-    hidden_e, normed_e, activ, gpre, keep_e, send, vec_e, upb_e = ffn_rows(0, ctx_e, "ffn_rows_early", gnt_l[:1])
+    hidden_e, normed_e, activ, gpre, upb_e = ffn_rows(0, ctx_e, "ffn_rows_early", gnt_l[:1])
+    keep_e, send, back, _ = ffn_back(gpre, saved_e[-1], "ffn_back_early")
     gnt_e = cores(send, n_tensor)
-    share, f_keep, f_send = call(
+    share, *halves, gnt_l, vec_e = call(
         functools.partial(ffn_early_kernel, 0),
-        [(x.shape, BF)] + [((chunk, width), BF)] * 2,
-        (place, activ, gpre, normed_e, w_down, g, share, up_l, down_l), "ffn_early", 1e9,
-    )
-    ffn = Chain(f_keep, f_send, n_dp)
-    gnt_l, gnt_e = work(place, [("sum", 0, *gnt_l), ("sum", 0, keep_e, gnt_e)], "add_early", (f_keep,))
+        [(x.shape, BF)] + [((width // 2, ff), BF)] * 2 + [((ff // 2, width), BF)] * 2 + [((block, width), BF), ((3, width), FL)],
+        (place, activ, gpre, normed_e, w_down, g, back, hidden_e, share, up_l, down_l, *gnt_l), "ffn_early", 1e9,
+    )
     gnt_l = (gnt_l, cores(gnt_l, n_tensor))
+    up_keep, up_send, down_keep, down_send = halves
+    up_got = swap(up_send, "dp", n_dp, 1)
+    down_got = swap(down_send, "dp", n_dp, 2)
+    (gnt_e,) = work(place, [("sum", 0, keep_e, gnt_e)], "add_early", (up_keep,))
     gnt_e = chips(gnt_e, n_tensor)
 
     sums = [((wide, total), FL), ((wide, total), FL), ((wide, width), FL), ((wide, width), FL), ((chunk, wide), BF)]
@@ -684,57 +730,78 @@
         [((chunk, width), FL), *sums, ((2, wide), FL), ((chunk, width), BF), ((2, width), FL)],
         back_args(hidden_l, gnt_l, saved_l), "back_late", 8e9, turn_scr,
     )
-    gnt_e, *results = work(place, [("sum", 0, *gnt_e), ffn.job()], "add_middle", (vec,))
-    ffn.take(results)
+    gnt_e, up_keep, up_send, down_keep, down_send = work(
+        place, [("sum", 0, *gnt_e), ("halve", 1, up_keep, up_got), ("halve", 0, down_keep, down_got)], "add_middle", (vec,)
+    )
+    up_got = swap(up_send, "dp", n_dp, 2)
+    down_got = swap(down_send, "dp", n_dp, 1)
     gnt_e = (gnt_e, cores(gnt_e, n_tensor))
-    size = max(16, -(-5 * wide // n_dp // 16) * 16)
-    gh_e, keep, send, a_keep, a_send = call(
-        functools.partial(back_early_kernel, 0, block, heads, mem_len, n_tensor, size),
-        [((chunk, width), FL), *[((seq_len, width), BF)] * 2, *[((n_dp // 2 * (size + small), width), BF)] * 2],
-        (*back_args(hidden_e, gnt_e, saved_e), mem, normed, dk, dv, dpos, dout, dq, bias, part, vec, vec_l, vec_e, upb_l,
-         upb_e, share),
-        "back_early", 6e9, [pltpu.VMEM(s, d) for s, d in (*sums, ((2, width), FL), ((2, wide), FL))] + turn_scr,
-    )
-    attn = Chain(a_keep, a_send, n_dp)
-    send = cores(send, n_tensor)
-    rows, *results = work(place, [("sum", 0, keep, send), ffn.job()], "step_ffn")
-    ffn.take(results)
-    rows = chips(rows, n_tensor)
-    count = 0
-    while not attn.last():
-        chains = [attn] + [c for c in (ffn,) if not c.last()]
-        jobs = [attn.job("split")] + [c.job() for c in chains[1:]]
-        if attn.done == attn.steps:
+    groups = n_dp // 2
+    size = max(16, -(-5 * wide // groups // 16) * 16)
+    gh_e, dk, dv, dpos, dout, dq_e, bias = call(
+        functools.partial(back_early_kernel, 0, block, heads, mem_len),
+        [((chunk, width), FL), *sums, ((2, wide), FL)],
+        (*back_args(hidden_e, gnt_e, saved_e)[:-2], dk, dv, dpos, dout, bias), "back_early", 6e9, turn_scr,
+    )
+    keep, send, a_keep, a_send, f_rows = call(
+        functools.partial(back_end_kernel, 0, block, heads, mem_len, n_tensor, size),
+        [*[((seq_len, width), BF)] * 2, *[((groups // 2 * (size + small), width), BF)] * 2, ((chunk // 2, width), BF)],
+        (place, x, weights, mem, normed, dk, dv, dpos, dout, dq_e, bias, dq, part, vec, vec_l, vec_e, upb_l, upb_e, share,
+         up_keep, up_got, down_keep, down_got),
+        "back_end", 6e9, [pltpu.VMEM((2, width), FL)],
+    )
+    bits = list(range((n_dp - 1).bit_length()))
+    attn = Chain(a_keep, a_send, bits, n_dp, "split")
+    if len(bits) > 3:
+        f_rows, f_send = work(place, [("halve", 2, f_rows, jnp.zeros_like(f_rows))], "halve_ffn")
+    else:
+        f_send = f_rows
+    ffn = Chain(f_rows, f_send, bits[2:], n_dp, "two" if len(bits) == 3 else "sum")
+    rows = (keep, cores(send, n_tensor))
+    count, stage = 0, 0
+    while attn.left() > 0:
+        jobs = [attn.job()]
+        if stage == 0:
+            jobs.append(ffn.job())
+        elif stage < 3:
+            jobs += [("join", 2 - stage, up, up_got), ("join", stage - 1, down, down_got)]
+        if count == 0 or attn.left() == 1:
             jobs.append(("sum", 0, *rows))
         results = work(place, jobs, f"step_{count}")
-        if attn.done == attn.steps:
-            rows = results.pop()
-            rows = (rows, cores(rows, n_tensor))
-        if attn.done == attn.steps - 1:
+        if attn.job()[0] == "split":
             totals = results.pop(1)
             totals = [totals] + [swap(totals, "tensor", n_tensor, k) for k in range(1, n_tensor)]
-        for c in chains:
-            c.take(results)
+        if count == 0 or attn.left() == 1:
+            rows = results.pop()
+            rows = (rows, (other_chips if count == 0 else cores)(rows, n_tensor))
+        attn.take(results)
+        if stage == 0 and ffn.left() > 0:
+            ffn.take(results)
+        elif stage < 3:
+            up, down = results if len(results) == 2 else (results[0][: chunk // 4], results[0][chunk // 4 :])
+            if stage < 2:
+                up_got, down_got = swap(up, "dp", n_dp, 2 >> stage), swap(down, "dp", n_dp, 1 << stage)
+            stage += 1
         count += 1
+    output, input_grad = call(
+        functools.partial(finish_kernel, block), [(x.shape, BF)] * 2,
+        (place, x, attn_gain, gh_e, gh_l, hidden_e, hidden_l, *rows, down_bias), "finish", 1e8,
+        out_space=pltpu.HBM,
+    )
+    output_there = pltpu.with_memory_space_constraint(output, pltpu.HBM)
     vecs = call(
         functools.partial(small_kernel, heads, n_tensor),
-        [((1, width), FL)] * 5 + [((heads, HEAD), FL)] * 2 + [((1, ff), FL)], totals, "small", 1e6,
+        [((1, width), FL)] * 5 + [((heads, HEAD), FL)] * 2 + [((1, ff), FL)], totals, "small", 1e6, after=(output_there,),
     )
     g_up, g_down = call(
-        ffn_grads_kernel, [((width, ff), FL), ((ff, width), FL)], (place, ffn.rows, ffn.got), "ffn_grads", 1e6,
-        after=vecs[:1], out_space=pltpu.HBM,
+        ffn_grads_kernel, [((width, ff), FL), ((ff, width), FL)], (up, down), "ffn_grads", 1e6,
+        out_space=pltpu.HBM, after=vecs[5:6],
     )
     g_up_there = pltpu.with_memory_space_constraint(g_up, pltpu.HBM)
-    output, input_grad = call(
-        functools.partial(finish_kernel, block), [(x.shape, BF)] * 2,
-        (place, x, attn_gain, gh_e, gh_l, hidden_e, hidden_l, *rows, down_bias), "finish", 1e8, after=(g_up_there,),
-        out_space=pltpu.HBM,
-    )
-    output_there = pltpu.with_memory_space_constraint(output, pltpu.HBM)
     g_query, g_key, g_value, g_pos, g_out = call(
         functools.partial(weights_kernel, wide, attn.bit()),
         [((width, wide), FL)] * 4 + [((wide, width), FL)], (place, attn.rows, attn.got), "weights", 1e6,
-        [pltpu.VMEM((n_dp * size, width), FL)], after=(output_there,), out_space=pltpu.HBM,
+        [pltpu.VMEM((groups * size, width), FL)], after=(g_up_there,), out_space=pltpu.HBM,
     )
     return (
         output[None],

time: 135 us -> 123 us (0.911)
  starting transfers between devices: 35.6 us -> 30.2 us
  Pallas kernels: 58.8 us -> 53.9 us
  waiting for transfers between devices: 38.6 us -> 36.3 us
    ppermute x33 -> x35, starting transfers between devices: 35.6 us -> 30.2 us  [swap(): return lax.ppermute(rows, axis, [(i, i ^ bit) for i in range(size)])]
    pallas_call x22 -> x23, Pallas kernels: 58.8 us -> 53.9 us  [call(): pl.pallas_call(body, out_shape=[out_space(s, d) if out_space else jax.Sha...]
    ppermute x33 -> x35, waiting for transfers between devices: 38.6 us -> 36.3 us  [swap(): return lax.ppermute(rows, axis, [(i, i ^ bit) for i in range(size)])]
  transfers between devices with their start and end apart: 33 -> 35, of which waited for: 17 -> 10; matrix products, arithmetic and copies ran while one was open for 0% -> 0% of each run, Pallas kernels for 23% -> 29%
where the time goes in v1:
time: 123 us
  Pallas kernels  53.9 us (44%)
  waiting for transfers between devices  36.3 us (30%)
  starting transfers between devices  30.2 us (25%)
  between operations  1.55 us (1%)
    pallas_call x23, Pallas kernels, call(): pl.pallas_call(body, out_shape=[out_space(s, d) if out_space else jax.Sha...  53.9 us
    ppermute x35, waiting for transfers between devices, swap(): return lax.ppermute(rows, axis, [(i, i ^ bit) for i in range(size)])  36.3 us
    ppermute x35, starting transfers between devices, swap(): return lax.ppermute(rows, axis, [(i, i ^ bit) for i in range(size)])  30.2 us
  transfers between devices with their start and end apart: 35, of which 10 were waited for; matrix products, arithmetic and copies ran while one was open for 0% of the time, Pallas kernels for 29%

profile of v1, /device:TPU:0, one launch (start us, length us, event | category | flops | bytes accessed | tf_op | source)
XLA Modules:
  0.0 122.7 jit_solution(2259046380639940801)
XLA Ops:
  1.3 0.1 pad_add_fusion.refs_0_
  1.4 9.3 %front.1 = (bf16[1024,512]{1,0:T(8,128)(2,1)S(1)}, bf16[512,512]{1,0:T(8,128)(2,1)S(1)}, bf16[1024,512]{1,0:T(8,128)(2,1)S(1)}, bf16[512,384]{1,0:T(8,128)(2,1)S...) custom-call(s32[2]{0:T(128)S(1)} %pad_add_fusion.refs_0_, ...), custom_call_target="tpu_custom_call" | custom-call | flops 1 | bytes 1 | tf_op jit(solution)/shard_map/front/pallas_call | solution.py:527
  10.7 3.0 %collective-permute-start.3 = (bf16[512,128]{1,0:T(8,128)(2,1)S(1)}, bf16[512,128]{1,0:T(8,128)(2,1)S(1)}, u32[]{:S(2)}, u32[]{:S(2)}) collective-permute-start(bf16[512,128]{1,0:T(8,128)(2,1)S(1)} %get-tuple-element.140.refs_2_.refs_7_), channel_id=1, source_target_pairs={{0,2},{1,3},{2,0},{3,1},{4,6},{5,7},{6,4},{7,5},{8,10},{9,11},{10,... | collective-permute-start | bytes 393224 | tf_op jit(solution)/shard_map/ppermute | solution.py:540
  13.8 1.2 collective-permute-start.6
  14.9 0.7 collective-permute-start.5
  15.6 4.1 %second.1 = (bf16[2,512,640]{2,1,0:T(8,128)(2,1)S(1)}, bf16[512,128]{1,0:T(8,128)(2,1)S(1)}, bf16[2,512,1024]{2,1,0:T(8,128)(2,1)S(1)}, bf16[512,128]{1,0:T(8,128)(2,1)S(1)}) custom-call(s32[1]{0:T(128)S(6)} %copy.39.refs_1_.refs_0_, bf16[1536,512]{1,0:T(8,128)(2,1)S(1)} %get-tuple-element.131.refs_1_.refs_4_, ...), custom_call_target="tpu_custom_call" | custom-call | flops 1 | bytes 1 | tf_op jit(solution)/shard_map/second/pallas_call | solution.py:527
  19.8 0.6 collective-permute-start.4
  20.3 0.1 collective-permute-done.7.refs_9_
  20.5 0.2 collective-permute-start.1
  20.6 2.2 %collective-permute-done.6.refs_8_ = bf16[128,512]{1,0:T(8,128)(2,1)S(1)} collective-permute-done((bf16[128,512]{1,0:T(8,128)(2,1)S(1)}, bf16[128,512]{1,0:T(8,128)(2,1)S(1)}, u32[]{:S(2)}, u32[]{:S(2)}) %collective-permute-start.6) | collective-permute-done | bytes 131104 | tf_op jit(solution)/shard_map/ppermute | solution.py:540
  22.9 2.6 %ffn_rows_late.1 = (f32[512,512]{1,0:T(8,128)S(1)}, bf16[512,512]{1,0:T(8,128)(2,1)S(1)}, bf16[512,512]{1,0:T(8,128)(2,1)S(1)}, bf16[512,512]{1,0:T(8,128)(2,1)S(1)}, f32[1,512]{1,0:T(1,128)S(1)}) custom-call(s32[2]{0:T(128)S(1)} %pad_add_fusion.refs_0_, bf16[1024,512]{1,0:T(8,128)(2,1)S(1)} %get-tuple-element.129.refs_1_.refs_16_, ...), custom_call_target="tpu_custom_call" | custom-call | flops 1 | bytes 1 | tf_op jit(solution)/shard_map/ffn_rows_late/pallas_call | solution.py:527
  25.5 0.9 collective-permute-done.1.refs_3_.refs_4_
  26.4 1.4 %ffn_back_late.1 = (bf16[256,512]{1,0:T(8,128)(2,1)S(1)}, bf16[256,512]{1,0:T(8,128)(2,1)S(1)}, f32[512,512]{1,0:T(8,128)S(1)}, bf16[512,128]{1,0:T(8,128)(2,1)S(1)}) custom-call(s32[2]{0:T(128)S(1)} %pad_add_fusion.refs_0_, bf16[512,512]{1,0:T(8,128)(2,1)S(1)} %get-tuple-element.147.refs_1_.refs_2_, ...), custom_call_target="tpu_custom_call" | custom-call | flops 1 | bytes 1 | tf_op jit(solution)/shard_map/ffn_back_late/pallas_call | solution.py:527
  27.9 0.1 collective-permute-start.9
  28.0 0.5 collective-permute-start
  28.4 0.1 collective-permute-start.8
  28.5 1.6 %ffn_late.1 = (bf16[512,512]{1,0:T(8,128)(2,1)S(1)}, f32[512,512]{1,0:T(8,128)S(1)}, f32[512,512]{1,0:T(8,128)S(1)}, f32[3,512]{1,0:T(4,128)S(1)}) custom-call(s32[2]{0:T(128)S(1)} %pad_add_fusion.refs_0_, bf16[512,512]{1,0:T(8,128)(2,1)S(1)} %get-tuple-element.151.refs_1_, bf16[512,512]{1,0:T(8,128)(2,1)S(1)} %get-tuple-element.147.refs_1_.refs_2_, ...), custom_call_target="tpu_custom_call" | custom-call | flops 1 | bytes 1 | tf_op jit(solution)/shard_map/ffn_late/pallas_call | solution.py:527
  30.1 0.6 add_late.1.refs_16_.refs_11_
  30.7 0.9 collective-permute-start.11
  31.6 2.6 %ffn_rows_early.1 = (f32[512,512]{1,0:T(8,128)S(1)}, bf16[512,512]{1,0:T(8,128)(2,1)S(1)}, bf16[512,512]{1,0:T(8,128)(2,1)S(1)}, bf16[512,512]{1,0:T(8,128)(2,1)S(1)}, f32[1,512]{1,0:T(1,128)S(1)}) custom-call(s32[2]{0:T(128)S(1)} %pad_add_fusion.refs_0_, bf16[1024,512]{1,0:T(8,128)(2,1)S(1)} %get-tuple-element.129.refs_1_.refs_16_, ...), custom_call_target="tpu_custom_call" | custom-call | flops 1 | bytes 1 | tf_op jit(solution)/shard_map/ffn_rows_early/pallas_call | solution.py:527
  34.2 1.9 %ffn_back_early.1 = (bf16[256,512]{1,0:T(8,128)(2,1)S(1)}, bf16[256,512]{1,0:T(8,128)(2,1)S(1)}, f32[512,512]{1,0:T(8,128)S(1)}, bf16[512,128]{1,0:T(8,128)(2,1)}) custom-call(s32[2]{0:T(128)S(1)} %pad_add_fusion.refs_0_, bf16[512,512]{1,0:T(8,128)(2,1)S(1)} %get-tuple-element.157.refs_1_.refs_2_, bf16[512,512]{1,0:T(8,128)(2,1)S(1)} %get-tuple-element.143.refs_12_.refs_2_, ...), custom_call_target="tpu_custom_call" | custom-call | flops 1 | bytes 1 | tf_op jit(solution)/shard_map/ffn_back_early/pallas_call | solution.py:527
  36.1 0.2 collective-permute-start.10
  36.3 3.2 %collective-permute-done.11.refs_12_ = bf16[256,512]{1,0:T(8,128)(2,1)S(1)} collective-permute-done((bf16[256,512]{1,0:T(8,128)(2,1)S(1)}, bf16[256,512]{1,0:T(8,128)(2,1)S(1)}, u32[]{:S(2)}, u32[]{:S(2)}) %collective-permute-start.11) | collective-permute-done | bytes 262176 | tf_op jit(solution)/shard_map/ppermute | solution.py:540
  39.5 2.4 %ffn_early.1 = (bf16[1024,512]{1,0:T(8,128)(2,1)S(1)}, bf16[256,512]{1,0:T(8,128)(2,1)S(1)}, bf16[256,512]{1,0:T(8,128)(2,1)S(1)}, bf16[256,512]{1,0:T(8,128)(2,...) custom-call(s32[2]{0:T(128)S(1)} %pad_add_fusion.refs_0_, ...), custom_call_target="tpu_custom_call" | custom-call | flops 1 | bytes 1 | tf_op jit(solution)/shard_map/ffn_early/pallas_call | solution.py:527
  41.8 0.1 collective-permute-start.15
  41.9 0.6 add_early.1.refs_1_
  42.5 0.9 collective-permute-start.12
  43.4 1.5 %collective-permute-start.13 = (bf16[256,512]{1,0:T(8,128)(2,1)S(1)}, bf16[256,512]{1,0:T(8,128)(2,1)S(1)}, u32[]{:S(2)}, u32[]{:S(2)}) collective-permute-start(bf16[256,512]{1,0:T(8,128)(2,1)S(1)} %get-tuple-element.166), channel_id=1, source_target_pairs={{0,4},{4,0},{8,12},{12,8},{16,20},{20,16},{24,28},{28,24},{1,5},{5... | collective-permute-start | bytes 786440 | tf_op jit(solution)/shard_map/ppermute | solution.py:540
  44.9 1.6 %collective-permute-start.14 = (bf16[256,512]{1,0:T(8,128)(2,1)S(1)}, bf16[256,512]{1,0:T(8,128)(2,1)S(1)}, u32[]{:S(2)}, u32[]{:S(2)}) collective-permute-start(bf16[256,512]{1,0:T(8,128)(2,1)S(1)} %get-tuple-element.168), channel_id=1, source_target_pairs={{0,8},{4,12},{8,0},{12,4},{16,24},{20,28},{24,16},{28,20},{1,9},{5... | collective-permute-start | bytes 786440 | tf_op jit(solution)/shard_map/ppermute | solution.py:540
  46.5 6.8 %back_late.1 = (f32[512,512]{1,0:T(8,128)S(1)}, f32[128,1536]{1,0:T(8,128)S(1)}, f32[128,1536]{1,0:T(8,128)S(1)}, f32[128,512]{1,0:T(8,128)S(1)}, f32[128,512]{1...) custom-call(s32[2]{0:T(128)S(1)} %pad_add_fusion.refs_0_, ...), custom_call_target="tpu_custom_call" | custom-call | flops 1 | bytes 1 | tf_op jit(solution)/shard_map/back_late/pallas_call | solution.py:527
  53.3 1.1 add_middle.1
  54.4 0.1 collective-permute-start.16
  54.5 1.4 %collective-permute-start.17 = (bf16[128,512]{1,0:T(8,128)(2,1)S(1)}, bf16[128,512]{1,0:T(8,128)(2,1)S(1)}, u32[]{:S(2)}, u32[]{:S(2)}) collective-permute-start(bf16[128,512]{1,0:T(8,128)(2,1)S(1)} %get-tuple-element.201), channel_id=1, source_target_pairs={{0,8},{4,12},{8,0},{12,4},{16,24},{20,28},{24,16},{28,20},{1,9},{5... | collective-permute-start | bytes 393224 | tf_op jit(solution)/shard_map/ppermute | solution.py:540
  55.8 0.5 collective-permute-start.18
  56.4 5.0 %back_early.1 = (f32[512,512]{1,0:T(8,128)S(1)}, f32[128,1536]{1,0:T(8,128)S(1)}, f32[128,1536]{1,0:T(8,128)S(1)}, f32[128,512]{1,0:T(8,128)S(1)}, f32[128,512]{...) custom-call(s32[2]{0:T(128)S(1)} %pad_add_fusion.refs_0_, ...), custom_call_target="tpu_custom_call" | custom-call | flops 1 | bytes 1 | tf_op jit(solution)/shard_map/back_early/pallas_call | solution.py:527
  61.4 3.0 %back_end.1 = (bf16[1024,512]{1,0:T(8,128)(2,1)S(1)}, bf16[1024,512]{1,0:T(8,128)(2,1)S(1)}, bf16[352,512]{1,0:T(8,128)(2,1)S(1)}, bf16[352,512]{1,0:T(8,128)(2,1)S(1)}, bf16[256,512]{1,0:T(8,128)(2,1)S(1)}) custom-call(s32[2]{0:T(128)S(1)} %pad_add_fusion.refs_0_, bf16[1024,512]{1,0:T(8,128)(2,1)S(1)} %get-tuple-element.129.refs_1_.refs_16_, ...), custom_call_target="tpu_custom_call" | custom-call | flops 1 | bytes 1 | tf_op jit(solution)/shard_map/back_end/pallas_call | solution.py:527
  64.3 0.1 collective-permute-start.21
  64.4 1.6 %collective-permute-start.19 = (bf16[352,512]{1,0:T(8,128)(2,1)S(1)}, bf16[352,512]{1,0:T(8,128)(2,1)S(1)}, u32[]{:S(2)}, u32[]{:S(2)}) collective-permute-start(bf16[352,512]{1,0:T(8,128)(2,1)S(1)} %get-tuple-element.205), channel_id=1, source_target_pairs={{0,4},{4,0},{8,12},{12,8},{16,20},{20,16},{24,28},{28,24},{1,5},{5... | collective-permute-start | bytes 1081352 | tf_op jit(solution)/shard_map/ppermute | solution.py:540
  66.0 2.6 %collective-permute-start.20 = (bf16[256,512]{1,0:T(8,128)(2,1)S(1)}, bf16[256,512]{1,0:T(8,128)(2,1)S(1)}, u32[]{:S(2)}, u32[]{:S(2)}) collective-permute-start(bf16[256,512]{1,0:T(8,128)(2,1)S(1)} %get-tuple-element.206.refs_3_), channel_id=1, source_target_pairs={{0,16},{4,20},{8,24},{12,28},{16,0},{20,4},{24,8},{28,12},{1,17},{... | collective-permute-start | bytes 786440 | tf_op jit(solution)/shard_map/ppermute | solution.py:540
  68.6 12.3 %collective-permute-done.20.refs_4_ = bf16[256,512]{1,0:T(8,128)(2,1)S(1)} collective-permute-done((bf16[256,512]{1,0:T(8,128)(2,1)S(1)}, bf16[256,512]{1,0:T(8,128)(2,1)S(1)}, u32[]{:S(2)}, u32[]{:S(2)}) %collective-permute-start.20) | collective-permute-done | bytes 262176 | tf_op jit(solution)/shard_map/ppermute | solution.py:540
  80.9 1.0 step_0.1
  81.9 1.3 %collective-permute-start.29 = (bf16[1024,512]{1,0:T(8,128)(2,1)S(1)}, bf16[1024,512]{1,0:T(8,128)(2,1)S(1)}, u32[]{:S(2)}, u32[]{:S(2)}) collective-permute-start(bf16[1024,512]{1,0:T(8,128)(2,1)S(1)} %get-tuple-element.217.refs_3_), channel_id=1, source_target_pairs={{0,2},{1,3},{2,0},{3,1},{4,6},{5,7},{6,4},{7,5},{8,10},{9,11},{10,... | collective-permute-start | bytes 3145736 | tf_op jit(solution)/shard_map/ppermute | solution.py:540
  83.2 2.0 %collective-permute-start.23 = (bf16[128,512]{1,0:T(8,128)(2,1)S(1)}, bf16[128,512]{1,0:T(8,128)(2,1)S(1)}, u32[]{:S(2)}, u32[]{:S(2)}) collective-permute-start(bf16[128,512]{1,0:T(8,128)(2,1)S(1)} %get-tuple-element.211.refs_3_), channel_id=1, source_target_pairs={{0,8},{4,12},{8,0},{12,4},{16,24},{20,28},{24,16},{28,20},{1,9},{5... | collective-permute-start | bytes 393224 | tf_op jit(solution)/shard_map/ppermute | solution.py:540
  85.3 0.5 collective-permute-start.24
  85.8 6.3 %collective-permute-done.23.refs_4_ = bf16[128,512]{1,0:T(8,128)(2,1)S(1)} collective-permute-done((bf16[128,512]{1,0:T(8,128)(2,1)S(1)}, bf16[128,512]{1,0:T(8,128)(2,1)S(1)}, u32[]{:S(2)}, u32[]{:S(2)}) %collective-permute-start.23) | collective-permute-done | bytes 131104 | tf_op jit(solution)/shard_map/ppermute | solution.py:540
  92.1 0.7 step_1.1
  92.8 0.4 collective-permute-start.26
  93.2 0.3 collective-permute-start.27
  93.5 3.0 %collective-permute-start.25 = (bf16[176,512]{1,0:T(8,128)(2,1)S(1)}, bf16[176,512]{1,0:T(8,128)(2,1)S(1)}, u32[]{:S(2)}, u32[]{:S(2)}) collective-permute-start(bf16[176,512]{1,0:T(8,128)(2,1)S(1)} %get-tuple-element.213.refs_1_), channel_id=1, source_target_pairs={{0,16},{4,20},{8,24},{12,28},{16,0},{20,4},{24,8},{28,12},{1,17},{... | collective-permute-start | bytes 540680 | tf_op jit(solution)/shard_map/ppermute | solution.py:540
  96.5 5.4 %collective-permute-done.25.refs_2_ = bf16[176,512]{1,0:T(8,128)(2,1)S(1)} collective-permute-done((bf16[176,512]{1,0:T(8,128)(2,1)S(1)}, bf16[176,512]{1,0:T(8,128)(2,1)S(1)}, u32[]{:S(2)}, u32[]{:S(2)}) %collective-permute-start.25) | collective-permute-done | bytes 180256 | tf_op jit(solution)/shard_map/ppermute | solution.py:540
  101.9 1.7 %collective-permute-done.27.refs_6_ = bf16[256,512]{1,0:T(8,128)(2,1)S(1)} collective-permute-done((bf16[256,512]{1,0:T(8,128)(2,1)S(1)}, bf16[256,512]{1,0:T(8,128)(2,1)S(1)}, u32[]{:S(2)}, u32[]{:S(2)}) %collective-permute-start.27) | collective-permute-done | bytes 262176 | tf_op jit(solution)/shard_map/ppermute | solution.py:540
  103.7 0.9 step_2.1
  104.5 1.5 %collective-permute-start.28 = (bf16[160,512]{1,0:T(8,128)(2,1)S(1)}, bf16[160,512]{1,0:T(8,128)(2,1)S(1)}, u32[]{:S(2)}, u32[]{:S(2)}) collective-permute-start(bf16[160,512]{1,0:T(8,128)(2,1)S(1)} %get-tuple-element.216.refs_1_), channel_id=1, source_target_pairs={{0,8},{4,12},{8,0},{12,4},{16,24},{20,28},{24,16},{28,20},{1,9},{5... | collective-permute-start | bytes 491528 | tf_op jit(solution)/shard_map/ppermute | solution.py:540
  106.0 3.9 %collective-permute-done.28.refs_2_ = bf16[160,512]{1,0:T(8,128)(2,1)S(1)} collective-permute-done((bf16[160,512]{1,0:T(8,128)(2,1)S(1)}, bf16[160,512]{1,0:T(8,128)(2,1)S(1)}, u32[]{:S(2)}, u32[]{:S(2)}) %collective-permute-start.28) | collective-permute-done | bytes 163872 | tf_op jit(solution)/shard_map/ppermute | solution.py:540
  109.9 0.9 step_3.1
  110.9 1.7 %collective-permute-start.34 = (bf16[320,512]{1,0:T(8,128)(2,1)S(1)}, bf16[320,512]{1,0:T(8,128)(2,1)S(1)}, u32[]{:S(2)}, u32[]{:S(2)}) collective-permute-start(bf16[320,512]{1,0:T(8,128)(2,1)S(1)} %get-tuple-element.225.refs_1_), channel_id=1, source_target_pairs={{0,4},{4,0},{8,12},{12,8},{16,20},{20,16},{24,28},{28,24},{1,5},{5... | collective-permute-start | bytes 983048 | tf_op jit(solution)/shard_map/ppermute | solution.py:540
  112.6 0.6 collective-permute-start.33
  113.2 1.2 collective-permute-start.32
  114.5 3.7 %finish.1 = (bf16[1024,512]{1,0:T(8,128)(2,1)}, bf16[1024,512]{1,0:T(8,128)(2,1)}) custom-call(s32[2]{0:T(128)S(1)} %pad_add_fusion.refs_0_, bf16[1024,512]{1,0:T(8,128)(2,1)S(1)} %get-tuple-element.129.refs_1_.refs_16_, f32[1,512]{1,0:T(1,128)S(1)} %get-tuple-element.130.refs_2_, f32[512,512]{1,0:T(8,128)S(1)} %get-tuple-element.184.refs_3_, ...), custom_call_target="tpu_custom_call" | custom-call | flops 1 | bytes 1 | tf_op jit(solution)/shard_map/finish/pallas_call | solution.py:527
  118.2 0.6 small.1
  118.8 0.7 copy-done.1
  119.5 1.4 %ffn_grads.1 = (f32[512,512]{1,0:T(8,128)}, f32[512,512]{1,0:T(8,128)}) custom-call(bf16[512,512]{1,0:T(8,128)(2,1)S(1)} %get-tuple-element.226.refs_0_, bf16[512,512]{1,0:T(8,128)(2,1)S(1)} %get-tuple-element.227.refs_1_, f32[2,64]{1,0:T(2,128)S(1)} %copy-done.1), custom_call_target="tpu_custom_call" | custom-call | flops 1 | bytes 1 | tf_op jit(solution)/shard_map/ffn_grads/pallas_call | solution.py:527
  120.9 0.1 collective-permute-done.34.refs_2_
  121.0 1.7 %weights.1 = (f32[512,128]{1,0:T(8,128)}, f32[512,128]{1,0:T(8,128)}, f32[512,128]{1,0:T(8,128)}, f32[512,128]{1,0:T(8,128)}, f32[128,512]{1,0:T(8,128)}) custom-call(s32[2]{0:T(128)S(1)} %pad_add_fusion.refs_0_, bf16[320,512]{1,0:T(8,128)(2,1)S(1)} %get-tuple-element.225.refs_1_, bf16[320,512]{1,0:T(8,128)(2,1)S(1)} %collective-permute-done.34.refs_2_, ...), custom_call_target="tpu_custom_call" | custom-call | flops 1 | bytes 1 | tf_op jit(solution)/shard_map/weights/pallas_call | solution.py:527
  (34 shorter events, 0.2 us)
Async XLA Ops:
  1.4 12.4 %copy-start = (bf16[128,512]{1,0:T(8,128)(2,1)S(1)}, bf16[128,512]{1,0:T(8,128)(2,1)}, u32[]{:S(2)}) copy-start(bf16[128,512]{1,0:T(8,128)(2,1)} %refs_6_.5) | copy-start | bytes 393220
  10.7 9.0 %collective-permute-start.3 = (bf16[512,128]{1,0:T(8,128)(2,1)S(1)}, bf16[512,128]{1,0:T(8,128)(2,1)S(1)}, u32[]{:S(2)}, u32[]{:S(2)}) collective-permute-start(bf16[512,128]{1,0:T(8,128)(2,1)S(1)} %get-tuple-element.140.refs_2_.refs_7_), channel_id=1, source_target_pairs={{0,2},{1,3},{2,0},{3,1},{4,6},{5,7},{6,4},{7,5},{8,10},{9,11},{10,... | collective-permute-start | bytes 393224 | tf_op jit(solution)/shard_map/ppermute | solution.py:540
  13.8 6.7 %collective-permute-start.7 = (bf16[128,512]{1,0:T(8,128)(2,1)S(1)}, bf16[128,512]{1,0:T(8,128)(2,1)S(1)}, u32[]{:S(2)}, u32[]{:S(2)}) collective-permute-start(bf16[128,512]{1,0:T(8,128)(2,1)S(1)} %copy-done), channel_id=1, source_target_pairs={{0,3},{1,2},{2,1},{3,0},{4,7},{5,6},{6,5},{7,4},{8,11},{9,10},{10,... | collective-permute-start | bytes 393224 | tf_op jit(solution)/shard_map/ppermute | solution.py:540
  13.8 9.1 %collective-permute-start.6 = (bf16[128,512]{1,0:T(8,128)(2,1)S(1)}, bf16[128,512]{1,0:T(8,128)(2,1)S(1)}, u32[]{:S(2)}, u32[]{:S(2)}) collective-permute-start(bf16[128,512]{1,0:T(8,128)(2,1)S(1)} %copy-done), channel_id=1, source_target_pairs={{0,2},{1,3},{2,0},{3,1},{4,6},{5,7},{6,4},{7,5},{8,10},{9,11},{10,... | collective-permute-start | bytes 393224 | tf_op jit(solution)/shard_map/ppermute | solution.py:540
  14.9 7.9 %collective-permute-start.5 = (bf16[128,512]{1,0:T(8,128)(2,1)S(1)}, bf16[128,512]{1,0:T(8,128)(2,1)S(1)}, u32[]{:S(2)}, u32[]{:S(2)}) collective-permute-start(bf16[128,512]{1,0:T(8,128)(2,1)S(1)} %copy-done), channel_id=1, source_target_pairs={{0,1},{1,0},{2,3},{3,2},{4,5},{5,4},{6,7},{7,6},{8,9},{9,8},{10,11... | collective-permute-start | bytes 393224 | tf_op jit(solution)/shard_map/ppermute | solution.py:540
  15.6 7.3 %collective-permute-start.2 = (bf16[512,128]{1,0:T(8,128)(2,1)S(1)}, bf16[512,128]{1,0:T(8,128)(2,1)S(1)}, u32[]{:S(2)}, u32[]{:S(2)}) collective-permute-start(bf16[512,128]{1,0:T(8,128)(2,1)S(1)} %get-tuple-element.140.refs_2_.refs_7_), channel_id=1, source_target_pairs={{0,1},{1,0},{2,3},{3,2},{4,5},{5,4},{6,7},{7,6},{8,9},{9,8},{10,11... | collective-permute-start | bytes 393224 | tf_op jit(solution)/shard_map/ppermute | solution.py:540
  19.8 3.1 %collective-permute-start.4 = (bf16[512,128]{1,0:T(8,128)(2,1)S(1)}, bf16[512,128]{1,0:T(8,128)(2,1)S(1)}, u32[]{:S(2)}, u32[]{:S(2)}) collective-permute-start(bf16[512,128]{1,0:T(8,128)(2,1)S(1)} %relay_late.1), channel_id=1, source_target_pairs={{0,1},{1,0},{2,3},{3,2},{4,5},{5,4},{6,7},{7,6},{8,9},{9,8},{10,11... | collective-permute-start | bytes 393224 | tf_op jit(solution)/shard_map/ppermute | solution.py:540
  20.5 6.0 %collective-permute-start.1 = (bf16[512,128]{1,0:T(8,128)(2,1)S(1)}, bf16[512,128]{1,0:T(8,128)(2,1)S(1)}, u32[]{:S(2)}, u32[]{:S(2)}) collective-permute-start(bf16[512,128]{1,0:T(8,128)(2,1)S(1)} %get-tuple-element.139.refs_1_.refs_16_.refs_2_.refs_3_.refs_7_), channel_id=1, source_target_pairs={{0,2},{1,3},{2,0},{3,1},{4,6},{5,7},{6,4},{7,5},{8,10},{9,11},{10,... | collective-permute-start | bytes 393224 | tf_op jit(solution)/shard_map/ppermute | solution.py:540
  27.9 2.3 %collective-permute-start.9 = (bf16[256,512]{1,0:T(8,128)(2,1)S(1)}, bf16[256,512]{1,0:T(8,128)(2,1)S(1)}, u32[]{:S(2)}, u32[]{:S(2)}) collective-permute-start(bf16[256,512]{1,0:T(8,128)(2,1)S(1)} %get-tuple-element.150), channel_id=1, source_target_pairs={{0,1},{1,0},{2,3},{3,2},{4,5},{5,4},{6,7},{7,6},{8,9},{9,8},{10,11... | collective-permute-start | bytes 786440 | tf_op jit(solution)/shard_map/ppermute | solution.py:540
  28.0 3.7 %collective-permute-start = (bf16[512,128]{1,0:T(8,128)(2,1)S(1)}, bf16[512,128]{1,0:T(8,128)(2,1)S(1)}, u32[]{:S(2)}, u32[]{:S(2)}) collective-permute-start(bf16[512,128]{1,0:T(8,128)(2,1)S(1)} %get-tuple-element.139.refs_1_.refs_16_.refs_2_.refs_3_.refs_7_), channel_id=1, source_target_pairs={{0,1},{1,0},{2,3},{3,2},{4,5},{5,4},{6,7},{7,6},{8,9},{9,8},{10,11... | collective-permute-start | bytes 393224 | tf_op jit(solution)/shard_map/ppermute | solution.py:540
  28.4 3.2 %collective-permute-start.8 = (bf16[512,128]{1,0:T(8,128)(2,1)S(1)}, bf16[512,128]{1,0:T(8,128)(2,1)S(1)}, u32[]{:S(2)}, u32[]{:S(2)}) collective-permute-start(bf16[512,128]{1,0:T(8,128)(2,1)S(1)} %get-tuple-element.148), channel_id=1, source_target_pairs={{0,1},{1,0},{2,3},{3,2},{4,5},{5,4},{6,7},{7,6},{8,9},{9,8},{10,11... | collective-permute-start | bytes 393224 | tf_op jit(solution)/shard_map/ppermute | solution.py:540
  30.7 8.7 %collective-permute-start.11 = (bf16[256,512]{1,0:T(8,128)(2,1)S(1)}, bf16[256,512]{1,0:T(8,128)(2,1)S(1)}, u32[]{:S(2)}, u32[]{:S(2)}) collective-permute-start(bf16[256,512]{1,0:T(8,128)(2,1)S(1)} %add_late.1.refs_16_.refs_11_), channel_id=1, source_target_pairs={{0,2},{1,3},{2,0},{3,1},{4,6},{5,7},{6,4},{7,5},{8,10},{9,11},{10,... | collective-permute-start | bytes 786440 | tf_op jit(solution)/shard_map/ppermute | solution.py:540
  36.1 5.8 %collective-permute-start.10 = (bf16[256,512]{1,0:T(8,128)(2,1)S(1)}, bf16[256,512]{1,0:T(8,128)(2,1)S(1)}, u32[]{:S(2)}, u32[]{:S(2)}) collective-permute-start(bf16[256,512]{1,0:T(8,128)(2,1)S(1)} %get-tuple-element.159), channel_id=1, source_target_pairs={{0,1},{1,0},{2,3},{3,2},{4,5},{5,4},{6,7},{7,6},{8,9},{9,8},{10,11... | collective-permute-start | bytes 786440 | tf_op jit(solution)/shard_map/ppermute | solution.py:540
  41.8 4.6 %collective-permute-start.15 = (bf16[256,512]{1,0:T(8,128)(2,1)S(1)}, bf16[256,512]{1,0:T(8,128)(2,1)S(1)}, u32[]{:S(2)}, u32[]{:S(2)}) collective-permute-start(bf16[256,512]{1,0:T(8,128)(2,1)S(1)} %get-tuple-element.169.refs_2_), channel_id=1, source_target_pairs={{0,1},{1,0},{2,3},{3,2},{4,5},{5,4},{6,7},{7,6},{8,9},{9,8},{10,11... | collective-permute-start | bytes 786440 | tf_op jit(solution)/shard_map/ppermute | solution.py:540
  42.5 10.7 %collective-permute-start.12 = (bf16[256,512]{1,0:T(8,128)(2,1)S(1)}, bf16[256,512]{1,0:T(8,128)(2,1)S(1)}, u32[]{:S(2)}, u32[]{:S(2)}) collective-permute-start(bf16[256,512]{1,0:T(8,128)(2,1)S(1)} %add_early.1.refs_1_), channel_id=1, source_target_pairs={{0,2},{1,3},{2,0},{3,1},{4,6},{5,7},{6,4},{7,5},{8,10},{9,11},{10,... | collective-permute-start | bytes 786440 | tf_op jit(solution)/shard_map/ppermute | solution.py:540
  43.4 9.9 %collective-permute-start.13 = (bf16[256,512]{1,0:T(8,128)(2,1)S(1)}, bf16[256,512]{1,0:T(8,128)(2,1)S(1)}, u32[]{:S(2)}, u32[]{:S(2)}) collective-permute-start(bf16[256,512]{1,0:T(8,128)(2,1)S(1)} %get-tuple-element.166), channel_id=1, source_target_pairs={{0,4},{4,0},{8,12},{12,8},{16,20},{20,16},{24,28},{28,24},{1,5},{5... | collective-permute-start | bytes 786440 | tf_op jit(solution)/shard_map/ppermute | solution.py:540
  44.9 8.4 %collective-permute-start.14 = (bf16[256,512]{1,0:T(8,128)(2,1)S(1)}, bf16[256,512]{1,0:T(8,128)(2,1)S(1)}, u32[]{:S(2)}, u32[]{:S(2)}) collective-permute-start(bf16[256,512]{1,0:T(8,128)(2,1)S(1)} %get-tuple-element.168), channel_id=1, source_target_pairs={{0,8},{4,12},{8,0},{12,4},{16,24},{20,28},{24,16},{28,20},{1,9},{5... | collective-permute-start | bytes 786440 | tf_op jit(solution)/shard_map/ppermute | solution.py:540
  54.4 2.0 %collective-permute-start.16 = (bf16[256,512]{1,0:T(8,128)(2,1)S(1)}, bf16[256,512]{1,0:T(8,128)(2,1)S(1)}, u32[]{:S(2)}, u32[]{:S(2)}) collective-permute-start(bf16[256,512]{1,0:T(8,128)(2,1)S(1)} %get-tuple-element.175.refs_2_), channel_id=1, source_target_pairs={{0,1},{1,0},{2,3},{3,2},{4,5},{5,4},{6,7},{7,6},{8,9},{9,8},{10,11... | collective-permute-start | bytes 786440 | tf_op jit(solution)/shard_map/ppermute | solution.py:540
  54.5 6.9 %collective-permute-start.17 = (bf16[128,512]{1,0:T(8,128)(2,1)S(1)}, bf16[128,512]{1,0:T(8,128)(2,1)S(1)}, u32[]{:S(2)}, u32[]{:S(2)}) collective-permute-start(bf16[128,512]{1,0:T(8,128)(2,1)S(1)} %get-tuple-element.201), channel_id=1, source_target_pairs={{0,8},{4,12},{8,0},{12,4},{16,24},{20,28},{24,16},{28,20},{1,9},{5... | collective-permute-start | bytes 393224 | tf_op jit(solution)/shard_map/ppermute | solution.py:540
  55.8 5.6 %collective-permute-start.18 = (bf16[128,512]{1,0:T(8,128)(2,1)S(1)}, bf16[128,512]{1,0:T(8,128)(2,1)S(1)}, u32[]{:S(2)}, u32[]{:S(2)}) collective-permute-start(bf16[128,512]{1,0:T(8,128)(2,1)S(1)} %get-tuple-element.203), channel_id=1, source_target_pairs={{0,4},{4,0},{8,12},{12,8},{16,20},{20,16},{24,28},{28,24},{1,5},{5... | collective-permute-start | bytes 393224 | tf_op jit(solution)/shard_map/ppermute | solution.py:540
  64.3 16.6 %collective-permute-start.21 = (bf16[1024,512]{1,0:T(8,128)(2,1)S(1)}, bf16[1024,512]{1,0:T(8,128)(2,1)S(1)}, u32[]{:S(2)}, u32[]{:S(2)}) collective-permute-start(bf16[1024,512]{1,0:T(8,128)(2,1)S(1)} %get-tuple-element.208), channel_id=1, source_target_pairs={{0,1},{1,0},{2,3},{3,2},{4,5},{5,4},{6,7},{7,6},{8,9},{9,8},{10,11... | collective-permute-start | bytes 3145736 | tf_op jit(solution)/shard_map/ppermute | solution.py:540
  64.4 16.5 %collective-permute-start.19 = (bf16[352,512]{1,0:T(8,128)(2,1)S(1)}, bf16[352,512]{1,0:T(8,128)(2,1)S(1)}, u32[]{:S(2)}, u32[]{:S(2)}) collective-permute-start(bf16[352,512]{1,0:T(8,128)(2,1)S(1)} %get-tuple-element.205), channel_id=1, source_target_pairs={{0,4},{4,0},{8,12},{12,8},{16,20},{20,16},{24,28},{28,24},{1,5},{5... | collective-permute-start | bytes 1081352 | tf_op jit(solution)/shard_map/ppermute | solution.py:540
  66.0 14.9 %collective-permute-start.20 = (bf16[256,512]{1,0:T(8,128)(2,1)S(1)}, bf16[256,512]{1,0:T(8,128)(2,1)S(1)}, u32[]{:S(2)}, u32[]{:S(2)}) collective-permute-start(bf16[256,512]{1,0:T(8,128)(2,1)S(1)} %get-tuple-element.206.refs_3_), channel_id=1, source_target_pairs={{0,16},{4,20},{8,24},{12,28},{16,0},{20,4},{24,8},{28,12},{1,17},{... | collective-permute-start | bytes 786440 | tf_op jit(solution)/shard_map/ppermute | solution.py:540
  81.9 28.0 %collective-permute-start.29 = (bf16[1024,512]{1,0:T(8,128)(2,1)S(1)}, bf16[1024,512]{1,0:T(8,128)(2,1)S(1)}, u32[]{:S(2)}, u32[]{:S(2)}) collective-permute-start(bf16[1024,512]{1,0:T(8,128)(2,1)S(1)} %get-tuple-element.217.refs_3_), channel_id=1, source_target_pairs={{0,2},{1,3},{2,0},{3,1},{4,6},{5,7},{6,4},{7,5},{8,10},{9,11},{10,... | collective-permute-start | bytes 3145736 | tf_op jit(solution)/shard_map/ppermute | solution.py:540
  83.2 8.8 %collective-permute-start.22 = (bf16[176,512]{1,0:T(8,128)(2,1)S(1)}, bf16[176,512]{1,0:T(8,128)(2,1)S(1)}, u32[]{:S(2)}, u32[]{:S(2)}) collective-permute-start(bf16[176,512]{1,0:T(8,128)(2,1)S(1)} %get-tuple-element.210), channel_id=1, source_target_pairs={{0,8},{4,12},{8,0},{12,4},{16,24},{20,28},{24,16},{28,20},{1,9},{5... | collective-permute-start | bytes 540680 | tf_op jit(solution)/shard_map/ppermute | solution.py:540
  83.2 8.8 %collective-permute-start.23 = (bf16[128,512]{1,0:T(8,128)(2,1)S(1)}, bf16[128,512]{1,0:T(8,128)(2,1)S(1)}, u32[]{:S(2)}, u32[]{:S(2)}) collective-permute-start(bf16[128,512]{1,0:T(8,128)(2,1)S(1)} %get-tuple-element.211.refs_3_), channel_id=1, source_target_pairs={{0,8},{4,12},{8,0},{12,4},{16,24},{20,28},{24,16},{28,20},{1,9},{5... | collective-permute-start | bytes 393224 | tf_op jit(solution)/shard_map/ppermute | solution.py:540
  85.3 6.8 %collective-permute-start.24 = (bf16[128,512]{1,0:T(8,128)(2,1)S(1)}, bf16[128,512]{1,0:T(8,128)(2,1)S(1)}, u32[]{:S(2)}, u32[]{:S(2)}) collective-permute-start(bf16[128,512]{1,0:T(8,128)(2,1)S(1)} %get-tuple-element.212.refs_5_), channel_id=1, source_target_pairs={{0,4},{4,0},{8,12},{12,8},{16,20},{20,16},{24,28},{28,24},{1,5},{5... | collective-permute-start | bytes 393224 | tf_op jit(solution)/shard_map/ppermute | solution.py:540
  92.8 9.1 %collective-permute-start.26 = (bf16[256,512]{1,0:T(8,128)(2,1)S(1)}, bf16[256,512]{1,0:T(8,128)(2,1)S(1)}, u32[]{:S(2)}, u32[]{:S(2)}) collective-permute-start(bf16[256,512]{1,0:T(8,128)(2,1)S(1)} %get-tuple-element.214.refs_3_), channel_id=1, source_target_pairs={{0,4},{4,0},{8,12},{12,8},{16,20},{20,16},{24,28},{28,24},{1,5},{5... | collective-permute-start | bytes 786440 | tf_op jit(solution)/shard_map/ppermute | solution.py:540
  93.2 10.5 %collective-permute-start.27 = (bf16[256,512]{1,0:T(8,128)(2,1)S(1)}, bf16[256,512]{1,0:T(8,128)(2,1)S(1)}, u32[]{:S(2)}, u32[]{:S(2)}) collective-permute-start(bf16[256,512]{1,0:T(8,128)(2,1)S(1)} %get-tuple-element.215.refs_5_), channel_id=1, source_target_pairs={{0,8},{4,12},{8,0},{12,4},{16,24},{20,28},{24,16},{28,20},{1,9},{5... | collective-permute-start | bytes 786440 | tf_op jit(solution)/shard_map/ppermute | solution.py:540
  93.5 8.4 %collective-permute-start.25 = (bf16[176,512]{1,0:T(8,128)(2,1)S(1)}, bf16[176,512]{1,0:T(8,128)(2,1)S(1)}, u32[]{:S(2)}, u32[]{:S(2)}) collective-permute-start(bf16[176,512]{1,0:T(8,128)(2,1)S(1)} %get-tuple-element.213.refs_1_), channel_id=1, source_target_pairs={{0,16},{4,20},{8,24},{12,28},{16,0},{20,4},{24,8},{28,12},{1,17},{... | collective-permute-start | bytes 540680 | tf_op jit(solution)/shard_map/ppermute | solution.py:540
  104.5 5.4 %collective-permute-start.28 = (bf16[160,512]{1,0:T(8,128)(2,1)S(1)}, bf16[160,512]{1,0:T(8,128)(2,1)S(1)}, u32[]{:S(2)}, u32[]{:S(2)}) collective-permute-start(bf16[160,512]{1,0:T(8,128)(2,1)S(1)} %get-tuple-element.216.refs_1_), channel_id=1, source_target_pairs={{0,8},{4,12},{8,0},{12,4},{16,24},{20,28},{24,16},{28,20},{1,9},{5... | collective-permute-start | bytes 491528 | tf_op jit(solution)/shard_map/ppermute | solution.py:540
  110.8 3.7 %collective-permute-start.30 = (bf16[1024,512]{1,0:T(8,128)(2,1)S(1)}, bf16[1024,512]{1,0:T(8,128)(2,1)S(1)}, u32[]{:S(2)}, u32[]{:S(2)}) collective-permute-start(bf16[1024,512]{1,0:T(8,128)(2,1)S(1)} %get-tuple-element.218.refs_7_), channel_id=1, source_target_pairs={{0,1},{1,0},{2,3},{3,2},{4,5},{5,4},{6,7},{7,6},{8,9},{9,8},{10,11... | collective-permute-start | bytes 3145736 | tf_op jit(solution)/shard_map/ppermute | solution.py:540
  110.9 10.1 %collective-permute-start.34 = (bf16[320,512]{1,0:T(8,128)(2,1)S(1)}, bf16[320,512]{1,0:T(8,128)(2,1)S(1)}, u32[]{:S(2)}, u32[]{:S(2)}) collective-permute-start(bf16[320,512]{1,0:T(8,128)(2,1)S(1)} %get-tuple-element.225.refs_1_), channel_id=1, source_target_pairs={{0,4},{4,0},{8,12},{12,8},{16,20},{20,16},{24,28},{28,24},{1,5},{5... | collective-permute-start | bytes 983048 | tf_op jit(solution)/shard_map/ppermute | solution.py:540
  112.6 5.6 %collective-permute-start.33 = (f32[16,512]{1,0:T(8,128)S(1)}, f32[16,512]{1,0:T(8,128)S(1)}, u32[]{:S(2)}, u32[]{:S(2)}) collective-permute-start(f32[16,512]{1,0:T(8,128)S(1)} %get-tuple-element.222.refs_0_), channel_id=1, source_target_pairs={{0,3},{1,2},{2,1},{3,0},{4,7},{5,6},{6,5},{7,4},{8,11},{9,10},{10,... | collective-permute-start | bytes 98312 | tf_op jit(solution)/shard_map/ppermute | solution.py:540
  113.2 5.0 %collective-permute-start.32 = (f32[16,512]{1,0:T(8,128)S(1)}, f32[16,512]{1,0:T(8,128)S(1)}, u32[]{:S(2)}, u32[]{:S(2)}) collective-permute-start(f32[16,512]{1,0:T(8,128)S(1)} %get-tuple-element.222.refs_0_), channel_id=1, source_target_pairs={{0,2},{1,3},{2,0},{3,1},{4,6},{5,7},{6,4},{7,5},{8,10},{9,11},{10,... | collective-permute-start | bytes 98312 | tf_op jit(solution)/shard_map/ppermute | solution.py:540
  114.4 3.8 %collective-permute-start.31 = (f32[16,512]{1,0:T(8,128)S(1)}, f32[16,512]{1,0:T(8,128)S(1)}, u32[]{:S(2)}, u32[]{:S(2)}) collective-permute-start(f32[16,512]{1,0:T(8,128)S(1)} %get-tuple-element.222.refs_0_), channel_id=1, source_target_pairs={{0,1},{1,0},{2,3},{3,2},{4,5},{5,4},{6,7},{7,6},{8,9},{9,8},{10,11... | collective-permute-start | bytes 98312 | tf_op jit(solution)/shard_map/ppermute | solution.py:540
  118.8 0.7 copy-start.1

commit v2 on v1

v2 whole, which is shorter than its diff:
```python
import functools

import jax
import jax.numpy as jnp
import numpy as np
from jax import lax
from jax.experimental import pallas as pl
from jax.experimental.pallas import tpu as pltpu
from jax.sharding import PartitionSpec as P

HEAD = 64
BF = jnp.bfloat16
FL = jnp.float32
eps_norm = 1e-05
neg_fill = -1e30
VMEM_LIMIT = 24 * 1024 * 1024
small = 16
UNROLL = [2, 2, 2]
STEP_COST = 5e9


def mm(left, right):
    return lax.dot_general(left, right, (((1,), (0,)), ((), ())), preferred_element_type=FL)


def mm_t(left, right):
    return lax.dot_general(left, right, (((1,), (1,)), ((), ())), preferred_element_type=FL)


def t_mm(left, right):
    return lax.dot_general(left, right, (((0,), (0,)), ((), ())), preferred_element_type=FL)


def norm_parts(rows):
    center = rows - jnp.mean(rows, axis=-1, keepdims=True)
    spread = jnp.mean(center * center, axis=-1, keepdims=True)
    inv = lax.rsqrt(spread + eps_norm)
    return center * inv, inv


def norm_back(scaled, unit, inv):
    flat = jnp.mean(scaled, axis=-1, keepdims=True)
    along = jnp.mean(scaled * unit, axis=-1, keepdims=True)
    return inv * (scaled - flat - unit * along)


def head_lanes(wide, h):
    lane = lax.broadcasted_iota(jnp.int32, (1, wide), 1)
    return (lane >= h * HEAD) & (lane < (h + 1) * HEAD)


def col_sum(rows):
    return jnp.sum(rows, axis=0, keepdims=True)


def fine_mm(left, right, product):
    high = left.astype(BF)
    low = (left - high.astype(FL)).astype(BF)
    return product(high, right) + product(low, right)


def norm_sums(weighted, shift_sum, gain, shift):
    return (weighted - shift * shift_sum) / gain, shift_sum


def loop(count, body, unroll=1):
    def step(i, carry):
        body(i)
        return carry

    lax.fori_loop(0, count, step, 0, unroll=unroll)


def rows_of(i, size):
    return pl.ds(pl.multiple_of(i * size, size), size)


def by_core(core, part, keep_ref, send_ref, rows, at):
    @pl.when(core == part)
    def _():
        keep_ref[at, :] = rows

    @pl.when(core != part)
    def _():
        send_ref[at, :] = rows


def added(left, right):
    return (left.astype(FL) + right.astype(FL)).astype(BF)


def make_queries(normed, spots, at, refs, heads):
    w_ref, wpos_ref, bu, bv, sin_ref, cos_ref, qb_ref, qv_ref = refs
    wide = heads * HEAD
    scale = HEAD ** (-0.5)
    query = mm(normed, w_ref[:, :wide]).astype(BF).astype(FL)
    query_u = (query + bu).astype(BF).astype(FL) * scale
    query_v = (query + bv).astype(BF).astype(FL) * scale
    qv_ref[at, :] = query_v.astype(BF)
    sin = sin_ref[spots, :]
    cos = cos_ref[spots, :]
    half = sin.shape[1]
    for h in range(heads):
        lanes = head_lanes(wide, h)
        qb_ref[h, at, :wide] = jnp.where(lanes, query_u, 0.0).astype(BF)
        coef = mm_t(jnp.where(lanes, query_v, 0.0).astype(BF), wpos_ref[...])
        on_sin, on_cos = coef[:, :half], coef[:, half:]
        qb_ref[h, at, wide : wide + half] = (on_sin * sin + on_cos * cos).astype(BF)
        qb_ref[h, at, wide + half :] = (on_cos * sin - on_sin * cos).astype(BF)


def attend(first, block, mem_len, heads, count, qb_ref, kt_ref, v_ref, probs_ref, ctx_ref, ctx_scr):
    wide = heads * HEAD
    rows = qb_ref.shape[1]
    for part in range(rows // block):
        at = slice(part * block, (part + 1) * block)
        start = first + part * block
        seen = mem_len + start + block

        def one_head(h):
            scores = mm_t(qb_ref[h, at, :], kt_ref[:seen, :])
            query_pos = start + lax.broadcasted_iota(jnp.int32, (block, 1), 0)
            limit = jnp.minimum(query_pos, count - 1)
            key_pos = lax.broadcasted_iota(jnp.int32, (block, seen - mem_len), 1)
            scores = jnp.concatenate(
                [scores[:, :mem_len], jnp.where(key_pos <= limit, scores[:, mem_len:], neg_fill)], axis=1
            )
            expo = jnp.exp(scores - jnp.max(scores, axis=-1, keepdims=True))
            probs = (expo * (1.0 / jnp.sum(expo, axis=-1, keepdims=True))).astype(BF)
            probs_ref[h, at, :seen] = probs
            found = mm(probs, v_ref[:seen, :])
            ctx_scr[...] = jnp.where(head_lanes(wide, h), found, ctx_scr[...])

        loop(heads, one_head, UNROLL[2])
        ctx_ref[at, :] = ctx_scr[...].astype(BF)


def front_kernel(
    block, heads,
    place_ref, x_in, mem_in, g_in, wq_in, wk_in, wv_in, wpos_in, wup_in, wdown_in, wout_in,
    shift_in, gain_in, fgain_in, fshift_in, upb_in, downb_in, bu_in, bv_in, table_in, sin_in, cos_in,
    x_ref, g_ref, w_ref, wpos_ref, wup_ref, wdown_ref, wout_ref, shift_ref, gain_ref, fgain_ref, fshift_ref, upb_ref,
    downb_ref, sin_ref, cos_ref, bias_ref, normed_ref, kt_ref, v_ref,
    mem_ref, bu_ref, bv_ref, sems,
):
    wide = heads * HEAD
    mem_len = mem_in.shape[0]
    seq_len = x_in.shape[0]
    todo = [
        (mem_in, mem_ref), (gain_in, gain_ref), (shift_in, shift_ref), (wk_in, w_ref.at[:, wide : 2 * wide]),
        (wv_in, w_ref.at[:, 2 * wide :]), (x_in, x_ref), (wq_in, w_ref.at[:, :wide]), (bu_in, bu_ref), (bv_in, bv_ref),
        (wpos_in, wpos_ref), (sin_in, sin_ref), (cos_in, cos_ref), (table_in, kt_ref.at[:, wide:]),
        (wout_in, wout_ref), (wup_in, wup_ref), (wdown_in, wdown_ref), (g_in, g_ref), (fgain_in, fgain_ref),
        (fshift_in, fshift_ref), (upb_in, upb_ref), (downb_in, downb_ref),
    ]
    copies = [pltpu.make_async_copy(src, dst, sems.at[i]) for i, (src, dst) in enumerate(todo)]
    for copy in copies:
        copy.start()
    for copy in copies[:5]:
        copy.wait()

    def project(rows_ref, at, to):
        unit, _ = norm_parts(rows_ref[at, :].astype(FL))
        normed = (unit * gain_ref[...] + shift_ref[...]).astype(BF)
        normed_ref[to, :] = normed
        pair = mm(normed, w_ref[:, wide:]).astype(BF)
        kt_ref[to, :wide] = pair[:, :wide]
        v_ref[to, :] = pair[:, wide:]

    def some_memory(i):
        project(mem_ref, rows_of(i, block), rows_of(i, block))

    def some_rows(i):
        project(x_ref, rows_of(i, block), rows_of(i + mem_len // block, block))

    loop(mem_len // block, some_memory, UNROLL[0])
    for copy in copies[5:7]:
        copy.wait()
    loop(seq_len // block, some_rows, UNROLL[0])
    for copy in copies[7:]:
        copy.wait()
    bias_ref[0:1, :] = jnp.concatenate([bu_ref[h : h + 1, :] for h in range(heads)], axis=1)
    bias_ref[1:2, :] = jnp.concatenate([bv_ref[h : h + 1, :] for h in range(heads)], axis=1)


def attend_kernel(
    first, block, heads, mem_len,
    count_ref, normed_ref, kt_ref, v_ref, w_ref, wpos_ref, bias_ref, sin_ref, cos_ref,
    qb_ref, qv_ref, probs_ref, ctx_ref, ctx_scr,
):
    def some_queries(i):
        at = rows_of(i, block)
        spots = rows_of(i + first // block, block)
        make_queries(
            normed_ref[rows_of(i + (mem_len + first) // block, block), :], spots, at,
            (w_ref, wpos_ref, bias_ref[0:1, :], bias_ref[1:2, :], sin_ref, cos_ref, qb_ref, qv_ref), heads,
        )

    loop(qb_ref.shape[1] // block, some_queries, UNROLL[1])
    attend(first, block, mem_len, heads, count_ref[0], qb_ref, kt_ref, v_ref, probs_ref, ctx_ref, ctx_scr)


def relay_kernel(ctx_ref, w_ref, out_ref):
    size, wide = ctx_ref.shape
    out_ref[:size, :] = ctx_ref[...]
    for k in range(w_ref.shape[1] // wide):
        at = size + k * w_ref.shape[0]
        out_ref[at : at + w_ref.shape[0], :] = w_ref[:, k * wide : (k + 1) * wide]


def ffn_rows_kernel(
    first, block, roles, relay,
    place_ref, x_ref, c0_ref, c1_ref, c2_ref, c3_ref, o0_ref, o1_ref, o2_ref, o3_ref, gain_ref, shift_ref, up_ref,
    upb_ref, down_ref, g_ref, *refs,
):
    if relay:
        ctx_in, *refs = refs
        *refs, ctx_out = refs
        ctx_out[...] = ctx_in[...]
    core = place_ref[0]
    wide = c0_ref.shape[1]
    size = c0_ref.shape[0]
    blocks = [o3_ref[at : at + wide, :] for at in range(o3_ref.shape[0] - size, o3_ref.shape[0], wide)]
    o3 = jnp.concatenate(blocks, axis=1)
    for role, hidden_ref, normed_ref, activ_ref, gpre_ref, vec_ref, share_ref in zip(roles, *[iter(refs)] * 6):
        half = core if role == "keep" else 1 - core
        at = rows_of(half, block)
        spots = rows_of(half + first // block, block)
        attended = mm(c0_ref[at, :], o0_ref[...]) + mm(c1_ref[at, :], o1_ref[...])
        attended = attended + (mm(c2_ref[at, :], o2_ref[...]) + mm(c3_ref[at, :], o3))
        hidden = x_ref[spots, :].astype(FL) + attended
        hidden_ref[...] = hidden
        unit, _ = norm_parts(hidden)
        normed = (unit * gain_ref[...] + shift_ref[...]).astype(BF)
        normed_ref[...] = normed
        pre = mm(normed, up_ref[...]) + upb_ref[...]
        cdf = 0.5 + 0.5 * lax.erf(pre * np.float32(0.5**0.5))
        activ_ref[...] = (pre * cdf).astype(BF)
        slope = cdf + pre * jnp.exp(-0.5 * pre * pre) * np.float32((2 * np.pi) ** -0.5)
        grad_pre = (mm_t(g_ref[spots, :], down_ref[...]) * slope).astype(BF)
        gpre_ref[...] = grad_pre
        back = mm_t(grad_pre, up_ref[...])
        share_ref[...] = back.astype(BF)
        vec_ref[0:1, :] = col_sum(back * unit)
        vec_ref[1:2, :] = col_sum(back)


def ffn_weights(first, place_ref, g_ref, down_ref, saved, shares):
    core = place_ref[0]
    block = shares[0].shape[0]
    total = None
    for role, (normed_ref, activ_ref, gpre_ref, vec_ref), share_ref in zip(("send", "keep"), saved, shares):
        half = core if role == "keep" else 1 - core
        grads = g_ref[rows_of(half + first // block, block), :]
        activ = activ_ref[...]
        share_ref[...] = mm(activ, down_ref[...]).astype(BF)
        vecs = jnp.concatenate([vec_ref[...], col_sum(grads.astype(FL))], axis=0)
        new = [t_mm(normed_ref[...], gpre_ref[...]), t_mm(activ, grads), vecs, col_sum(gpre_ref[...].astype(FL))]
        total = new if total is None else [old + part for old, part in zip(total, new)]
    return total


def ffn_late_kernel(first, place_ref, g_ref, down_ref, *refs):
    found = ffn_weights(first, place_ref, g_ref, down_ref, (refs[:4], refs[4:8]), refs[8:10])
    for ref, value in zip(refs[10:], found):
        ref[...] = value


def ffn_early_kernel(first, place_ref, g_ref, down_ref, *refs):
    found = ffn_weights(first, place_ref, g_ref, down_ref, (refs[:4], refs[4:8]), refs[12:14])
    up, down, vec, upb = (value + old[...] for value, old in zip(found, refs[8:12]))
    up_keep, up_send, down_keep, down_send, vec_ref, upb_out = refs[14:]
    halve(place_ref, 0, up.astype(BF), up_keep, up_send)
    halve(place_ref, 1, down.astype(BF), down_keep, down_send)
    vec_ref[...] = vec
    upb_out[...] = upb


def back_rows(
    first, block, heads, mem_len, place_ref, hid_s, hid_k, mine_ref, other_ref, g_ref, fgain_ref, wout_ref, ctx_ref,
    probs_ref, qb_ref, qv_ref, kt_ref, v_ref, wpos_ref, sin_ref, cos_ref,
    gh_ref, dk_ref, dv_ref, dpos_ref, dout_ref, dq_ref, bias_ref, grad_u, grad_v,
):
    core = place_ref[0]
    wide = heads * HEAD
    half = sin_ref.shape[1]
    scale = HEAD ** (-0.5)
    for part in range(2):
        at = slice(part * block, (part + 1) * block)
        spots = slice(first + part * block, first + (part + 1) * block)
        seen = mem_len + first + (part + 1) * block
        unit, inv = norm_parts(jnp.where(core == part, hid_k[...], hid_s[...]))
        summed = jnp.where(core == part, mine_ref[...].astype(FL), other_ref[...].astype(FL))
        grad_hidden = g_ref[spots, :].astype(FL) + norm_back(summed * fgain_ref[...], unit, inv)
        gh_ref[at, :] = grad_hidden
        gh = grad_hidden.astype(BF)
        context = ctx_ref[at, :]
        grad_context = mm_t(gh, wout_ref[...]).astype(BF).astype(FL)
        dout_ref[...] += t_mm(context, gh)
        along_context = grad_context * context.astype(FL)

        def one_head(h):
            lanes = head_lanes(wide, h)
            delta = jnp.sum(jnp.where(lanes, along_context, 0.0), axis=-1, keepdims=True)
            own = jnp.where(lanes, grad_context, 0.0).astype(BF)
            probs = probs_ref[h, at, :seen]
            grad_score = (probs.astype(FL) * (mm_t(own, v_ref[:seen, :]) - delta)).astype(BF)
            dv_ref[:, :seen] += t_mm(own, probs)
            dk_ref[:, :seen] += t_mm(qb_ref[h, at, :wide], grad_score)
            spread = mm(grad_score, kt_ref[:seen, :])
            grad_u[...] = jnp.where(lanes, spread[:, :wide], grad_u[...])
            sin = sin_ref[spots, :]
            cos = cos_ref[spots, :]
            on_cos, on_sin = spread[:, wide : wide + half], spread[:, wide + half :]
            turned = jnp.concatenate(
                [(on_cos * sin - on_sin * cos).astype(BF), (on_cos * cos + on_sin * sin).astype(BF)], axis=1
            )
            grad_v[...] = jnp.where(lanes, mm(turned, wpos_ref[...]), grad_v[...])
            query_v = jnp.where(lanes, qv_ref[at, :].astype(FL), 0.0).astype(BF)
            dpos_ref[...] += t_mm(query_v, turned)

        loop(heads, one_head, 2)
        bias_ref[0:1, :] += col_sum(grad_u[...]) * scale
        bias_ref[1:2, :] += col_sum(grad_v[...]) * scale
        dq_ref[at, :] = ((grad_u[...] + grad_v[...]) * scale).astype(BF)


def back_share(cols, dq_rows, dk_ref, dv_ref, weights):
    pair = [dk_ref[:, cols].T.astype(BF), dv_ref[:, cols].T.astype(BF)]
    return mm_t(jnp.concatenate([dq_rows, *pair], axis=1), weights).astype(BF)


def back_late_kernel(
    first, block, heads, mem_len,
    place_ref, hid_s, hid_k, mine_ref, other_ref, g_ref, fgain_ref, wout_ref, ctx_ref, probs_ref, qb_ref, qv_ref, kt_ref,
    v_ref, wpos_ref, sin_ref, cos_ref, w_ref,
    gh_ref, dk_ref, dv_ref, dpos_ref, dout_ref, dq_ref, bias_ref, share_ref, grad_u, grad_v,
):
    for ref in (dk_ref, dv_ref, dpos_ref, dout_ref, bias_ref):
        ref[...] = jnp.zeros(ref.shape, FL)
    back_rows(
        first, block, heads, mem_len, place_ref, hid_s, hid_k, mine_ref, other_ref, g_ref, fgain_ref, wout_ref, ctx_ref,
        probs_ref, qb_ref, qv_ref, kt_ref, v_ref, wpos_ref, sin_ref, cos_ref,
        gh_ref, dk_ref, dv_ref, dpos_ref, dout_ref, dq_ref, bias_ref, grad_u, grad_v,
    )
    for part in range(2):
        at = slice(part * block, (part + 1) * block)
        cols = slice(mem_len + first + part * block, mem_len + first + (part + 1) * block)
        share_ref[at, :] = back_share(cols, dq_ref[at, :], dk_ref, dv_ref, w_ref[...])


def back_early_kernel(
    first, block, heads, mem_len,
    place_ref, hid_s, hid_k, mine_ref, other_ref, g_ref, fgain_ref, wout_ref, ctx_ref, probs_ref, qb_ref, qv_ref, kt_ref,
    v_ref, wpos_ref, sin_ref, cos_ref, dk_in, dv_in, dpos_in, dout_in, bias_in,
    gh_ref, dk_ref, dv_ref, dpos_ref, dout_ref, dq_ref, bias_ref, grad_u, grad_v,
):
    for ref, old in ((dk_ref, dk_in), (dv_ref, dv_in), (dpos_ref, dpos_in), (dout_ref, dout_in), (bias_ref, bias_in)):
        ref[...] = old[...]
    back_rows(
        first, block, heads, mem_len, place_ref, hid_s, hid_k, mine_ref, other_ref, g_ref, fgain_ref, wout_ref, ctx_ref,
        probs_ref, qb_ref, qv_ref, kt_ref, v_ref, wpos_ref, sin_ref, cos_ref,
        gh_ref, dk_ref, dv_ref, dpos_ref, dout_ref, dq_ref, bias_ref, grad_u, grad_v,
    )


def back_end_kernel(
    first, block, heads, mem_len, n_tensor, size,
    place_ref, w_ref, normed_ref, shift_ref, gain_ref, dk_ref, dv_ref, dpos_ref, dout_ref, dq_ref, bias_ref, dq_in,
    late_ref, fvec_ref, upb_ref, e_send, e_keep, l_send, l_keep, up_keep, up_got, down_keep, down_got,
    keep_ref, send_ref, a_keep, a_send, f_ref,
):
    half = up_keep.shape[0]
    f_ref[:half, :] = added(up_keep[...], up_got[...])
    f_ref[half:, :] = added(down_keep[...], down_got[...])
    wide = heads * HEAD
    core = place_ref[0]
    for part in range(2):
        at = slice(part * block, (part + 1) * block)
        by_core(core, part, keep_ref, send_ref, late_ref[at, :], slice(block, 2 * block))
    keep_ref[2 * block : 3 * block, :] = e_keep[...]
    keep_ref[3 * block :, :] = l_keep[...]
    send_ref[2 * block : 3 * block, :] = e_send[...]
    send_ref[3 * block :, :] = l_send[...]
    normed = normed_ref[...]
    width = normed.shape[1]
    dq_all = jnp.concatenate([dq_ref[...], dq_in[...]], axis=0)
    dk, dv = dk_ref[...].astype(BF), dv_ref[...].astype(BF)
    grads = [t_mm(dq_all, normed[mem_len:]), mm(dk, normed), mm(dv, normed), dpos_ref[...], dout_ref[...]]
    grads = jnp.concatenate(grads, axis=0)
    turned = w_ref[...].astype(FL).T
    shift_sum = fine_mm(col_sum(dq_all.astype(FL)), turned[:wide].astype(BF), mm)
    for i, part in enumerate((dk, dv)):
        shift_sum += col_sum(turned[(i + 1) * wide : (i + 2) * wide] * jnp.sum(part.astype(FL), axis=1, keepdims=True))
    sums = norm_sums(col_sum(turned * grads[: 3 * wide]), shift_sum, gain_ref[...], shift_ref[...])
    for part in range(2):
        at = slice(part * block, (part + 1) * block)
        cols = slice(mem_len + first + part * block, mem_len + first + (part + 1) * block)
        back = back_share(cols, dq_ref[at, :], dk_ref, dv_ref, w_ref[...])
        by_core(core, part, keep_ref, send_ref, back, slice(0, block))
    wider = jnp.zeros((1, width - wide), FL)
    rows = [*sums, fvec_ref[0:2, :], fvec_ref[2:3, :] * (1.0 / n_tensor)]
    rows += [jnp.concatenate([bias_ref[i : i + 1, :], wider], axis=1) for i in range(2)]
    for i in range(upb_ref.shape[1] // width):
        rows.append(upb_ref[:, i * width : (i + 1) * width])
    rows.append(jnp.zeros((small - 7 - upb_ref.shape[1] // width, width), FL))
    rows = jnp.concatenate(rows, axis=0).astype(BF)
    step = size + small
    for d in range(2 * a_keep.shape[0] // step):
        here = max(0, min(size, 5 * wide - d * size))
        piece = [grads[d * size : d * size + here].astype(BF)] if here else []
        piece += [jnp.zeros((size - here, width), BF)] if here < size else []
        piece = jnp.concatenate([*piece, rows], axis=0)
        per_half = a_keep.shape[0] // step
        at = slice(d % per_half * step, (d % per_half + 1) * step)
        by_core(place_ref[1] & 1, d // per_half, a_keep, a_send, piece, at)


def last_kernel(
    wide, heads, n_tensor, place_ref, a_mine, a_got, down_mine, down_got, *refs
):
    totals, refs = refs[:n_tensor], refs[n_tensor:]
    down_out, outs, smalls = refs[0], refs[1:6], refs[6:14]
    down_scr, rows_scr, turned_scr, sems = refs[14:]
    copies = []

    def send(src, dst):
        copies.append(pltpu.make_async_copy(src, dst, sems.at[len(copies)]))
        copies[-1].start()

    join(place_ref, 1, down_mine, down_got, down_scr)
    send(down_scr, down_out)
    join(place_ref, 0, a_mine, a_got, rows_scr)
    send(rows_scr.at[pl.ds(4 * wide, wide), :], outs[4])
    for i in range(4):
        turned_scr[i] = rows_scr[i * wide : (i + 1) * wide, :].T
        send(turned_scr.at[i], outs[i])
    mine = totals[0]
    total = mine[...]
    for other in totals[1:]:
        total = total + other[...]
    for i in range(5):
        smalls[i][...] = total[i : i + 1, :]
    for k in range(2):
        for h in range(heads):
            smalls[5 + k][h : h + 1, :] = mine[5 + k : 6 + k, h * HEAD : (h + 1) * HEAD]
    width = mine.shape[1]
    for i in range(smalls[7].shape[1] // width):
        smalls[7][:, i * width : (i + 1) * width] = mine[7 + i : 8 + i, :]
    for copy in copies:
        copy.wait()


def finish_kernel(
    block, place_ref, x_ref, gain_ref, gh_e, gh_l, hid_es, hid_ek, hid_ls, hid_lk, mine_ref, other_ref, bias_ref, up_ref,
    out_ref, grad_ref, up_out, out_scr, grad_scr, up_scr, sems,
):
    core = place_ref[0]
    copies = []

    def send(src, dst):
        copies.append(pltpu.make_async_copy(src, dst, sems.at[len(copies)]))
        copies[-1].start()

    up_scr[...] = up_ref[...].astype(FL)
    send(up_scr, up_out)
    for first, gh_ref, hid_s, hid_k in ((0, gh_e, hid_es, hid_ek), (1, gh_l, hid_ls, hid_lk)):
        for part in range(2):
            at = slice(part * block, (part + 1) * block)
            spots = pl.ds((2 * first + part) * block, block)

            def summed(group):
                rows = slice(group * block, (group + 1) * block)
                return jnp.where(core == part, mine_ref[rows, :].astype(FL), other_ref[rows, :].astype(FL))

            hidden = jnp.where(core == part, hid_k[...], hid_s[...])
            out_scr[spots, :] = (hidden + summed(first + 2) + bias_ref[...]).astype(BF)
            send(out_scr.at[spots, :], out_ref.at[spots, :])
            unit, inv = norm_parts(x_ref[spots, :].astype(FL))
            grad_scr[spots, :] = (gh_ref[at, :] + norm_back(summed(first) * gain_ref[...], unit, inv)).astype(BF)
            send(grad_scr.at[spots, :], grad_ref.at[spots, :])
    for copy in copies:
        copy.wait()


def halve(place_ref, bit, total, keep_ref, send_ref):
    size = total.shape[0] // 2
    high = (place_ref[1] >> bit) & 1
    by_core(high, 0, keep_ref, send_ref, total[:size], slice(None))
    by_core(high, 1, keep_ref, send_ref, total[size:], slice(None))


def join(place_ref, bit, mine_ref, got_ref, out_ref):
    size = mine_ref.shape[0]
    high = ((place_ref[1] >> bit) & 1) == 1
    mine, got = mine_ref[...].astype(FL), got_ref[...].astype(FL)
    out_ref[:size, :] = jnp.where(high, got, mine).astype(out_ref.dtype)
    out_ref[size:, :] = jnp.where(high, mine, got).astype(out_ref.dtype)


SMEM = pl.BlockSpec(memory_space=pltpu.SMEM)
SPECS = {s: pl.BlockSpec(memory_space=s) for s in (pltpu.VMEM, pltpu.HBM)}


def call(kernel, outs, args, name, flops, scratch=(), space=pltpu.VMEM, after=(), far=0):
    count, extra = len(args), len(after)

    def body(*refs):
        kernel(*refs[:count], *refs[count + extra :])

    specs = [SMEM if a.dtype == jnp.int32 else SPECS[space] for a in args]
    specs += [pl.BlockSpec(memory_space=pl.ANY)] * extra
    if space is pltpu.HBM:
        args = [a if a.dtype == jnp.int32 else pltpu.with_memory_space_constraint(a, space) for a in args]
    return pl.pallas_call(
        body,
        out_shape=[pltpu.HBM(s, d) if i < far else jax.ShapeDtypeStruct(s, d) for i, (s, d) in enumerate(outs)],
        in_specs=specs,
        out_specs=[SPECS[pltpu.HBM]] * far + [SPECS[pltpu.VMEM]] * (len(outs) - far),
        scratch_shapes=scratch,
        compiler_params=pltpu.CompilerParams(vmem_limit_bytes=VMEM_LIMIT),
        cost_estimate=pl.CostEstimate(flops=int(flops), bytes_accessed=1, transcendentals=0),
        name=name,
    )(*args, *after)


def swap(rows, axis, size, bit):
    return lax.ppermute(rows, axis, [(i, i ^ bit) for i in range(size)])


def work_kernel(jobs, place_ref, *refs):
    ins, outs = refs[: 2 * len(jobs)], list(refs[2 * len(jobs) :])
    for i, (kind, bit) in enumerate(jobs):
        mine, got = ins[2 * i : 2 * i + 2]
        if kind == "halve":
            halve(place_ref, bit, added(mine[...], got[...]), outs.pop(0), outs.pop(0))
        elif kind == "join":
            join(place_ref, bit, mine, got, outs.pop(0))
        elif kind == "sum":
            outs.pop(0)[...] = added(mine[...], got[...])
        elif kind == "copy":
            outs.pop(0)[...] = mine[...]
        else:
            total = mine[...].astype(FL) + got[...].astype(FL)
            size = outs[0].shape[0]
            for part in (total[:size], total[size:]):
                out = outs.pop(0)
                out[...] = part.astype(out.dtype)


def work(place, jobs, name, after=(), cost=1):
    outs = []
    for kind, _, mine, _ in jobs:
        size, width = mine.shape
        outs += {
            "halve": [((size // 2, width), BF)] * 2,
            "two": [((size // 2, width), BF)] * 2,
            "join": [((2 * size, width), BF)],
            "sum": [((size, width), BF)],
            "copy": [((size, width), mine.dtype)],
            "split": [((size - small, width), BF), ((small, width), FL)],
        }[kind]
    args = [a for job in jobs for a in job[2:]]
    return list(
        call(functools.partial(work_kernel, [job[:2] for job in jobs]), outs, (place, *args), name, cost, after=after)
    )


class Chain:
    def __init__(self, rows, send, bits, n_dp, end="sum"):
        self.rows, self.send, self.bits, self.n_dp, self.end, self.done = rows, send, bits, n_dp, end, 0
        self.start()

    def bit(self):
        return self.bits[min(self.done, 2 * len(self.bits) - 2 - self.done)]

    def start(self):
        self.got = swap(self.send, "dp", self.n_dp, 1 << self.bit())

    def left(self):
        return 2 * len(self.bits) - 2 - self.done

    def job(self):
        last = len(self.bits) - 1
        if self.done < last - 1:
            kind, bit = "halve", self.bits[self.done + 1]
        elif self.done <= last:
            kind, bit = (self.end if self.done == last else "sum"), 0
        else:
            kind, bit = "join", self.bit()
        return kind, bit, self.rows, self.got

    def take(self, results):
        kind = self.job()[0]
        self.rows = self.send = results.pop(0)
        if kind == "halve":
            self.send = results.pop(0)
        self.done += 1
        if self.left() >= 0:
            self.start()


def cores(rows, n_tensor):
    return swap(rows, "tensor", n_tensor, 1)


def other_chips(rows, n_tensor):
    return swap(rows, "tensor", n_tensor, 2)


def chips(rows, n_tensor):
    return rows, other_chips(rows, n_tensor)


def split_at(*parts):
    (items,) = (p for p in parts if not isinstance(p, int))
    places = [0, *(p for p in parts if isinstance(p, int)), len(items)]
    return [items[start:end] for start, end in zip(places, places[1:])]


def per_device(n_dp, n_tensor, *args):
    (inputs, memory, counts, attn_gain, attn_shift, w_query, w_key, w_value, w_pos, bias_u, bias_v, w_out,
     ffn_gain, ffn_shift, w_up, up_bias, w_down, down_bias, out_grad) = args
    _, seq_len, width = inputs.shape
    mem_len = memory.shape[1]
    total = mem_len + seq_len
    wide = w_query.shape[1]
    heads = wide // HEAD
    ff = w_up.shape[1]
    chunk = seq_len // 2
    block = chunk // 2
    late = chunk
    place = jnp.stack([lax.axis_index("tensor") & 1, lax.axis_index("dp")]).astype(jnp.int32)
    x, mem, g = inputs[0], memory[0], out_grad[0]
    row = lambda v: v.reshape(1, -1)

    freq = 1.0 / 10000.0 ** (np.arange(0, width, 2, dtype=np.float64) / width)
    key_phase = np.arange(total)[:, None] * freq[None, :]
    table = jnp.asarray(np.concatenate([np.cos(key_phase), np.sin(key_phase)], axis=1).astype(BF))
    row_phase = (np.arange(seq_len) + mem_len)[:, None] * freq[None, :]
    sin = jnp.asarray(np.sin(row_phase).astype(np.float32))
    cos = jnp.asarray(np.cos(row_phase).astype(np.float32))

    outs_of = [w_out, cores(w_out, n_tensor), swap(w_out, "tensor", n_tensor, 2)]

    def attend_outs(seen):
        return [((heads, chunk, wide + width), BF), ((chunk, wide), BF), ((heads, chunk, seen), BF), ((chunk, wide), BF)]

    ctx_scr = pltpu.VMEM((block, wide), FL)
    vectors = [row(v) for v in (attn_shift, attn_gain, ffn_gain, ffn_shift, up_bias, down_bias)]
    copied = [
        *[(a.shape, BF) for a in (x, g)], ((width, 3 * wide), BF), *[(a.shape, BF) for a in (w_pos, w_up, w_down, w_out)],
        *[(a.shape, FL) for a in (*vectors, sin, cos)], ((2, wide), FL),
    ]
    found = call(
        functools.partial(front_kernel, block, heads),
        [*copied, ((total, width), BF), ((total, wide + width), BF), ((total, wide), BF)],
        (place, x, mem, g, w_query, w_key, w_value, w_pos, w_up, w_down, w_out, *vectors, bias_u, bias_v, table, sin,
         cos), "front", 1,
        [pltpu.VMEM(mem.shape, BF)] + [pltpu.VMEM(bias_u.shape, FL)] * 2 + [pltpu.SemaphoreType.DMA((21,))], pltpu.HBM,
    )
    x, g, weights, w_pos, w_up, w_down, w_out = found[:7]
    attn_shift, attn_gain, ffn_gain, ffn_shift, up_bias, down_bias, sin, cos, biases, normed, keys, values = found[7:]

    def attend_chunk(first, name, cost, after):
        return call(
            functools.partial(attend_kernel, first, block, heads, mem_len),
            attend_outs(mem_len + first + chunk),
            (counts, normed, keys, values, weights, w_pos, biases, sin, cos), name, cost, [ctx_scr], after=after,
        )

    saved_l = attend_chunk(late, "attend_late", 1, ())
    ctx_l = [saved_l[-1], cores(saved_l[-1], n_tensor), swap(saved_l[-1], "tensor", n_tensor, 2)]
    saved_e = attend_chunk(0, "attend_early", 5e9, outs_of[1:])
    ctx_e = [saved_e[-1], cores(saved_e[-1], n_tensor), swap(saved_e[-1], "tensor", n_tensor, 2)]
    (relay,) = call(
        relay_kernel, [((chunk + width, wide), BF)], (ctx_l[2], outs_of[2]), "relay_late", 1, after=saved_e[-1:]
    )
    relay = cores(relay, n_tensor)
    ctx_l.append(relay)
    outs_of.append(relay)
    half_outs = [
        ((block, width), FL), ((block, width), BF), ((block, ff), BF), ((block, ff), BF), ((2, width), FL),
        ((block, width), BF),
    ]

    def ffn_rows(first, ctx, roles, name, beside=(), after=(), cost=1):
        found = call(
            functools.partial(ffn_rows_kernel, first, block, roles, len(beside)),
            half_outs * len(roles) + [(r.shape, BF) for r in beside],
            (place, x, *ctx, *outs_of, ffn_gain, ffn_shift, w_up, up_bias, w_down, g, *beside), name, cost, after=after,
        )
        return *(found[i : i + 6] for i in range(0, 6 * len(roles), 6)), *found[6 * len(roles) :]

    sum_outs = [((width, ff), FL), ((ff, width), FL), ((3, width), FL), ((1, ff), FL)]
    (send_l,) = ffn_rows(late, ctx_l, ("send",), "ffn_send_late")
    gnt_l = cores(send_l[-1], n_tensor)
    keep_l, relay = ffn_rows(late, ctx_l, ("keep",), "ffn_keep_late", ctx_e[2:3], send_l[-1:], 5e9)
    ctx_e.append(cores(relay, n_tensor))
    (gnt_l,) = work(place, [("sum", 0, keep_l[-1], gnt_l)], "add_late")
    gnt_l = chips(gnt_l, n_tensor)
    shares_l, sums_l = split_at(2, call(
        functools.partial(ffn_late_kernel, late),
        [((block, width), BF)] * 2 + sum_outs, (place, g, w_down, *send_l[1:5], *keep_l[1:5]), "ffn_late", 1,
        after=gnt_l[:1],
    ))
    send_e, keep_e = ffn_rows(0, ctx_e, ("send", "keep"), "ffn_rows_early", after=sums_l[3:4])
    gnt_e = cores(send_e[-1], n_tensor)
    shares_e, halves, vecs = split_at(2, call(
        functools.partial(ffn_early_kernel, 0),
        [((block, width), BF)] * 2 + [((width // 2, ff), BF)] * 2 + [((ff // 2, width), BF)] * 2
        + [((3, width), FL), ((1, ff), FL)],
        (place, g, w_down, *send_e[1:5], *keep_e[1:5], *sums_l), "ffn_early", 1,
    ), 6)
    up_keep, up_send, down_keep, down_send = halves
    up_got = swap(up_send, "dp", n_dp, 1)
    down_got = swap(down_send, "dp", n_dp, 2)
    (gnt_l,) = work(place, [("sum", 0, *gnt_l)], "add_late_chips", (up_keep,), 5e9)
    gnt_l = (gnt_l, cores(gnt_l, n_tensor))
    (gnt_e,) = work(place, [("sum", 0, keep_e[-1], gnt_e)], "add_early", gnt_l[:1])
    gnt_e = chips(gnt_e, n_tensor)
    hidden_l, hidden_e = (send_l[0], keep_l[0]), (send_e[0], keep_e[0])

    sums = [((wide, total), FL), ((wide, total), FL), ((wide, width), FL), ((wide, width), FL), ((chunk, wide), BF)]
    turn_scr = [ctx_scr, ctx_scr]

    def back_args(hidden, gnt, saved):
        qb, qv, probs, ctx = saved
        return (place, *hidden, *gnt, g, ffn_gain, w_out, ctx, probs, qb, qv, keys, values, w_pos, sin, cos, weights)

    gh_l, dk, dv, dpos, dout, dq, bias, part = call(
        functools.partial(back_late_kernel, late, block, heads, mem_len),
        [((chunk, width), FL), *sums, ((2, wide), FL), ((chunk, width), BF)],
        back_args(hidden_l, gnt_l, saved_l), "back_late", 1, turn_scr,
    )
    gnt_e, up_keep, up_send, down_keep, down_send = work(
        place, [("sum", 0, *gnt_e), ("halve", 1, up_keep, up_got), ("halve", 0, down_keep, down_got)], "add_middle", (bias,)
    )
    up_got = swap(up_send, "dp", n_dp, 2)
    down_got = swap(down_send, "dp", n_dp, 1)
    gnt_e = (gnt_e, cores(gnt_e, n_tensor))
    groups = n_dp // 2
    size = max(16, -(-5 * wide // groups // 16) * 16)
    gh_e, dk, dv, dpos, dout, dq_e, bias = call(
        functools.partial(back_early_kernel, 0, block, heads, mem_len),
        [((chunk, width), FL), *sums, ((2, wide), FL)],
        (*back_args(hidden_e, gnt_e, saved_e)[:-1], dk, dv, dpos, dout, bias), "back_early", 1, turn_scr,
    )
    keep, send, a_keep, a_send, f_rows = call(
        functools.partial(back_end_kernel, 0, block, heads, mem_len, n_tensor, size),
        [*[((seq_len, width), BF)] * 2, *[((groups // 2 * (size + small), width), BF)] * 2, ((chunk // 2, width), BF)],
        (place, weights, normed, attn_shift, attn_gain, dk, dv, dpos, dout, dq_e, bias, dq, part, *vecs, *shares_e,
         *shares_l, up_keep, up_got, down_keep, down_got), "back_end", 1,
    )
    bits = list(range((n_dp - 1).bit_length()))
    attn = Chain(a_keep, a_send, bits, n_dp, "split")
    if len(bits) > 3:
        f_rows, f_send = work(place, [("halve", 2, f_rows, jnp.zeros_like(f_rows))], "halve_ffn")
    else:
        f_send = f_rows
    ffn = Chain(f_rows, f_send, bits[2:], n_dp, "two" if len(bits) == 3 else "sum")
    rows = (keep, cores(send, n_tensor))
    count, stage = 0, 0
    while attn.left() > 0:
        jobs = [attn.job()]
        if count == 0:
            pass
        elif stage == 0:
            jobs.append(ffn.job())
        elif stage == 1:
            jobs += [("join", 1, up, up_got), ("join", 0, down, down_got)]
        elif stage == 2:
            jobs += [("join", 0, up, up_got), ("copy", 0, down, down)]
        if attn.left() == 1:
            jobs.append(("copy", 0, totals, totals))
        if count == 0 or attn.left() == 1:
            jobs.append(("sum", 0, *rows))
        results = work(place, jobs, f"step_{count}", cost=STEP_COST if count == 2 else 1)
        if attn.job()[0] == "split":
            totals = results.pop(1)
        if count == 0 or attn.left() == 1:
            rows = results.pop()
            rows = (rows, (other_chips if count == 0 else cores)(rows, n_tensor))
        if attn.left() == 1:
            totals = results.pop()
            totals = [totals] + [swap(totals, "tensor", n_tensor, k) for k in range(1, n_tensor)]
        attn.take(results)
        if count == 0:
            pass
        elif stage == 0 and ffn.left() > 0:
            ffn.take(results)
        elif stage == 0:
            up, down = results if len(results) == 2 else (results[0][: chunk // 4], results[0][chunk // 4 :])
            up_got, down_got = swap(up, "dp", n_dp, 2), swap(down, "dp", n_dp, 1)
            stage = 1
        elif stage == 1:
            up, down = results
            up_got = swap(up, "dp", n_dp, 1)
            stage = 2
        elif stage == 2:
            up, down = results
            down_got = swap(down, "dp", n_dp, 2)
            stage = 3
        count += 1
    output, input_grad, g_up = call(
        functools.partial(finish_kernel, block), [(x.shape, BF)] * 2 + [((width, ff), FL)],
        (place, x, attn_gain, gh_e, gh_l, *hidden_e, *hidden_l, *rows, down_bias, up), "finish", 1,
        [pltpu.VMEM(x.shape, BF)] * 2 + [pltpu.VMEM((width, ff), FL), pltpu.SemaphoreType.DMA((9,))],
        after=(attn.rows,), far=3,
    )
    output_there = pltpu.with_memory_space_constraint(output, pltpu.HBM)
    g_down, g_query, g_key, g_value, g_pos, g_out, *vecs = call(
        functools.partial(last_kernel, wide, heads, n_tensor),
        [((ff, width), FL)] + [((width, wide), FL)] * 4 + [((wide, width), FL)]
        + [((1, width), FL)] * 5 + [((heads, HEAD), FL)] * 2 + [((1, ff), FL)],
        (place, attn.rows, attn.got, down, down_got, *totals), "last", 1,
        [pltpu.VMEM((ff, width), FL), pltpu.VMEM((groups * size, width), FL), pltpu.VMEM((4, width, wide), FL),
         pltpu.SemaphoreType.DMA((6,))],
        after=(output_there,), far=6,
    )
    return (
        output[None],
        input_grad[None],
        vecs[0].reshape(-1),
        vecs[1].reshape(-1),
        g_query,
        g_key,
        g_value,
        g_pos,
        vecs[5],
        vecs[6],
        g_out,
        vecs[2].reshape(-1),
        vecs[3].reshape(-1),
        g_up,
        vecs[7].reshape(-1),
        g_down,
        vecs[4].reshape(-1),
    )


def solution(mesh):
    split, whole = P(None, "tensor"), P()
    return jax.shard_map(
        functools.partial(per_device, mesh.shape["dp"], mesh.shape["tensor"]),
        mesh=mesh,
        in_specs=(
            P("dp", None, None), P("dp", None, None), P("dp"), whole, whole, split, split, split, split,
            P("tensor", None), P("tensor", None), P("tensor", None), whole, whole, split, P("tensor"),
            P("tensor", None), whole, P("dp", None, None),
        ),
        out_specs=(
            P("dp", None, None), P("dp", None, None), whole, whole, split, split, split, split,
            P("tensor", None), P("tensor", None), P("tensor", None), whole, whole, split, P("tensor"),
            P("tensor", None), whole,
        ),
        check_vma=False,
    )
```

time: 123 us -> 114 us (0.927)
  starting transfers between devices: 30.2 us -> 26.8 us
  Pallas kernels: 53.9 us -> 51.3 us
  waiting for transfers between devices: 36.3 us -> 34.1 us
    ppermute x35 -> x34, starting transfers between devices: 30.2 us -> 26.8 us  [swap(): return lax.ppermute(rows, axis, [(i, i ^ bit) for i in range(size)])]
    pallas_call x23 -> x22, Pallas kernels: 53.9 us -> 51.3 us  [call(): pl.pallas_call(body, out_shape=[pltpu.HBM(s, d) if i < far else jax.Shape...]
    ppermute x35 -> x34, waiting for transfers between devices: 36.3 us -> 34.1 us  [swap(): return lax.ppermute(rows, axis, [(i, i ^ bit) for i in range(size)])]
  transfers between devices with their start and end apart: 35 -> 34, of which waited for: 10 -> 15; matrix products, arithmetic and copies ran while one was open for 0% -> 0% of each run, Pallas kernels for 29% -> 38%
where the time goes in v2:
time: 114 us
  Pallas kernels  51.3 us (45%)
  waiting for transfers between devices  34.1 us (30%)
  starting transfers between devices  26.8 us (24%)
  between operations  1.77 us (2%)
    pallas_call x22, Pallas kernels, call(): pl.pallas_call(body, out_shape=[pltpu.HBM(s, d) if i < far else jax.Shape...  51.3 us
    ppermute x34, waiting for transfers between devices, swap(): return lax.ppermute(rows, axis, [(i, i ^ bit) for i in range(size)])  34.1 us
    ppermute x34, starting transfers between devices, swap(): return lax.ppermute(rows, axis, [(i, i ^ bit) for i in range(size)])  26.8 us
  transfers between devices with their start and end apart: 34, of which 15 were waited for; matrix products, arithmetic and copies ran while one was open for 0% of the time, Pallas kernels for 38%

profile of v2, /device:TPU:0, one launch (start us, length us, event | category | flops | bytes accessed | tf_op | source)
XLA Modules:
  0.0 114.1 jit_solution(1877194766996258439)
XLA Ops:
  0.7 3.0 %collective-permute-start.1 = (bf16[128,512]{1,0:T(8,128)(2,1)}, bf16[128,512]{1,0:T(8,128)(2,1)S(1)}, u32[]{:S(2)}, u32[]{:S(2)}) collective-permute-start(bf16[128,512]{1,0:T(8,128)(2,1)} %refs_6_.7), channel_id=1, source_target_pairs={{0,2},{1,3},{2,0},{3,1},{4,6},{5,7},{6,4},{7,5},{8,10},{9,11},{10,... | collective-permute-start | bytes 393224 | tf_op jit(solution)/shard_map/ppermute | solution.py:528
  3.7 0.1 pad_add_fusion.refs_0_
  3.8 4.2 %front.1 = (bf16[1024,512]{1,0:T(8,128)(2,1)S(1)}, bf16[1024,512]{1,0:T(8,128)(2,1)S(1)}, bf16[512,384]{1,0:T(8,128)(2,1)S(1)}, bf16[512,128]{1,0:T(8,128)(2,1)S...) custom-call(s32[2]{0:T(128)S(1)} %pad_add_fusion.refs_0_, ...), custom_call_target="tpu_custom_call" | custom-call | flops 1 | bytes 1 | tf_op jit(solution)/shard_map/front/pallas_call | solution.py:515
  8.6 5.7 %attend_late.1 = (bf16[2,512,640]{2,1,0:T(8,128)(2,1)S(1)}, bf16[512,128]{1,0:T(8,128)(2,1)S(1)}, bf16[2,512,1536]{2,1,0:T(8,128)(2,1)S(1)}, bf16[512,128]{1,0:T(8,128)(2,1)S(1)}) custom-call(s32[1]{0:T(128)S(6)} %copy.39.refs_0_, bf16[1536,512]{1,0:T(8,128)(2,1)S(1)} %get-tuple-element.142.refs_1_.refs_2_, ...), custom_call_target="tpu_custom_call" | custom-call | flops 1 | bytes 1 | tf_op jit(solution)/shard_map/attend_late/pallas_call | solution.py:515
  14.3 0.2 collective-permute-start.5
  14.5 4.1 %attend_early.1 = (bf16[2,512,640]{2,1,0:T(8,128)(2,1)S(1)}, bf16[512,128]{1,0:T(8,128)(2,1)S(1)}, bf16[2,512,1024]{2,1,0:T(8,128)(2,1)S(1)}, bf16[512,128]{1,0:T(8,128)(2,1)S(1)}) custom-call(s32[1]{0:T(128)S(6)} %copy.39.refs_0_, bf16[1536,512]{1,0:T(8,128)(2,1)S(1)} %get-tuple-element.142.refs_1_.refs_2_, ...), custom_call_target="tpu_custom_call" | custom-call | flops 5000000000 | bytes 1 | tf_op jit(solution)/shard_map/attend_early/pallas_call | solution.py:515
  18.6 1.7 %collective-permute-done.5.refs_0_.refs_4_ = bf16[512,128]{1,0:T(8,128)(2,1)S(1)} collective-permute-done((bf16[512,128]{1,0:T(8,128)(2,1)S(1)}, bf16[512,128]{1,0:T(8,128)(2,1)S(1)}, u32[]{:S(2)}, u32[]{:S(2)}) %collective-permute-start.5) | collective-permute-done | bytes 131104 | tf_op jit(solution)/shard_map/ppermute | solution.py:528
  20.3 0.1 collective-permute-start.6
  20.4 0.5 collective-permute-start.4
  20.9 0.3 collective-permute-start.3
  21.2 0.9 collective-permute-done.4.refs_3_
  22.1 1.9 %ffn_send_late.1 = (f32[256,512]{1,0:T(8,128)S(1)}, bf16[256,512]{1,0:T(8,128)(2,1)S(1)}, bf16[256,512]{1,0:T(8,128)(2,1)S(1)}, bf16[256,512]{1,0:T(8,128)(2,1)S...) custom-call(s32[2]{0:T(128)S(1)} %pad_add_fusion.refs_0_, bf16[1024,512]{1,0:T(8,128)(2,1)S(1)} %get-tuple-element.140.refs_1_, ...), custom_call_target="tpu_custom_call" | custom-call | flops 1 | bytes 1 | tf_op jit(solution)/shard_map/ffn_send_late/pallas_call | solution.py:515
  24.0 0.2 collective-permute-start.8
  24.2 2.2 %collective-permute-done.3.refs_16_.refs_4_ = bf16[512,128]{1,0:T(8,128)(2,1)S(1)} collective-permute-done((bf16[512,128]{1,0:T(8,128)(2,1)S(1)}, bf16[512,128]{1,0:T(8,128)(2,1)S(1)}, u32[]{:S(2)}, u32[]{:S(2)}) %collective-permute-start.3) | collective-permute-done | bytes 131104 | tf_op jit(solution)/shard_map/ppermute | solution.py:528
  26.4 1.9 %ffn_keep_late.1 = (f32[256,512]{1,0:T(8,128)S(1)}, bf16[256,512]{1,0:T(8,128)(2,1)S(1)}, bf16[256,512]{1,0:T(8,128)(2,1)S(1)}, bf16[256,512]{1,0:T(8,128)(2,1)S...) custom-call(s32[2]{0:T(128)S(1)} %pad_add_fusion.refs_0_, ...), custom_call_target="tpu_custom_call" | custom-call | flops 5000000000 | bytes 1 | tf_op jit(solution)/shard_map/ffn_keep_late/pallas_call | solution.py:515
  28.3 0.6 add_late.1.refs_11_.refs_1_
  28.9 0.5 collective-permute-start.10
  29.4 0.5 collective-permute-start.7
  29.9 1.5 %ffn_late.1 = (bf16[256,512]{1,0:T(8,128)(2,1)S(1)}, bf16[256,512]{1,0:T(8,128)(2,1)S(1)}, f32[512,512]{1,0:T(8,128)S(1)}, f32[512,512]{1,0:T(8,128)S(1)}, f32[3,512]{1,0:T(4,128)S(1)}, /*index=5*/f32[1,512]{1,0:T(1,128)S(1)}) custom-call(s32[2]{0:T(128)S(1)} %pad_add_fusion.refs_0_, bf16[1024,512]{1,0:T(8,128)(2,1)S(1)} %get-tuple-element.157.refs_15_.refs_1_.refs_5_, ...), custom_call_target="tpu_custom_call" | custom-call | flops 1 | bytes 1 | tf_op jit(solution)/shard_map/ffn_late/pallas_call | solution.py:515
  31.4 3.2 %ffn_rows_early.1 = (f32[256,512]{1,0:T(8,128)S(1)}, bf16[256,512]{1,0:T(8,128)(2,1)S(1)}, bf16[256,512]{1,0:T(8,128)(2,1)S(1)}, bf16[256,512]{1,0:T(8,128)(2,1)...) custom-call(s32[2]{0:T(128)S(1)} %pad_add_fusion.refs_0_, ...), custom_call_target="tpu_custom_call" | custom-call | flops 1 | bytes 1 | tf_op jit(solution)/shard_map/ffn_rows_early/pallas_call | solution.py:515
  34.7 1.7 %ffn_early.1 = (bf16[256,512]{1,0:T(8,128)(2,1)S(1)}, bf16[256,512]{1,0:T(8,128)(2,1)S(1)}, bf16[256,512]{1,0:T(8,128)(2,1)S(1)}, bf16[256,512]{1,0:T(8,128)(2,1...) custom-call(s32[2]{0:T(128)S(1)} %pad_add_fusion.refs_0_, ...), custom_call_target="tpu_custom_call" | custom-call | flops 1 | bytes 1 | tf_op jit(solution)/shard_map/ffn_early/pallas_call | solution.py:515
  36.4 0.6 add_late_chips.1.refs_3_
  37.0 0.5 collective-permute-start.14
  37.6 1.6 %collective-permute-start.12 = (bf16[256,512]{1,0:T(8,128)(2,1)S(1)}, bf16[256,512]{1,0:T(8,128)(2,1)S(1)}, u32[]{:S(2)}, u32[]{:S(2)}) collective-permute-start(bf16[256,512]{1,0:T(8,128)(2,1)S(1)} %get-tuple-element.186), channel_id=1, source_target_pairs={{0,4},{4,0},{8,12},{12,8},{16,20},{20,16},{24,28},{28,24},{1,5},{5... | collective-permute-start | bytes 786440 | tf_op jit(solution)/shard_map/ppermute | solution.py:528
  39.2 1.6 %collective-permute-start.13 = (bf16[256,512]{1,0:T(8,128)(2,1)S(1)}, bf16[256,512]{1,0:T(8,128)(2,1)S(1)}, u32[]{:S(2)}, u32[]{:S(2)}) collective-permute-start(bf16[256,512]{1,0:T(8,128)(2,1)S(1)} %get-tuple-element.188), channel_id=1, source_target_pairs={{0,8},{4,12},{8,0},{12,4},{16,24},{20,28},{24,16},{28,20},{1,9},{5... | collective-permute-start | bytes 786440 | tf_op jit(solution)/shard_map/ppermute | solution.py:528
  40.8 0.6 add_early.1.refs_1_
  41.4 1.6 %collective-permute-start.11 = (bf16[256,512]{1,0:T(8,128)(2,1)S(1)}, bf16[256,512]{1,0:T(8,128)(2,1)S(1)}, u32[]{:S(2)}, u32[]{:S(2)}) collective-permute-start(bf16[256,512]{1,0:T(8,128)(2,1)S(1)} %add_early.1.refs_1_), channel_id=1, source_target_pairs={{0,2},{1,3},{2,0},{3,1},{4,6},{5,7},{6,4},{7,5},{8,10},{9,11},{10,... | collective-permute-start | bytes 786440 | tf_op jit(solution)/shard_map/ppermute | solution.py:528
  43.0 6.7 %back_late.1 = (f32[512,512]{1,0:T(8,128)S(1)}, f32[128,1536]{1,0:T(8,128)S(1)}, f32[128,1536]{1,0:T(8,128)S(1)}, f32[128,512]{1,0:T(8,128)S(1)}, f32[128,512]{1...) custom-call(s32[2]{0:T(128)S(1)} %pad_add_fusion.refs_0_, ...), custom_call_target="tpu_custom_call" | custom-call | flops 1 | bytes 1 | tf_op jit(solution)/shard_map/back_late/pallas_call | solution.py:515
  49.7 1.1 add_middle.1
  50.9 0.5 collective-permute-start.16
  51.4 0.5 collective-permute-start.17
  51.9 0.5 collective-permute-done.15.refs_4_
  52.4 5.0 %back_early.1 = (f32[512,512]{1,0:T(8,128)S(1)}, f32[128,1536]{1,0:T(8,128)S(1)}, f32[128,1536]{1,0:T(8,128)S(1)}, f32[128,512]{1,0:T(8,128)S(1)}, f32[128,512]{...) custom-call(s32[2]{0:T(128)S(1)} %pad_add_fusion.refs_0_, ...), custom_call_target="tpu_custom_call" | custom-call | flops 1 | bytes 1 | tf_op jit(solution)/shard_map/back_early/pallas_call | solution.py:515
  57.4 2.3 %back_end.1 = (bf16[1024,512]{1,0:T(8,128)(2,1)S(1)}, bf16[1024,512]{1,0:T(8,128)(2,1)S(1)}, bf16[352,512]{1,0:T(8,128)(2,1)S(1)}, bf16[352,512]{1,0:T(8,128)(2,1)S(1)}, bf16[256,512]{1,0:T(8,128)(2,1)S(1)}) custom-call(s32[2]{0:T(128)S(1)} %pad_add_fusion.refs_0_, bf16[512,384]{1,0:T(8,128)(2,1)S(1)} %get-tuple-element.145.refs_4_.refs_17_.refs_1_, ...), custom_call_target="tpu_custom_call" | custom-call | flops 1 | bytes 1 | tf_op jit(solution)/shard_map/back_end/pallas_call | solution.py:515
  59.8 0.2 collective-permute-start.19
  60.0 0.9 collective-permute-start.18
  60.9 2.6 %collective-permute-start.21 = (bf16[256,512]{1,0:T(8,128)(2,1)S(1)}, bf16[256,512]{1,0:T(8,128)(2,1)S(1)}, u32[]{:S(2)}, u32[]{:S(2)}) collective-permute-start(bf16[256,512]{1,0:T(8,128)(2,1)S(1)} %get-tuple-element.231.refs_3_), channel_id=1, source_target_pairs={{0,16},{4,20},{8,24},{12,28},{16,0},{20,4},{24,8},{28,12},{1,17},{... | collective-permute-start | bytes 786440 | tf_op jit(solution)/shard_map/ppermute | solution.py:528
  63.5 7.1 %collective-permute-done.18.refs_2_ = bf16[352,512]{1,0:T(8,128)(2,1)S(1)} collective-permute-done((bf16[352,512]{1,0:T(8,128)(2,1)S(1)}, bf16[352,512]{1,0:T(8,128)(2,1)S(1)}, u32[]{:S(2)}, u32[]{:S(2)}) %collective-permute-start.18) | collective-permute-done | bytes 360480 | tf_op jit(solution)/shard_map/ppermute | solution.py:528
  70.7 1.0 step_0.1
  71.6 1.2 %collective-permute-start.20 = (bf16[176,512]{1,0:T(8,128)(2,1)S(1)}, bf16[176,512]{1,0:T(8,128)(2,1)S(1)}, u32[]{:S(2)}, u32[]{:S(2)}) collective-permute-start(bf16[176,512]{1,0:T(8,128)(2,1)S(1)} %get-tuple-element.230), channel_id=1, source_target_pairs={{0,8},{4,12},{8,0},{12,4},{16,24},{20,28},{24,16},{28,20},{1,9},{5... | collective-permute-start | bytes 540680 | tf_op jit(solution)/shard_map/ppermute | solution.py:528
  72.8 1.0 collective-permute-start.27
  73.8 2.1 %collective-permute-done.21.refs_4_ = bf16[256,512]{1,0:T(8,128)(2,1)S(1)} collective-permute-done((bf16[256,512]{1,0:T(8,128)(2,1)S(1)}, bf16[256,512]{1,0:T(8,128)(2,1)S(1)}, u32[]{:S(2)}, u32[]{:S(2)}) %collective-permute-start.21) | collective-permute-done | bytes 262176 | tf_op jit(solution)/shard_map/ppermute | solution.py:528
  75.9 3.8 %collective-permute-done.20.refs_2_ = bf16[176,512]{1,0:T(8,128)(2,1)S(1)} collective-permute-done((bf16[176,512]{1,0:T(8,128)(2,1)S(1)}, bf16[176,512]{1,0:T(8,128)(2,1)S(1)}, u32[]{:S(2)}, u32[]{:S(2)}) %collective-permute-start.20) | collective-permute-done | bytes 180256 | tf_op jit(solution)/shard_map/ppermute | solution.py:528
  79.7 0.6 step_1.1
  80.3 1.6 %collective-permute-start.22 = (bf16[176,512]{1,0:T(8,128)(2,1)S(1)}, bf16[176,512]{1,0:T(8,128)(2,1)S(1)}, u32[]{:S(2)}, u32[]{:S(2)}) collective-permute-start(bf16[176,512]{1,0:T(8,128)(2,1)S(1)} %get-tuple-element.232.refs_1_), channel_id=1, source_target_pairs={{0,16},{4,20},{8,24},{12,28},{16,0},{20,4},{24,8},{28,12},{1,17},{... | collective-permute-start | bytes 540680 | tf_op jit(solution)/shard_map/ppermute | solution.py:528
  82.0 2.5 %collective-permute-start.23 = (bf16[128,512]{1,0:T(8,128)(2,1)S(1)}, bf16[128,512]{1,0:T(8,128)(2,1)S(1)}, u32[]{:S(2)}, u32[]{:S(2)}) collective-permute-start(bf16[128,512]{1,0:T(8,128)(2,1)S(1)} %get-tuple-element.233.refs_3_), channel_id=1, source_target_pairs={{0,8},{4,12},{8,0},{12,4},{16,24},{20,28},{24,16},{28,20},{1,9},{5... | collective-permute-start | bytes 393224 | tf_op jit(solution)/shard_map/ppermute | solution.py:528
  84.5 0.7 collective-permute-start.24
  85.1 3.7 %collective-permute-done.23.refs_4_ = bf16[128,512]{1,0:T(8,128)(2,1)S(1)} collective-permute-done((bf16[128,512]{1,0:T(8,128)(2,1)S(1)}, bf16[128,512]{1,0:T(8,128)(2,1)S(1)}, u32[]{:S(2)}, u32[]{:S(2)}) %collective-permute-start.23) | collective-permute-done | bytes 131104 | tf_op jit(solution)/shard_map/ppermute | solution.py:528
  88.8 0.6 collective-permute-done.24.refs_6_
  89.4 2.2 %collective-permute-done.22.refs_2_ = bf16[176,512]{1,0:T(8,128)(2,1)S(1)} collective-permute-done((bf16[176,512]{1,0:T(8,128)(2,1)S(1)}, bf16[176,512]{1,0:T(8,128)(2,1)S(1)}, u32[]{:S(2)}, u32[]{:S(2)}) %collective-permute-start.22) | collective-permute-done | bytes 180256 | tf_op jit(solution)/shard_map/ppermute | solution.py:528
  91.6 0.7 step_2.1
  92.4 1.0 collective-permute-start.26
  93.4 5.3 %collective-permute-done.25.refs_2_ = bf16[160,512]{1,0:T(8,128)(2,1)S(1)} collective-permute-done((bf16[160,512]{1,0:T(8,128)(2,1)S(1)}, bf16[160,512]{1,0:T(8,128)(2,1)S(1)}, u32[]{:S(2)}, u32[]{:S(2)}) %collective-permute-start.25) | collective-permute-done | bytes 163872 | tf_op jit(solution)/shard_map/ppermute | solution.py:528
  98.7 1.1 collective-permute-done.26.refs_4_
  99.8 1.0 step_3.1
  100.9 1.4 %collective-permute-start.29 = (bf16[320,512]{1,0:T(8,128)(2,1)S(1)}, bf16[320,512]{1,0:T(8,128)(2,1)S(1)}, u32[]{:S(2)}, u32[]{:S(2)}) collective-permute-start(bf16[320,512]{1,0:T(8,128)(2,1)S(1)} %get-tuple-element.243.refs_13_.refs_1_), channel_id=1, source_target_pairs={{0,4},{4,0},{8,12},{12,8},{16,20},{20,16},{24,28},{28,24},{1,5},{5... | collective-permute-start | bytes 983048 | tf_op jit(solution)/shard_map/ppermute | solution.py:528
  102.3 0.2 collective-permute-start.31
  102.4 1.0 collective-permute-start.32
  103.4 0.1 collective-permute-done.28.refs_10_
  103.6 0.7 collective-permute-start.33
  104.3 4.0 %finish.1 = (bf16[1024,512]{1,0:T(8,128)(2,1)}, bf16[1024,512]{1,0:T(8,128)(2,1)}, f32[512,512]{1,0:T(8,128)}) custom-call(s32[2]{0:T(128)S(1)} %pad_add_fusion.refs_0_, bf16[1024,512]{1,0:T(8,128)(2,1)S(1)} %get-tuple-element.140.refs_1_, f32[1,512]{1,0:T(1,128)S(1)} %get-tuple-element.141.refs_4_.refs_2_, f32[512,512]{1,0:T(8,128)S(1)} %get-tuple-element.204.refs_3_, ...), custom_call_target="tpu_custom_call" | custom-call | flops 1 | bytes 1 | tf_op jit(solution)/shard_map/finish/pallas_call | solution.py:515
  108.3 2.3 %collective-permute-done.30.refs_4_ = bf16[256,512]{1,0:T(8,128)(2,1)S(1)} collective-permute-done((bf16[256,512]{1,0:T(8,128)(2,1)S(1)}, bf16[256,512]{1,0:T(8,128)(2,1)S(1)}, u32[]{:S(2)}, u32[]{:S(2)}) %collective-permute-start.30) | collective-permute-done | bytes 262176 | tf_op jit(solution)/shard_map/ppermute | solution.py:528
  110.6 0.4 collective-permute-done.29.refs_2_
  111.0 2.9 %last.1 = (f32[512,512]{1,0:T(8,128)}, f32[512,128]{1,0:T(8,128)}, f32[512,128]{1,0:T(8,128)}, f32[512,128]{1,0:T(8,128)}, f32[512,128]{1,0:T(8,128)}, /*index=5...) custom-call(s32[2]{0:T(128)S(1)} %pad_add_fusion.refs_0_, ...), custom_call_target="tpu_custom_call" | custom-call | flops 1 | bytes 1 | tf_op jit(solution)/shard_map/last/pallas_call | solution.py:515
  (29 shorter events, 0.3 us)
Async XLA Ops:
  0.7 13.8 %collective-permute-start.1 = (bf16[128,512]{1,0:T(8,128)(2,1)}, bf16[128,512]{1,0:T(8,128)(2,1)S(1)}, u32[]{:S(2)}, u32[]{:S(2)}) collective-permute-start(bf16[128,512]{1,0:T(8,128)(2,1)} %refs_6_.7), channel_id=1, source_target_pairs={{0,2},{1,3},{2,0},{3,1},{4,6},{5,7},{6,4},{7,5},{8,10},{9,11},{10,... | collective-permute-start | bytes 393224 | tf_op jit(solution)/shard_map/ppermute | solution.py:528
  3.7 10.8 %collective-permute-start = (bf16[128,512]{1,0:T(8,128)(2,1)}, bf16[128,512]{1,0:T(8,128)(2,1)S(1)}, u32[]{:S(2)}, u32[]{:S(2)}) collective-permute-start(bf16[128,512]{1,0:T(8,128)(2,1)} %refs_6_.7), channel_id=1, source_target_pairs={{0,1},{1,0},{2,3},{3,2},{4,5},{5,4},{6,7},{7,6},{8,9},{9,8},{10,11... | collective-permute-start | bytes 393224 | tf_op jit(solution)/shard_map/ppermute | solution.py:528
  14.3 7.8 %copy-start = (bf16[128,512]{1,0:T(8,128)(2,1)S(1)}, bf16[128,512]{1,0:T(8,128)(2,1)}, u32[]{:S(2)}) copy-start(bf16[128,512]{1,0:T(8,128)(2,1)} %refs_6_.7) | copy-start | bytes 393220
  14.3 6.0 %collective-permute-start.5 = (bf16[512,128]{1,0:T(8,128)(2,1)S(1)}, bf16[512,128]{1,0:T(8,128)(2,1)S(1)}, u32[]{:S(2)}, u32[]{:S(2)}) collective-permute-start(bf16[512,128]{1,0:T(8,128)(2,1)S(1)} %get-tuple-element.151.refs_2_.refs_8_), channel_id=1, source_target_pairs={{0,2},{1,3},{2,0},{3,1},{4,6},{5,7},{6,4},{7,5},{8,10},{9,11},{10,... | collective-permute-start | bytes 393224 | tf_op jit(solution)/shard_map/ppermute | solution.py:528
  20.3 1.8 %collective-permute-start.6 = (bf16[1024,128]{1,0:T(8,128)(2,1)S(1)}, bf16[1024,128]{1,0:T(8,128)(2,1)S(1)}, u32[]{:S(2)}, u32[]{:S(2)}) collective-permute-start(bf16[1024,128]{1,0:T(8,128)(2,1)S(1)} %relay_late.1), channel_id=1, source_target_pairs={{0,1},{1,0},{2,3},{3,2},{4,5},{5,4},{6,7},{7,6},{8,9},{9,8},{10,11... | collective-permute-start | bytes 786440 | tf_op jit(solution)/shard_map/ppermute | solution.py:528
  20.4 1.7 %collective-permute-start.4 = (bf16[512,128]{1,0:T(8,128)(2,1)S(1)}, bf16[512,128]{1,0:T(8,128)(2,1)S(1)}, u32[]{:S(2)}, u32[]{:S(2)}) collective-permute-start(bf16[512,128]{1,0:T(8,128)(2,1)S(1)} %get-tuple-element.151.refs_2_.refs_8_), channel_id=1, source_target_pairs={{0,1},{1,0},{2,3},{3,2},{4,5},{5,4},{6,7},{7,6},{8,9},{9,8},{10,11... | collective-permute-start | bytes 393224 | tf_op jit(solution)/shard_map/ppermute | solution.py:528
  20.9 5.5 %collective-permute-start.3 = (bf16[512,128]{1,0:T(8,128)(2,1)S(1)}, bf16[512,128]{1,0:T(8,128)(2,1)S(1)}, u32[]{:S(2)}, u32[]{:S(2)}) collective-permute-start(bf16[512,128]{1,0:T(8,128)(2,1)S(1)} %get-tuple-element.150.refs_2_.refs_8_), channel_id=1, source_target_pairs={{0,2},{1,3},{2,0},{3,1},{4,6},{5,7},{6,4},{7,5},{8,10},{9,11},{10,... | collective-permute-start | bytes 393224 | tf_op jit(solution)/shard_map/ppermute | solution.py:528
  24.0 4.3 %collective-permute-start.8 = (bf16[256,512]{1,0:T(8,128)(2,1)S(1)}, bf16[256,512]{1,0:T(8,128)(2,1)S(1)}, u32[]{:S(2)}, u32[]{:S(2)}) collective-permute-start(bf16[256,512]{1,0:T(8,128)(2,1)S(1)} %get-tuple-element.158.refs_17_), channel_id=1, source_target_pairs={{0,1},{1,0},{2,3},{3,2},{4,5},{5,4},{6,7},{7,6},{8,9},{9,8},{10,11... | collective-permute-start | bytes 786440 | tf_op jit(solution)/shard_map/ppermute | solution.py:528
  28.9 7.5 %collective-permute-start.10 = (bf16[256,512]{1,0:T(8,128)(2,1)S(1)}, bf16[256,512]{1,0:T(8,128)(2,1)S(1)}, u32[]{:S(2)}, u32[]{:S(2)}) collective-permute-start(bf16[256,512]{1,0:T(8,128)(2,1)S(1)} %add_late.1.refs_11_.refs_1_), channel_id=1, source_target_pairs={{0,2},{1,3},{2,0},{3,1},{4,6},{5,7},{6,4},{7,5},{8,10},{9,11},{10,... | collective-permute-start | bytes 786440 | tf_op jit(solution)/shard_map/ppermute | solution.py:528
  29.4 2.0 %collective-permute-start.2 = (bf16[512,128]{1,0:T(8,128)(2,1)S(1)}, bf16[512,128]{1,0:T(8,128)(2,1)S(1)}, u32[]{:S(2)}, u32[]{:S(2)}) collective-permute-start(bf16[512,128]{1,0:T(8,128)(2,1)S(1)} %get-tuple-element.150.refs_2_.refs_8_), channel_id=1, source_target_pairs={{0,1},{1,0},{2,3},{3,2},{4,5},{5,4},{6,7},{7,6},{8,9},{9,8},{10,11... | collective-permute-start | bytes 393224 | tf_op jit(solution)/shard_map/ppermute | solution.py:528
  29.4 2.1 %collective-permute-start.7 = (bf16[512,128]{1,0:T(8,128)(2,1)S(1)}, bf16[512,128]{1,0:T(8,128)(2,1)S(1)}, u32[]{:S(2)}, u32[]{:S(2)}) collective-permute-start(bf16[512,128]{1,0:T(8,128)(2,1)S(1)} %get-tuple-element.159), channel_id=1, source_target_pairs={{0,1},{1,0},{2,3},{3,2},{4,5},{5,4},{6,7},{7,6},{8,9},{9,8},{10,11... | collective-permute-start | bytes 393224 | tf_op jit(solution)/shard_map/ppermute | solution.py:528
  34.7 6.1 %collective-permute-start.9 = (bf16[256,512]{1,0:T(8,128)(2,1)S(1)}, bf16[256,512]{1,0:T(8,128)(2,1)S(1)}, u32[]{:S(2)}, u32[]{:S(2)}) collective-permute-start(bf16[256,512]{1,0:T(8,128)(2,1)S(1)} %get-tuple-element.173), channel_id=1, source_target_pairs={{0,1},{1,0},{2,3},{3,2},{4,5},{5,4},{6,7},{7,6},{8,9},{9,8},{10,11... | collective-permute-start | bytes 786440 | tf_op jit(solution)/shard_map/ppermute | solution.py:528
  37.0 5.9 %collective-permute-start.14 = (bf16[256,512]{1,0:T(8,128)(2,1)S(1)}, bf16[256,512]{1,0:T(8,128)(2,1)S(1)}, u32[]{:S(2)}, u32[]{:S(2)}) collective-permute-start(bf16[256,512]{1,0:T(8,128)(2,1)S(1)} %add_late_chips.1.refs_3_), channel_id=1, source_target_pairs={{0,1},{1,0},{2,3},{3,2},{4,5},{5,4},{6,7},{7,6},{8,9},{9,8},{10,11... | collective-permute-start | bytes 786440 | tf_op jit(solution)/shard_map/ppermute | solution.py:528
  37.6 12.1 %collective-permute-start.12 = (bf16[256,512]{1,0:T(8,128)(2,1)S(1)}, bf16[256,512]{1,0:T(8,128)(2,1)S(1)}, u32[]{:S(2)}, u32[]{:S(2)}) collective-permute-start(bf16[256,512]{1,0:T(8,128)(2,1)S(1)} %get-tuple-element.186), channel_id=1, source_target_pairs={{0,4},{4,0},{8,12},{12,8},{16,20},{20,16},{24,28},{28,24},{1,5},{5... | collective-permute-start | bytes 786440 | tf_op jit(solution)/shard_map/ppermute | solution.py:528
  39.2 10.5 %collective-permute-start.13 = (bf16[256,512]{1,0:T(8,128)(2,1)S(1)}, bf16[256,512]{1,0:T(8,128)(2,1)S(1)}, u32[]{:S(2)}, u32[]{:S(2)}) collective-permute-start(bf16[256,512]{1,0:T(8,128)(2,1)S(1)} %get-tuple-element.188), channel_id=1, source_target_pairs={{0,8},{4,12},{8,0},{12,4},{16,24},{20,28},{24,16},{28,20},{1,9},{5... | collective-permute-start | bytes 786440 | tf_op jit(solution)/shard_map/ppermute | solution.py:528
  41.4 8.3 %collective-permute-start.11 = (bf16[256,512]{1,0:T(8,128)(2,1)S(1)}, bf16[256,512]{1,0:T(8,128)(2,1)S(1)}, u32[]{:S(2)}, u32[]{:S(2)}) collective-permute-start(bf16[256,512]{1,0:T(8,128)(2,1)S(1)} %add_early.1.refs_1_), channel_id=1, source_target_pairs={{0,2},{1,3},{2,0},{3,1},{4,6},{5,7},{6,4},{7,5},{8,10},{9,11},{10,... | collective-permute-start | bytes 786440 | tf_op jit(solution)/shard_map/ppermute | solution.py:528
  50.8 1.6 %collective-permute-start.15 = (bf16[256,512]{1,0:T(8,128)(2,1)S(1)}, bf16[256,512]{1,0:T(8,128)(2,1)S(1)}, u32[]{:S(2)}, u32[]{:S(2)}) collective-permute-start(bf16[256,512]{1,0:T(8,128)(2,1)S(1)} %get-tuple-element.196.refs_3_), channel_id=1, source_target_pairs={{0,1},{1,0},{2,3},{3,2},{4,5},{5,4},{6,7},{7,6},{8,9},{9,8},{10,11... | collective-permute-start | bytes 786440 | tf_op jit(solution)/shard_map/ppermute | solution.py:528
  50.9 6.6 %collective-permute-start.16 = (bf16[128,512]{1,0:T(8,128)(2,1)S(1)}, bf16[128,512]{1,0:T(8,128)(2,1)S(1)}, u32[]{:S(2)}, u32[]{:S(2)}) collective-permute-start(bf16[128,512]{1,0:T(8,128)(2,1)S(1)} %get-tuple-element.222), channel_id=1, source_target_pairs={{0,8},{4,12},{8,0},{12,4},{16,24},{20,28},{24,16},{28,20},{1,9},{5... | collective-permute-start | bytes 393224 | tf_op jit(solution)/shard_map/ppermute | solution.py:528
  51.4 6.1 %collective-permute-start.17 = (bf16[128,512]{1,0:T(8,128)(2,1)S(1)}, bf16[128,512]{1,0:T(8,128)(2,1)S(1)}, u32[]{:S(2)}, u32[]{:S(2)}) collective-permute-start(bf16[128,512]{1,0:T(8,128)(2,1)S(1)} %get-tuple-element.224), channel_id=1, source_target_pairs={{0,4},{4,0},{8,12},{12,8},{16,20},{20,16},{24,28},{28,24},{1,5},{5... | collective-permute-start | bytes 393224 | tf_op jit(solution)/shard_map/ppermute | solution.py:528
  59.8 10.9 %collective-permute-start.19 = (bf16[1024,512]{1,0:T(8,128)(2,1)S(1)}, bf16[1024,512]{1,0:T(8,128)(2,1)S(1)}, u32[]{:S(2)}, u32[]{:S(2)}) collective-permute-start(bf16[1024,512]{1,0:T(8,128)(2,1)S(1)} %get-tuple-element.228), channel_id=1, source_target_pairs={{0,1},{1,0},{2,3},{3,2},{4,5},{5,4},{6,7},{7,6},{8,9},{9,8},{10,11... | collective-permute-start | bytes 3145736 | tf_op jit(solution)/shard_map/ppermute | solution.py:528
  60.0 10.7 %collective-permute-start.18 = (bf16[352,512]{1,0:T(8,128)(2,1)S(1)}, bf16[352,512]{1,0:T(8,128)(2,1)S(1)}, u32[]{:S(2)}, u32[]{:S(2)}) collective-permute-start(bf16[352,512]{1,0:T(8,128)(2,1)S(1)} %get-tuple-element.226), channel_id=1, source_target_pairs={{0,4},{4,0},{8,12},{12,8},{16,20},{20,16},{24,28},{28,24},{1,5},{5... | collective-permute-start | bytes 1081352 | tf_op jit(solution)/shard_map/ppermute | solution.py:528
  60.9 15.0 %collective-permute-start.21 = (bf16[256,512]{1,0:T(8,128)(2,1)S(1)}, bf16[256,512]{1,0:T(8,128)(2,1)S(1)}, u32[]{:S(2)}, u32[]{:S(2)}) collective-permute-start(bf16[256,512]{1,0:T(8,128)(2,1)S(1)} %get-tuple-element.231.refs_3_), channel_id=1, source_target_pairs={{0,16},{4,20},{8,24},{12,28},{16,0},{20,4},{24,8},{28,12},{1,17},{... | collective-permute-start | bytes 786440 | tf_op jit(solution)/shard_map/ppermute | solution.py:528
  71.6 8.1 %collective-permute-start.20 = (bf16[176,512]{1,0:T(8,128)(2,1)S(1)}, bf16[176,512]{1,0:T(8,128)(2,1)S(1)}, u32[]{:S(2)}, u32[]{:S(2)}) collective-permute-start(bf16[176,512]{1,0:T(8,128)(2,1)S(1)} %get-tuple-element.230), channel_id=1, source_target_pairs={{0,8},{4,12},{8,0},{12,4},{16,24},{20,28},{24,16},{28,20},{1,9},{5... | collective-permute-start | bytes 540680 | tf_op jit(solution)/shard_map/ppermute | solution.py:528
  72.8 27.0 %collective-permute-start.27 = (bf16[1024,512]{1,0:T(8,128)(2,1)S(1)}, bf16[1024,512]{1,0:T(8,128)(2,1)S(1)}, u32[]{:S(2)}, u32[]{:S(2)}) collective-permute-start(bf16[1024,512]{1,0:T(8,128)(2,1)S(1)} %get-tuple-element.239.refs_9_), channel_id=1, source_target_pairs={{0,2},{1,3},{2,0},{3,1},{4,6},{5,7},{6,4},{7,5},{8,10},{9,11},{10,... | collective-permute-start | bytes 3145736 | tf_op jit(solution)/shard_map/ppermute | solution.py:528
  80.3 11.3 %collective-permute-start.22 = (bf16[176,512]{1,0:T(8,128)(2,1)S(1)}, bf16[176,512]{1,0:T(8,128)(2,1)S(1)}, u32[]{:S(2)}, u32[]{:S(2)}) collective-permute-start(bf16[176,512]{1,0:T(8,128)(2,1)S(1)} %get-tuple-element.232.refs_1_), channel_id=1, source_target_pairs={{0,16},{4,20},{8,24},{12,28},{16,0},{20,4},{24,8},{28,12},{1,17},{... | collective-permute-start | bytes 540680 | tf_op jit(solution)/shard_map/ppermute | solution.py:528
  82.0 6.8 %collective-permute-start.23 = (bf16[128,512]{1,0:T(8,128)(2,1)S(1)}, bf16[128,512]{1,0:T(8,128)(2,1)S(1)}, u32[]{:S(2)}, u32[]{:S(2)}) collective-permute-start(bf16[128,512]{1,0:T(8,128)(2,1)S(1)} %get-tuple-element.233.refs_3_), channel_id=1, source_target_pairs={{0,8},{4,12},{8,0},{12,4},{16,24},{20,28},{24,16},{28,20},{1,9},{5... | collective-permute-start | bytes 393224 | tf_op jit(solution)/shard_map/ppermute | solution.py:528
  84.5 5.0 %collective-permute-start.24 = (bf16[128,512]{1,0:T(8,128)(2,1)S(1)}, bf16[128,512]{1,0:T(8,128)(2,1)S(1)}, u32[]{:S(2)}, u32[]{:S(2)}) collective-permute-start(bf16[128,512]{1,0:T(8,128)(2,1)S(1)} %get-tuple-element.234.refs_5_), channel_id=1, source_target_pairs={{0,4},{4,0},{8,12},{12,8},{16,20},{20,16},{24,28},{28,24},{1,5},{5... | collective-permute-start | bytes 393224 | tf_op jit(solution)/shard_map/ppermute | solution.py:528
  92.4 7.5 %collective-permute-start.26 = (bf16[256,512]{1,0:T(8,128)(2,1)S(1)}, bf16[256,512]{1,0:T(8,128)(2,1)S(1)}, u32[]{:S(2)}, u32[]{:S(2)}) collective-permute-start(bf16[256,512]{1,0:T(8,128)(2,1)S(1)} %get-tuple-element.236.refs_3_), channel_id=1, source_target_pairs={{0,4},{4,0},{8,12},{12,8},{16,20},{20,16},{24,28},{28,24},{1,5},{5... | collective-permute-start | bytes 786440 | tf_op jit(solution)/shard_map/ppermute | solution.py:528
  93.4 5.3 %collective-permute-start.25 = (bf16[160,512]{1,0:T(8,128)(2,1)S(1)}, bf16[160,512]{1,0:T(8,128)(2,1)S(1)}, u32[]{:S(2)}, u32[]{:S(2)}) collective-permute-start(bf16[160,512]{1,0:T(8,128)(2,1)S(1)} %get-tuple-element.235.refs_1_), channel_id=1, source_target_pairs={{0,8},{4,12},{8,0},{12,4},{16,24},{20,28},{24,16},{28,20},{1,9},{5... | collective-permute-start | bytes 491528 | tf_op jit(solution)/shard_map/ppermute | solution.py:528
  100.8 2.7 %collective-permute-start.28 = (bf16[1024,512]{1,0:T(8,128)(2,1)S(1)}, bf16[1024,512]{1,0:T(8,128)(2,1)S(1)}, u32[]{:S(2)}, u32[]{:S(2)}) collective-permute-start(bf16[1024,512]{1,0:T(8,128)(2,1)S(1)} %get-tuple-element.240.refs_9_), channel_id=1, source_target_pairs={{0,1},{1,0},{2,3},{3,2},{4,5},{5,4},{6,7},{7,6},{8,9},{9,8},{10,11... | collective-permute-start | bytes 3145736 | tf_op jit(solution)/shard_map/ppermute | solution.py:528
  100.9 10.1 %collective-permute-start.29 = (bf16[320,512]{1,0:T(8,128)(2,1)S(1)}, bf16[320,512]{1,0:T(8,128)(2,1)S(1)}, u32[]{:S(2)}, u32[]{:S(2)}) collective-permute-start(bf16[320,512]{1,0:T(8,128)(2,1)S(1)} %get-tuple-element.243.refs_13_.refs_1_), channel_id=1, source_target_pairs={{0,4},{4,0},{8,12},{12,8},{16,20},{20,16},{24,28},{28,24},{1,5},{5... | collective-permute-start | bytes 983048 | tf_op jit(solution)/shard_map/ppermute | solution.py:528
  102.3 8.4 %collective-permute-start.30 = (bf16[256,512]{1,0:T(8,128)(2,1)S(1)}, bf16[256,512]{1,0:T(8,128)(2,1)S(1)}, u32[]{:S(2)}, u32[]{:S(2)}) collective-permute-start(bf16[256,512]{1,0:T(8,128)(2,1)S(1)} %get-tuple-element.246.refs_3_), channel_id=1, source_target_pairs={{0,8},{4,12},{8,0},{12,4},{16,24},{20,28},{24,16},{28,20},{1,9},{5... | collective-permute-start | bytes 786440 | tf_op jit(solution)/shard_map/ppermute | solution.py:528
  102.3 6.0 %collective-permute-start.31 = (f32[16,512]{1,0:T(8,128)S(1)}, f32[16,512]{1,0:T(8,128)S(1)}, u32[]{:S(2)}, u32[]{:S(2)}) collective-permute-start(f32[16,512]{1,0:T(8,128)S(1)} %get-tuple-element.247.refs_5_), channel_id=1, source_target_pairs={{0,1},{1,0},{2,3},{3,2},{4,5},{5,4},{6,7},{7,6},{8,9},{9,8},{10,11... | collective-permute-start | bytes 98312 | tf_op jit(solution)/shard_map/ppermute | solution.py:528
  102.4 5.8 %collective-permute-start.32 = (f32[16,512]{1,0:T(8,128)S(1)}, f32[16,512]{1,0:T(8,128)S(1)}, u32[]{:S(2)}, u32[]{:S(2)}) collective-permute-start(f32[16,512]{1,0:T(8,128)S(1)} %get-tuple-element.247.refs_5_), channel_id=1, source_target_pairs={{0,2},{1,3},{2,0},{3,1},{4,6},{5,7},{6,4},{7,5},{8,10},{9,11},{10,... | collective-permute-start | bytes 98312 | tf_op jit(solution)/shard_map/ppermute | solution.py:528
  103.6 4.7 %collective-permute-start.33 = (f32[16,512]{1,0:T(8,128)S(1)}, f32[16,512]{1,0:T(8,128)S(1)}, u32[]{:S(2)}, u32[]{:S(2)}) collective-permute-start(f32[16,512]{1,0:T(8,128)S(1)} %get-tuple-element.247.refs_5_), channel_id=1, source_target_pairs={{0,3},{1,2},{2,1},{3,0},{4,7},{5,6},{6,5},{7,4},{8,11},{9,10},{10,... | collective-permute-start | bytes 98312 | tf_op jit(solution)/shard_map/ppermute | solution.py:528

commit v3 on v2

--- a/solution.py
+++ b/solution.py
@@ -499,14 +499,18 @@
 
 
 SMEM = pl.BlockSpec(memory_space=pltpu.SMEM)
+PLACE = object()
 SPECS = {s: pl.BlockSpec(memory_space=s) for s in (pltpu.VMEM, pltpu.HBM)}
 
 
 def call(kernel, outs, args, name, flops, scratch=(), space=pltpu.VMEM, after=(), far=0):
+    placed = args[0] is PLACE
+    args = args[1:] if placed else args
     count, extra = len(args), len(after)
 
     def body(*refs):
-        kernel(*refs[:count], *refs[count + extra :])
+        place = [(lax.axis_index("tensor") & 1, lax.axis_index("dp"))] if placed else []
+        kernel(*place, *refs[:count], *refs[count + extra :])
 
     specs = [SMEM if a.dtype == jnp.int32 else SPECS[space] for a in args]
     specs += [pl.BlockSpec(memory_space=pl.ANY)] * extra
@@ -630,7 +634,7 @@
     chunk = seq_len // 2
     block = chunk // 2
     late = chunk
-    place = jnp.stack([lax.axis_index("tensor") & 1, lax.axis_index("dp")]).astype(jnp.int32)
+    place = PLACE
     x, mem, g = inputs[0], memory[0], out_grad[0]
     row = lambda v: v.reshape(1, -1)
 

time: 114 us -> 107 us (0.939)
  Pallas kernels: 51.3 us -> 41.4 us
  waiting for transfers between devices: 34.1 us -> 38.2 us
  starting transfers between devices: 26.8 us -> 25.6 us
    pallas_call x22, Pallas kernels: 51.3 us -> 41.4 us  [call(): pl.pallas_call(body, out_shape=[pltpu.HBM(s, d) if i < far else jax.Shape...]
    ppermute x34, waiting for transfers between devices: 34.1 us -> 38.2 us  [swap(): return lax.ppermute(rows, axis, [(i, i ^ bit) for i in range(size)])]
    ppermute x34, starting transfers between devices: 26.8 us -> 25.6 us  [swap(): return lax.ppermute(rows, axis, [(i, i ^ bit) for i in range(size)])]
  transfers between devices with their start and end apart: 34 -> 34, of which waited for: 15 -> 17; matrix products, arithmetic and copies ran while one was open for 0% -> 0% of each run, Pallas kernels for 38% -> 34%
where the time goes in v3:
time: 107 us
  Pallas kernels  41.4 us (39%)
  waiting for transfers between devices  38.2 us (36%)
  starting transfers between devices  25.6 us (24%)
  between operations  1.74 us (2%)
    pallas_call x22, Pallas kernels, call(): pl.pallas_call(body, out_shape=[pltpu.HBM(s, d) if i < far else jax.Shape...  41.4 us
    ppermute x34, waiting for transfers between devices, swap(): return lax.ppermute(rows, axis, [(i, i ^ bit) for i in range(size)])  38.2 us
    ppermute x34, starting transfers between devices, swap(): return lax.ppermute(rows, axis, [(i, i ^ bit) for i in range(size)])  25.6 us
  transfers between devices with their start and end apart: 34, of which 17 were waited for; matrix products, arithmetic and copies ran while one was open for 0% of the time, Pallas kernels for 34%

profile of v3, /device:TPU:0, one launch (start us, length us, event | category | flops | bytes accessed | tf_op | source)
XLA Modules:
  0.0 107.0 jit_solution(5212357947507859988)
XLA Ops:
  0.7 3.0 %collective-permute-start.1 = (bf16[128,512]{1,0:T(8,128)(2,1)}, bf16[128,512]{1,0:T(8,128)(2,1)S(1)}, u32[]{:S(2)}, u32[]{:S(2)}) collective-permute-start(bf16[128,512]{1,0:T(8,128)(2,1)} %refs_5_.7), channel_id=1, source_target_pairs={{0,2},{1,3},{2,0},{3,1},{4,6},{5,7},{6,4},{7,5},{8,10},{9,11},{10,... | collective-permute-start | bytes 393224 | tf_op jit(solution)/shard_map/ppermute | solution.py:532
  3.7 3.6 %front.1 = (bf16[1024,512]{1,0:T(8,128)(2,1)S(1)}, bf16[1024,512]{1,0:T(8,128)(2,1)S(1)}, bf16[512,384]{1,0:T(8,128)(2,1)S(1)}, bf16[512,128]{1,0:T(8,128)(2,1)S...) custom-call(bf16[1024,512]{1,0:T(8,128)(2,1)} %bitcast.17, ...), custom_call_target="tpu_custom_call" | custom-call | flops 1 | bytes 1 | tf_op jit(solution)/shard_map/front/pallas_call | solution.py:519
  8.0 5.8 %attend_late.1 = (bf16[2,512,640]{2,1,0:T(8,128)(2,1)S(1)}, bf16[512,128]{1,0:T(8,128)(2,1)S(1)}, bf16[2,512,1536]{2,1,0:T(8,128)(2,1)S(1)}, bf16[512,128]{1,0:T(8,128)(2,1)S(1)}) custom-call(s32[1]{0:T(128)S(6)} %copy.39.refs_0_, bf16[1536,512]{1,0:T(8,128)(2,1)S(1)} %get-tuple-element.142.refs_1_, ...), custom_call_target="tpu_custom_call" | custom-call | flops 1 | bytes 1 | tf_op jit(solution)/shard_map/attend_late/pallas_call | solution.py:519
  13.8 0.2 collective-permute-start.5
  14.0 4.2 %attend_early.1 = (bf16[2,512,640]{2,1,0:T(8,128)(2,1)S(1)}, bf16[512,128]{1,0:T(8,128)(2,1)S(1)}, bf16[2,512,1024]{2,1,0:T(8,128)(2,1)S(1)}, bf16[512,128]{1,0:T(8,128)(2,1)S(1)}) custom-call(s32[1]{0:T(128)S(6)} %copy.39.refs_0_, bf16[1536,512]{1,0:T(8,128)(2,1)S(1)} %get-tuple-element.142.refs_1_, ...), custom_call_target="tpu_custom_call" | custom-call | flops 5000000000 | bytes 1 | tf_op jit(solution)/shard_map/attend_early/pallas_call | solution.py:519
  18.2 1.5 %collective-permute-done.5.refs_0_.refs_3_ = bf16[512,128]{1,0:T(8,128)(2,1)S(1)} collective-permute-done((bf16[512,128]{1,0:T(8,128)(2,1)S(1)}, bf16[512,128]{1,0:T(8,128)(2,1)S(1)}, u32[]{:S(2)}, u32[]{:S(2)}) %collective-permute-start.5) | collective-permute-done | bytes 131104 | tf_op jit(solution)/shard_map/ppermute | solution.py:532
  19.8 0.1 collective-permute-start.6
  19.9 0.5 collective-permute-start.4
  20.4 0.3 collective-permute-start.3
  20.7 0.9 collective-permute-done.4.refs_2_
  21.6 1.3 %ffn_send_late.1 = (f32[256,512]{1,0:T(8,128)S(1)}, bf16[256,512]{1,0:T(8,128)(2,1)S(1)}, bf16[256,512]{1,0:T(8,128)(2,1)S(1)}, bf16[256,512]{1,0:T(8,128)(2,1)S...) custom-call(bf16[1024,512]{1,0:T(8,128)(2,1)S(1)} %get-tuple-element.140.refs_0_, ...), custom_call_target="tpu_custom_call" | custom-call | flops 1 | bytes 1 | tf_op jit(solution)/shard_map/ffn_send_late/pallas_call | solution.py:519
  22.9 0.2 collective-permute-start.8
  23.1 2.8 %collective-permute-done.3.refs_15_.refs_3_ = bf16[512,128]{1,0:T(8,128)(2,1)S(1)} collective-permute-done((bf16[512,128]{1,0:T(8,128)(2,1)S(1)}, bf16[512,128]{1,0:T(8,128)(2,1)S(1)}, u32[]{:S(2)}, u32[]{:S(2)}) %collective-permute-start.3) | collective-permute-done | bytes 131104 | tf_op jit(solution)/shard_map/ppermute | solution.py:532
  25.9 1.3 %ffn_keep_late.1 = (f32[256,512]{1,0:T(8,128)S(1)}, bf16[256,512]{1,0:T(8,128)(2,1)S(1)}, bf16[256,512]{1,0:T(8,128)(2,1)S(1)}, bf16[256,512]{1,0:T(8,128)(2,1)S...) custom-call(bf16[1024,512]{1,0:T(8,128)(2,1)S(1)} %get-tuple-element.140.refs_0_, ...), custom_call_target="tpu_custom_call" | custom-call | flops 5000000000 | bytes 1 | tf_op jit(solution)/shard_map/ffn_keep_late/pallas_call | solution.py:519
  27.3 0.5 collective-permute-start.10
  27.8 0.5 collective-permute-start.7
  28.3 1.0 ffn_late.1
  29.3 2.6 %ffn_rows_early.1 = (f32[256,512]{1,0:T(8,128)S(1)}, bf16[256,512]{1,0:T(8,128)(2,1)S(1)}, bf16[256,512]{1,0:T(8,128)(2,1)S(1)}, bf16[256,512]{1,0:T(8,128)(2,1)...) custom-call(bf16[1024,512]{1,0:T(8,128)(2,1)S(1)} %get-tuple-element, ...), custom_call_target="tpu_custom_call" | custom-call | flops 1 | bytes 1 | tf_op jit(solution)/shard_map/ffn_rows_early/pallas_call | solution.py:519
  32.0 0.4 collective-permute-start.9
  32.4 1.1 %ffn_early.1 = (bf16[256,512]{1,0:T(8,128)(2,1)S(1)}, bf16[256,512]{1,0:T(8,128)(2,1)S(1)}, bf16[256,512]{1,0:T(8,128)(2,1)S(1)}, bf16[256,512]{1,0:T(8,128)(2,1...) custom-call(bf16[1024,512]{1,0:T(8,128)(2,1)S(1)} %get-tuple-element, ...), custom_call_target="tpu_custom_call" | custom-call | flops 1 | bytes 1 | tf_op jit(solution)/shard_map/ffn_early/pallas_call | solution.py:519
  33.5 1.3 %collective-permute-done.10.refs_1_ = bf16[256,512]{1,0:T(8,128)(2,1)S(1)} collective-permute-done((bf16[256,512]{1,0:T(8,128)(2,1)S(1)}, bf16[256,512]{1,0:T(8,128)(2,1)S(1)}, u32[]{:S(2)}, u32[]{:S(2)}) %collective-permute-start.10) | collective-permute-done | bytes 262176 | tf_op jit(solution)/shard_map/ppermute | solution.py:532
  34.8 0.1 collective-permute-start.14
  34.9 1.6 %collective-permute-start.12 = (bf16[256,512]{1,0:T(8,128)(2,1)S(1)}, bf16[256,512]{1,0:T(8,128)(2,1)S(1)}, u32[]{:S(2)}, u32[]{:S(2)}) collective-permute-start(bf16[256,512]{1,0:T(8,128)(2,1)S(1)} %get-tuple-element.186), channel_id=1, source_target_pairs={{0,4},{4,0},{8,12},{12,8},{16,20},{20,16},{24,28},{28,24},{1,5},{5... | collective-permute-start | bytes 786440 | tf_op jit(solution)/shard_map/ppermute | solution.py:532
  36.5 1.6 %collective-permute-start.13 = (bf16[256,512]{1,0:T(8,128)(2,1)S(1)}, bf16[256,512]{1,0:T(8,128)(2,1)S(1)}, u32[]{:S(2)}, u32[]{:S(2)}) collective-permute-start(bf16[256,512]{1,0:T(8,128)(2,1)S(1)} %get-tuple-element.188), channel_id=1, source_target_pairs={{0,8},{4,12},{8,0},{12,4},{16,24},{20,28},{24,16},{28,20},{1,9},{5... | collective-permute-start | bytes 786440 | tf_op jit(solution)/shard_map/ppermute | solution.py:532
  38.1 0.6 collective-permute-start.11
  38.7 6.4 %back_late.1 = (f32[512,512]{1,0:T(8,128)S(1)}, f32[128,1536]{1,0:T(8,128)S(1)}, f32[128,1536]{1,0:T(8,128)S(1)}, f32[128,512]{1,0:T(8,128)S(1)}, f32[128,512]{1...) custom-call(f32[256,512]{1,0:T(8,128)S(1)} %get-tuple-element.189.refs_0_.refs_6_,, ...), custom_call_target="tpu_custom_call" | custom-call | flops 1 | bytes 1 | tf_op jit(solution)/shard_map/back_late/pallas_call | solution.py:519
  45.1 1.2 %collective-permute-done.11.refs_1_ = bf16[256,512]{1,0:T(8,128)(2,1)S(1)} collective-permute-done((bf16[256,512]{1,0:T(8,128)(2,1)S(1)}, bf16[256,512]{1,0:T(8,128)(2,1)S(1)}, u32[]{:S(2)}, u32[]{:S(2)}) %collective-permute-start.11) | collective-permute-done | bytes 262176 | tf_op jit(solution)/shard_map/ppermute | solution.py:532
  46.3 0.5 add_middle.1
  46.8 0.1 collective-permute-start.15
  46.9 0.5 collective-permute-start.16
  47.4 0.5 collective-permute-start.17
  47.9 0.5 collective-permute-done.15.refs_3_
  48.4 4.6 %back_early.1 = (f32[512,512]{1,0:T(8,128)S(1)}, f32[128,1536]{1,0:T(8,128)S(1)}, f32[128,1536]{1,0:T(8,128)S(1)}, f32[128,512]{1,0:T(8,128)S(1)}, f32[128,512]{...) custom-call(f32[256,512]{1,0:T(8,128)S(1)} %get-tuple-element.170.refs_0_.refs_4_, ...), custom_call_target="tpu_custom_call" | custom-call | flops 1 | bytes 1 | tf_op jit(solution)/shard_map/back_early/pallas_call | solution.py:519
  53.1 1.8 %back_end.1 = (bf16[1024,512]{1,0:T(8,128)(2,1)S(1)}, bf16[1024,512]{1,0:T(8,128)(2,1)S(1)}, bf16[352,512]{1,0:T(8,128)(2,1)S(1)}, bf16[352,512]{1,0:T(8,128)(2,1)S(1)}, bf16[256,512]{1,0:T(8,128)(2,1)S(1)}) custom-call(bf16[512,384]{1,0:T(8,128)(2,1)S(1)} %get-tuple-element.145.refs_4_.refs_16_.refs_0_, bf16[1536,512]{1,0:T(8,128)(2,1)S(1)} %get-tuple-element.142.refs_1_, ...), custom_call_target="tpu_custom_call" | custom-call | flops 1 | bytes 1 | tf_op jit(solution)/shard_map/back_end/pallas_call | solution.py:519
  54.8 0.2 collective-permute-start.19
  55.1 0.9 collective-permute-start.18
  56.0 2.6 %collective-permute-start.21 = (bf16[256,512]{1,0:T(8,128)(2,1)S(1)}, bf16[256,512]{1,0:T(8,128)(2,1)S(1)}, u32[]{:S(2)}, u32[]{:S(2)}) collective-permute-start(bf16[256,512]{1,0:T(8,128)(2,1)S(1)} %get-tuple-element.231.refs_2_), channel_id=1, source_target_pairs={{0,16},{4,20},{8,24},{12,28},{16,0},{20,4},{24,8},{28,12},{1,17},{... | collective-permute-start | bytes 786440 | tf_op jit(solution)/shard_map/ppermute | solution.py:532
  58.6 7.1 %collective-permute-done.18.refs_1_ = bf16[352,512]{1,0:T(8,128)(2,1)S(1)} collective-permute-done((bf16[352,512]{1,0:T(8,128)(2,1)S(1)}, bf16[352,512]{1,0:T(8,128)(2,1)S(1)}, u32[]{:S(2)}, u32[]{:S(2)}) %collective-permute-start.18) | collective-permute-done | bytes 360480 | tf_op jit(solution)/shard_map/ppermute | solution.py:532
  65.7 0.5 step_0.1
  66.2 1.6 %collective-permute-start.20 = (bf16[176,512]{1,0:T(8,128)(2,1)S(1)}, bf16[176,512]{1,0:T(8,128)(2,1)S(1)}, u32[]{:S(2)}, u32[]{:S(2)}) collective-permute-start(bf16[176,512]{1,0:T(8,128)(2,1)S(1)} %get-tuple-element.230), channel_id=1, source_target_pairs={{0,8},{4,12},{8,0},{12,4},{16,24},{20,28},{24,16},{28,20},{1,9},{5... | collective-permute-start | bytes 540680 | tf_op jit(solution)/shard_map/ppermute | solution.py:532
  67.8 0.5 collective-permute-start.27
  68.3 2.7 %collective-permute-done.21.refs_3_ = bf16[256,512]{1,0:T(8,128)(2,1)S(1)} collective-permute-done((bf16[256,512]{1,0:T(8,128)(2,1)S(1)}, bf16[256,512]{1,0:T(8,128)(2,1)S(1)}, u32[]{:S(2)}, u32[]{:S(2)}) %collective-permute-start.21) | collective-permute-done | bytes 262176 | tf_op jit(solution)/shard_map/ppermute | solution.py:532
  71.0 3.8 %collective-permute-done.20.refs_1_ = bf16[176,512]{1,0:T(8,128)(2,1)S(1)} collective-permute-done((bf16[176,512]{1,0:T(8,128)(2,1)S(1)}, bf16[176,512]{1,0:T(8,128)(2,1)S(1)}, u32[]{:S(2)}, u32[]{:S(2)}) %collective-permute-start.20) | collective-permute-done | bytes 180256 | tf_op jit(solution)/shard_map/ppermute | solution.py:532
  74.8 0.1 step_1.1
  74.9 1.6 %collective-permute-start.22 = (bf16[176,512]{1,0:T(8,128)(2,1)S(1)}, bf16[176,512]{1,0:T(8,128)(2,1)S(1)}, u32[]{:S(2)}, u32[]{:S(2)}) collective-permute-start(bf16[176,512]{1,0:T(8,128)(2,1)S(1)} %get-tuple-element.232.refs_0_), channel_id=1, source_target_pairs={{0,16},{4,20},{8,24},{12,28},{16,0},{20,4},{24,8},{28,12},{1,17},{... | collective-permute-start | bytes 540680 | tf_op jit(solution)/shard_map/ppermute | solution.py:532
  76.5 2.5 %collective-permute-start.23 = (bf16[128,512]{1,0:T(8,128)(2,1)S(1)}, bf16[128,512]{1,0:T(8,128)(2,1)S(1)}, u32[]{:S(2)}, u32[]{:S(2)}) collective-permute-start(bf16[128,512]{1,0:T(8,128)(2,1)S(1)} %get-tuple-element.233.refs_2_), channel_id=1, source_target_pairs={{0,8},{4,12},{8,0},{12,4},{16,24},{20,28},{24,16},{28,20},{1,9},{5... | collective-permute-start | bytes 393224 | tf_op jit(solution)/shard_map/ppermute | solution.py:532
  79.0 1.0 collective-permute-start.24
  80.0 3.4 %collective-permute-done.23.refs_3_ = bf16[128,512]{1,0:T(8,128)(2,1)S(1)} collective-permute-done((bf16[128,512]{1,0:T(8,128)(2,1)S(1)}, bf16[128,512]{1,0:T(8,128)(2,1)S(1)}, u32[]{:S(2)}, u32[]{:S(2)}) %collective-permute-start.23) | collective-permute-done | bytes 131104 | tf_op jit(solution)/shard_map/ppermute | solution.py:532
  83.3 0.6 collective-permute-done.24.refs_5_
  84.0 2.2 %collective-permute-done.22.refs_1_ = bf16[176,512]{1,0:T(8,128)(2,1)S(1)} collective-permute-done((bf16[176,512]{1,0:T(8,128)(2,1)S(1)}, bf16[176,512]{1,0:T(8,128)(2,1)S(1)}, u32[]{:S(2)}, u32[]{:S(2)}) %collective-permute-start.22) | collective-permute-done | bytes 180256 | tf_op jit(solution)/shard_map/ppermute | solution.py:532
  86.2 0.2 step_2.1
  86.3 1.1 collective-permute-start.26
  87.4 5.3 %collective-permute-done.25.refs_1_ = bf16[160,512]{1,0:T(8,128)(2,1)S(1)} collective-permute-done((bf16[160,512]{1,0:T(8,128)(2,1)S(1)}, bf16[160,512]{1,0:T(8,128)(2,1)S(1)}, u32[]{:S(2)}, u32[]{:S(2)}) %collective-permute-start.25) | collective-permute-done | bytes 163872 | tf_op jit(solution)/shard_map/ppermute | solution.py:532
  92.7 1.1 %collective-permute-done.26.refs_3_ = bf16[256,512]{1,0:T(8,128)(2,1)S(1)} collective-permute-done((bf16[256,512]{1,0:T(8,128)(2,1)S(1)}, bf16[256,512]{1,0:T(8,128)(2,1)S(1)}, u32[]{:S(2)}, u32[]{:S(2)}) %collective-permute-start.26) | collective-permute-done | bytes 262176 | tf_op jit(solution)/shard_map/ppermute | solution.py:532
  93.8 0.5 step_3.1
  94.3 1.1 collective-permute-start.29
  95.4 0.5 collective-permute-start.30
  95.9 0.5 collective-permute-start.32
  96.4 0.6 collective-permute-done.28.refs_9_
  97.0 0.8 collective-permute-start.33
  97.8 3.4 %finish.1 = (bf16[1024,512]{1,0:T(8,128)(2,1)}, bf16[1024,512]{1,0:T(8,128)(2,1)}, f32[512,512]{1,0:T(8,128)}) custom-call(bf16[1024,512]{1,0:T(8,128)(2,1)S(1)} %get-tuple-element.140.refs_0_, f32[1,512]{1,0:T(1,128)S(1)} %get-tuple-element.141.refs_3_.refs_1_, f32[512,512]{1,0:T(8,128)S(1)} %get-tuple-element.204.refs_2_, ...), custom_call_target="tpu_custom_call" | custom-call | flops 1 | bytes 1 | tf_op jit(solution)/shard_map/finish/pallas_call | solution.py:519
  101.2 2.6 %collective-permute-done.30.refs_3_ = bf16[256,512]{1,0:T(8,128)(2,1)S(1)} collective-permute-done((bf16[256,512]{1,0:T(8,128)(2,1)S(1)}, bf16[256,512]{1,0:T(8,128)(2,1)S(1)}, u32[]{:S(2)}, u32[]{:S(2)}) %collective-permute-start.30) | collective-permute-done | bytes 262176 | tf_op jit(solution)/shard_map/ppermute | solution.py:532
  103.8 0.7 collective-permute-done.29.refs_1_
  104.5 2.3 %last.1 = (f32[512,512]{1,0:T(8,128)}, f32[512,128]{1,0:T(8,128)}, f32[512,128]{1,0:T(8,128)}, f32[512,128]{1,0:T(8,128)}, f32[512,128]{1,0:T(8,128)}, /*index=5...) custom-call(bf16[320,512]{1,0:T(8,128)(2,1)S(1)} %get-tuple-element., ...), custom_call_target="tpu_custom_call" | custom-call | flops 1 | bytes 1 | tf_op jit(solution)/shard_map/last/pallas_call | solution.py:519
  (28 shorter events, 0.4 us)
Async XLA Ops:
  0.7 13.4 %collective-permute-start.1 = (bf16[128,512]{1,0:T(8,128)(2,1)}, bf16[128,512]{1,0:T(8,128)(2,1)S(1)}, u32[]{:S(2)}, u32[]{:S(2)}) collective-permute-start(bf16[128,512]{1,0:T(8,128)(2,1)} %refs_5_.7), channel_id=1, source_target_pairs={{0,2},{1,3},{2,0},{3,1},{4,6},{5,7},{6,4},{7,5},{8,10},{9,11},{10,... | collective-permute-start | bytes 393224 | tf_op jit(solution)/shard_map/ppermute | solution.py:532
  3.7 10.3 %collective-permute-start = (bf16[128,512]{1,0:T(8,128)(2,1)}, bf16[128,512]{1,0:T(8,128)(2,1)S(1)}, u32[]{:S(2)}, u32[]{:S(2)}) collective-permute-start(bf16[128,512]{1,0:T(8,128)(2,1)} %refs_5_.7), channel_id=1, source_target_pairs={{0,1},{1,0},{2,3},{3,2},{4,5},{5,4},{6,7},{7,6},{8,9},{9,8},{10,11... | collective-permute-start | bytes 393224 | tf_op jit(solution)/shard_map/ppermute | solution.py:532
  13.8 7.8 %copy-start = (bf16[128,512]{1,0:T(8,128)(2,1)S(1)}, bf16[128,512]{1,0:T(8,128)(2,1)}, u32[]{:S(2)}) copy-start(bf16[128,512]{1,0:T(8,128)(2,1)} %refs_5_.7) | copy-start | bytes 393220
  13.8 6.0 %collective-permute-start.5 = (bf16[512,128]{1,0:T(8,128)(2,1)S(1)}, bf16[512,128]{1,0:T(8,128)(2,1)S(1)}, u32[]{:S(2)}, u32[]{:S(2)}) collective-permute-start(bf16[512,128]{1,0:T(8,128)(2,1)S(1)} %get-tuple-element.151.refs_1_.refs_7_), channel_id=1, source_target_pairs={{0,2},{1,3},{2,0},{3,1},{4,6},{5,7},{6,4},{7,5},{8,10},{9,11},{10,... | collective-permute-start | bytes 393224 | tf_op jit(solution)/shard_map/ppermute | solution.py:532
  19.8 1.8 %collective-permute-start.6 = (bf16[1024,128]{1,0:T(8,128)(2,1)S(1)}, bf16[1024,128]{1,0:T(8,128)(2,1)S(1)}, u32[]{:S(2)}, u32[]{:S(2)}) collective-permute-start(bf16[1024,128]{1,0:T(8,128)(2,1)S(1)} %relay_late.1), channel_id=1, source_target_pairs={{0,1},{1,0},{2,3},{3,2},{4,5},{5,4},{6,7},{7,6},{8,9},{9,8},{10,11... | collective-permute-start | bytes 786440 | tf_op jit(solution)/shard_map/ppermute | solution.py:532
  19.9 1.7 %collective-permute-start.4 = (bf16[512,128]{1,0:T(8,128)(2,1)S(1)}, bf16[512,128]{1,0:T(8,128)(2,1)S(1)}, u32[]{:S(2)}, u32[]{:S(2)}) collective-permute-start(bf16[512,128]{1,0:T(8,128)(2,1)S(1)} %get-tuple-element.151.refs_1_.refs_7_), channel_id=1, source_target_pairs={{0,1},{1,0},{2,3},{3,2},{4,5},{5,4},{6,7},{7,6},{8,9},{9,8},{10,11... | collective-permute-start | bytes 393224 | tf_op jit(solution)/shard_map/ppermute | solution.py:532
  20.4 5.5 %collective-permute-start.3 = (bf16[512,128]{1,0:T(8,128)(2,1)S(1)}, bf16[512,128]{1,0:T(8,128)(2,1)S(1)}, u32[]{:S(2)}, u32[]{:S(2)}) collective-permute-start(bf16[512,128]{1,0:T(8,128)(2,1)S(1)} %get-tuple-element.150.refs_2_.refs_1_.refs_7_), channel_id=1, source_target_pairs={{0,2},{1,3},{2,0},{3,1},{4,6},{5,7},{6,4},{7,5},{8,10},{9,11},{10,... | collective-permute-start | bytes 393224 | tf_op jit(solution)/shard_map/ppermute | solution.py:532
  22.9 4.3 %collective-permute-start.8 = (bf16[256,512]{1,0:T(8,128)(2,1)S(1)}, bf16[256,512]{1,0:T(8,128)(2,1)S(1)}, u32[]{:S(2)}, u32[]{:S(2)}) collective-permute-start(bf16[256,512]{1,0:T(8,128)(2,1)S(1)} %get-tuple-element.158.refs_16_), channel_id=1, source_target_pairs={{0,1},{1,0},{2,3},{3,2},{4,5},{5,4},{6,7},{7,6},{8,9},{9,8},{10,11... | collective-permute-start | bytes 786440 | tf_op jit(solution)/shard_map/ppermute | solution.py:532
  27.3 7.5 %collective-permute-start.10 = (bf16[256,512]{1,0:T(8,128)(2,1)S(1)}, bf16[256,512]{1,0:T(8,128)(2,1)S(1)}, u32[]{:S(2)}, u32[]{:S(2)}) collective-permute-start(bf16[256,512]{1,0:T(8,128)(2,1)S(1)} %add_late.1.refs_10_.refs_0_), channel_id=1, source_target_pairs={{0,2},{1,3},{2,0},{3,1},{4,6},{5,7},{6,4},{7,5},{8,10},{9,11},{10,... | collective-permute-start | bytes 786440 | tf_op jit(solution)/shard_map/ppermute | solution.py:532
  27.8 1.5 %collective-permute-start.2 = (bf16[512,128]{1,0:T(8,128)(2,1)S(1)}, bf16[512,128]{1,0:T(8,128)(2,1)S(1)}, u32[]{:S(2)}, u32[]{:S(2)}) collective-permute-start(bf16[512,128]{1,0:T(8,128)(2,1)S(1)} %get-tuple-element.150.refs_2_.refs_1_.refs_7_), channel_id=1, source_target_pairs={{0,1},{1,0},{2,3},{3,2},{4,5},{5,4},{6,7},{7,6},{8,9},{9,8},{10,11... | collective-permute-start | bytes 393224 | tf_op jit(solution)/shard_map/ppermute | solution.py:532
  27.8 1.5 %collective-permute-start.7 = (bf16[512,128]{1,0:T(8,128)(2,1)S(1)}, bf16[512,128]{1,0:T(8,128)(2,1)S(1)}, u32[]{:S(2)}, u32[]{:S(2)}) collective-permute-start(bf16[512,128]{1,0:T(8,128)(2,1)S(1)} %get-tuple-element.159), channel_id=1, source_target_pairs={{0,1},{1,0},{2,3},{3,2},{4,5},{5,4},{6,7},{7,6},{8,9},{9,8},{10,11... | collective-permute-start | bytes 393224 | tf_op jit(solution)/shard_map/ppermute | solution.py:532
  32.0 6.1 %collective-permute-start.9 = (bf16[256,512]{1,0:T(8,128)(2,1)S(1)}, bf16[256,512]{1,0:T(8,128)(2,1)S(1)}, u32[]{:S(2)}, u32[]{:S(2)}) collective-permute-start(bf16[256,512]{1,0:T(8,128)(2,1)S(1)} %get-tuple-element.173), channel_id=1, source_target_pairs={{0,1},{1,0},{2,3},{3,2},{4,5},{5,4},{6,7},{7,6},{8,9},{9,8},{10,11... | collective-permute-start | bytes 786440 | tf_op jit(solution)/shard_map/ppermute | solution.py:532
  34.8 3.9 %collective-permute-start.14 = (bf16[256,512]{1,0:T(8,128)(2,1)S(1)}, bf16[256,512]{1,0:T(8,128)(2,1)S(1)}, u32[]{:S(2)}, u32[]{:S(2)}) collective-permute-start(bf16[256,512]{1,0:T(8,128)(2,1)S(1)} %add_late_chips.1.refs_2_), channel_id=1, source_target_pairs={{0,1},{1,0},{2,3},{3,2},{4,5},{5,4},{6,7},{7,6},{8,9},{9,8},{10,11... | collective-permute-start | bytes 786440 | tf_op jit(solution)/shard_map/ppermute | solution.py:532
  34.9 10.2 %collective-permute-start.12 = (bf16[256,512]{1,0:T(8,128)(2,1)S(1)}, bf16[256,512]{1,0:T(8,128)(2,1)S(1)}, u32[]{:S(2)}, u32[]{:S(2)}) collective-permute-start(bf16[256,512]{1,0:T(8,128)(2,1)S(1)} %get-tuple-element.186), channel_id=1, source_target_pairs={{0,4},{4,0},{8,12},{12,8},{16,20},{20,16},{24,28},{28,24},{1,5},{5... | collective-permute-start | bytes 786440 | tf_op jit(solution)/shard_map/ppermute | solution.py:532
  36.5 8.6 %collective-permute-start.13 = (bf16[256,512]{1,0:T(8,128)(2,1)S(1)}, bf16[256,512]{1,0:T(8,128)(2,1)S(1)}, u32[]{:S(2)}, u32[]{:S(2)}) collective-permute-start(bf16[256,512]{1,0:T(8,128)(2,1)S(1)} %get-tuple-element.188), channel_id=1, source_target_pairs={{0,8},{4,12},{8,0},{12,4},{16,24},{20,28},{24,16},{28,20},{1,9},{5... | collective-permute-start | bytes 786440 | tf_op jit(solution)/shard_map/ppermute | solution.py:532
  38.1 8.2 %collective-permute-start.11 = (bf16[256,512]{1,0:T(8,128)(2,1)S(1)}, bf16[256,512]{1,0:T(8,128)(2,1)S(1)}, u32[]{:S(2)}, u32[]{:S(2)}) collective-permute-start(bf16[256,512]{1,0:T(8,128)(2,1)S(1)} %add_early.1.refs_0_), channel_id=1, source_target_pairs={{0,2},{1,3},{2,0},{3,1},{4,6},{5,7},{6,4},{7,5},{8,10},{9,11},{10,... | collective-permute-start | bytes 786440 | tf_op jit(solution)/shard_map/ppermute | solution.py:532
  46.8 1.6 %collective-permute-start.15 = (bf16[256,512]{1,0:T(8,128)(2,1)S(1)}, bf16[256,512]{1,0:T(8,128)(2,1)S(1)}, u32[]{:S(2)}, u32[]{:S(2)}) collective-permute-start(bf16[256,512]{1,0:T(8,128)(2,1)S(1)} %get-tuple-element.196.refs_2_), channel_id=1, source_target_pairs={{0,1},{1,0},{2,3},{3,2},{4,5},{5,4},{6,7},{7,6},{8,9},{9,8},{10,11... | collective-permute-start | bytes 786440 | tf_op jit(solution)/shard_map/ppermute | solution.py:532
  46.9 6.2 %collective-permute-start.16 = (bf16[128,512]{1,0:T(8,128)(2,1)S(1)}, bf16[128,512]{1,0:T(8,128)(2,1)S(1)}, u32[]{:S(2)}, u32[]{:S(2)}) collective-permute-start(bf16[128,512]{1,0:T(8,128)(2,1)S(1)} %get-tuple-element.222), channel_id=1, source_target_pairs={{0,8},{4,12},{8,0},{12,4},{16,24},{20,28},{24,16},{28,20},{1,9},{5... | collective-permute-start | bytes 393224 | tf_op jit(solution)/shard_map/ppermute | solution.py:532
  47.4 5.7 %collective-permute-start.17 = (bf16[128,512]{1,0:T(8,128)(2,1)S(1)}, bf16[128,512]{1,0:T(8,128)(2,1)S(1)}, u32[]{:S(2)}, u32[]{:S(2)}) collective-permute-start(bf16[128,512]{1,0:T(8,128)(2,1)S(1)} %get-tuple-element.224), channel_id=1, source_target_pairs={{0,4},{4,0},{8,12},{12,8},{16,20},{20,16},{24,28},{28,24},{1,5},{5... | collective-permute-start | bytes 393224 | tf_op jit(solution)/shard_map/ppermute | solution.py:532
  54.8 10.9 %collective-permute-start.19 = (bf16[1024,512]{1,0:T(8,128)(2,1)S(1)}, bf16[1024,512]{1,0:T(8,128)(2,1)S(1)}, u32[]{:S(2)}, u32[]{:S(2)}) collective-permute-start(bf16[1024,512]{1,0:T(8,128)(2,1)S(1)} %get-tuple-element.228), channel_id=1, source_target_pairs={{0,1},{1,0},{2,3},{3,2},{4,5},{5,4},{6,7},{7,6},{8,9},{9,8},{10,11... | collective-permute-start | bytes 3145736 | tf_op jit(solution)/shard_map/ppermute | solution.py:532
  55.1 10.7 %collective-permute-start.18 = (bf16[352,512]{1,0:T(8,128)(2,1)S(1)}, bf16[352,512]{1,0:T(8,128)(2,1)S(1)}, u32[]{:S(2)}, u32[]{:S(2)}) collective-permute-start(bf16[352,512]{1,0:T(8,128)(2,1)S(1)} %get-tuple-element.226), channel_id=1, source_target_pairs={{0,4},{4,0},{8,12},{12,8},{16,20},{20,16},{24,28},{28,24},{1,5},{5... | collective-permute-start | bytes 1081352 | tf_op jit(solution)/shard_map/ppermute | solution.py:532
  56.0 15.0 %collective-permute-start.21 = (bf16[256,512]{1,0:T(8,128)(2,1)S(1)}, bf16[256,512]{1,0:T(8,128)(2,1)S(1)}, u32[]{:S(2)}, u32[]{:S(2)}) collective-permute-start(bf16[256,512]{1,0:T(8,128)(2,1)S(1)} %get-tuple-element.231.refs_2_), channel_id=1, source_target_pairs={{0,16},{4,20},{8,24},{12,28},{16,0},{20,4},{24,8},{28,12},{1,17},{... | collective-permute-start | bytes 786440 | tf_op jit(solution)/shard_map/ppermute | solution.py:532
  66.2 8.6 %collective-permute-start.20 = (bf16[176,512]{1,0:T(8,128)(2,1)S(1)}, bf16[176,512]{1,0:T(8,128)(2,1)S(1)}, u32[]{:S(2)}, u32[]{:S(2)}) collective-permute-start(bf16[176,512]{1,0:T(8,128)(2,1)S(1)} %get-tuple-element.230), channel_id=1, source_target_pairs={{0,8},{4,12},{8,0},{12,4},{16,24},{20,28},{24,16},{28,20},{1,9},{5... | collective-permute-start | bytes 540680 | tf_op jit(solution)/shard_map/ppermute | solution.py:532
  67.8 26.0 %collective-permute-start.27 = (bf16[1024,512]{1,0:T(8,128)(2,1)S(1)}, bf16[1024,512]{1,0:T(8,128)(2,1)S(1)}, u32[]{:S(2)}, u32[]{:S(2)}) collective-permute-start(bf16[1024,512]{1,0:T(8,128)(2,1)S(1)} %get-tuple-element.239.refs_8_), channel_id=1, source_target_pairs={{0,2},{1,3},{2,0},{3,1},{4,6},{5,7},{6,4},{7,5},{8,10},{9,11},{10,... | collective-permute-start | bytes 3145736 | tf_op jit(solution)/shard_map/ppermute | solution.py:532
  74.9 11.3 %collective-permute-start.22 = (bf16[176,512]{1,0:T(8,128)(2,1)S(1)}, bf16[176,512]{1,0:T(8,128)(2,1)S(1)}, u32[]{:S(2)}, u32[]{:S(2)}) collective-permute-start(bf16[176,512]{1,0:T(8,128)(2,1)S(1)} %get-tuple-element.232.refs_0_), channel_id=1, source_target_pairs={{0,16},{4,20},{8,24},{12,28},{16,0},{20,4},{24,8},{28,12},{1,17},{... | collective-permute-start | bytes 540680 | tf_op jit(solution)/shard_map/ppermute | solution.py:532
  76.5 6.8 %collective-permute-start.23 = (bf16[128,512]{1,0:T(8,128)(2,1)S(1)}, bf16[128,512]{1,0:T(8,128)(2,1)S(1)}, u32[]{:S(2)}, u32[]{:S(2)}) collective-permute-start(bf16[128,512]{1,0:T(8,128)(2,1)S(1)} %get-tuple-element.233.refs_2_), channel_id=1, source_target_pairs={{0,8},{4,12},{8,0},{12,4},{16,24},{20,28},{24,16},{28,20},{1,9},{5... | collective-permute-start | bytes 393224 | tf_op jit(solution)/shard_map/ppermute | solution.py:532
  79.0 5.0 %collective-permute-start.24 = (bf16[128,512]{1,0:T(8,128)(2,1)S(1)}, bf16[128,512]{1,0:T(8,128)(2,1)S(1)}, u32[]{:S(2)}, u32[]{:S(2)}) collective-permute-start(bf16[128,512]{1,0:T(8,128)(2,1)S(1)} %get-tuple-element.234.refs_4_), channel_id=1, source_target_pairs={{0,4},{4,0},{8,12},{12,8},{16,20},{20,16},{24,28},{28,24},{1,5},{5... | collective-permute-start | bytes 393224 | tf_op jit(solution)/shard_map/ppermute | solution.py:532
  86.3 7.5 %collective-permute-start.26 = (bf16[256,512]{1,0:T(8,128)(2,1)S(1)}, bf16[256,512]{1,0:T(8,128)(2,1)S(1)}, u32[]{:S(2)}, u32[]{:S(2)}) collective-permute-start(bf16[256,512]{1,0:T(8,128)(2,1)S(1)} %get-tuple-element.236.refs_2_), channel_id=1, source_target_pairs={{0,4},{4,0},{8,12},{12,8},{16,20},{20,16},{24,28},{28,24},{1,5},{5... | collective-permute-start | bytes 786440 | tf_op jit(solution)/shard_map/ppermute | solution.py:532
  87.4 5.3 %collective-permute-start.25 = (bf16[160,512]{1,0:T(8,128)(2,1)S(1)}, bf16[160,512]{1,0:T(8,128)(2,1)S(1)}, u32[]{:S(2)}, u32[]{:S(2)}) collective-permute-start(bf16[160,512]{1,0:T(8,128)(2,1)S(1)} %get-tuple-element.235.refs_0_), channel_id=1, source_target_pairs={{0,8},{4,12},{8,0},{12,4},{16,24},{20,28},{24,16},{28,20},{1,9},{5... | collective-permute-start | bytes 491528 | tf_op jit(solution)/shard_map/ppermute | solution.py:532
  94.3 2.7 %collective-permute-start.28 = (bf16[1024,512]{1,0:T(8,128)(2,1)S(1)}, bf16[1024,512]{1,0:T(8,128)(2,1)S(1)}, u32[]{:S(2)}, u32[]{:S(2)}) collective-permute-start(bf16[1024,512]{1,0:T(8,128)(2,1)S(1)} %get-tuple-element.240.refs_8_), channel_id=1, source_target_pairs={{0,1},{1,0},{2,3},{3,2},{4,5},{5,4},{6,7},{7,6},{8,9},{9,8},{10,11... | collective-permute-start | bytes 3145736 | tf_op jit(solution)/shard_map/ppermute | solution.py:532
  94.3 10.1 %collective-permute-start.29 = (bf16[320,512]{1,0:T(8,128)(2,1)S(1)}, bf16[320,512]{1,0:T(8,128)(2,1)S(1)}, u32[]{:S(2)}, u32[]{:S(2)}) collective-permute-start(bf16[320,512]{1,0:T(8,128)(2,1)S(1)} %get-tuple-element.243.refs_12_.refs_0_), channel_id=1, source_target_pairs={{0,4},{4,0},{8,12},{12,8},{16,20},{20,16},{24,28},{28,24},{1,5},{5... | collective-permute-start | bytes 983048 | tf_op jit(solution)/shard_map/ppermute | solution.py:532
  95.4 8.4 %collective-permute-start.30 = (bf16[256,512]{1,0:T(8,128)(2,1)S(1)}, bf16[256,512]{1,0:T(8,128)(2,1)S(1)}, u32[]{:S(2)}, u32[]{:S(2)}) collective-permute-start(bf16[256,512]{1,0:T(8,128)(2,1)S(1)} %get-tuple-element.246.refs_2_), channel_id=1, source_target_pairs={{0,8},{4,12},{8,0},{12,4},{16,24},{20,28},{24,16},{28,20},{1,9},{5... | collective-permute-start | bytes 786440 | tf_op jit(solution)/shard_map/ppermute | solution.py:532
  95.9 5.2 %collective-permute-start.31 = (f32[16,512]{1,0:T(8,128)S(1)}, f32[16,512]{1,0:T(8,128)S(1)}, u32[]{:S(2)}, u32[]{:S(2)}) collective-permute-start(f32[16,512]{1,0:T(8,128)S(1)} %get-tuple-element.247.refs_4_), channel_id=1, source_target_pairs={{0,1},{1,0},{2,3},{3,2},{4,5},{5,4},{6,7},{7,6},{8,9},{9,8},{10,11... | collective-permute-start | bytes 98312 | tf_op jit(solution)/shard_map/ppermute | solution.py:532
  95.9 5.2 %collective-permute-start.32 = (f32[16,512]{1,0:T(8,128)S(1)}, f32[16,512]{1,0:T(8,128)S(1)}, u32[]{:S(2)}, u32[]{:S(2)}) collective-permute-start(f32[16,512]{1,0:T(8,128)S(1)} %get-tuple-element.247.refs_4_), channel_id=1, source_target_pairs={{0,2},{1,3},{2,0},{3,1},{4,6},{5,7},{6,4},{7,5},{8,10},{9,11},{10,... | collective-permute-start | bytes 98312 | tf_op jit(solution)/shard_map/ppermute | solution.py:532
  97.0 4.2 %collective-permute-start.33 = (f32[16,512]{1,0:T(8,128)S(1)}, f32[16,512]{1,0:T(8,128)S(1)}, u32[]{:S(2)}, u32[]{:S(2)}) collective-permute-start(f32[16,512]{1,0:T(8,128)S(1)} %get-tuple-element.247.refs_4_), channel_id=1, source_target_pairs={{0,3},{1,2},{2,1},{3,0},{4,7},{5,6},{6,5},{7,4},{8,11},{9,10},{10,... | collective-permute-start | bytes 98312 | tf_op jit(solution)/shard_map/ppermute | solution.py:532

commit v4 on v3

--- a/solution.py
+++ b/solution.py
@@ -209,14 +209,10 @@
 
 
 def ffn_rows_kernel(
-    first, block, roles, relay,
+    first, block, roles,
     place_ref, x_ref, c0_ref, c1_ref, c2_ref, c3_ref, o0_ref, o1_ref, o2_ref, o3_ref, gain_ref, shift_ref, up_ref,
     upb_ref, down_ref, g_ref, *refs,
 ):
-    if relay:
-        ctx_in, *refs = refs
-        *refs, ctx_out = refs
-        ctx_out[...] = ctx_in[...]
     core = place_ref[0]
     wide = c0_ref.shape[1]
     size = c0_ref.shape[0]
@@ -688,20 +684,20 @@
         ((block, width), BF),
     ]
 
-    def ffn_rows(first, ctx, roles, name, beside=(), after=(), cost=1):
+    def ffn_rows(first, ctx, roles, name, after=()):
         found = call(
-            functools.partial(ffn_rows_kernel, first, block, roles, len(beside)),
-            half_outs * len(roles) + [(r.shape, BF) for r in beside],
-            (place, x, *ctx, *outs_of, ffn_gain, ffn_shift, w_up, up_bias, w_down, g, *beside), name, cost, after=after,
+            functools.partial(ffn_rows_kernel, first, block, roles), half_outs * len(roles),
+            (place, x, *ctx, *outs_of, ffn_gain, ffn_shift, w_up, up_bias, w_down, g), name, 1, after=after,
         )
-        return *(found[i : i + 6] for i in range(0, 6 * len(roles), 6)), *found[6 * len(roles) :]
+        return [found[i : i + 6] for i in range(0, 6 * len(roles), 6)]
 
     sum_outs = [((width, ff), FL), ((ff, width), FL), ((3, width), FL), ((1, ff), FL)]
     (send_l,) = ffn_rows(late, ctx_l, ("send",), "ffn_send_late")
     gnt_l = cores(send_l[-1], n_tensor)
-    keep_l, relay = ffn_rows(late, ctx_l, ("keep",), "ffn_keep_late", ctx_e[2:3], send_l[-1:], 5e9)
+    (keep_l,) = ffn_rows(late, ctx_l, ("keep",), "ffn_keep_late", after=send_l[-1:])
+    (relay,) = work(place, [("copy", 0, ctx_e[2], ctx_e[2])], "relay_early", keep_l[-1:], 5e9)
     ctx_e.append(cores(relay, n_tensor))
-    (gnt_l,) = work(place, [("sum", 0, keep_l[-1], gnt_l)], "add_late")
+    (gnt_l,) = work(place, [("sum", 0, keep_l[-1], gnt_l)], "add_late", (relay,))
     gnt_l = chips(gnt_l, n_tensor)
     shares_l, sums_l = split_at(2, call(
         functools.partial(ffn_late_kernel, late),

time: 107 us -> 106 us (level)
  waiting for transfers between devices: 38.2 us -> 36.9 us
    ppermute x34, waiting for transfers between devices: 38.2 us -> 36.9 us  [swap(): return lax.ppermute(rows, axis, [(i, i ^ bit) for i in range(size)])]
    pallas_call x22 -> x23, Pallas kernels: 41.4 us -> 41.5 us  [call(): pl.pallas_call(body, out_shape=[pltpu.HBM(s, d) if i < far else jax.Shape...]
where the time goes in v4:
time: 106 us
  Pallas kernels  41.5 us (39%)
  waiting for transfers between devices  36.9 us (35%)
  starting transfers between devices  25.7 us (24%)
  between operations  1.74 us (2%)
    pallas_call x23, Pallas kernels, call(): pl.pallas_call(body, out_shape=[pltpu.HBM(s, d) if i < far else jax.Shape...  41.5 us
    ppermute x34, waiting for transfers between devices, swap(): return lax.ppermute(rows, axis, [(i, i ^ bit) for i in range(size)])  36.9 us
    ppermute x34, starting transfers between devices, swap(): return lax.ppermute(rows, axis, [(i, i ^ bit) for i in range(size)])  25.7 us
  transfers between devices with their start and end apart: 34, of which 17 were waited for; matrix products, arithmetic and copies ran while one was open for 0% of the time, Pallas kernels for 34%

profile of v4, /device:TPU:0, one launch (start us, length us, event | category | flops | bytes accessed | tf_op | source)
XLA Modules:
  0.0 105.7 jit_solution(16574520961583126013)
XLA Ops:
  0.7 3.0 %collective-permute-start.1 = (bf16[128,512]{1,0:T(8,128)(2,1)}, bf16[128,512]{1,0:T(8,128)(2,1)S(1)}, u32[]{:S(2)}, u32[]{:S(2)}) collective-permute-start(bf16[128,512]{1,0:T(8,128)(2,1)} %refs_5_.7), channel_id=1, source_target_pairs={{0,2},{1,3},{2,0},{3,1},{4,6},{5,7},{6,4},{7,5},{8,10},{9,11},{10,... | collective-permute-start | bytes 393224 | tf_op jit(solution)/shard_map/ppermute | solution.py:528
  3.7 3.6 %front.1 = (bf16[1024,512]{1,0:T(8,128)(2,1)S(1)}, bf16[1024,512]{1,0:T(8,128)(2,1)S(1)}, bf16[512,384]{1,0:T(8,128)(2,1)S(1)}, bf16[512,128]{1,0:T(8,128)(2,1)S...) custom-call(bf16[1024,512]{1,0:T(8,128)(2,1)} %bitcast.17, ...), custom_call_target="tpu_custom_call" | custom-call | flops 1 | bytes 1 | tf_op jit(solution)/shard_map/front/pallas_call | solution.py:515
  8.0 5.8 %attend_late.1 = (bf16[2,512,640]{2,1,0:T(8,128)(2,1)S(1)}, bf16[512,128]{1,0:T(8,128)(2,1)S(1)}, bf16[2,512,1536]{2,1,0:T(8,128)(2,1)S(1)}, bf16[512,128]{1,0:T(8,128)(2,1)S(1)}) custom-call(s32[1]{0:T(128)S(6)} %copy.39.refs_0_, bf16[1536,512]{1,0:T(8,128)(2,1)S(1)} %get-tuple-element.141.refs_1_, ...), custom_call_target="tpu_custom_call" | custom-call | flops 1 | bytes 1 | tf_op jit(solution)/shard_map/attend_late/pallas_call | solution.py:515
  13.8 0.2 collective-permute-start.5
  14.0 4.2 %attend_early.1 = (bf16[2,512,640]{2,1,0:T(8,128)(2,1)S(1)}, bf16[512,128]{1,0:T(8,128)(2,1)S(1)}, bf16[2,512,1024]{2,1,0:T(8,128)(2,1)S(1)}, bf16[512,128]{1,0:T(8,128)(2,1)S(1)}) custom-call(s32[1]{0:T(128)S(6)} %copy.39.refs_0_, bf16[1536,512]{1,0:T(8,128)(2,1)S(1)} %get-tuple-element.141.refs_1_, ...), custom_call_target="tpu_custom_call" | custom-call | flops 5000000000 | bytes 1 | tf_op jit(solution)/shard_map/attend_early/pallas_call | solution.py:515
  18.2 1.6 %collective-permute-done.5.refs_0_.refs_3_ = bf16[512,128]{1,0:T(8,128)(2,1)S(1)} collective-permute-done((bf16[512,128]{1,0:T(8,128)(2,1)S(1)}, bf16[512,128]{1,0:T(8,128)(2,1)S(1)}, u32[]{:S(2)}, u32[]{:S(2)}) %collective-permute-start.5) | collective-permute-done | bytes 131104 | tf_op jit(solution)/shard_map/ppermute | solution.py:528
  19.8 0.1 collective-permute-start.6
  19.9 0.5 collective-permute-start.4
  20.4 0.3 collective-permute-start.3
  20.7 0.9 collective-permute-done.4.refs_2_
  21.6 1.3 %ffn_send_late.1 = (f32[256,512]{1,0:T(8,128)S(1)}, bf16[256,512]{1,0:T(8,128)(2,1)S(1)}, bf16[256,512]{1,0:T(8,128)(2,1)S(1)}, bf16[256,512]{1,0:T(8,128)(2,1)S...) custom-call(bf16[1024,512]{1,0:T(8,128)(2,1)S(1)} %get-tuple-element.139.refs_0_, ...), custom_call_target="tpu_custom_call" | custom-call | flops 1 | bytes 1 | tf_op jit(solution)/shard_map/ffn_send_late/pallas_call | solution.py:515
  22.9 0.2 collective-permute-start.8
  23.1 1.3 %ffn_keep_late.1 = (f32[256,512]{1,0:T(8,128)S(1)}, bf16[256,512]{1,0:T(8,128)(2,1)S(1)}, bf16[256,512]{1,0:T(8,128)(2,1)S(1)}, bf16[256,512]{1,0:T(8,128)(2,1)S...) custom-call(bf16[1024,512]{1,0:T(8,128)(2,1)S(1)} %get-tuple-element.139.refs_0_, ...), custom_call_target="tpu_custom_call" | custom-call | flops 1 | bytes 1 | tf_op jit(solution)/shard_map/ffn_keep_late/pallas_call | solution.py:515
  24.4 1.4 %collective-permute-done.3.refs_0_.refs_1_.refs_3_ = bf16[512,128]{1,0:T(8,128)(2,1)S(1)} collective-permute-done((bf16[512,128]{1,0:T(8,128)(2,1)S(1)}, bf16[512,128]{1,0:T(8,128)(2,1)S(1)}, u32[]{:S(2)}, u32[]{:S(2)}) %collective-permute-start.3) | collective-permute-done | bytes 131104 | tf_op jit(solution)/shard_map/ppermute | solution.py:528
  25.9 0.1 add_late.1.refs_10_.refs_0_
  26.0 0.6 collective-permute-start.10
  26.5 0.5 collective-permute-start.7
  27.0 1.0 ffn_late.1
  28.1 2.7 %ffn_rows_early.1 = (f32[256,512]{1,0:T(8,128)S(1)}, bf16[256,512]{1,0:T(8,128)(2,1)S(1)}, bf16[256,512]{1,0:T(8,128)(2,1)S(1)}, bf16[256,512]{1,0:T(8,128)(2,1)...) custom-call(bf16[1024,512]{1,0:T(8,128)(2,1)S(1)} %get-tuple-element, ...), custom_call_target="tpu_custom_call" | custom-call | flops 1 | bytes 1 | tf_op jit(solution)/shard_map/ffn_rows_early/pallas_call | solution.py:515
  30.7 0.4 collective-permute-start.9
  31.1 1.1 %ffn_early.1 = (bf16[256,512]{1,0:T(8,128)(2,1)S(1)}, bf16[256,512]{1,0:T(8,128)(2,1)S(1)}, bf16[256,512]{1,0:T(8,128)(2,1)S(1)}, bf16[256,512]{1,0:T(8,128)(2,1...) custom-call(bf16[1024,512]{1,0:T(8,128)(2,1)S(1)} %get-tuple-element, ...), custom_call_target="tpu_custom_call" | custom-call | flops 1 | bytes 1 | tf_op jit(solution)/shard_map/ffn_early/pallas_call | solution.py:515
  32.3 1.2 %collective-permute-done.10.refs_1_ = bf16[256,512]{1,0:T(8,128)(2,1)S(1)} collective-permute-done((bf16[256,512]{1,0:T(8,128)(2,1)S(1)}, bf16[256,512]{1,0:T(8,128)(2,1)S(1)}, u32[]{:S(2)}, u32[]{:S(2)}) %collective-permute-start.10) | collective-permute-done | bytes 262176 | tf_op jit(solution)/shard_map/ppermute | solution.py:528
  33.5 0.1 collective-permute-start.14
  33.6 1.6 %collective-permute-start.12 = (bf16[256,512]{1,0:T(8,128)(2,1)S(1)}, bf16[256,512]{1,0:T(8,128)(2,1)S(1)}, u32[]{:S(2)}, u32[]{:S(2)}) collective-permute-start(bf16[256,512]{1,0:T(8,128)(2,1)S(1)} %get-tuple-element.184), channel_id=1, source_target_pairs={{0,4},{4,0},{8,12},{12,8},{16,20},{20,16},{24,28},{28,24},{1,5},{5... | collective-permute-start | bytes 786440 | tf_op jit(solution)/shard_map/ppermute | solution.py:528
  35.2 1.6 %collective-permute-start.13 = (bf16[256,512]{1,0:T(8,128)(2,1)S(1)}, bf16[256,512]{1,0:T(8,128)(2,1)S(1)}, u32[]{:S(2)}, u32[]{:S(2)}) collective-permute-start(bf16[256,512]{1,0:T(8,128)(2,1)S(1)} %get-tuple-element.186), channel_id=1, source_target_pairs={{0,8},{4,12},{8,0},{12,4},{16,24},{20,28},{24,16},{28,20},{1,9},{5... | collective-permute-start | bytes 786440 | tf_op jit(solution)/shard_map/ppermute | solution.py:528
  36.8 0.6 collective-permute-start.11
  37.4 6.4 %back_late.1 = (f32[512,512]{1,0:T(8,128)S(1)}, f32[128,1536]{1,0:T(8,128)S(1)}, f32[128,1536]{1,0:T(8,128)S(1)}, f32[128,512]{1,0:T(8,128)S(1)}, f32[128,512]{1...) custom-call(f32[256,512]{1,0:T(8,128)S(1)} %get-tuple-element.187.refs_0_.refs_6_,, ...), custom_call_target="tpu_custom_call" | custom-call | flops 1 | bytes 1 | tf_op jit(solution)/shard_map/back_late/pallas_call | solution.py:515
  43.9 1.1 %collective-permute-done.11.refs_1_ = bf16[256,512]{1,0:T(8,128)(2,1)S(1)} collective-permute-done((bf16[256,512]{1,0:T(8,128)(2,1)S(1)}, bf16[256,512]{1,0:T(8,128)(2,1)S(1)}, u32[]{:S(2)}, u32[]{:S(2)}) %collective-permute-start.11) | collective-permute-done | bytes 262176 | tf_op jit(solution)/shard_map/ppermute | solution.py:528
  45.0 0.5 add_middle.1
  45.6 0.5 collective-permute-start.16
  46.1 0.5 collective-permute-start.17
  46.7 0.5 collective-permute-done.15.refs_3_
  47.1 4.6 %back_early.1 = (f32[512,512]{1,0:T(8,128)S(1)}, f32[128,1536]{1,0:T(8,128)S(1)}, f32[128,1536]{1,0:T(8,128)S(1)}, f32[128,512]{1,0:T(8,128)S(1)}, f32[128,512]{...) custom-call(f32[256,512]{1,0:T(8,128)S(1)} %get-tuple-element.168.refs_0_.refs_4_, ...), custom_call_target="tpu_custom_call" | custom-call | flops 1 | bytes 1 | tf_op jit(solution)/shard_map/back_early/pallas_call | solution.py:515
  51.8 1.8 %back_end.1 = (bf16[1024,512]{1,0:T(8,128)(2,1)S(1)}, bf16[1024,512]{1,0:T(8,128)(2,1)S(1)}, bf16[352,512]{1,0:T(8,128)(2,1)S(1)}, bf16[352,512]{1,0:T(8,128)(2,1)S(1)}, bf16[256,512]{1,0:T(8,128)(2,1)S(1)}) custom-call(bf16[512,384]{1,0:T(8,128)(2,1)S(1)} %get-tuple-element.144.refs_4_.refs_16_.refs_0_, bf16[1536,512]{1,0:T(8,128)(2,1)S(1)} %get-tuple-element.141.refs_1_, ...), custom_call_target="tpu_custom_call" | custom-call | flops 1 | bytes 1 | tf_op jit(solution)/shard_map/back_end/pallas_call | solution.py:515
  53.6 0.2 collective-permute-start.19
  53.8 1.0 collective-permute-start.18
  54.8 2.6 %collective-permute-start.21 = (bf16[256,512]{1,0:T(8,128)(2,1)S(1)}, bf16[256,512]{1,0:T(8,128)(2,1)S(1)}, u32[]{:S(2)}, u32[]{:S(2)}) collective-permute-start(bf16[256,512]{1,0:T(8,128)(2,1)S(1)} %get-tuple-element.229.refs_2_), channel_id=1, source_target_pairs={{0,16},{4,20},{8,24},{12,28},{16,0},{20,4},{24,8},{28,12},{1,17},{... | collective-permute-start | bytes 786440 | tf_op jit(solution)/shard_map/ppermute | solution.py:528
  57.4 7.1 %collective-permute-done.18.refs_1_ = bf16[352,512]{1,0:T(8,128)(2,1)S(1)} collective-permute-done((bf16[352,512]{1,0:T(8,128)(2,1)S(1)}, bf16[352,512]{1,0:T(8,128)(2,1)S(1)}, u32[]{:S(2)}, u32[]{:S(2)}) %collective-permute-start.18) | collective-permute-done | bytes 360480 | tf_op jit(solution)/shard_map/ppermute | solution.py:528
  64.5 0.5 step_0.1
  64.9 1.5 %collective-permute-start.20 = (bf16[176,512]{1,0:T(8,128)(2,1)S(1)}, bf16[176,512]{1,0:T(8,128)(2,1)S(1)}, u32[]{:S(2)}, u32[]{:S(2)}) collective-permute-start(bf16[176,512]{1,0:T(8,128)(2,1)S(1)} %get-tuple-element.228), channel_id=1, source_target_pairs={{0,8},{4,12},{8,0},{12,4},{16,24},{20,28},{24,16},{28,20},{1,9},{5... | collective-permute-start | bytes 540680 | tf_op jit(solution)/shard_map/ppermute | solution.py:528
  66.5 0.6 collective-permute-start.27
  67.0 2.7 %collective-permute-done.21.refs_3_ = bf16[256,512]{1,0:T(8,128)(2,1)S(1)} collective-permute-done((bf16[256,512]{1,0:T(8,128)(2,1)S(1)}, bf16[256,512]{1,0:T(8,128)(2,1)S(1)}, u32[]{:S(2)}, u32[]{:S(2)}) %collective-permute-start.21) | collective-permute-done | bytes 262176 | tf_op jit(solution)/shard_map/ppermute | solution.py:528
  69.8 3.8 %collective-permute-done.20.refs_1_ = bf16[176,512]{1,0:T(8,128)(2,1)S(1)} collective-permute-done((bf16[176,512]{1,0:T(8,128)(2,1)S(1)}, bf16[176,512]{1,0:T(8,128)(2,1)S(1)}, u32[]{:S(2)}, u32[]{:S(2)}) %collective-permute-start.20) | collective-permute-done | bytes 180256 | tf_op jit(solution)/shard_map/ppermute | solution.py:528
  73.5 0.1 step_1.1
  73.6 1.6 %collective-permute-start.22 = (bf16[176,512]{1,0:T(8,128)(2,1)S(1)}, bf16[176,512]{1,0:T(8,128)(2,1)S(1)}, u32[]{:S(2)}, u32[]{:S(2)}) collective-permute-start(bf16[176,512]{1,0:T(8,128)(2,1)S(1)} %get-tuple-element.230.refs_0_), channel_id=1, source_target_pairs={{0,16},{4,20},{8,24},{12,28},{16,0},{20,4},{24,8},{28,12},{1,17},{... | collective-permute-start | bytes 540680 | tf_op jit(solution)/shard_map/ppermute | solution.py:528
  75.3 2.5 %collective-permute-start.23 = (bf16[128,512]{1,0:T(8,128)(2,1)S(1)}, bf16[128,512]{1,0:T(8,128)(2,1)S(1)}, u32[]{:S(2)}, u32[]{:S(2)}) collective-permute-start(bf16[128,512]{1,0:T(8,128)(2,1)S(1)} %get-tuple-element.231.refs_2_), channel_id=1, source_target_pairs={{0,8},{4,12},{8,0},{12,4},{16,24},{20,28},{24,16},{28,20},{1,9},{5... | collective-permute-start | bytes 393224 | tf_op jit(solution)/shard_map/ppermute | solution.py:528
  77.7 1.0 collective-permute-start.24
  78.7 3.4 %collective-permute-done.23.refs_3_ = bf16[128,512]{1,0:T(8,128)(2,1)S(1)} collective-permute-done((bf16[128,512]{1,0:T(8,128)(2,1)S(1)}, bf16[128,512]{1,0:T(8,128)(2,1)S(1)}, u32[]{:S(2)}, u32[]{:S(2)}) %collective-permute-start.23) | collective-permute-done | bytes 131104 | tf_op jit(solution)/shard_map/ppermute | solution.py:528
  82.1 0.6 collective-permute-done.24.refs_5_
  82.7 2.2 %collective-permute-done.22.refs_1_ = bf16[176,512]{1,0:T(8,128)(2,1)S(1)} collective-permute-done((bf16[176,512]{1,0:T(8,128)(2,1)S(1)}, bf16[176,512]{1,0:T(8,128)(2,1)S(1)}, u32[]{:S(2)}, u32[]{:S(2)}) %collective-permute-start.22) | collective-permute-done | bytes 180256 | tf_op jit(solution)/shard_map/ppermute | solution.py:528
  84.9 0.2 step_2.1
  85.1 1.0 collective-permute-start.26
  86.1 5.3 %collective-permute-done.25.refs_1_ = bf16[160,512]{1,0:T(8,128)(2,1)S(1)} collective-permute-done((bf16[160,512]{1,0:T(8,128)(2,1)S(1)}, bf16[160,512]{1,0:T(8,128)(2,1)S(1)}, u32[]{:S(2)}, u32[]{:S(2)}) %collective-permute-start.25) | collective-permute-done | bytes 163872 | tf_op jit(solution)/shard_map/ppermute | solution.py:528
  91.5 1.1 %collective-permute-done.26.refs_3_ = bf16[256,512]{1,0:T(8,128)(2,1)S(1)} collective-permute-done((bf16[256,512]{1,0:T(8,128)(2,1)S(1)}, bf16[256,512]{1,0:T(8,128)(2,1)S(1)}, u32[]{:S(2)}, u32[]{:S(2)}) %collective-permute-start.26) | collective-permute-done | bytes 262176 | tf_op jit(solution)/shard_map/ppermute | solution.py:528
  92.6 0.5 step_3.1
  93.1 1.0 collective-permute-start.29
  94.2 0.5 collective-permute-start.30
  94.7 0.5 collective-permute-start.32
  95.2 0.6 collective-permute-done.28.refs_9_
  95.8 0.8 collective-permute-start.33
  96.5 3.4 %finish.1 = (bf16[1024,512]{1,0:T(8,128)(2,1)}, bf16[1024,512]{1,0:T(8,128)(2,1)}, f32[512,512]{1,0:T(8,128)}) custom-call(bf16[1024,512]{1,0:T(8,128)(2,1)S(1)} %get-tuple-element.139.refs_0_, f32[1,512]{1,0:T(1,128)S(1)} %get-tuple-element.140.refs_3_.refs_1_, f32[512,512]{1,0:T(8,128)S(1)} %get-tuple-element.202.refs_2_, ...), custom_call_target="tpu_custom_call" | custom-call | flops 1 | bytes 1 | tf_op jit(solution)/shard_map/finish/pallas_call | solution.py:515
  99.9 2.6 %collective-permute-done.30.refs_3_ = bf16[256,512]{1,0:T(8,128)(2,1)S(1)} collective-permute-done((bf16[256,512]{1,0:T(8,128)(2,1)S(1)}, bf16[256,512]{1,0:T(8,128)(2,1)S(1)}, u32[]{:S(2)}, u32[]{:S(2)}) %collective-permute-start.30) | collective-permute-done | bytes 262176 | tf_op jit(solution)/shard_map/ppermute | solution.py:528
  102.5 0.7 collective-permute-done.29.refs_1_
  103.2 2.3 %last.1 = (f32[512,512]{1,0:T(8,128)}, f32[512,128]{1,0:T(8,128)}, f32[512,128]{1,0:T(8,128)}, f32[512,128]{1,0:T(8,128)}, f32[512,128]{1,0:T(8,128)}, /*index=5...) custom-call(bf16[320,512]{1,0:T(8,128)(2,1)S(1)} %get-tuple-element., ...), custom_call_target="tpu_custom_call" | custom-call | flops 1 | bytes 1 | tf_op jit(solution)/shard_map/last/pallas_call | solution.py:515
  (29 shorter events, 0.4 us)
Async XLA Ops:
  0.7 13.4 %collective-permute-start.1 = (bf16[128,512]{1,0:T(8,128)(2,1)}, bf16[128,512]{1,0:T(8,128)(2,1)S(1)}, u32[]{:S(2)}, u32[]{:S(2)}) collective-permute-start(bf16[128,512]{1,0:T(8,128)(2,1)} %refs_5_.7), channel_id=1, source_target_pairs={{0,2},{1,3},{2,0},{3,1},{4,6},{5,7},{6,4},{7,5},{8,10},{9,11},{10,... | collective-permute-start | bytes 393224 | tf_op jit(solution)/shard_map/ppermute | solution.py:528
  3.7 10.3 %collective-permute-start = (bf16[128,512]{1,0:T(8,128)(2,1)}, bf16[128,512]{1,0:T(8,128)(2,1)S(1)}, u32[]{:S(2)}, u32[]{:S(2)}) collective-permute-start(bf16[128,512]{1,0:T(8,128)(2,1)} %refs_5_.7), channel_id=1, source_target_pairs={{0,1},{1,0},{2,3},{3,2},{4,5},{5,4},{6,7},{7,6},{8,9},{9,8},{10,11... | collective-permute-start | bytes 393224 | tf_op jit(solution)/shard_map/ppermute | solution.py:528
  13.8 7.8 %copy-start = (bf16[128,512]{1,0:T(8,128)(2,1)S(1)}, bf16[128,512]{1,0:T(8,128)(2,1)}, u32[]{:S(2)}) copy-start(bf16[128,512]{1,0:T(8,128)(2,1)} %refs_5_.7) | copy-start | bytes 393220
  13.8 6.0 %collective-permute-start.5 = (bf16[512,128]{1,0:T(8,128)(2,1)S(1)}, bf16[512,128]{1,0:T(8,128)(2,1)S(1)}, u32[]{:S(2)}, u32[]{:S(2)}) collective-permute-start(bf16[512,128]{1,0:T(8,128)(2,1)S(1)} %get-tuple-element.150.refs_1_.refs_7_), channel_id=1, source_target_pairs={{0,2},{1,3},{2,0},{3,1},{4,6},{5,7},{6,4},{7,5},{8,10},{9,11},{10,... | collective-permute-start | bytes 393224 | tf_op jit(solution)/shard_map/ppermute | solution.py:528
  19.8 1.8 %collective-permute-start.6 = (bf16[1024,128]{1,0:T(8,128)(2,1)S(1)}, bf16[1024,128]{1,0:T(8,128)(2,1)S(1)}, u32[]{:S(2)}, u32[]{:S(2)}) collective-permute-start(bf16[1024,128]{1,0:T(8,128)(2,1)S(1)} %relay_late.1), channel_id=1, source_target_pairs={{0,1},{1,0},{2,3},{3,2},{4,5},{5,4},{6,7},{7,6},{8,9},{9,8},{10,11... | collective-permute-start | bytes 786440 | tf_op jit(solution)/shard_map/ppermute | solution.py:528
  19.9 1.7 %collective-permute-start.4 = (bf16[512,128]{1,0:T(8,128)(2,1)S(1)}, bf16[512,128]{1,0:T(8,128)(2,1)S(1)}, u32[]{:S(2)}, u32[]{:S(2)}) collective-permute-start(bf16[512,128]{1,0:T(8,128)(2,1)S(1)} %get-tuple-element.150.refs_1_.refs_7_), channel_id=1, source_target_pairs={{0,1},{1,0},{2,3},{3,2},{4,5},{5,4},{6,7},{7,6},{8,9},{9,8},{10,11... | collective-permute-start | bytes 393224 | tf_op jit(solution)/shard_map/ppermute | solution.py:528
  20.4 5.5 %collective-permute-start.3 = (bf16[512,128]{1,0:T(8,128)(2,1)S(1)}, bf16[512,128]{1,0:T(8,128)(2,1)S(1)}, u32[]{:S(2)}, u32[]{:S(2)}) collective-permute-start(bf16[512,128]{1,0:T(8,128)(2,1)S(1)} %get-tuple-element.149.refs_2_.refs_1_.refs_7_), channel_id=1, source_target_pairs={{0,2},{1,3},{2,0},{3,1},{4,6},{5,7},{6,4},{7,5},{8,10},{9,11},{10,... | collective-permute-start | bytes 393224 | tf_op jit(solution)/shard_map/ppermute | solution.py:528
  22.9 3.0 %collective-permute-start.8 = (bf16[256,512]{1,0:T(8,128)(2,1)S(1)}, bf16[256,512]{1,0:T(8,128)(2,1)S(1)}, u32[]{:S(2)}, u32[]{:S(2)}) collective-permute-start(bf16[256,512]{1,0:T(8,128)(2,1)S(1)} %get-tuple-element.157.refs_15_), channel_id=1, source_target_pairs={{0,1},{1,0},{2,3},{3,2},{4,5},{5,4},{6,7},{7,6},{8,9},{9,8},{10,11... | collective-permute-start | bytes 786440 | tf_op jit(solution)/shard_map/ppermute | solution.py:528
  26.0 7.5 %collective-permute-start.10 = (bf16[256,512]{1,0:T(8,128)(2,1)S(1)}, bf16[256,512]{1,0:T(8,128)(2,1)S(1)}, u32[]{:S(2)}, u32[]{:S(2)}) collective-permute-start(bf16[256,512]{1,0:T(8,128)(2,1)S(1)} %add_late.1.refs_10_.refs_0_), channel_id=1, source_target_pairs={{0,2},{1,3},{2,0},{3,1},{4,6},{5,7},{6,4},{7,5},{8,10},{9,11},{10,... | collective-permute-start | bytes 786440 | tf_op jit(solution)/shard_map/ppermute | solution.py:528
  26.5 1.5 %collective-permute-start.2 = (bf16[512,128]{1,0:T(8,128)(2,1)S(1)}, bf16[512,128]{1,0:T(8,128)(2,1)S(1)}, u32[]{:S(2)}, u32[]{:S(2)}) collective-permute-start(bf16[512,128]{1,0:T(8,128)(2,1)S(1)} %get-tuple-element.149.refs_2_.refs_1_.refs_7_), channel_id=1, source_target_pairs={{0,1},{1,0},{2,3},{3,2},{4,5},{5,4},{6,7},{7,6},{8,9},{9,8},{10,11... | collective-permute-start | bytes 393224 | tf_op jit(solution)/shard_map/ppermute | solution.py:528
  26.5 1.5 %collective-permute-start.7 = (bf16[512,128]{1,0:T(8,128)(2,1)S(1)}, bf16[512,128]{1,0:T(8,128)(2,1)S(1)}, u32[]{:S(2)}, u32[]{:S(2)}) collective-permute-start(bf16[512,128]{1,0:T(8,128)(2,1)S(1)} %relay_early.1.refs_2_), channel_id=1, source_target_pairs={{0,1},{1,0},{2,3},{3,2},{4,5},{5,4},{6,7},{7,6},{8,9},{9,8},{10,11... | collective-permute-start | bytes 393224 | tf_op jit(solution)/shard_map/ppermute | solution.py:528
  30.7 6.0 %collective-permute-start.9 = (bf16[256,512]{1,0:T(8,128)(2,1)S(1)}, bf16[256,512]{1,0:T(8,128)(2,1)S(1)}, u32[]{:S(2)}, u32[]{:S(2)}) collective-permute-start(bf16[256,512]{1,0:T(8,128)(2,1)S(1)} %get-tuple-element.171), channel_id=1, source_target_pairs={{0,1},{1,0},{2,3},{3,2},{4,5},{5,4},{6,7},{7,6},{8,9},{9,8},{10,11... | collective-permute-start | bytes 786440 | tf_op jit(solution)/shard_map/ppermute | solution.py:528
  33.5 3.9 %collective-permute-start.14 = (bf16[256,512]{1,0:T(8,128)(2,1)S(1)}, bf16[256,512]{1,0:T(8,128)(2,1)S(1)}, u32[]{:S(2)}, u32[]{:S(2)}) collective-permute-start(bf16[256,512]{1,0:T(8,128)(2,1)S(1)} %add_late_chips.1.refs_2_), channel_id=1, source_target_pairs={{0,1},{1,0},{2,3},{3,2},{4,5},{5,4},{6,7},{7,6},{8,9},{9,8},{10,11... | collective-permute-start | bytes 786440 | tf_op jit(solution)/shard_map/ppermute | solution.py:528
  33.6 10.2 %collective-permute-start.12 = (bf16[256,512]{1,0:T(8,128)(2,1)S(1)}, bf16[256,512]{1,0:T(8,128)(2,1)S(1)}, u32[]{:S(2)}, u32[]{:S(2)}) collective-permute-start(bf16[256,512]{1,0:T(8,128)(2,1)S(1)} %get-tuple-element.184), channel_id=1, source_target_pairs={{0,4},{4,0},{8,12},{12,8},{16,20},{20,16},{24,28},{28,24},{1,5},{5... | collective-permute-start | bytes 786440 | tf_op jit(solution)/shard_map/ppermute | solution.py:528
  35.2 8.7 %collective-permute-start.13 = (bf16[256,512]{1,0:T(8,128)(2,1)S(1)}, bf16[256,512]{1,0:T(8,128)(2,1)S(1)}, u32[]{:S(2)}, u32[]{:S(2)}) collective-permute-start(bf16[256,512]{1,0:T(8,128)(2,1)S(1)} %get-tuple-element.186), channel_id=1, source_target_pairs={{0,8},{4,12},{8,0},{12,4},{16,24},{20,28},{24,16},{28,20},{1,9},{5... | collective-permute-start | bytes 786440 | tf_op jit(solution)/shard_map/ppermute | solution.py:528
  36.8 8.2 %collective-permute-start.11 = (bf16[256,512]{1,0:T(8,128)(2,1)S(1)}, bf16[256,512]{1,0:T(8,128)(2,1)S(1)}, u32[]{:S(2)}, u32[]{:S(2)}) collective-permute-start(bf16[256,512]{1,0:T(8,128)(2,1)S(1)} %add_early.1.refs_0_), channel_id=1, source_target_pairs={{0,2},{1,3},{2,0},{3,1},{4,6},{5,7},{6,4},{7,5},{8,10},{9,11},{10,... | collective-permute-start | bytes 786440 | tf_op jit(solution)/shard_map/ppermute | solution.py:528
  45.5 1.6 %collective-permute-start.15 = (bf16[256,512]{1,0:T(8,128)(2,1)S(1)}, bf16[256,512]{1,0:T(8,128)(2,1)S(1)}, u32[]{:S(2)}, u32[]{:S(2)}) collective-permute-start(bf16[256,512]{1,0:T(8,128)(2,1)S(1)} %get-tuple-element.194.refs_2_), channel_id=1, source_target_pairs={{0,1},{1,0},{2,3},{3,2},{4,5},{5,4},{6,7},{7,6},{8,9},{9,8},{10,11... | collective-permute-start | bytes 786440 | tf_op jit(solution)/shard_map/ppermute | solution.py:528
  45.6 6.2 %collective-permute-start.16 = (bf16[128,512]{1,0:T(8,128)(2,1)S(1)}, bf16[128,512]{1,0:T(8,128)(2,1)S(1)}, u32[]{:S(2)}, u32[]{:S(2)}) collective-permute-start(bf16[128,512]{1,0:T(8,128)(2,1)S(1)} %get-tuple-element.220), channel_id=1, source_target_pairs={{0,8},{4,12},{8,0},{12,4},{16,24},{20,28},{24,16},{28,20},{1,9},{5... | collective-permute-start | bytes 393224 | tf_op jit(solution)/shard_map/ppermute | solution.py:528
  46.1 5.7 %collective-permute-start.17 = (bf16[128,512]{1,0:T(8,128)(2,1)S(1)}, bf16[128,512]{1,0:T(8,128)(2,1)S(1)}, u32[]{:S(2)}, u32[]{:S(2)}) collective-permute-start(bf16[128,512]{1,0:T(8,128)(2,1)S(1)} %get-tuple-element.222), channel_id=1, source_target_pairs={{0,4},{4,0},{8,12},{12,8},{16,20},{20,16},{24,28},{28,24},{1,5},{5... | collective-permute-start | bytes 393224 | tf_op jit(solution)/shard_map/ppermute | solution.py:528
  53.6 10.9 %collective-permute-start.19 = (bf16[1024,512]{1,0:T(8,128)(2,1)S(1)}, bf16[1024,512]{1,0:T(8,128)(2,1)S(1)}, u32[]{:S(2)}, u32[]{:S(2)}) collective-permute-start(bf16[1024,512]{1,0:T(8,128)(2,1)S(1)} %get-tuple-element.226), channel_id=1, source_target_pairs={{0,1},{1,0},{2,3},{3,2},{4,5},{5,4},{6,7},{7,6},{8,9},{9,8},{10,11... | collective-permute-start | bytes 3145736 | tf_op jit(solution)/shard_map/ppermute | solution.py:528
  53.8 10.7 %collective-permute-start.18 = (bf16[352,512]{1,0:T(8,128)(2,1)S(1)}, bf16[352,512]{1,0:T(8,128)(2,1)S(1)}, u32[]{:S(2)}, u32[]{:S(2)}) collective-permute-start(bf16[352,512]{1,0:T(8,128)(2,1)S(1)} %get-tuple-element.224), channel_id=1, source_target_pairs={{0,4},{4,0},{8,12},{12,8},{16,20},{20,16},{24,28},{28,24},{1,5},{5... | collective-permute-start | bytes 1081352 | tf_op jit(solution)/shard_map/ppermute | solution.py:528
  54.8 15.0 %collective-permute-start.21 = (bf16[256,512]{1,0:T(8,128)(2,1)S(1)}, bf16[256,512]{1,0:T(8,128)(2,1)S(1)}, u32[]{:S(2)}, u32[]{:S(2)}) collective-permute-start(bf16[256,512]{1,0:T(8,128)(2,1)S(1)} %get-tuple-element.229.refs_2_), channel_id=1, source_target_pairs={{0,16},{4,20},{8,24},{12,28},{16,0},{20,4},{24,8},{28,12},{1,17},{... | collective-permute-start | bytes 786440 | tf_op jit(solution)/shard_map/ppermute | solution.py:528
  64.9 8.6 %collective-permute-start.20 = (bf16[176,512]{1,0:T(8,128)(2,1)S(1)}, bf16[176,512]{1,0:T(8,128)(2,1)S(1)}, u32[]{:S(2)}, u32[]{:S(2)}) collective-permute-start(bf16[176,512]{1,0:T(8,128)(2,1)S(1)} %get-tuple-element.228), channel_id=1, source_target_pairs={{0,8},{4,12},{8,0},{12,4},{16,24},{20,28},{24,16},{28,20},{1,9},{5... | collective-permute-start | bytes 540680 | tf_op jit(solution)/shard_map/ppermute | solution.py:528
  66.5 26.1 %collective-permute-start.27 = (bf16[1024,512]{1,0:T(8,128)(2,1)S(1)}, bf16[1024,512]{1,0:T(8,128)(2,1)S(1)}, u32[]{:S(2)}, u32[]{:S(2)}) collective-permute-start(bf16[1024,512]{1,0:T(8,128)(2,1)S(1)} %get-tuple-element.237.refs_8_), channel_id=1, source_target_pairs={{0,2},{1,3},{2,0},{3,1},{4,6},{5,7},{6,4},{7,5},{8,10},{9,11},{10,... | collective-permute-start | bytes 3145736 | tf_op jit(solution)/shard_map/ppermute | solution.py:528
  73.6 11.3 %collective-permute-start.22 = (bf16[176,512]{1,0:T(8,128)(2,1)S(1)}, bf16[176,512]{1,0:T(8,128)(2,1)S(1)}, u32[]{:S(2)}, u32[]{:S(2)}) collective-permute-start(bf16[176,512]{1,0:T(8,128)(2,1)S(1)} %get-tuple-element.230.refs_0_), channel_id=1, source_target_pairs={{0,16},{4,20},{8,24},{12,28},{16,0},{20,4},{24,8},{28,12},{1,17},{... | collective-permute-start | bytes 540680 | tf_op jit(solution)/shard_map/ppermute | solution.py:528
  75.3 6.8 %collective-permute-start.23 = (bf16[128,512]{1,0:T(8,128)(2,1)S(1)}, bf16[128,512]{1,0:T(8,128)(2,1)S(1)}, u32[]{:S(2)}, u32[]{:S(2)}) collective-permute-start(bf16[128,512]{1,0:T(8,128)(2,1)S(1)} %get-tuple-element.231.refs_2_), channel_id=1, source_target_pairs={{0,8},{4,12},{8,0},{12,4},{16,24},{20,28},{24,16},{28,20},{1,9},{5... | collective-permute-start | bytes 393224 | tf_op jit(solution)/shard_map/ppermute | solution.py:528
  77.7 5.0 %collective-permute-start.24 = (bf16[128,512]{1,0:T(8,128)(2,1)S(1)}, bf16[128,512]{1,0:T(8,128)(2,1)S(1)}, u32[]{:S(2)}, u32[]{:S(2)}) collective-permute-start(bf16[128,512]{1,0:T(8,128)(2,1)S(1)} %get-tuple-element.232.refs_4_), channel_id=1, source_target_pairs={{0,4},{4,0},{8,12},{12,8},{16,20},{20,16},{24,28},{28,24},{1,5},{5... | collective-permute-start | bytes 393224 | tf_op jit(solution)/shard_map/ppermute | solution.py:528
  85.1 7.5 %collective-permute-start.26 = (bf16[256,512]{1,0:T(8,128)(2,1)S(1)}, bf16[256,512]{1,0:T(8,128)(2,1)S(1)}, u32[]{:S(2)}, u32[]{:S(2)}) collective-permute-start(bf16[256,512]{1,0:T(8,128)(2,1)S(1)} %get-tuple-element.234.refs_2_), channel_id=1, source_target_pairs={{0,4},{4,0},{8,12},{12,8},{16,20},{20,16},{24,28},{28,24},{1,5},{5... | collective-permute-start | bytes 786440 | tf_op jit(solution)/shard_map/ppermute | solution.py:528
  86.1 5.3 %collective-permute-start.25 = (bf16[160,512]{1,0:T(8,128)(2,1)S(1)}, bf16[160,512]{1,0:T(8,128)(2,1)S(1)}, u32[]{:S(2)}, u32[]{:S(2)}) collective-permute-start(bf16[160,512]{1,0:T(8,128)(2,1)S(1)} %get-tuple-element.233.refs_0_), channel_id=1, source_target_pairs={{0,8},{4,12},{8,0},{12,4},{16,24},{20,28},{24,16},{28,20},{1,9},{5... | collective-permute-start | bytes 491528 | tf_op jit(solution)/shard_map/ppermute | solution.py:528
  93.0 2.7 %collective-permute-start.28 = (bf16[1024,512]{1,0:T(8,128)(2,1)S(1)}, bf16[1024,512]{1,0:T(8,128)(2,1)S(1)}, u32[]{:S(2)}, u32[]{:S(2)}) collective-permute-start(bf16[1024,512]{1,0:T(8,128)(2,1)S(1)} %get-tuple-element.238.refs_8_), channel_id=1, source_target_pairs={{0,1},{1,0},{2,3},{3,2},{4,5},{5,4},{6,7},{7,6},{8,9},{9,8},{10,11... | collective-permute-start | bytes 3145736 | tf_op jit(solution)/shard_map/ppermute | solution.py:528
  93.1 10.1 %collective-permute-start.29 = (bf16[320,512]{1,0:T(8,128)(2,1)S(1)}, bf16[320,512]{1,0:T(8,128)(2,1)S(1)}, u32[]{:S(2)}, u32[]{:S(2)}) collective-permute-start(bf16[320,512]{1,0:T(8,128)(2,1)S(1)} %get-tuple-element.241.refs_12_.refs_0_), channel_id=1, source_target_pairs={{0,4},{4,0},{8,12},{12,8},{16,20},{20,16},{24,28},{28,24},{1,5},{5... | collective-permute-start | bytes 983048 | tf_op jit(solution)/shard_map/ppermute | solution.py:528
  94.2 8.4 %collective-permute-start.30 = (bf16[256,512]{1,0:T(8,128)(2,1)S(1)}, bf16[256,512]{1,0:T(8,128)(2,1)S(1)}, u32[]{:S(2)}, u32[]{:S(2)}) collective-permute-start(bf16[256,512]{1,0:T(8,128)(2,1)S(1)} %get-tuple-element.244.refs_2_), channel_id=1, source_target_pairs={{0,8},{4,12},{8,0},{12,4},{16,24},{20,28},{24,16},{28,20},{1,9},{5... | collective-permute-start | bytes 786440 | tf_op jit(solution)/shard_map/ppermute | solution.py:528
  94.7 5.2 %collective-permute-start.31 = (f32[16,512]{1,0:T(8,128)S(1)}, f32[16,512]{1,0:T(8,128)S(1)}, u32[]{:S(2)}, u32[]{:S(2)}) collective-permute-start(f32[16,512]{1,0:T(8,128)S(1)} %get-tuple-element.245.refs_4_), channel_id=1, source_target_pairs={{0,1},{1,0},{2,3},{3,2},{4,5},{5,4},{6,7},{7,6},{8,9},{9,8},{10,11... | collective-permute-start | bytes 98312 | tf_op jit(solution)/shard_map/ppermute | solution.py:528
  94.7 5.2 %collective-permute-start.32 = (f32[16,512]{1,0:T(8,128)S(1)}, f32[16,512]{1,0:T(8,128)S(1)}, u32[]{:S(2)}, u32[]{:S(2)}) collective-permute-start(f32[16,512]{1,0:T(8,128)S(1)} %get-tuple-element.245.refs_4_), channel_id=1, source_target_pairs={{0,2},{1,3},{2,0},{3,1},{4,6},{5,7},{6,4},{7,5},{8,10},{9,11},{10,... | collective-permute-start | bytes 98312 | tf_op jit(solution)/shard_map/ppermute | solution.py:528
  95.8 4.2 %collective-permute-start.33 = (f32[16,512]{1,0:T(8,128)S(1)}, f32[16,512]{1,0:T(8,128)S(1)}, u32[]{:S(2)}, u32[]{:S(2)}) collective-permute-start(f32[16,512]{1,0:T(8,128)S(1)} %get-tuple-element.245.refs_4_), channel_id=1, source_target_pairs={{0,3},{1,2},{2,1},{3,0},{4,7},{5,6},{6,5},{7,4},{8,11},{9,10},{10,... | collective-permute-start | bytes 98312 | tf_op jit(solution)/shard_map/ppermute | solution.py:528

commit v5 on v4

--- a/solution.py
+++ b/solution.py
@@ -364,7 +364,7 @@
     first, block, heads, mem_len, n_tensor, size,
     place_ref, w_ref, normed_ref, shift_ref, gain_ref, dk_ref, dv_ref, dpos_ref, dout_ref, dq_ref, bias_ref, dq_in,
     late_ref, fvec_ref, upb_ref, e_send, e_keep, l_send, l_keep, up_keep, up_got, down_keep, down_got,
-    keep_ref, send_ref, a_keep, a_send, f_ref,
+    keep_ref, send_ref, a_keep, a_send, b_keep, b_send, f_ref,
 ):
     half = up_keep.shape[0]
     f_ref[:half, :] = added(up_keep[...], up_got[...])
@@ -401,32 +401,27 @@
         rows.append(upb_ref[:, i * width : (i + 1) * width])
     rows.append(jnp.zeros((small - 7 - upb_ref.shape[1] // width, width), FL))
     rows = jnp.concatenate(rows, axis=0).astype(BF)
-    step = size + small
-    for d in range(2 * a_keep.shape[0] // step):
-        here = max(0, min(size, 5 * wide - d * size))
-        piece = [grads[d * size : d * size + here].astype(BF)] if here else []
-        piece += [jnp.zeros((size - here, width), BF)] if here < size else []
-        piece = jnp.concatenate([*piece, rows], axis=0)
-        per_half = a_keep.shape[0] // step
-        at = slice(d % per_half * step, (d % per_half + 1) * step)
-        by_core(place_ref[1] & 1, d // per_half, a_keep, a_send, piece, at)
-
-
-def last_kernel(
-    wide, heads, n_tensor, place_ref, a_mine, a_got, down_mine, down_got, *refs
-):
+    for d in range(4):
+        piece = jnp.concatenate([grads[d * size : (d + 1) * size].astype(BF), rows], axis=0)
+        at = slice(d % 2 * (size + small), (d % 2 + 1) * (size + small))
+        by_core(place_ref[1] & 1, d // 2, a_keep, a_send, piece, at)
+        piece = grads[(d + 4) * size : (d + 5) * size].astype(BF)
+        by_core((place_ref[1] >> 1) & 1, d // 2, b_keep, b_send, piece, slice(d % 2 * size, (d % 2 + 1) * size))
+
+
+def last_kernel(wide, heads, n_tensor, place_ref, a_mine, a_got, b_mine, b_got, *refs):
     totals, refs = refs[:n_tensor], refs[n_tensor:]
-    down_out, outs, smalls = refs[0], refs[1:6], refs[6:14]
-    down_scr, rows_scr, turned_scr, sems = refs[14:]
+    outs, smalls = refs[:5], refs[5:13]
+    rows_scr, turned_scr, sems = refs[13:]
     copies = []
 
     def send(src, dst):
         copies.append(pltpu.make_async_copy(src, dst, sems.at[len(copies)]))
         copies[-1].start()
 
-    join(place_ref, 1, down_mine, down_got, down_scr)
-    send(down_scr, down_out)
-    join(place_ref, 0, a_mine, a_got, rows_scr)
+    half = rows_scr.shape[0] // 2
+    join(place_ref, 0, a_mine, a_got, rows_scr.at[pl.ds(0, half), :])
+    join(place_ref, 1, b_mine, b_got, rows_scr.at[pl.ds(half, half), :])
     send(rows_scr.at[pl.ds(4 * wide, wide), :], outs[4])
     for i in range(4):
         turned_scr[i] = rows_scr[i * wide : (i + 1) * wide, :].T
@@ -449,7 +444,7 @@
 
 def finish_kernel(
     block, place_ref, x_ref, gain_ref, gh_e, gh_l, hid_es, hid_ek, hid_ls, hid_lk, mine_ref, other_ref, bias_ref, up_ref,
-    out_ref, grad_ref, up_out, out_scr, grad_scr, up_scr, sems,
+    down_ref, out_ref, grad_ref, up_out, down_out, out_scr, grad_scr, up_scr, down_scr, sems,
 ):
     core = place_ref[0]
     copies = []
@@ -460,6 +455,8 @@
 
     up_scr[...] = up_ref[...].astype(FL)
     send(up_scr, up_out)
+    down_scr[...] = down_ref[...].astype(FL)
+    send(down_scr, down_out)
     for first, gh_ref, hid_s, hid_k in ((0, gh_e, hid_es, hid_ek), (1, gh_l, hid_ls, hid_lk)):
         for part in range(2):
             at = slice(part * block, (part + 1) * block)
@@ -529,9 +526,9 @@
 
 
 def work_kernel(jobs, place_ref, *refs):
-    ins, outs = refs[: 2 * len(jobs)], list(refs[2 * len(jobs) :])
-    for i, (kind, bit) in enumerate(jobs):
-        mine, got = ins[2 * i : 2 * i + 2]
+    outs = list(refs)
+    ins = [[outs.pop(0) for _ in range(count)] for _, _, count in jobs]
+    for (kind, bit, _), (mine, got, *more) in zip(jobs, ins):
         if kind == "halve":
             halve(place_ref, bit, added(mine[...], got[...]), outs.pop(0), outs.pop(0))
         elif kind == "join":
@@ -540,6 +537,17 @@
             outs.pop(0)[...] = added(mine[...], got[...])
         elif kind == "copy":
             outs.pop(0)[...] = mine[...]
+        elif kind == "pack":
+            out = outs.pop(0)
+            size = mine.shape[0]
+            out[:size, :] = added(mine[...], got[...])
+            out[size:, :] = added(more[0][...], more[1][...])
+        elif kind == "three":
+            total = mine[...].astype(FL) + got[...].astype(FL)
+            size = outs[0].shape[0]
+            for start, end in ((0, size), (size, size + small), (size + small, 2 * size + small)):
+                out = outs.pop(0)
+                out[...] = total[start:end].astype(out.dtype)
         else:
             total = mine[...].astype(FL) + got[...].astype(FL)
             size = outs[0].shape[0]
@@ -550,7 +558,7 @@
 
 def work(place, jobs, name, after=(), cost=1):
     outs = []
-    for kind, _, mine, _ in jobs:
+    for kind, _, mine, *others in jobs:
         size, width = mine.shape
         outs += {
             "halve": [((size // 2, width), BF)] * 2,
@@ -558,11 +566,12 @@
             "join": [((2 * size, width), BF)],
             "sum": [((size, width), BF)],
             "copy": [((size, width), mine.dtype)],
-            "split": [((size - small, width), BF), ((small, width), FL)],
+            "pack": [((size + others[-1].shape[0], width), BF)],
+            "three": [(((size - small) // 2, width), BF), ((small, width), FL), (((size - small) // 2, width), BF)],
         }[kind]
     args = [a for job in jobs for a in job[2:]]
     return list(
-        call(functools.partial(work_kernel, [job[:2] for job in jobs]), outs, (place, *args), name, cost, after=after)
+        call(functools.partial(work_kernel, [(*job[:2], len(job) - 2) for job in jobs]), outs, (place, *args), name, cost, after=after)
     )
 
 
@@ -739,84 +748,71 @@
     up_got = swap(up_send, "dp", n_dp, 2)
     down_got = swap(down_send, "dp", n_dp, 1)
     gnt_e = (gnt_e, cores(gnt_e, n_tensor))
-    groups = n_dp // 2
-    size = max(16, -(-5 * wide // groups // 16) * 16)
+    size = 5 * wide // 8
     gh_e, dk, dv, dpos, dout, dq_e, bias = call(
         functools.partial(back_early_kernel, 0, block, heads, mem_len),
         [((chunk, width), FL), *sums, ((2, wide), FL)],
         (*back_args(hidden_e, gnt_e, saved_e)[:-1], dk, dv, dpos, dout, bias), "back_early", 1, turn_scr,
     )
-    keep, send, a_keep, a_send, f_rows = call(
+    pieces = [((2 * (size + small), width), BF)] * 2 + [((2 * size, width), BF)] * 2
+    keep, send, a_keep, a_send, b_keep, b_send, f_rows = call(
         functools.partial(back_end_kernel, 0, block, heads, mem_len, n_tensor, size),
-        [*[((seq_len, width), BF)] * 2, *[((groups // 2 * (size + small), width), BF)] * 2, ((chunk // 2, width), BF)],
+        [*[((seq_len, width), BF)] * 2, *pieces, ((chunk // 2, width), BF)],
         (place, weights, normed, attn_shift, attn_gain, dk, dv, dpos, dout, dq_e, bias, dq, part, *vecs, *shares_e,
          *shares_l, up_keep, up_got, down_keep, down_got), "back_end", 1,
     )
+
+    def pair(rows, bit):
+        return swap(rows, "dp", n_dp, 1 << bit)
+
     bits = list(range((n_dp - 1).bit_length()))
-    attn = Chain(a_keep, a_send, bits, n_dp, "split")
+    a_got, b_got = pair(a_send, 0), pair(b_send, 1)
     if len(bits) > 3:
         f_rows, f_send = work(place, [("halve", 2, f_rows, jnp.zeros_like(f_rows))], "halve_ffn")
     else:
         f_send = f_rows
     ffn = Chain(f_rows, f_send, bits[2:], n_dp, "two" if len(bits) == 3 else "sum")
     rows = (keep, cores(send, n_tensor))
-    count, stage = 0, 0
-    while attn.left() > 0:
-        jobs = [attn.job()]
-        if count == 0:
-            pass
-        elif stage == 0:
-            jobs.append(ffn.job())
-        elif stage == 1:
-            jobs += [("join", 1, up, up_got), ("join", 0, down, down_got)]
-        elif stage == 2:
-            jobs += [("join", 0, up, up_got), ("copy", 0, down, down)]
-        if attn.left() == 1:
-            jobs.append(("copy", 0, totals, totals))
-        if count == 0 or attn.left() == 1:
-            jobs.append(("sum", 0, *rows))
-        results = work(place, jobs, f"step_{count}", cost=STEP_COST if count == 2 else 1)
-        if attn.job()[0] == "split":
-            totals = results.pop(1)
-        if count == 0 or attn.left() == 1:
-            rows = results.pop()
-            rows = (rows, (other_chips if count == 0 else cores)(rows, n_tensor))
-        if attn.left() == 1:
-            totals = results.pop()
-            totals = [totals] + [swap(totals, "tensor", n_tensor, k) for k in range(1, n_tensor)]
-        attn.take(results)
-        if count == 0:
-            pass
-        elif stage == 0 and ffn.left() > 0:
-            ffn.take(results)
-        elif stage == 0:
-            up, down = results if len(results) == 2 else (results[0][: chunk // 4], results[0][chunk // 4 :])
-            up_got, down_got = swap(up, "dp", n_dp, 2), swap(down, "dp", n_dp, 1)
-            stage = 1
-        elif stage == 1:
-            up, down = results
-            up_got = swap(up, "dp", n_dp, 1)
-            stage = 2
-        elif stage == 2:
-            up, down = results
-            down_got = swap(down, "dp", n_dp, 2)
-            stage = 3
-        count += 1
-    output, input_grad, g_up = call(
-        functools.partial(finish_kernel, block), [(x.shape, BF)] * 2 + [((width, ff), FL)],
-        (place, x, attn_gain, gh_e, gh_l, *hidden_e, *hidden_l, *rows, down_bias, up), "finish", 1,
-        [pltpu.VMEM(x.shape, BF)] * 2 + [pltpu.VMEM((width, ff), FL), pltpu.SemaphoreType.DMA((9,))],
-        after=(attn.rows,), far=3,
+    a_keep, a_send, b_keep, b_send, rows = work(
+        place, [("halve", 1, a_keep, a_got), ("halve", 0, b_keep, b_got), ("sum", 0, *rows)], "step_0"
+    )
+    rows = (rows, other_chips(rows, n_tensor))
+    while ffn.left() > 0:
+        ffn.take(work(place, [ffn.job()], "step_ffn"))
+    attn, *halves = work(
+        place, [("pack", 0, a_keep, pair(a_send, 1), b_keep, pair(b_send, 0)), ffn.job()], "step_1"
+    )
+    up, down = halves if len(halves) == 2 else (halves[0][: chunk // 4], halves[0][chunk // 4 :])
+    for bit in bits[2:-1]:
+        (attn,) = work(place, [("sum", 0, attn, pair(attn, bit))], f"step_1_{bit}")
+    a_rows, totals, b_rows, up, down = work(
+        place,
+        [("three", 0, attn, pair(attn, bits[-1])), ("join", 1, up, pair(up, 1)), ("join", 0, down, pair(down, 0))],
+        "step_2", cost=STEP_COST,
+    )
+    a_rows, b_rows, up, down, totals, summed = work(
+        place,
+        [("join", 1, a_rows, pair(a_rows, 1)), ("join", 0, b_rows, pair(b_rows, 0)), ("join", 0, up, pair(up, 0)),
+         ("join", 1, down, pair(down, 1)), ("copy", 0, totals, totals), ("sum", 0, *rows)],
+        "step_3",
+    )
+    rows = (summed, cores(summed, n_tensor))
+    totals = [totals] + [swap(totals, "tensor", n_tensor, k) for k in range(1, n_tensor)]
+    output, input_grad, g_up, g_down = call(
+        functools.partial(finish_kernel, block), [(x.shape, BF)] * 2 + [((width, ff), FL), ((ff, width), FL)],
+        (place, x, attn_gain, gh_e, gh_l, *hidden_e, *hidden_l, *rows, down_bias, up, down), "finish", 1,
+        [pltpu.VMEM(x.shape, BF)] * 2 + [pltpu.VMEM((width, ff), FL), pltpu.VMEM((ff, width), FL),
+                                         pltpu.SemaphoreType.DMA((10,))],
+        after=(a_rows,), far=4,
     )
     output_there = pltpu.with_memory_space_constraint(output, pltpu.HBM)
-    g_down, g_query, g_key, g_value, g_pos, g_out, *vecs = call(
+    g_query, g_key, g_value, g_pos, g_out, *vecs = call(
         functools.partial(last_kernel, wide, heads, n_tensor),
-        [((ff, width), FL)] + [((width, wide), FL)] * 4 + [((wide, width), FL)]
+        [((width, wide), FL)] * 4 + [((wide, width), FL)]
         + [((1, width), FL)] * 5 + [((heads, HEAD), FL)] * 2 + [((1, ff), FL)],
-        (place, attn.rows, attn.got, down, down_got, *totals), "last", 1,
-        [pltpu.VMEM((ff, width), FL), pltpu.VMEM((groups * size, width), FL), pltpu.VMEM((4, width, wide), FL),
-         pltpu.SemaphoreType.DMA((6,))],
-        after=(output_there,), far=6,
+        (place, a_rows, pair(a_rows, 0), b_rows, pair(b_rows, 1), *totals), "last", 1,
+        [pltpu.VMEM((5 * wide, width), FL), pltpu.VMEM((4, width, wide), FL), pltpu.SemaphoreType.DMA((5,))],
+        after=(output_there,), far=5,
     )
     return (
         output[None],

time: 106 us -> 102 us (0.962)
  waiting for transfers between devices: 36.9 us -> 27.2 us
  starting transfers between devices: 25.7 us -> 31.9 us
    ppermute x34 -> x38, waiting for transfers between devices: 36.9 us -> 27.2 us  [swap(): return lax.ppermute(rows, axis, [(i, i ^ bit) for i in range(size)])]
    ppermute x34 -> x38, starting transfers between devices: 25.7 us -> 31.9 us  [swap(): return lax.ppermute(rows, axis, [(i, i ^ bit) for i in range(size)])]
  transfers between devices with their start and end apart: 34 -> 38, of which waited for: 17 -> 13; matrix products, arithmetic and copies ran while one was open for 0% -> 0% of each run, Pallas kernels for 34% -> 36%
where the time goes in v5:
time: 102 us
  Pallas kernels  41.2 us (40%)
  starting transfers between devices  31.9 us (31%)
  waiting for transfers between devices  27.2 us (27%)
  between operations  1.77 us (2%)
    pallas_call x23, Pallas kernels, call(): pl.pallas_call(body, out_shape=[pltpu.HBM(s, d) if i < far else jax.Shape...  41.2 us
    ppermute x38, starting transfers between devices, swap(): return lax.ppermute(rows, axis, [(i, i ^ bit) for i in range(size)])  31.9 us
    ppermute x38, waiting for transfers between devices, swap(): return lax.ppermute(rows, axis, [(i, i ^ bit) for i in range(size)])  27.2 us
  transfers between devices with their start and end apart: 38, of which 13 were waited for; matrix products, arithmetic and copies ran while one was open for 0% of the time, Pallas kernels for 36%

profile of v5, /device:TPU:0, one launch (start us, length us, event | category | flops | bytes accessed | tf_op | source)
XLA Modules:
  0.0 102.1 jit_solution(1641191462242740760)
XLA Ops:
  0.7 3.0 %collective-permute-start.1 = (bf16[128,512]{1,0:T(8,128)(2,1)}, bf16[128,512]{1,0:T(8,128)(2,1)S(1)}, u32[]{:S(2)}, u32[]{:S(2)}) collective-permute-start(bf16[128,512]{1,0:T(8,128)(2,1)} %refs_5_.7), channel_id=1, source_target_pairs={{0,2},{1,3},{2,0},{3,1},{4,6},{5,7},{6,4},{7,5},{8,10},{9,11},{10,... | collective-permute-start | bytes 393224 | tf_op jit(solution)/shard_map/ppermute | solution.py:525
  3.7 3.6 %front.1 = (bf16[1024,512]{1,0:T(8,128)(2,1)S(1)}, bf16[1024,512]{1,0:T(8,128)(2,1)S(1)}, bf16[512,384]{1,0:T(8,128)(2,1)S(1)}, bf16[512,128]{1,0:T(8,128)(2,1)S...) custom-call(bf16[1024,512]{1,0:T(8,128)(2,1)} %bitcast.17, ...), custom_call_target="tpu_custom_call" | custom-call | flops 1 | bytes 1 | tf_op jit(solution)/shard_map/front/pallas_call | solution.py:512
  8.0 5.8 %attend_late.1 = (bf16[2,512,640]{2,1,0:T(8,128)(2,1)S(1)}, bf16[512,128]{1,0:T(8,128)(2,1)S(1)}, bf16[2,512,1536]{2,1,0:T(8,128)(2,1)S(1)}, bf16[512,128]{1,0:T(8,128)(2,1)S(1)}) custom-call(s32[1]{0:T(128)S(6)} %copy.39.refs_0_, bf16[1536,512]{1,0:T(8,128)(2,1)S(1)} %get-tuple-element.147.refs_1_, ...), custom_call_target="tpu_custom_call" | custom-call | flops 1 | bytes 1 | tf_op jit(solution)/shard_map/attend_late/pallas_call | solution.py:512
  13.8 0.2 collective-permute-start.5
  14.0 4.2 %attend_early.1 = (bf16[2,512,640]{2,1,0:T(8,128)(2,1)S(1)}, bf16[512,128]{1,0:T(8,128)(2,1)S(1)}, bf16[2,512,1024]{2,1,0:T(8,128)(2,1)S(1)}, bf16[512,128]{1,0:T(8,128)(2,1)S(1)}) custom-call(s32[1]{0:T(128)S(6)} %copy.39.refs_0_, bf16[1536,512]{1,0:T(8,128)(2,1)S(1)} %get-tuple-element.147.refs_1_, ...), custom_call_target="tpu_custom_call" | custom-call | flops 5000000000 | bytes 1 | tf_op jit(solution)/shard_map/attend_early/pallas_call | solution.py:512
  18.2 1.6 %collective-permute-done.5.refs_0_.refs_3_ = bf16[512,128]{1,0:T(8,128)(2,1)S(1)} collective-permute-done((bf16[512,128]{1,0:T(8,128)(2,1)S(1)}, bf16[512,128]{1,0:T(8,128)(2,1)S(1)}, u32[]{:S(2)}, u32[]{:S(2)}) %collective-permute-start.5) | collective-permute-done | bytes 131104 | tf_op jit(solution)/shard_map/ppermute | solution.py:525
  19.8 0.1 collective-permute-start.6
  19.9 0.5 collective-permute-start.4
  20.4 0.3 collective-permute-start.3
  20.7 0.9 collective-permute-done.4.refs_2_
  21.6 1.3 %ffn_send_late.1 = (f32[256,512]{1,0:T(8,128)S(1)}, bf16[256,512]{1,0:T(8,128)(2,1)S(1)}, bf16[256,512]{1,0:T(8,128)(2,1)S(1)}, bf16[256,512]{1,0:T(8,128)(2,1)S...) custom-call(bf16[1024,512]{1,0:T(8,128)(2,1)S(1)} %get-tuple-element.145.refs_0_, ...), custom_call_target="tpu_custom_call" | custom-call | flops 1 | bytes 1 | tf_op jit(solution)/shard_map/ffn_send_late/pallas_call | solution.py:512
  22.9 0.2 collective-permute-start.8
  23.1 1.3 %ffn_keep_late.1 = (f32[256,512]{1,0:T(8,128)S(1)}, bf16[256,512]{1,0:T(8,128)(2,1)S(1)}, bf16[256,512]{1,0:T(8,128)(2,1)S(1)}, bf16[256,512]{1,0:T(8,128)(2,1)S...) custom-call(bf16[1024,512]{1,0:T(8,128)(2,1)S(1)} %get-tuple-element.145.refs_0_, ...), custom_call_target="tpu_custom_call" | custom-call | flops 1 | bytes 1 | tf_op jit(solution)/shard_map/ffn_keep_late/pallas_call | solution.py:512
  24.4 1.4 %collective-permute-done.3.refs_0_.refs_1_.refs_3_ = bf16[512,128]{1,0:T(8,128)(2,1)S(1)} collective-permute-done((bf16[512,128]{1,0:T(8,128)(2,1)S(1)}, bf16[512,128]{1,0:T(8,128)(2,1)S(1)}, u32[]{:S(2)}, u32[]{:S(2)}) %collective-permute-start.3) | collective-permute-done | bytes 131104 | tf_op jit(solution)/shard_map/ppermute | solution.py:525
  25.9 0.1 add_late.1.refs_10_.refs_0_
  26.0 0.6 collective-permute-start.10
  26.5 0.5 collective-permute-start.7
  27.0 1.0 ffn_late.1
  28.1 2.7 %ffn_rows_early.1 = (f32[256,512]{1,0:T(8,128)S(1)}, bf16[256,512]{1,0:T(8,128)(2,1)S(1)}, bf16[256,512]{1,0:T(8,128)(2,1)S(1)}, bf16[256,512]{1,0:T(8,128)(2,1)...) custom-call(bf16[1024,512]{1,0:T(8,128)(2,1)S(1)} %get-tuple-element, ...), custom_call_target="tpu_custom_call" | custom-call | flops 1 | bytes 1 | tf_op jit(solution)/shard_map/ffn_rows_early/pallas_call | solution.py:512
  30.7 0.4 collective-permute-start.9
  31.1 1.1 %ffn_early.1 = (bf16[256,512]{1,0:T(8,128)(2,1)S(1)}, bf16[256,512]{1,0:T(8,128)(2,1)S(1)}, bf16[256,512]{1,0:T(8,128)(2,1)S(1)}, bf16[256,512]{1,0:T(8,128)(2,1...) custom-call(bf16[1024,512]{1,0:T(8,128)(2,1)S(1)} %get-tuple-element, ...), custom_call_target="tpu_custom_call" | custom-call | flops 1 | bytes 1 | tf_op jit(solution)/shard_map/ffn_early/pallas_call | solution.py:512
  32.3 1.2 %collective-permute-done.10.refs_1_ = bf16[256,512]{1,0:T(8,128)(2,1)S(1)} collective-permute-done((bf16[256,512]{1,0:T(8,128)(2,1)S(1)}, bf16[256,512]{1,0:T(8,128)(2,1)S(1)}, u32[]{:S(2)}, u32[]{:S(2)}) %collective-permute-start.10) | collective-permute-done | bytes 262176 | tf_op jit(solution)/shard_map/ppermute | solution.py:525
  33.5 0.1 collective-permute-start.14
  33.6 1.6 %collective-permute-start.12 = (bf16[256,512]{1,0:T(8,128)(2,1)S(1)}, bf16[256,512]{1,0:T(8,128)(2,1)S(1)}, u32[]{:S(2)}, u32[]{:S(2)}) collective-permute-start(bf16[256,512]{1,0:T(8,128)(2,1)S(1)} %get-tuple-element.190), channel_id=1, source_target_pairs={{0,4},{4,0},{8,12},{12,8},{16,20},{20,16},{24,28},{28,24},{1,5},{5... | collective-permute-start | bytes 786440 | tf_op jit(solution)/shard_map/ppermute | solution.py:525
  35.2 1.6 %collective-permute-start.13 = (bf16[256,512]{1,0:T(8,128)(2,1)S(1)}, bf16[256,512]{1,0:T(8,128)(2,1)S(1)}, u32[]{:S(2)}, u32[]{:S(2)}) collective-permute-start(bf16[256,512]{1,0:T(8,128)(2,1)S(1)} %get-tuple-element.192), channel_id=1, source_target_pairs={{0,8},{4,12},{8,0},{12,4},{16,24},{20,28},{24,16},{28,20},{1,9},{5... | collective-permute-start | bytes 786440 | tf_op jit(solution)/shard_map/ppermute | solution.py:525
  36.8 0.6 collective-permute-start.11
  37.4 6.4 %back_late.1 = (f32[512,512]{1,0:T(8,128)S(1)}, f32[128,1536]{1,0:T(8,128)S(1)}, f32[128,1536]{1,0:T(8,128)S(1)}, f32[128,512]{1,0:T(8,128)S(1)}, f32[128,512]{1...) custom-call(f32[256,512]{1,0:T(8,128)S(1)} %get-tuple-element.193.refs_0_.refs_6_,, ...), custom_call_target="tpu_custom_call" | custom-call | flops 1 | bytes 1 | tf_op jit(solution)/shard_map/back_late/pallas_call | solution.py:512
  43.9 1.1 %collective-permute-done.11.refs_1_ = bf16[256,512]{1,0:T(8,128)(2,1)S(1)} collective-permute-done((bf16[256,512]{1,0:T(8,128)(2,1)S(1)}, bf16[256,512]{1,0:T(8,128)(2,1)S(1)}, u32[]{:S(2)}, u32[]{:S(2)}) %collective-permute-start.11) | collective-permute-done | bytes 262176 | tf_op jit(solution)/shard_map/ppermute | solution.py:525
  45.0 0.5 add_middle.1
  45.6 0.5 collective-permute-start.16
  46.1 0.5 collective-permute-start.17
  46.7 0.5 collective-permute-done.15.refs_3_
  47.1 4.6 %back_early.1 = (f32[512,512]{1,0:T(8,128)S(1)}, f32[128,1536]{1,0:T(8,128)S(1)}, f32[128,1536]{1,0:T(8,128)S(1)}, f32[128,512]{1,0:T(8,128)S(1)}, f32[128,512]{...) custom-call(f32[256,512]{1,0:T(8,128)S(1)} %get-tuple-element.174.refs_0_.refs_4_, ...), custom_call_target="tpu_custom_call" | custom-call | flops 1 | bytes 1 | tf_op jit(solution)/shard_map/back_early/pallas_call | solution.py:512
  51.8 1.8 %back_end.1 = (bf16[1024,512]{1,0:T(8,128)(2,1)S(1)}, bf16[1024,512]{1,0:T(8,128)(2,1)S(1)}, bf16[192,512]{1,0:T(8,128)(2,1)S(1)}, bf16[192,512]{1,0:T(8,128)(2,...) custom-call(bf16[512,384]{1,0:T(8,128)(2,1)S(1)} %get-tuple-element.150.refs_4_.ref, ...), custom_call_target="tpu_custom_call" | custom-call | flops 1 | bytes 1 | tf_op jit(solution)/shard_map/back_end/pallas_call | solution.py:512
  53.6 0.2 collective-permute-start.20
  53.8 1.0 collective-permute-start.18
  54.8 1.6 %collective-permute-start.19 = (bf16[160,512]{1,0:T(8,128)(2,1)S(1)}, bf16[160,512]{1,0:T(8,128)(2,1)S(1)}, u32[]{:S(2)}, u32[]{:S(2)}) collective-permute-start(bf16[160,512]{1,0:T(8,128)(2,1)S(1)} %get-tuple-element.232), channel_id=1, source_target_pairs={{0,8},{4,12},{8,0},{12,4},{16,24},{20,28},{24,16},{28,20},{1,9},{5... | collective-permute-start | bytes 491528 | tf_op jit(solution)/shard_map/ppermute | solution.py:525
  56.3 2.6 %collective-permute-start.23 = (bf16[256,512]{1,0:T(8,128)(2,1)S(1)}, bf16[256,512]{1,0:T(8,128)(2,1)S(1)}, u32[]{:S(2)}, u32[]{:S(2)}) collective-permute-start(bf16[256,512]{1,0:T(8,128)(2,1)S(1)} %get-tuple-element.239.refs_4_), channel_id=1, source_target_pairs={{0,16},{4,20},{8,24},{12,28},{16,0},{20,4},{24,8},{28,12},{1,17},{... | collective-permute-start | bytes 786440 | tf_op jit(solution)/shard_map/ppermute | solution.py:525
  58.9 5.5 %collective-permute-done.19.refs_3_ = bf16[160,512]{1,0:T(8,128)(2,1)S(1)} collective-permute-done((bf16[160,512]{1,0:T(8,128)(2,1)S(1)}, bf16[160,512]{1,0:T(8,128)(2,1)S(1)}, u32[]{:S(2)}, u32[]{:S(2)}) %collective-permute-start.19) | collective-permute-done | bytes 163872 | tf_op jit(solution)/shard_map/ppermute | solution.py:525
  64.4 0.4 step_0.1
  64.9 0.6 collective-permute-start.31
  65.5 1.1 %collective-permute-start.22 = (bf16[80,512]{1,0:T(8,128)(2,1)S(1)}, bf16[80,512]{1,0:T(8,128)(2,1)S(1)}, u32[]{:S(2)}, u32[]{:S(2)}) collective-permute-start(bf16[80,512]{1,0:T(8,128)(2,1)S(1)} %get-tuple-element.238), channel_id=1, source_target_pairs={{0,4},{4,0},{8,12},{12,8},{16,20},{20,16},{24,28},{28,24},{1,5},{5... | collective-permute-start | bytes 245768 | tf_op jit(solution)/shard_map/ppermute | solution.py:525
  66.6 4.5 %collective-permute-done.23.refs_5_ = bf16[256,512]{1,0:T(8,128)(2,1)S(1)} collective-permute-done((bf16[256,512]{1,0:T(8,128)(2,1)S(1)}, bf16[256,512]{1,0:T(8,128)(2,1)S(1)}, u32[]{:S(2)}, u32[]{:S(2)}) %collective-permute-start.23) | collective-permute-done | bytes 262176 | tf_op jit(solution)/shard_map/ppermute | solution.py:525
  71.1 0.7 collective-permute-done.21.refs_1_
  71.8 0.1 step_1.1
  71.9 1.3 %collective-permute-start.24 = (bf16[176,512]{1,0:T(8,128)(2,1)S(1)}, bf16[176,512]{1,0:T(8,128)(2,1)S(1)}, u32[]{:S(2)}, u32[]{:S(2)}) collective-permute-start(bf16[176,512]{1,0:T(8,128)(2,1)S(1)} %get-tuple-element.240.refs_0_), channel_id=1, source_target_pairs={{0,16},{4,20},{8,24},{12,28},{16,0},{20,4},{24,8},{28,12},{1,17},{... | collective-permute-start | bytes 540680 | tf_op jit(solution)/shard_map/ppermute | solution.py:525
  73.2 2.5 %collective-permute-start.25 = (bf16[128,512]{1,0:T(8,128)(2,1)S(1)}, bf16[128,512]{1,0:T(8,128)(2,1)S(1)}, u32[]{:S(2)}, u32[]{:S(2)}) collective-permute-start(bf16[128,512]{1,0:T(8,128)(2,1)S(1)} %get-tuple-element.241.refs_2_), channel_id=1, source_target_pairs={{0,8},{4,12},{8,0},{12,4},{16,24},{20,28},{24,16},{28,20},{1,9},{5... | collective-permute-start | bytes 393224 | tf_op jit(solution)/shard_map/ppermute | solution.py:525
  75.7 0.9 collective-permute-start.26
  76.6 2.7 %collective-permute-done.25.refs_3_ = bf16[128,512]{1,0:T(8,128)(2,1)S(1)} collective-permute-done((bf16[128,512]{1,0:T(8,128)(2,1)S(1)}, bf16[128,512]{1,0:T(8,128)(2,1)S(1)}, u32[]{:S(2)}, u32[]{:S(2)}) %collective-permute-start.25) | collective-permute-done | bytes 131104 | tf_op jit(solution)/shard_map/ppermute | solution.py:525
  79.3 1.3 %collective-permute-done.26.refs_5_ = bf16[128,512]{1,0:T(8,128)(2,1)S(1)} collective-permute-done((bf16[128,512]{1,0:T(8,128)(2,1)S(1)}, bf16[128,512]{1,0:T(8,128)(2,1)S(1)}, u32[]{:S(2)}, u32[]{:S(2)}) %collective-permute-start.26) | collective-permute-done | bytes 131104 | tf_op jit(solution)/shard_map/ppermute | solution.py:525
  80.7 0.8 collective-permute-done.24.refs_1_
  81.4 0.2 step_2.1
  81.6 1.0 collective-permute-start.29
  82.6 0.2 collective-permute-start.30
  82.8 1.8 %collective-permute-start.27 = (bf16[80,512]{1,0:T(8,128)(2,1)S(1)}, bf16[80,512]{1,0:T(8,128)(2,1)S(1)}, u32[]{:S(2)}, u32[]{:S(2)}) collective-permute-start(bf16[80,512]{1,0:T(8,128)(2,1)S(1)} %get-tuple-element.243.refs_0_), channel_id=1, source_target_pairs={{0,8},{4,12},{8,0},{12,4},{16,24},{20,28},{24,16},{28,20},{1,9},{5... | collective-permute-start | bytes 245768 | tf_op jit(solution)/shard_map/ppermute | solution.py:525
  84.6 1.1 %collective-permute-start.28 = (bf16[80,512]{1,0:T(8,128)(2,1)S(1)}, bf16[80,512]{1,0:T(8,128)(2,1)S(1)}, u32[]{:S(2)}, u32[]{:S(2)}) collective-permute-start(bf16[80,512]{1,0:T(8,128)(2,1)S(1)} %get-tuple-element.244.refs_2_), channel_id=1, source_target_pairs={{0,4},{4,0},{8,12},{12,8},{16,20},{20,16},{24,28},{28,24},{1,5},{5... | collective-permute-start | bytes 245768 | tf_op jit(solution)/shard_map/ppermute | solution.py:525
  85.7 4.9 %collective-permute-done.27.refs_1_ = bf16[80,512]{1,0:T(8,128)(2,1)S(1)} collective-permute-done((bf16[80,512]{1,0:T(8,128)(2,1)S(1)}, bf16[80,512]{1,0:T(8,128)(2,1)S(1)}, u32[]{:S(2)}, u32[]{:S(2)}) %collective-permute-start.27) | collective-permute-done | bytes 81952 | tf_op jit(solution)/shard_map/ppermute | solution.py:525
  90.6 0.6 step_3.1
  91.3 1.2 %collective-permute-start.33 = (bf16[160,512]{1,0:T(8,128)(2,1)S(1)}, bf16[160,512]{1,0:T(8,128)(2,1)S(1)}, u32[]{:S(2)}, u32[]{:S(2)}) collective-permute-start(bf16[160,512]{1,0:T(8,128)(2,1)S(1)} %get-tuple-element.253.refs_13_.refs_0_), channel_id=1, source_target_pairs={{0,4},{4,0},{8,12},{12,8},{16,20},{20,16},{24,28},{28,24},{1,5},{5... | collective-permute-start | bytes 491528 | tf_op jit(solution)/shard_map/ppermute | solution.py:525
  92.5 1.7 %collective-permute-start.34 = (bf16[160,512]{1,0:T(8,128)(2,1)S(1)}, bf16[160,512]{1,0:T(8,128)(2,1)S(1)}, u32[]{:S(2)}, u32[]{:S(2)}) collective-permute-start(bf16[160,512]{1,0:T(8,128)(2,1)S(1)} %get-tuple-element.256.refs_2_), channel_id=1, source_target_pairs={{0,8},{4,12},{8,0},{12,4},{16,24},{20,28},{24,16},{28,20},{1,9},{5... | collective-permute-start | bytes 491528 | tf_op jit(solution)/shard_map/ppermute | solution.py:525
  94.3 2.2 %collective-permute-start.36 = (f32[16,512]{1,0:T(8,128)S(1)}, f32[16,512]{1,0:T(8,128)S(1)}, u32[]{:S(2)}, u32[]{:S(2)}) collective-permute-start(f32[16,512]{1,0:T(8,128)S(1)} %get-tuple-element.257.refs_4_), channel_id=1, source_target_pairs={{0,2},{1,3},{2,0},{3,1},{4,6},{5,7},{6,4},{7,5},{8,10},{9,11},{10,... | collective-permute-start | bytes 98312 | tf_op jit(solution)/shard_map/ppermute | solution.py:525
  96.4 0.1 collective-permute-start.37
  96.6 3.4 %finish.1 = (bf16[1024,512]{1,0:T(8,128)(2,1)}, bf16[1024,512]{1,0:T(8,128)(2,1)}, f32[512,512]{1,0:T(8,128)}, f32[512,512]{1,0:T(8,128)}) custom-call(bf16[1024,512]{1,0:T(8,128)(2,1)S(1)} %get-tuple-element.145.refs_0_, f32[1,512]{1,0:T(1,128)S(1)} %get-tuple-element.146.refs_3_.refs_1_, f32[512,512]{1,0:T(8,128)S(1)} %get-tuple-element.208.refs_2_, ...), custom_call_target="tpu_custom_call" | custom-call | flops 1 | bytes 1 | tf_op jit(solution)/shard_map/finish/pallas_call | solution.py:512
  100.1 1.9 %last.1 = (f32[512,128]{1,0:T(8,128)}, f32[512,128]{1,0:T(8,128)}, f32[512,128]{1,0:T(8,128)}, f32[512,128]{1,0:T(8,128)}, f32[128,512]{1,0:T(8,128)}, /*index=5...) custom-call(bf16[160,512]{1,0:T(8,128)(2,1)S(1)} %get-tuple-element., ...), custom_call_target="tpu_custom_call" | custom-call | flops 1 | bytes 1 | tf_op jit(solution)/shard_map/last/pallas_call | solution.py:512
  (37 shorter events, 0.4 us)
Async XLA Ops:
  0.7 13.4 %collective-permute-start.1 = (bf16[128,512]{1,0:T(8,128)(2,1)}, bf16[128,512]{1,0:T(8,128)(2,1)S(1)}, u32[]{:S(2)}, u32[]{:S(2)}) collective-permute-start(bf16[128,512]{1,0:T(8,128)(2,1)} %refs_5_.7), channel_id=1, source_target_pairs={{0,2},{1,3},{2,0},{3,1},{4,6},{5,7},{6,4},{7,5},{8,10},{9,11},{10,... | collective-permute-start | bytes 393224 | tf_op jit(solution)/shard_map/ppermute | solution.py:525
  3.7 10.3 %collective-permute-start = (bf16[128,512]{1,0:T(8,128)(2,1)}, bf16[128,512]{1,0:T(8,128)(2,1)S(1)}, u32[]{:S(2)}, u32[]{:S(2)}) collective-permute-start(bf16[128,512]{1,0:T(8,128)(2,1)} %refs_5_.7), channel_id=1, source_target_pairs={{0,1},{1,0},{2,3},{3,2},{4,5},{5,4},{6,7},{7,6},{8,9},{9,8},{10,11... | collective-permute-start | bytes 393224 | tf_op jit(solution)/shard_map/ppermute | solution.py:525
  13.8 7.8 %copy-start = (bf16[128,512]{1,0:T(8,128)(2,1)S(1)}, bf16[128,512]{1,0:T(8,128)(2,1)}, u32[]{:S(2)}) copy-start(bf16[128,512]{1,0:T(8,128)(2,1)} %refs_5_.7) | copy-start | bytes 393220
  13.8 6.0 %collective-permute-start.5 = (bf16[512,128]{1,0:T(8,128)(2,1)S(1)}, bf16[512,128]{1,0:T(8,128)(2,1)S(1)}, u32[]{:S(2)}, u32[]{:S(2)}) collective-permute-start(bf16[512,128]{1,0:T(8,128)(2,1)S(1)} %get-tuple-element.156.refs_1_.refs_7_), channel_id=1, source_target_pairs={{0,2},{1,3},{2,0},{3,1},{4,6},{5,7},{6,4},{7,5},{8,10},{9,11},{10,... | collective-permute-start | bytes 393224 | tf_op jit(solution)/shard_map/ppermute | solution.py:525
  19.8 1.8 %collective-permute-start.6 = (bf16[1024,128]{1,0:T(8,128)(2,1)S(1)}, bf16[1024,128]{1,0:T(8,128)(2,1)S(1)}, u32[]{:S(2)}, u32[]{:S(2)}) collective-permute-start(bf16[1024,128]{1,0:T(8,128)(2,1)S(1)} %relay_late.1), channel_id=1, source_target_pairs={{0,1},{1,0},{2,3},{3,2},{4,5},{5,4},{6,7},{7,6},{8,9},{9,8},{10,11... | collective-permute-start | bytes 786440 | tf_op jit(solution)/shard_map/ppermute | solution.py:525
  19.9 1.7 %collective-permute-start.4 = (bf16[512,128]{1,0:T(8,128)(2,1)S(1)}, bf16[512,128]{1,0:T(8,128)(2,1)S(1)}, u32[]{:S(2)}, u32[]{:S(2)}) collective-permute-start(bf16[512,128]{1,0:T(8,128)(2,1)S(1)} %get-tuple-element.156.refs_1_.refs_7_), channel_id=1, source_target_pairs={{0,1},{1,0},{2,3},{3,2},{4,5},{5,4},{6,7},{7,6},{8,9},{9,8},{10,11... | collective-permute-start | bytes 393224 | tf_op jit(solution)/shard_map/ppermute | solution.py:525
  20.4 5.5 %collective-permute-start.3 = (bf16[512,128]{1,0:T(8,128)(2,1)S(1)}, bf16[512,128]{1,0:T(8,128)(2,1)S(1)}, u32[]{:S(2)}, u32[]{:S(2)}) collective-permute-start(bf16[512,128]{1,0:T(8,128)(2,1)S(1)} %get-tuple-element.155.refs_2_.refs_1_.refs_7_), channel_id=1, source_target_pairs={{0,2},{1,3},{2,0},{3,1},{4,6},{5,7},{6,4},{7,5},{8,10},{9,11},{10,... | collective-permute-start | bytes 393224 | tf_op jit(solution)/shard_map/ppermute | solution.py:525
  22.9 3.0 %collective-permute-start.8 = (bf16[256,512]{1,0:T(8,128)(2,1)S(1)}, bf16[256,512]{1,0:T(8,128)(2,1)S(1)}, u32[]{:S(2)}, u32[]{:S(2)}) collective-permute-start(bf16[256,512]{1,0:T(8,128)(2,1)S(1)} %get-tuple-element.163.refs_15_), channel_id=1, source_target_pairs={{0,1},{1,0},{2,3},{3,2},{4,5},{5,4},{6,7},{7,6},{8,9},{9,8},{10,11... | collective-permute-start | bytes 786440 | tf_op jit(solution)/shard_map/ppermute | solution.py:525
  26.0 7.5 %collective-permute-start.10 = (bf16[256,512]{1,0:T(8,128)(2,1)S(1)}, bf16[256,512]{1,0:T(8,128)(2,1)S(1)}, u32[]{:S(2)}, u32[]{:S(2)}) collective-permute-start(bf16[256,512]{1,0:T(8,128)(2,1)S(1)} %add_late.1.refs_10_.refs_0_), channel_id=1, source_target_pairs={{0,2},{1,3},{2,0},{3,1},{4,6},{5,7},{6,4},{7,5},{8,10},{9,11},{10,... | collective-permute-start | bytes 786440 | tf_op jit(solution)/shard_map/ppermute | solution.py:525
  26.5 1.5 %collective-permute-start.2 = (bf16[512,128]{1,0:T(8,128)(2,1)S(1)}, bf16[512,128]{1,0:T(8,128)(2,1)S(1)}, u32[]{:S(2)}, u32[]{:S(2)}) collective-permute-start(bf16[512,128]{1,0:T(8,128)(2,1)S(1)} %get-tuple-element.155.refs_2_.refs_1_.refs_7_), channel_id=1, source_target_pairs={{0,1},{1,0},{2,3},{3,2},{4,5},{5,4},{6,7},{7,6},{8,9},{9,8},{10,11... | collective-permute-start | bytes 393224 | tf_op jit(solution)/shard_map/ppermute | solution.py:525
  26.5 1.5 %collective-permute-start.7 = (bf16[512,128]{1,0:T(8,128)(2,1)S(1)}, bf16[512,128]{1,0:T(8,128)(2,1)S(1)}, u32[]{:S(2)}, u32[]{:S(2)}) collective-permute-start(bf16[512,128]{1,0:T(8,128)(2,1)S(1)} %relay_early.1.refs_2_), channel_id=1, source_target_pairs={{0,1},{1,0},{2,3},{3,2},{4,5},{5,4},{6,7},{7,6},{8,9},{9,8},{10,11... | collective-permute-start | bytes 393224 | tf_op jit(solution)/shard_map/ppermute | solution.py:525
  30.7 6.0 %collective-permute-start.9 = (bf16[256,512]{1,0:T(8,128)(2,1)S(1)}, bf16[256,512]{1,0:T(8,128)(2,1)S(1)}, u32[]{:S(2)}, u32[]{:S(2)}) collective-permute-start(bf16[256,512]{1,0:T(8,128)(2,1)S(1)} %get-tuple-element.177), channel_id=1, source_target_pairs={{0,1},{1,0},{2,3},{3,2},{4,5},{5,4},{6,7},{7,6},{8,9},{9,8},{10,11... | collective-permute-start | bytes 786440 | tf_op jit(solution)/shard_map/ppermute | solution.py:525
  33.5 3.9 %collective-permute-start.14 = (bf16[256,512]{1,0:T(8,128)(2,1)S(1)}, bf16[256,512]{1,0:T(8,128)(2,1)S(1)}, u32[]{:S(2)}, u32[]{:S(2)}) collective-permute-start(bf16[256,512]{1,0:T(8,128)(2,1)S(1)} %add_late_chips.1.refs_2_), channel_id=1, source_target_pairs={{0,1},{1,0},{2,3},{3,2},{4,5},{5,4},{6,7},{7,6},{8,9},{9,8},{10,11... | collective-permute-start | bytes 786440 | tf_op jit(solution)/shard_map/ppermute | solution.py:525
  33.6 10.2 %collective-permute-start.12 = (bf16[256,512]{1,0:T(8,128)(2,1)S(1)}, bf16[256,512]{1,0:T(8,128)(2,1)S(1)}, u32[]{:S(2)}, u32[]{:S(2)}) collective-permute-start(bf16[256,512]{1,0:T(8,128)(2,1)S(1)} %get-tuple-element.190), channel_id=1, source_target_pairs={{0,4},{4,0},{8,12},{12,8},{16,20},{20,16},{24,28},{28,24},{1,5},{5... | collective-permute-start | bytes 786440 | tf_op jit(solution)/shard_map/ppermute | solution.py:525
  35.2 8.7 %collective-permute-start.13 = (bf16[256,512]{1,0:T(8,128)(2,1)S(1)}, bf16[256,512]{1,0:T(8,128)(2,1)S(1)}, u32[]{:S(2)}, u32[]{:S(2)}) collective-permute-start(bf16[256,512]{1,0:T(8,128)(2,1)S(1)} %get-tuple-element.192), channel_id=1, source_target_pairs={{0,8},{4,12},{8,0},{12,4},{16,24},{20,28},{24,16},{28,20},{1,9},{5... | collective-permute-start | bytes 786440 | tf_op jit(solution)/shard_map/ppermute | solution.py:525
  36.8 8.2 %collective-permute-start.11 = (bf16[256,512]{1,0:T(8,128)(2,1)S(1)}, bf16[256,512]{1,0:T(8,128)(2,1)S(1)}, u32[]{:S(2)}, u32[]{:S(2)}) collective-permute-start(bf16[256,512]{1,0:T(8,128)(2,1)S(1)} %add_early.1.refs_0_), channel_id=1, source_target_pairs={{0,2},{1,3},{2,0},{3,1},{4,6},{5,7},{6,4},{7,5},{8,10},{9,11},{10,... | collective-permute-start | bytes 786440 | tf_op jit(solution)/shard_map/ppermute | solution.py:525
  45.5 1.6 %collective-permute-start.15 = (bf16[256,512]{1,0:T(8,128)(2,1)S(1)}, bf16[256,512]{1,0:T(8,128)(2,1)S(1)}, u32[]{:S(2)}, u32[]{:S(2)}) collective-permute-start(bf16[256,512]{1,0:T(8,128)(2,1)S(1)} %get-tuple-element.200.refs_2_), channel_id=1, source_target_pairs={{0,1},{1,0},{2,3},{3,2},{4,5},{5,4},{6,7},{7,6},{8,9},{9,8},{10,11... | collective-permute-start | bytes 786440 | tf_op jit(solution)/shard_map/ppermute | solution.py:525
  45.6 6.2 %collective-permute-start.16 = (bf16[128,512]{1,0:T(8,128)(2,1)S(1)}, bf16[128,512]{1,0:T(8,128)(2,1)S(1)}, u32[]{:S(2)}, u32[]{:S(2)}) collective-permute-start(bf16[128,512]{1,0:T(8,128)(2,1)S(1)} %get-tuple-element.226), channel_id=1, source_target_pairs={{0,8},{4,12},{8,0},{12,4},{16,24},{20,28},{24,16},{28,20},{1,9},{5... | collective-permute-start | bytes 393224 | tf_op jit(solution)/shard_map/ppermute | solution.py:525
  46.1 5.7 %collective-permute-start.17 = (bf16[128,512]{1,0:T(8,128)(2,1)S(1)}, bf16[128,512]{1,0:T(8,128)(2,1)S(1)}, u32[]{:S(2)}, u32[]{:S(2)}) collective-permute-start(bf16[128,512]{1,0:T(8,128)(2,1)S(1)} %get-tuple-element.228), channel_id=1, source_target_pairs={{0,4},{4,0},{8,12},{12,8},{16,20},{20,16},{24,28},{28,24},{1,5},{5... | collective-permute-start | bytes 393224 | tf_op jit(solution)/shard_map/ppermute | solution.py:525
  53.6 10.9 %collective-permute-start.20 = (bf16[1024,512]{1,0:T(8,128)(2,1)S(1)}, bf16[1024,512]{1,0:T(8,128)(2,1)S(1)}, u32[]{:S(2)}, u32[]{:S(2)}) collective-permute-start(bf16[1024,512]{1,0:T(8,128)(2,1)S(1)} %get-tuple-element.234), channel_id=1, source_target_pairs={{0,1},{1,0},{2,3},{3,2},{4,5},{5,4},{6,7},{7,6},{8,9},{9,8},{10,11... | collective-permute-start | bytes 3145736 | tf_op jit(solution)/shard_map/ppermute | solution.py:525
  53.8 10.6 %collective-permute-start.18 = (bf16[192,512]{1,0:T(8,128)(2,1)S(1)}, bf16[192,512]{1,0:T(8,128)(2,1)S(1)}, u32[]{:S(2)}, u32[]{:S(2)}) collective-permute-start(bf16[192,512]{1,0:T(8,128)(2,1)S(1)} %get-tuple-element.230), channel_id=1, source_target_pairs={{0,4},{4,0},{8,12},{12,8},{16,20},{20,16},{24,28},{28,24},{1,5},{5... | collective-permute-start | bytes 589832 | tf_op jit(solution)/shard_map/ppermute | solution.py:525
  54.8 9.7 %collective-permute-start.19 = (bf16[160,512]{1,0:T(8,128)(2,1)S(1)}, bf16[160,512]{1,0:T(8,128)(2,1)S(1)}, u32[]{:S(2)}, u32[]{:S(2)}) collective-permute-start(bf16[160,512]{1,0:T(8,128)(2,1)S(1)} %get-tuple-element.232), channel_id=1, source_target_pairs={{0,8},{4,12},{8,0},{12,4},{16,24},{20,28},{24,16},{28,20},{1,9},{5... | collective-permute-start | bytes 491528 | tf_op jit(solution)/shard_map/ppermute | solution.py:525
  56.3 14.8 %collective-permute-start.23 = (bf16[256,512]{1,0:T(8,128)(2,1)S(1)}, bf16[256,512]{1,0:T(8,128)(2,1)S(1)}, u32[]{:S(2)}, u32[]{:S(2)}) collective-permute-start(bf16[256,512]{1,0:T(8,128)(2,1)S(1)} %get-tuple-element.239.refs_4_), channel_id=1, source_target_pairs={{0,16},{4,20},{8,24},{12,28},{16,0},{20,4},{24,8},{28,12},{1,17},{... | collective-permute-start | bytes 786440 | tf_op jit(solution)/shard_map/ppermute | solution.py:525
  64.9 25.7 %collective-permute-start.31 = (bf16[1024,512]{1,0:T(8,128)(2,1)S(1)}, bf16[1024,512]{1,0:T(8,128)(2,1)S(1)}, u32[]{:S(2)}, u32[]{:S(2)}) collective-permute-start(bf16[1024,512]{1,0:T(8,128)(2,1)S(1)} %get-tuple-element.248.refs_10_), channel_id=1, source_target_pairs={{0,2},{1,3},{2,0},{3,1},{4,6},{5,7},{6,4},{7,5},{8,10},{9,11},{10,... | collective-permute-start | bytes 3145736 | tf_op jit(solution)/shard_map/ppermute | solution.py:525
  65.5 6.3 %collective-permute-start.21 = (bf16[96,512]{1,0:T(8,128)(2,1)S(1)}, bf16[96,512]{1,0:T(8,128)(2,1)S(1)}, u32[]{:S(2)}, u32[]{:S(2)}) collective-permute-start(bf16[96,512]{1,0:T(8,128)(2,1)S(1)} %get-tuple-element.236), channel_id=1, source_target_pairs={{0,8},{4,12},{8,0},{12,4},{16,24},{20,28},{24,16},{28,20},{1,9},{5... | collective-permute-start | bytes 294920 | tf_op jit(solution)/shard_map/ppermute | solution.py:525
  65.5 5.6 %collective-permute-start.22 = (bf16[80,512]{1,0:T(8,128)(2,1)S(1)}, bf16[80,512]{1,0:T(8,128)(2,1)S(1)}, u32[]{:S(2)}, u32[]{:S(2)}) collective-permute-start(bf16[80,512]{1,0:T(8,128)(2,1)S(1)} %get-tuple-element.238), channel_id=1, source_target_pairs={{0,4},{4,0},{8,12},{12,8},{16,20},{20,16},{24,28},{28,24},{1,5},{5... | collective-permute-start | bytes 245768 | tf_op jit(solution)/shard_map/ppermute | solution.py:525
  71.9 9.5 %collective-permute-start.24 = (bf16[176,512]{1,0:T(8,128)(2,1)S(1)}, bf16[176,512]{1,0:T(8,128)(2,1)S(1)}, u32[]{:S(2)}, u32[]{:S(2)}) collective-permute-start(bf16[176,512]{1,0:T(8,128)(2,1)S(1)} %get-tuple-element.240.refs_0_), channel_id=1, source_target_pairs={{0,16},{4,20},{8,24},{12,28},{16,0},{20,4},{24,8},{28,12},{1,17},{... | collective-permute-start | bytes 540680 | tf_op jit(solution)/shard_map/ppermute | solution.py:525
  73.2 6.1 %collective-permute-start.25 = (bf16[128,512]{1,0:T(8,128)(2,1)S(1)}, bf16[128,512]{1,0:T(8,128)(2,1)S(1)}, u32[]{:S(2)}, u32[]{:S(2)}) collective-permute-start(bf16[128,512]{1,0:T(8,128)(2,1)S(1)} %get-tuple-element.241.refs_2_), channel_id=1, source_target_pairs={{0,8},{4,12},{8,0},{12,4},{16,24},{20,28},{24,16},{28,20},{1,9},{5... | collective-permute-start | bytes 393224 | tf_op jit(solution)/shard_map/ppermute | solution.py:525
  75.7 5.0 %collective-permute-start.26 = (bf16[128,512]{1,0:T(8,128)(2,1)S(1)}, bf16[128,512]{1,0:T(8,128)(2,1)S(1)}, u32[]{:S(2)}, u32[]{:S(2)}) collective-permute-start(bf16[128,512]{1,0:T(8,128)(2,1)S(1)} %get-tuple-element.242.refs_4_), channel_id=1, source_target_pairs={{0,4},{4,0},{8,12},{12,8},{16,20},{20,16},{24,28},{28,24},{1,5},{5... | collective-permute-start | bytes 393224 | tf_op jit(solution)/shard_map/ppermute | solution.py:525
  81.6 9.0 %collective-permute-start.29 = (bf16[256,512]{1,0:T(8,128)(2,1)S(1)}, bf16[256,512]{1,0:T(8,128)(2,1)S(1)}, u32[]{:S(2)}, u32[]{:S(2)}) collective-permute-start(bf16[256,512]{1,0:T(8,128)(2,1)S(1)} %get-tuple-element.245.refs_4_), channel_id=1, source_target_pairs={{0,4},{4,0},{8,12},{12,8},{16,20},{20,16},{24,28},{28,24},{1,5},{5... | collective-permute-start | bytes 786440 | tf_op jit(solution)/shard_map/ppermute | solution.py:525
  82.6 8.0 %collective-permute-start.30 = (bf16[256,512]{1,0:T(8,128)(2,1)S(1)}, bf16[256,512]{1,0:T(8,128)(2,1)S(1)}, u32[]{:S(2)}, u32[]{:S(2)}) collective-permute-start(bf16[256,512]{1,0:T(8,128)(2,1)S(1)} %get-tuple-element.246.refs_6_), channel_id=1, source_target_pairs={{0,8},{4,12},{8,0},{12,4},{16,24},{20,28},{24,16},{28,20},{1,9},{5... | collective-permute-start | bytes 786440 | tf_op jit(solution)/shard_map/ppermute | solution.py:525
  82.8 7.8 %collective-permute-start.27 = (bf16[80,512]{1,0:T(8,128)(2,1)S(1)}, bf16[80,512]{1,0:T(8,128)(2,1)S(1)}, u32[]{:S(2)}, u32[]{:S(2)}) collective-permute-start(bf16[80,512]{1,0:T(8,128)(2,1)S(1)} %get-tuple-element.243.refs_0_), channel_id=1, source_target_pairs={{0,8},{4,12},{8,0},{12,4},{16,24},{20,28},{24,16},{28,20},{1,9},{5... | collective-permute-start | bytes 245768 | tf_op jit(solution)/shard_map/ppermute | solution.py:525
  84.6 6.0 %collective-permute-start.28 = (bf16[80,512]{1,0:T(8,128)(2,1)S(1)}, bf16[80,512]{1,0:T(8,128)(2,1)S(1)}, u32[]{:S(2)}, u32[]{:S(2)}) collective-permute-start(bf16[80,512]{1,0:T(8,128)(2,1)S(1)} %get-tuple-element.244.refs_2_), channel_id=1, source_target_pairs={{0,4},{4,0},{8,12},{12,8},{16,20},{20,16},{24,28},{28,24},{1,5},{5... | collective-permute-start | bytes 245768 | tf_op jit(solution)/shard_map/ppermute | solution.py:525
  91.2 5.2 %collective-permute-start.32 = (bf16[1024,512]{1,0:T(8,128)(2,1)S(1)}, bf16[1024,512]{1,0:T(8,128)(2,1)S(1)}, u32[]{:S(2)}, u32[]{:S(2)}) collective-permute-start(bf16[1024,512]{1,0:T(8,128)(2,1)S(1)} %get-tuple-element.249.refs_8_), channel_id=1, source_target_pairs={{0,1},{1,0},{2,3},{3,2},{4,5},{5,4},{6,7},{7,6},{8,9},{9,8},{10,11... | collective-permute-start | bytes 3145736 | tf_op jit(solution)/shard_map/ppermute | solution.py:525
  91.3 8.8 %collective-permute-start.33 = (bf16[160,512]{1,0:T(8,128)(2,1)S(1)}, bf16[160,512]{1,0:T(8,128)(2,1)S(1)}, u32[]{:S(2)}, u32[]{:S(2)}) collective-permute-start(bf16[160,512]{1,0:T(8,128)(2,1)S(1)} %get-tuple-element.253.refs_13_.refs_0_), channel_id=1, source_target_pairs={{0,4},{4,0},{8,12},{12,8},{16,20},{20,16},{24,28},{28,24},{1,5},{5... | collective-permute-start | bytes 491528 | tf_op jit(solution)/shard_map/ppermute | solution.py:525
  92.5 7.5 %collective-permute-start.34 = (bf16[160,512]{1,0:T(8,128)(2,1)S(1)}, bf16[160,512]{1,0:T(8,128)(2,1)S(1)}, u32[]{:S(2)}, u32[]{:S(2)}) collective-permute-start(bf16[160,512]{1,0:T(8,128)(2,1)S(1)} %get-tuple-element.256.refs_2_), channel_id=1, source_target_pairs={{0,8},{4,12},{8,0},{12,4},{16,24},{20,28},{24,16},{28,20},{1,9},{5... | collective-permute-start | bytes 491528 | tf_op jit(solution)/shard_map/ppermute | solution.py:525
  94.3 5.8 %collective-permute-start.35 = (f32[16,512]{1,0:T(8,128)S(1)}, f32[16,512]{1,0:T(8,128)S(1)}, u32[]{:S(2)}, u32[]{:S(2)}) collective-permute-start(f32[16,512]{1,0:T(8,128)S(1)} %get-tuple-element.257.refs_4_), channel_id=1, source_target_pairs={{0,1},{1,0},{2,3},{3,2},{4,5},{5,4},{6,7},{7,6},{8,9},{9,8},{10,11... | collective-permute-start | bytes 98312 | tf_op jit(solution)/shard_map/ppermute | solution.py:525
  94.3 5.8 %collective-permute-start.36 = (f32[16,512]{1,0:T(8,128)S(1)}, f32[16,512]{1,0:T(8,128)S(1)}, u32[]{:S(2)}, u32[]{:S(2)}) collective-permute-start(f32[16,512]{1,0:T(8,128)S(1)} %get-tuple-element.257.refs_4_), channel_id=1, source_target_pairs={{0,2},{1,3},{2,0},{3,1},{4,6},{5,7},{6,4},{7,5},{8,10},{9,11},{10,... | collective-permute-start | bytes 98312 | tf_op jit(solution)/shard_map/ppermute | solution.py:525
  96.4 3.6 %collective-permute-start.37 = (f32[16,512]{1,0:T(8,128)S(1)}, f32[16,512]{1,0:T(8,128)S(1)}, u32[]{:S(2)}, u32[]{:S(2)}) collective-permute-start(f32[16,512]{1,0:T(8,128)S(1)} %get-tuple-element.257.refs_4_), channel_id=1, source_target_pairs={{0,3},{1,2},{2,1},{3,0},{4,7},{5,6},{6,5},{7,4},{8,11},{9,10},{10,... | collective-permute-start | bytes 98312 | tf_op jit(solution)/shard_map/ppermute | solution.py:525

commit v6 on v5

--- a/solution.py
+++ b/solution.py
@@ -409,8 +409,7 @@
         by_core((place_ref[1] >> 1) & 1, d // 2, b_keep, b_send, piece, slice(d % 2 * size, (d % 2 + 1) * size))
 
 
-def last_kernel(wide, heads, n_tensor, place_ref, a_mine, a_got, b_mine, b_got, *refs):
-    totals, refs = refs[:n_tensor], refs[n_tensor:]
+def last_kernel(wide, heads, place_ref, a_mine, a_got, b_mine, b_got, mine, chip_ref, other_ref, *refs):
     outs, smalls = refs[:5], refs[5:13]
     rows_scr, turned_scr, sems = refs[13:]
     copies = []
@@ -426,10 +425,7 @@
     for i in range(4):
         turned_scr[i] = rows_scr[i * wide : (i + 1) * wide, :].T
         send(turned_scr.at[i], outs[i])
-    mine = totals[0]
-    total = mine[...]
-    for other in totals[1:]:
-        total = total + other[...]
+    total = chip_ref[...] + other_ref[...]
     for i in range(5):
         smalls[i][...] = total[i : i + 1, :]
     for k in range(2):
@@ -537,6 +533,11 @@
             outs.pop(0)[...] = added(mine[...], got[...])
         elif kind == "copy":
             outs.pop(0)[...] = mine[...]
+        elif kind == "plus":
+            total = mine[...] + got[...]
+            for other in more:
+                total = total + other[...]
+            outs.pop(0)[...] = total
         elif kind == "pack":
             out = outs.pop(0)
             size = mine.shape[0]
@@ -566,6 +567,7 @@
             "join": [((2 * size, width), BF)],
             "sum": [((size, width), BF)],
             "copy": [((size, width), mine.dtype)],
+            "plus": [((size, width), FL)],
             "pack": [((size + others[-1].shape[0], width), BF)],
             "three": [(((size - small) // 2, width), BF), ((small, width), FL), (((size - small) // 2, width), BF)],
         }[kind]
@@ -790,14 +792,13 @@
         [("three", 0, attn, pair(attn, bits[-1])), ("join", 1, up, pair(up, 1)), ("join", 0, down, pair(down, 0))],
         "step_2", cost=STEP_COST,
     )
-    a_rows, b_rows, up, down, totals, summed = work(
+    a_rows, b_rows, up, down, chip_totals, summed = work(
         place,
         [("join", 1, a_rows, pair(a_rows, 1)), ("join", 0, b_rows, pair(b_rows, 0)), ("join", 0, up, pair(up, 0)),
-         ("join", 1, down, pair(down, 1)), ("copy", 0, totals, totals), ("sum", 0, *rows)],
+         ("join", 1, down, pair(down, 1)), ("plus", 0, totals, cores(totals, n_tensor)), ("sum", 0, *rows)],
         "step_3",
     )
     rows = (summed, cores(summed, n_tensor))
-    totals = [totals] + [swap(totals, "tensor", n_tensor, k) for k in range(1, n_tensor)]
     output, input_grad, g_up, g_down = call(
         functools.partial(finish_kernel, block), [(x.shape, BF)] * 2 + [((width, ff), FL), ((ff, width), FL)],
         (place, x, attn_gain, gh_e, gh_l, *hidden_e, *hidden_l, *rows, down_bias, up, down), "finish", 1,
@@ -807,10 +808,10 @@
     )
     output_there = pltpu.with_memory_space_constraint(output, pltpu.HBM)
     g_query, g_key, g_value, g_pos, g_out, *vecs = call(
-        functools.partial(last_kernel, wide, heads, n_tensor),
+        functools.partial(last_kernel, wide, heads),
         [((width, wide), FL)] * 4 + [((wide, width), FL)]
         + [((1, width), FL)] * 5 + [((heads, HEAD), FL)] * 2 + [((1, ff), FL)],
-        (place, a_rows, pair(a_rows, 0), b_rows, pair(b_rows, 1), *totals), "last", 1,
+        (place, a_rows, pair(a_rows, 0), b_rows, pair(b_rows, 1), totals, *chips(chip_totals, n_tensor)), "last", 1,
         [pltpu.VMEM((5 * wide, width), FL), pltpu.VMEM((4, width, wide), FL), pltpu.SemaphoreType.DMA((5,))],
         after=(output_there,), far=5,
     )

time: 102 us -> 102 us (level)
    ppermute x38 -> x37, starting transfers between devices: 31.9 us -> 31.8 us  [swap(): return lax.ppermute(rows, axis, [(i, i ^ bit) for i in range(size)])]
    ppermute x38 -> x37, waiting for transfers between devices: 27.2 us -> 27.2 us  [swap(): return lax.ppermute(rows, axis, [(i, i ^ bit) for i in range(size)])]
  transfers between devices with their start and end apart: 38 -> 37, of which waited for: 13 -> 13; matrix products, arithmetic and copies ran while one was open for 0% -> 0% of each run, Pallas kernels for 36% -> 36%
where the time goes in v6:
time: 102 us
  Pallas kernels  41.2 us (40%)
  starting transfers between devices  31.8 us (31%)
  waiting for transfers between devices  27.2 us (27%)
  between operations  1.76 us (2%)
    pallas_call x23, Pallas kernels, call(): pl.pallas_call(body, out_shape=[pltpu.HBM(s, d) if i < far else jax.Shape...  41.2 us
    ppermute x37, starting transfers between devices, swap(): return lax.ppermute(rows, axis, [(i, i ^ bit) for i in range(size)])  31.8 us
    ppermute x37, waiting for transfers between devices, swap(): return lax.ppermute(rows, axis, [(i, i ^ bit) for i in range(size)])  27.2 us
  transfers between devices with their start and end apart: 37, of which 13 were waited for; matrix products, arithmetic and copies ran while one was open for 0% of the time, Pallas kernels for 36%

profile of v6, /device:TPU:0, one launch (start us, length us, event | category | flops | bytes accessed | tf_op | source)
XLA Modules:
  0.0 102.0 jit_solution(627272822547613579)
XLA Ops:
  0.7 3.0 %collective-permute-start.1 = (bf16[128,512]{1,0:T(8,128)(2,1)}, bf16[128,512]{1,0:T(8,128)(2,1)S(1)}, u32[]{:S(2)}, u32[]{:S(2)}) collective-permute-start(bf16[128,512]{1,0:T(8,128)(2,1)} %refs_5_.7), channel_id=1, source_target_pairs={{0,2},{1,3},{2,0},{3,1},{4,6},{5,7},{6,4},{7,5},{8,10},{9,11},{10,... | collective-permute-start | bytes 393224 | tf_op jit(solution)/shard_map/ppermute | solution.py:521
  3.7 3.6 %front.1 = (bf16[1024,512]{1,0:T(8,128)(2,1)S(1)}, bf16[1024,512]{1,0:T(8,128)(2,1)S(1)}, bf16[512,384]{1,0:T(8,128)(2,1)S(1)}, bf16[512,128]{1,0:T(8,128)(2,1)S...) custom-call(bf16[1024,512]{1,0:T(8,128)(2,1)} %bitcast.17, ...), custom_call_target="tpu_custom_call" | custom-call | flops 1 | bytes 1 | tf_op jit(solution)/shard_map/front/pallas_call | solution.py:508
  8.0 5.8 %attend_late.1 = (bf16[2,512,640]{2,1,0:T(8,128)(2,1)S(1)}, bf16[512,128]{1,0:T(8,128)(2,1)S(1)}, bf16[2,512,1536]{2,1,0:T(8,128)(2,1)S(1)}, bf16[512,128]{1,0:T(8,128)(2,1)S(1)}) custom-call(s32[1]{0:T(128)S(6)} %copy.39.refs_0_, bf16[1536,512]{1,0:T(8,128)(2,1)S(1)} %get-tuple-element.147.refs_1_, ...), custom_call_target="tpu_custom_call" | custom-call | flops 1 | bytes 1 | tf_op jit(solution)/shard_map/attend_late/pallas_call | solution.py:508
  13.8 0.2 collective-permute-start.5
  14.0 4.2 %attend_early.1 = (bf16[2,512,640]{2,1,0:T(8,128)(2,1)S(1)}, bf16[512,128]{1,0:T(8,128)(2,1)S(1)}, bf16[2,512,1024]{2,1,0:T(8,128)(2,1)S(1)}, bf16[512,128]{1,0:T(8,128)(2,1)S(1)}) custom-call(s32[1]{0:T(128)S(6)} %copy.39.refs_0_, bf16[1536,512]{1,0:T(8,128)(2,1)S(1)} %get-tuple-element.147.refs_1_, ...), custom_call_target="tpu_custom_call" | custom-call | flops 5000000000 | bytes 1 | tf_op jit(solution)/shard_map/attend_early/pallas_call | solution.py:508
  18.2 1.6 %collective-permute-done.5.refs_0_.refs_3_ = bf16[512,128]{1,0:T(8,128)(2,1)S(1)} collective-permute-done((bf16[512,128]{1,0:T(8,128)(2,1)S(1)}, bf16[512,128]{1,0:T(8,128)(2,1)S(1)}, u32[]{:S(2)}, u32[]{:S(2)}) %collective-permute-start.5) | collective-permute-done | bytes 131104 | tf_op jit(solution)/shard_map/ppermute | solution.py:521
  19.8 0.1 collective-permute-start.6
  19.9 0.5 collective-permute-start.4
  20.4 0.3 collective-permute-start.3
  20.7 0.9 collective-permute-done.4.refs_2_
  21.6 1.3 %ffn_send_late.1 = (f32[256,512]{1,0:T(8,128)S(1)}, bf16[256,512]{1,0:T(8,128)(2,1)S(1)}, bf16[256,512]{1,0:T(8,128)(2,1)S(1)}, bf16[256,512]{1,0:T(8,128)(2,1)S...) custom-call(bf16[1024,512]{1,0:T(8,128)(2,1)S(1)} %get-tuple-element.145.refs_0_, ...), custom_call_target="tpu_custom_call" | custom-call | flops 1 | bytes 1 | tf_op jit(solution)/shard_map/ffn_send_late/pallas_call | solution.py:508
  22.9 0.2 collective-permute-start.8
  23.1 1.3 %ffn_keep_late.1 = (f32[256,512]{1,0:T(8,128)S(1)}, bf16[256,512]{1,0:T(8,128)(2,1)S(1)}, bf16[256,512]{1,0:T(8,128)(2,1)S(1)}, bf16[256,512]{1,0:T(8,128)(2,1)S...) custom-call(bf16[1024,512]{1,0:T(8,128)(2,1)S(1)} %get-tuple-element.145.refs_0_, ...), custom_call_target="tpu_custom_call" | custom-call | flops 1 | bytes 1 | tf_op jit(solution)/shard_map/ffn_keep_late/pallas_call | solution.py:508
  24.4 1.4 %collective-permute-done.3.refs_0_.refs_1_.refs_3_ = bf16[512,128]{1,0:T(8,128)(2,1)S(1)} collective-permute-done((bf16[512,128]{1,0:T(8,128)(2,1)S(1)}, bf16[512,128]{1,0:T(8,128)(2,1)S(1)}, u32[]{:S(2)}, u32[]{:S(2)}) %collective-permute-start.3) | collective-permute-done | bytes 131104 | tf_op jit(solution)/shard_map/ppermute | solution.py:521
  25.9 0.1 add_late.1.refs_10_.refs_0_
  26.0 0.6 collective-permute-start.10
  26.5 0.5 collective-permute-start.7
  27.0 1.0 ffn_late.1
  28.1 2.7 %ffn_rows_early.1 = (f32[256,512]{1,0:T(8,128)S(1)}, bf16[256,512]{1,0:T(8,128)(2,1)S(1)}, bf16[256,512]{1,0:T(8,128)(2,1)S(1)}, bf16[256,512]{1,0:T(8,128)(2,1)...) custom-call(bf16[1024,512]{1,0:T(8,128)(2,1)S(1)} %get-tuple-element, ...), custom_call_target="tpu_custom_call" | custom-call | flops 1 | bytes 1 | tf_op jit(solution)/shard_map/ffn_rows_early/pallas_call | solution.py:508
  30.7 0.4 collective-permute-start.9
  31.1 1.1 %ffn_early.1 = (bf16[256,512]{1,0:T(8,128)(2,1)S(1)}, bf16[256,512]{1,0:T(8,128)(2,1)S(1)}, bf16[256,512]{1,0:T(8,128)(2,1)S(1)}, bf16[256,512]{1,0:T(8,128)(2,1...) custom-call(bf16[1024,512]{1,0:T(8,128)(2,1)S(1)} %get-tuple-element, ...), custom_call_target="tpu_custom_call" | custom-call | flops 1 | bytes 1 | tf_op jit(solution)/shard_map/ffn_early/pallas_call | solution.py:508
  32.3 1.2 %collective-permute-done.10.refs_1_ = bf16[256,512]{1,0:T(8,128)(2,1)S(1)} collective-permute-done((bf16[256,512]{1,0:T(8,128)(2,1)S(1)}, bf16[256,512]{1,0:T(8,128)(2,1)S(1)}, u32[]{:S(2)}, u32[]{:S(2)}) %collective-permute-start.10) | collective-permute-done | bytes 262176 | tf_op jit(solution)/shard_map/ppermute | solution.py:521
  33.5 0.1 collective-permute-start.14
  33.6 1.6 %collective-permute-start.12 = (bf16[256,512]{1,0:T(8,128)(2,1)S(1)}, bf16[256,512]{1,0:T(8,128)(2,1)S(1)}, u32[]{:S(2)}, u32[]{:S(2)}) collective-permute-start(bf16[256,512]{1,0:T(8,128)(2,1)S(1)} %get-tuple-element.190), channel_id=1, source_target_pairs={{0,4},{4,0},{8,12},{12,8},{16,20},{20,16},{24,28},{28,24},{1,5},{5... | collective-permute-start | bytes 786440 | tf_op jit(solution)/shard_map/ppermute | solution.py:521
  35.2 1.6 %collective-permute-start.13 = (bf16[256,512]{1,0:T(8,128)(2,1)S(1)}, bf16[256,512]{1,0:T(8,128)(2,1)S(1)}, u32[]{:S(2)}, u32[]{:S(2)}) collective-permute-start(bf16[256,512]{1,0:T(8,128)(2,1)S(1)} %get-tuple-element.192), channel_id=1, source_target_pairs={{0,8},{4,12},{8,0},{12,4},{16,24},{20,28},{24,16},{28,20},{1,9},{5... | collective-permute-start | bytes 786440 | tf_op jit(solution)/shard_map/ppermute | solution.py:521
  36.8 0.6 collective-permute-start.11
  37.4 6.4 %back_late.1 = (f32[512,512]{1,0:T(8,128)S(1)}, f32[128,1536]{1,0:T(8,128)S(1)}, f32[128,1536]{1,0:T(8,128)S(1)}, f32[128,512]{1,0:T(8,128)S(1)}, f32[128,512]{1...) custom-call(f32[256,512]{1,0:T(8,128)S(1)} %get-tuple-element.193.refs_0_.refs_6_,, ...), custom_call_target="tpu_custom_call" | custom-call | flops 1 | bytes 1 | tf_op jit(solution)/shard_map/back_late/pallas_call | solution.py:508
  43.9 1.1 %collective-permute-done.11.refs_1_ = bf16[256,512]{1,0:T(8,128)(2,1)S(1)} collective-permute-done((bf16[256,512]{1,0:T(8,128)(2,1)S(1)}, bf16[256,512]{1,0:T(8,128)(2,1)S(1)}, u32[]{:S(2)}, u32[]{:S(2)}) %collective-permute-start.11) | collective-permute-done | bytes 262176 | tf_op jit(solution)/shard_map/ppermute | solution.py:521
  45.0 0.5 add_middle.1
  45.5 0.1 collective-permute-start.15
  45.6 0.5 collective-permute-start.16
  46.1 0.5 collective-permute-start.17
  46.7 0.5 collective-permute-done.15.refs_3_
  47.1 4.6 %back_early.1 = (f32[512,512]{1,0:T(8,128)S(1)}, f32[128,1536]{1,0:T(8,128)S(1)}, f32[128,1536]{1,0:T(8,128)S(1)}, f32[128,512]{1,0:T(8,128)S(1)}, f32[128,512]{...) custom-call(f32[256,512]{1,0:T(8,128)S(1)} %get-tuple-element.174.refs_0_.refs_4_, ...), custom_call_target="tpu_custom_call" | custom-call | flops 1 | bytes 1 | tf_op jit(solution)/shard_map/back_early/pallas_call | solution.py:508
  51.8 1.8 %back_end.1 = (bf16[1024,512]{1,0:T(8,128)(2,1)S(1)}, bf16[1024,512]{1,0:T(8,128)(2,1)S(1)}, bf16[192,512]{1,0:T(8,128)(2,1)S(1)}, bf16[192,512]{1,0:T(8,128)(2,...) custom-call(bf16[512,384]{1,0:T(8,128)(2,1)S(1)} %get-tuple-element.150.refs_4_.ref, ...), custom_call_target="tpu_custom_call" | custom-call | flops 1 | bytes 1 | tf_op jit(solution)/shard_map/back_end/pallas_call | solution.py:508
  53.6 0.2 collective-permute-start.20
  53.8 1.0 collective-permute-start.18
  54.8 1.6 %collective-permute-start.19 = (bf16[160,512]{1,0:T(8,128)(2,1)S(1)}, bf16[160,512]{1,0:T(8,128)(2,1)S(1)}, u32[]{:S(2)}, u32[]{:S(2)}) collective-permute-start(bf16[160,512]{1,0:T(8,128)(2,1)S(1)} %get-tuple-element.232), channel_id=1, source_target_pairs={{0,8},{4,12},{8,0},{12,4},{16,24},{20,28},{24,16},{28,20},{1,9},{5... | collective-permute-start | bytes 491528 | tf_op jit(solution)/shard_map/ppermute | solution.py:521
  56.3 2.6 %collective-permute-start.23 = (bf16[256,512]{1,0:T(8,128)(2,1)S(1)}, bf16[256,512]{1,0:T(8,128)(2,1)S(1)}, u32[]{:S(2)}, u32[]{:S(2)}) collective-permute-start(bf16[256,512]{1,0:T(8,128)(2,1)S(1)} %get-tuple-element.239.refs_4_), channel_id=1, source_target_pairs={{0,16},{4,20},{8,24},{12,28},{16,0},{20,4},{24,8},{28,12},{1,17},{... | collective-permute-start | bytes 786440 | tf_op jit(solution)/shard_map/ppermute | solution.py:521
  58.9 5.5 %collective-permute-done.19.refs_3_ = bf16[160,512]{1,0:T(8,128)(2,1)S(1)} collective-permute-done((bf16[160,512]{1,0:T(8,128)(2,1)S(1)}, bf16[160,512]{1,0:T(8,128)(2,1)S(1)}, u32[]{:S(2)}, u32[]{:S(2)}) %collective-permute-start.19) | collective-permute-done | bytes 163872 | tf_op jit(solution)/shard_map/ppermute | solution.py:521
  64.4 0.4 step_0.1
  64.9 0.6 collective-permute-start.32
  65.5 1.1 %collective-permute-start.22 = (bf16[80,512]{1,0:T(8,128)(2,1)S(1)}, bf16[80,512]{1,0:T(8,128)(2,1)S(1)}, u32[]{:S(2)}, u32[]{:S(2)}) collective-permute-start(bf16[80,512]{1,0:T(8,128)(2,1)S(1)} %get-tuple-element.238), channel_id=1, source_target_pairs={{0,4},{4,0},{8,12},{12,8},{16,20},{20,16},{24,28},{28,24},{1,5},{5... | collective-permute-start | bytes 245768 | tf_op jit(solution)/shard_map/ppermute | solution.py:521
  66.6 4.5 %collective-permute-done.23.refs_5_ = bf16[256,512]{1,0:T(8,128)(2,1)S(1)} collective-permute-done((bf16[256,512]{1,0:T(8,128)(2,1)S(1)}, bf16[256,512]{1,0:T(8,128)(2,1)S(1)}, u32[]{:S(2)}, u32[]{:S(2)}) %collective-permute-start.23) | collective-permute-done | bytes 262176 | tf_op jit(solution)/shard_map/ppermute | solution.py:521
  71.1 0.7 collective-permute-done.21.refs_1_
  71.8 0.1 step_1.1
  71.9 1.3 %collective-permute-start.24 = (bf16[176,512]{1,0:T(8,128)(2,1)S(1)}, bf16[176,512]{1,0:T(8,128)(2,1)S(1)}, u32[]{:S(2)}, u32[]{:S(2)}) collective-permute-start(bf16[176,512]{1,0:T(8,128)(2,1)S(1)} %get-tuple-element.240.refs_0_), channel_id=1, source_target_pairs={{0,16},{4,20},{8,24},{12,28},{16,0},{20,4},{24,8},{28,12},{1,17},{... | collective-permute-start | bytes 540680 | tf_op jit(solution)/shard_map/ppermute | solution.py:521
  73.2 2.5 %collective-permute-start.25 = (bf16[128,512]{1,0:T(8,128)(2,1)S(1)}, bf16[128,512]{1,0:T(8,128)(2,1)S(1)}, u32[]{:S(2)}, u32[]{:S(2)}) collective-permute-start(bf16[128,512]{1,0:T(8,128)(2,1)S(1)} %get-tuple-element.241.refs_2_), channel_id=1, source_target_pairs={{0,8},{4,12},{8,0},{12,4},{16,24},{20,28},{24,16},{28,20},{1,9},{5... | collective-permute-start | bytes 393224 | tf_op jit(solution)/shard_map/ppermute | solution.py:521
  75.7 0.9 collective-permute-start.26
  76.6 2.7 %collective-permute-done.25.refs_3_ = bf16[128,512]{1,0:T(8,128)(2,1)S(1)} collective-permute-done((bf16[128,512]{1,0:T(8,128)(2,1)S(1)}, bf16[128,512]{1,0:T(8,128)(2,1)S(1)}, u32[]{:S(2)}, u32[]{:S(2)}) %collective-permute-start.25) | collective-permute-done | bytes 131104 | tf_op jit(solution)/shard_map/ppermute | solution.py:521
  79.3 1.3 %collective-permute-done.26.refs_5_ = bf16[128,512]{1,0:T(8,128)(2,1)S(1)} collective-permute-done((bf16[128,512]{1,0:T(8,128)(2,1)S(1)}, bf16[128,512]{1,0:T(8,128)(2,1)S(1)}, u32[]{:S(2)}, u32[]{:S(2)}) %collective-permute-start.26) | collective-permute-done | bytes 131104 | tf_op jit(solution)/shard_map/ppermute | solution.py:521
  80.7 0.8 collective-permute-done.24.refs_1_
  81.4 0.2 step_2.1
  81.6 1.0 collective-permute-start.29
  82.6 0.2 collective-permute-start.30
  82.8 1.8 %collective-permute-start.27 = (bf16[80,512]{1,0:T(8,128)(2,1)S(1)}, bf16[80,512]{1,0:T(8,128)(2,1)S(1)}, u32[]{:S(2)}, u32[]{:S(2)}) collective-permute-start(bf16[80,512]{1,0:T(8,128)(2,1)S(1)} %get-tuple-element.243.refs_0_), channel_id=1, source_target_pairs={{0,8},{4,12},{8,0},{12,4},{16,24},{20,28},{24,16},{28,20},{1,9},{5... | collective-permute-start | bytes 245768 | tf_op jit(solution)/shard_map/ppermute | solution.py:521
  84.6 1.1 %collective-permute-start.28 = (bf16[80,512]{1,0:T(8,128)(2,1)S(1)}, bf16[80,512]{1,0:T(8,128)(2,1)S(1)}, u32[]{:S(2)}, u32[]{:S(2)}) collective-permute-start(bf16[80,512]{1,0:T(8,128)(2,1)S(1)} %get-tuple-element.244.refs_2_), channel_id=1, source_target_pairs={{0,4},{4,0},{8,12},{12,8},{16,20},{20,16},{24,28},{28,24},{1,5},{5... | collective-permute-start | bytes 245768 | tf_op jit(solution)/shard_map/ppermute | solution.py:521
  85.7 4.9 %collective-permute-done.27.refs_1_ = bf16[80,512]{1,0:T(8,128)(2,1)S(1)} collective-permute-done((bf16[80,512]{1,0:T(8,128)(2,1)S(1)}, bf16[80,512]{1,0:T(8,128)(2,1)S(1)}, u32[]{:S(2)}, u32[]{:S(2)}) %collective-permute-start.27) | collective-permute-done | bytes 81952 | tf_op jit(solution)/shard_map/ppermute | solution.py:521
  90.6 0.6 step_3.1
  91.3 1.2 %collective-permute-start.34 = (bf16[160,512]{1,0:T(8,128)(2,1)S(1)}, bf16[160,512]{1,0:T(8,128)(2,1)S(1)}, u32[]{:S(2)}, u32[]{:S(2)}) collective-permute-start(bf16[160,512]{1,0:T(8,128)(2,1)S(1)} %get-tuple-element.253.refs_13_.refs_0_), channel_id=1, source_target_pairs={{0,4},{4,0},{8,12},{12,8},{16,20},{20,16},{24,28},{28,24},{1,5},{5... | collective-permute-start | bytes 491528 | tf_op jit(solution)/shard_map/ppermute | solution.py:521
  92.5 1.7 %collective-permute-start.35 = (bf16[160,512]{1,0:T(8,128)(2,1)S(1)}, bf16[160,512]{1,0:T(8,128)(2,1)S(1)}, u32[]{:S(2)}, u32[]{:S(2)}) collective-permute-start(bf16[160,512]{1,0:T(8,128)(2,1)S(1)} %get-tuple-element.256.refs_2_), channel_id=1, source_target_pairs={{0,8},{4,12},{8,0},{12,4},{16,24},{20,28},{24,16},{28,20},{1,9},{5... | collective-permute-start | bytes 491528 | tf_op jit(solution)/shard_map/ppermute | solution.py:521
  94.3 2.2 %collective-permute-start.36 = (f32[16,512]{1,0:T(8,128)S(1)}, f32[16,512]{1,0:T(8,128)S(1)}, u32[]{:S(2)}, u32[]{:S(2)}) collective-permute-start(f32[16,512]{1,0:T(8,128)S(1)} %get-tuple-element.257.refs_5_), channel_id=1, source_target_pairs={{0,2},{1,3},{2,0},{3,1},{4,6},{5,7},{6,4},{7,5},{8,10},{9,11},{10,... | collective-permute-start | bytes 98312 | tf_op jit(solution)/shard_map/ppermute | solution.py:521
  96.4 3.4 %finish.1 = (bf16[1024,512]{1,0:T(8,128)(2,1)}, bf16[1024,512]{1,0:T(8,128)(2,1)}, f32[512,512]{1,0:T(8,128)}, f32[512,512]{1,0:T(8,128)}) custom-call(bf16[1024,512]{1,0:T(8,128)(2,1)S(1)} %get-tuple-element.145.refs_0_, f32[1,512]{1,0:T(1,128)S(1)} %get-tuple-element.146.refs_3_.refs_1_, f32[512,512]{1,0:T(8,128)S(1)} %get-tuple-element.208.refs_2_, ...), custom_call_target="tpu_custom_call" | custom-call | flops 1 | bytes 1 | tf_op jit(solution)/shard_map/finish/pallas_call | solution.py:508
  99.9 1.9 %last.1 = (f32[512,128]{1,0:T(8,128)}, f32[512,128]{1,0:T(8,128)}, f32[512,128]{1,0:T(8,128)}, f32[512,128]{1,0:T(8,128)}, f32[128,512]{1,0:T(8,128)}, /*index=5...) custom-call(bf16[160,512]{1,0:T(8,128)(2,1)S(1)} %get-tuple-element., ...), custom_call_target="tpu_custom_call" | custom-call | flops 1 | bytes 1 | tf_op jit(solution)/shard_map/last/pallas_call | solution.py:508
  (35 shorter events, 0.3 us)
Async XLA Ops:
  0.7 13.4 %collective-permute-start.1 = (bf16[128,512]{1,0:T(8,128)(2,1)}, bf16[128,512]{1,0:T(8,128)(2,1)S(1)}, u32[]{:S(2)}, u32[]{:S(2)}) collective-permute-start(bf16[128,512]{1,0:T(8,128)(2,1)} %refs_5_.7), channel_id=1, source_target_pairs={{0,2},{1,3},{2,0},{3,1},{4,6},{5,7},{6,4},{7,5},{8,10},{9,11},{10,... | collective-permute-start | bytes 393224 | tf_op jit(solution)/shard_map/ppermute | solution.py:521
  3.7 10.3 %collective-permute-start = (bf16[128,512]{1,0:T(8,128)(2,1)}, bf16[128,512]{1,0:T(8,128)(2,1)S(1)}, u32[]{:S(2)}, u32[]{:S(2)}) collective-permute-start(bf16[128,512]{1,0:T(8,128)(2,1)} %refs_5_.7), channel_id=1, source_target_pairs={{0,1},{1,0},{2,3},{3,2},{4,5},{5,4},{6,7},{7,6},{8,9},{9,8},{10,11... | collective-permute-start | bytes 393224 | tf_op jit(solution)/shard_map/ppermute | solution.py:521
  13.8 7.8 %copy-start = (bf16[128,512]{1,0:T(8,128)(2,1)S(1)}, bf16[128,512]{1,0:T(8,128)(2,1)}, u32[]{:S(2)}) copy-start(bf16[128,512]{1,0:T(8,128)(2,1)} %refs_5_.7) | copy-start | bytes 393220
  13.8 6.0 %collective-permute-start.5 = (bf16[512,128]{1,0:T(8,128)(2,1)S(1)}, bf16[512,128]{1,0:T(8,128)(2,1)S(1)}, u32[]{:S(2)}, u32[]{:S(2)}) collective-permute-start(bf16[512,128]{1,0:T(8,128)(2,1)S(1)} %get-tuple-element.156.refs_1_.refs_7_), channel_id=1, source_target_pairs={{0,2},{1,3},{2,0},{3,1},{4,6},{5,7},{6,4},{7,5},{8,10},{9,11},{10,... | collective-permute-start | bytes 393224 | tf_op jit(solution)/shard_map/ppermute | solution.py:521
  19.8 1.8 %collective-permute-start.6 = (bf16[1024,128]{1,0:T(8,128)(2,1)S(1)}, bf16[1024,128]{1,0:T(8,128)(2,1)S(1)}, u32[]{:S(2)}, u32[]{:S(2)}) collective-permute-start(bf16[1024,128]{1,0:T(8,128)(2,1)S(1)} %relay_late.1), channel_id=1, source_target_pairs={{0,1},{1,0},{2,3},{3,2},{4,5},{5,4},{6,7},{7,6},{8,9},{9,8},{10,11... | collective-permute-start | bytes 786440 | tf_op jit(solution)/shard_map/ppermute | solution.py:521
  19.9 1.7 %collective-permute-start.4 = (bf16[512,128]{1,0:T(8,128)(2,1)S(1)}, bf16[512,128]{1,0:T(8,128)(2,1)S(1)}, u32[]{:S(2)}, u32[]{:S(2)}) collective-permute-start(bf16[512,128]{1,0:T(8,128)(2,1)S(1)} %get-tuple-element.156.refs_1_.refs_7_), channel_id=1, source_target_pairs={{0,1},{1,0},{2,3},{3,2},{4,5},{5,4},{6,7},{7,6},{8,9},{9,8},{10,11... | collective-permute-start | bytes 393224 | tf_op jit(solution)/shard_map/ppermute | solution.py:521
  20.4 5.5 %collective-permute-start.3 = (bf16[512,128]{1,0:T(8,128)(2,1)S(1)}, bf16[512,128]{1,0:T(8,128)(2,1)S(1)}, u32[]{:S(2)}, u32[]{:S(2)}) collective-permute-start(bf16[512,128]{1,0:T(8,128)(2,1)S(1)} %get-tuple-element.155.refs_2_.refs_1_.refs_7_), channel_id=1, source_target_pairs={{0,2},{1,3},{2,0},{3,1},{4,6},{5,7},{6,4},{7,5},{8,10},{9,11},{10,... | collective-permute-start | bytes 393224 | tf_op jit(solution)/shard_map/ppermute | solution.py:521
  22.9 3.0 %collective-permute-start.8 = (bf16[256,512]{1,0:T(8,128)(2,1)S(1)}, bf16[256,512]{1,0:T(8,128)(2,1)S(1)}, u32[]{:S(2)}, u32[]{:S(2)}) collective-permute-start(bf16[256,512]{1,0:T(8,128)(2,1)S(1)} %get-tuple-element.163.refs_15_), channel_id=1, source_target_pairs={{0,1},{1,0},{2,3},{3,2},{4,5},{5,4},{6,7},{7,6},{8,9},{9,8},{10,11... | collective-permute-start | bytes 786440 | tf_op jit(solution)/shard_map/ppermute | solution.py:521
  26.0 7.5 %collective-permute-start.10 = (bf16[256,512]{1,0:T(8,128)(2,1)S(1)}, bf16[256,512]{1,0:T(8,128)(2,1)S(1)}, u32[]{:S(2)}, u32[]{:S(2)}) collective-permute-start(bf16[256,512]{1,0:T(8,128)(2,1)S(1)} %add_late.1.refs_10_.refs_0_), channel_id=1, source_target_pairs={{0,2},{1,3},{2,0},{3,1},{4,6},{5,7},{6,4},{7,5},{8,10},{9,11},{10,... | collective-permute-start | bytes 786440 | tf_op jit(solution)/shard_map/ppermute | solution.py:521
  26.5 1.5 %collective-permute-start.2 = (bf16[512,128]{1,0:T(8,128)(2,1)S(1)}, bf16[512,128]{1,0:T(8,128)(2,1)S(1)}, u32[]{:S(2)}, u32[]{:S(2)}) collective-permute-start(bf16[512,128]{1,0:T(8,128)(2,1)S(1)} %get-tuple-element.155.refs_2_.refs_1_.refs_7_), channel_id=1, source_target_pairs={{0,1},{1,0},{2,3},{3,2},{4,5},{5,4},{6,7},{7,6},{8,9},{9,8},{10,11... | collective-permute-start | bytes 393224 | tf_op jit(solution)/shard_map/ppermute | solution.py:521
  26.5 1.5 %collective-permute-start.7 = (bf16[512,128]{1,0:T(8,128)(2,1)S(1)}, bf16[512,128]{1,0:T(8,128)(2,1)S(1)}, u32[]{:S(2)}, u32[]{:S(2)}) collective-permute-start(bf16[512,128]{1,0:T(8,128)(2,1)S(1)} %relay_early.1.refs_2_), channel_id=1, source_target_pairs={{0,1},{1,0},{2,3},{3,2},{4,5},{5,4},{6,7},{7,6},{8,9},{9,8},{10,11... | collective-permute-start | bytes 393224 | tf_op jit(solution)/shard_map/ppermute | solution.py:521
  30.7 6.0 %collective-permute-start.9 = (bf16[256,512]{1,0:T(8,128)(2,1)S(1)}, bf16[256,512]{1,0:T(8,128)(2,1)S(1)}, u32[]{:S(2)}, u32[]{:S(2)}) collective-permute-start(bf16[256,512]{1,0:T(8,128)(2,1)S(1)} %get-tuple-element.177), channel_id=1, source_target_pairs={{0,1},{1,0},{2,3},{3,2},{4,5},{5,4},{6,7},{7,6},{8,9},{9,8},{10,11... | collective-permute-start | bytes 786440 | tf_op jit(solution)/shard_map/ppermute | solution.py:521
  33.5 3.9 %collective-permute-start.14 = (bf16[256,512]{1,0:T(8,128)(2,1)S(1)}, bf16[256,512]{1,0:T(8,128)(2,1)S(1)}, u32[]{:S(2)}, u32[]{:S(2)}) collective-permute-start(bf16[256,512]{1,0:T(8,128)(2,1)S(1)} %add_late_chips.1.refs_2_), channel_id=1, source_target_pairs={{0,1},{1,0},{2,3},{3,2},{4,5},{5,4},{6,7},{7,6},{8,9},{9,8},{10,11... | collective-permute-start | bytes 786440 | tf_op jit(solution)/shard_map/ppermute | solution.py:521
  33.6 10.2 %collective-permute-start.12 = (bf16[256,512]{1,0:T(8,128)(2,1)S(1)}, bf16[256,512]{1,0:T(8,128)(2,1)S(1)}, u32[]{:S(2)}, u32[]{:S(2)}) collective-permute-start(bf16[256,512]{1,0:T(8,128)(2,1)S(1)} %get-tuple-element.190), channel_id=1, source_target_pairs={{0,4},{4,0},{8,12},{12,8},{16,20},{20,16},{24,28},{28,24},{1,5},{5... | collective-permute-start | bytes 786440 | tf_op jit(solution)/shard_map/ppermute | solution.py:521
  35.2 8.7 %collective-permute-start.13 = (bf16[256,512]{1,0:T(8,128)(2,1)S(1)}, bf16[256,512]{1,0:T(8,128)(2,1)S(1)}, u32[]{:S(2)}, u32[]{:S(2)}) collective-permute-start(bf16[256,512]{1,0:T(8,128)(2,1)S(1)} %get-tuple-element.192), channel_id=1, source_target_pairs={{0,8},{4,12},{8,0},{12,4},{16,24},{20,28},{24,16},{28,20},{1,9},{5... | collective-permute-start | bytes 786440 | tf_op jit(solution)/shard_map/ppermute | solution.py:521
  36.8 8.2 %collective-permute-start.11 = (bf16[256,512]{1,0:T(8,128)(2,1)S(1)}, bf16[256,512]{1,0:T(8,128)(2,1)S(1)}, u32[]{:S(2)}, u32[]{:S(2)}) collective-permute-start(bf16[256,512]{1,0:T(8,128)(2,1)S(1)} %add_early.1.refs_0_), channel_id=1, source_target_pairs={{0,2},{1,3},{2,0},{3,1},{4,6},{5,7},{6,4},{7,5},{8,10},{9,11},{10,... | collective-permute-start | bytes 786440 | tf_op jit(solution)/shard_map/ppermute | solution.py:521
  45.5 1.6 %collective-permute-start.15 = (bf16[256,512]{1,0:T(8,128)(2,1)S(1)}, bf16[256,512]{1,0:T(8,128)(2,1)S(1)}, u32[]{:S(2)}, u32[]{:S(2)}) collective-permute-start(bf16[256,512]{1,0:T(8,128)(2,1)S(1)} %get-tuple-element.200.refs_2_), channel_id=1, source_target_pairs={{0,1},{1,0},{2,3},{3,2},{4,5},{5,4},{6,7},{7,6},{8,9},{9,8},{10,11... | collective-permute-start | bytes 786440 | tf_op jit(solution)/shard_map/ppermute | solution.py:521
  45.6 6.2 %collective-permute-start.16 = (bf16[128,512]{1,0:T(8,128)(2,1)S(1)}, bf16[128,512]{1,0:T(8,128)(2,1)S(1)}, u32[]{:S(2)}, u32[]{:S(2)}) collective-permute-start(bf16[128,512]{1,0:T(8,128)(2,1)S(1)} %get-tuple-element.226), channel_id=1, source_target_pairs={{0,8},{4,12},{8,0},{12,4},{16,24},{20,28},{24,16},{28,20},{1,9},{5... | collective-permute-start | bytes 393224 | tf_op jit(solution)/shard_map/ppermute | solution.py:521
  46.1 5.7 %collective-permute-start.17 = (bf16[128,512]{1,0:T(8,128)(2,1)S(1)}, bf16[128,512]{1,0:T(8,128)(2,1)S(1)}, u32[]{:S(2)}, u32[]{:S(2)}) collective-permute-start(bf16[128,512]{1,0:T(8,128)(2,1)S(1)} %get-tuple-element.228), channel_id=1, source_target_pairs={{0,4},{4,0},{8,12},{12,8},{16,20},{20,16},{24,28},{28,24},{1,5},{5... | collective-permute-start | bytes 393224 | tf_op jit(solution)/shard_map/ppermute | solution.py:521
  53.6 10.9 %collective-permute-start.20 = (bf16[1024,512]{1,0:T(8,128)(2,1)S(1)}, bf16[1024,512]{1,0:T(8,128)(2,1)S(1)}, u32[]{:S(2)}, u32[]{:S(2)}) collective-permute-start(bf16[1024,512]{1,0:T(8,128)(2,1)S(1)} %get-tuple-element.234), channel_id=1, source_target_pairs={{0,1},{1,0},{2,3},{3,2},{4,5},{5,4},{6,7},{7,6},{8,9},{9,8},{10,11... | collective-permute-start | bytes 3145736 | tf_op jit(solution)/shard_map/ppermute | solution.py:521
  53.8 10.6 %collective-permute-start.18 = (bf16[192,512]{1,0:T(8,128)(2,1)S(1)}, bf16[192,512]{1,0:T(8,128)(2,1)S(1)}, u32[]{:S(2)}, u32[]{:S(2)}) collective-permute-start(bf16[192,512]{1,0:T(8,128)(2,1)S(1)} %get-tuple-element.230), channel_id=1, source_target_pairs={{0,4},{4,0},{8,12},{12,8},{16,20},{20,16},{24,28},{28,24},{1,5},{5... | collective-permute-start | bytes 589832 | tf_op jit(solution)/shard_map/ppermute | solution.py:521
  54.8 9.7 %collective-permute-start.19 = (bf16[160,512]{1,0:T(8,128)(2,1)S(1)}, bf16[160,512]{1,0:T(8,128)(2,1)S(1)}, u32[]{:S(2)}, u32[]{:S(2)}) collective-permute-start(bf16[160,512]{1,0:T(8,128)(2,1)S(1)} %get-tuple-element.232), channel_id=1, source_target_pairs={{0,8},{4,12},{8,0},{12,4},{16,24},{20,28},{24,16},{28,20},{1,9},{5... | collective-permute-start | bytes 491528 | tf_op jit(solution)/shard_map/ppermute | solution.py:521
  56.3 14.8 %collective-permute-start.23 = (bf16[256,512]{1,0:T(8,128)(2,1)S(1)}, bf16[256,512]{1,0:T(8,128)(2,1)S(1)}, u32[]{:S(2)}, u32[]{:S(2)}) collective-permute-start(bf16[256,512]{1,0:T(8,128)(2,1)S(1)} %get-tuple-element.239.refs_4_), channel_id=1, source_target_pairs={{0,16},{4,20},{8,24},{12,28},{16,0},{20,4},{24,8},{28,12},{1,17},{... | collective-permute-start | bytes 786440 | tf_op jit(solution)/shard_map/ppermute | solution.py:521
  64.9 25.7 %collective-permute-start.32 = (bf16[1024,512]{1,0:T(8,128)(2,1)S(1)}, bf16[1024,512]{1,0:T(8,128)(2,1)S(1)}, u32[]{:S(2)}, u32[]{:S(2)}) collective-permute-start(bf16[1024,512]{1,0:T(8,128)(2,1)S(1)} %get-tuple-element.248.refs_10_), channel_id=1, source_target_pairs={{0,2},{1,3},{2,0},{3,1},{4,6},{5,7},{6,4},{7,5},{8,10},{9,11},{10,... | collective-permute-start | bytes 3145736 | tf_op jit(solution)/shard_map/ppermute | solution.py:521
  65.5 6.3 %collective-permute-start.21 = (bf16[96,512]{1,0:T(8,128)(2,1)S(1)}, bf16[96,512]{1,0:T(8,128)(2,1)S(1)}, u32[]{:S(2)}, u32[]{:S(2)}) collective-permute-start(bf16[96,512]{1,0:T(8,128)(2,1)S(1)} %get-tuple-element.236), channel_id=1, source_target_pairs={{0,8},{4,12},{8,0},{12,4},{16,24},{20,28},{24,16},{28,20},{1,9},{5... | collective-permute-start | bytes 294920 | tf_op jit(solution)/shard_map/ppermute | solution.py:521
  65.5 5.6 %collective-permute-start.22 = (bf16[80,512]{1,0:T(8,128)(2,1)S(1)}, bf16[80,512]{1,0:T(8,128)(2,1)S(1)}, u32[]{:S(2)}, u32[]{:S(2)}) collective-permute-start(bf16[80,512]{1,0:T(8,128)(2,1)S(1)} %get-tuple-element.238), channel_id=1, source_target_pairs={{0,4},{4,0},{8,12},{12,8},{16,20},{20,16},{24,28},{28,24},{1,5},{5... | collective-permute-start | bytes 245768 | tf_op jit(solution)/shard_map/ppermute | solution.py:521
  71.9 9.5 %collective-permute-start.24 = (bf16[176,512]{1,0:T(8,128)(2,1)S(1)}, bf16[176,512]{1,0:T(8,128)(2,1)S(1)}, u32[]{:S(2)}, u32[]{:S(2)}) collective-permute-start(bf16[176,512]{1,0:T(8,128)(2,1)S(1)} %get-tuple-element.240.refs_0_), channel_id=1, source_target_pairs={{0,16},{4,20},{8,24},{12,28},{16,0},{20,4},{24,8},{28,12},{1,17},{... | collective-permute-start | bytes 540680 | tf_op jit(solution)/shard_map/ppermute | solution.py:521
  73.2 6.1 %collective-permute-start.25 = (bf16[128,512]{1,0:T(8,128)(2,1)S(1)}, bf16[128,512]{1,0:T(8,128)(2,1)S(1)}, u32[]{:S(2)}, u32[]{:S(2)}) collective-permute-start(bf16[128,512]{1,0:T(8,128)(2,1)S(1)} %get-tuple-element.241.refs_2_), channel_id=1, source_target_pairs={{0,8},{4,12},{8,0},{12,4},{16,24},{20,28},{24,16},{28,20},{1,9},{5... | collective-permute-start | bytes 393224 | tf_op jit(solution)/shard_map/ppermute | solution.py:521
  75.7 5.0 %collective-permute-start.26 = (bf16[128,512]{1,0:T(8,128)(2,1)S(1)}, bf16[128,512]{1,0:T(8,128)(2,1)S(1)}, u32[]{:S(2)}, u32[]{:S(2)}) collective-permute-start(bf16[128,512]{1,0:T(8,128)(2,1)S(1)} %get-tuple-element.242.refs_4_), channel_id=1, source_target_pairs={{0,4},{4,0},{8,12},{12,8},{16,20},{20,16},{24,28},{28,24},{1,5},{5... | collective-permute-start | bytes 393224 | tf_op jit(solution)/shard_map/ppermute | solution.py:521
  81.6 9.0 %collective-permute-start.29 = (bf16[256,512]{1,0:T(8,128)(2,1)S(1)}, bf16[256,512]{1,0:T(8,128)(2,1)S(1)}, u32[]{:S(2)}, u32[]{:S(2)}) collective-permute-start(bf16[256,512]{1,0:T(8,128)(2,1)S(1)} %get-tuple-element.245.refs_4_), channel_id=1, source_target_pairs={{0,4},{4,0},{8,12},{12,8},{16,20},{20,16},{24,28},{28,24},{1,5},{5... | collective-permute-start | bytes 786440 | tf_op jit(solution)/shard_map/ppermute | solution.py:521
  82.6 8.0 %collective-permute-start.30 = (bf16[256,512]{1,0:T(8,128)(2,1)S(1)}, bf16[256,512]{1,0:T(8,128)(2,1)S(1)}, u32[]{:S(2)}, u32[]{:S(2)}) collective-permute-start(bf16[256,512]{1,0:T(8,128)(2,1)S(1)} %get-tuple-element.246.refs_6_), channel_id=1, source_target_pairs={{0,8},{4,12},{8,0},{12,4},{16,24},{20,28},{24,16},{28,20},{1,9},{5... | collective-permute-start | bytes 786440 | tf_op jit(solution)/shard_map/ppermute | solution.py:521
  82.8 1.8 %collective-permute-start.31 = (f32[16,512]{1,0:T(8,128)S(1)}, f32[16,512]{1,0:T(8,128)S(1)}, u32[]{:S(2)}, u32[]{:S(2)}) collective-permute-start(f32[16,512]{1,0:T(8,128)S(1)} %get-tuple-element.247.refs_8_.refs_4_), channel_id=1, source_target_pairs={{0,1},{1,0},{2,3},{3,2},{4,5},{5,4},{6,7},{7,6},{8,9},{9,8},{10,11... | collective-permute-start | bytes 98312 | tf_op jit(solution)/shard_map/ppermute | solution.py:521
  82.8 7.8 %collective-permute-start.27 = (bf16[80,512]{1,0:T(8,128)(2,1)S(1)}, bf16[80,512]{1,0:T(8,128)(2,1)S(1)}, u32[]{:S(2)}, u32[]{:S(2)}) collective-permute-start(bf16[80,512]{1,0:T(8,128)(2,1)S(1)} %get-tuple-element.243.refs_0_), channel_id=1, source_target_pairs={{0,8},{4,12},{8,0},{12,4},{16,24},{20,28},{24,16},{28,20},{1,9},{5... | collective-permute-start | bytes 245768 | tf_op jit(solution)/shard_map/ppermute | solution.py:521
  84.6 6.0 %collective-permute-start.28 = (bf16[80,512]{1,0:T(8,128)(2,1)S(1)}, bf16[80,512]{1,0:T(8,128)(2,1)S(1)}, u32[]{:S(2)}, u32[]{:S(2)}) collective-permute-start(bf16[80,512]{1,0:T(8,128)(2,1)S(1)} %get-tuple-element.244.refs_2_), channel_id=1, source_target_pairs={{0,4},{4,0},{8,12},{12,8},{16,20},{20,16},{24,28},{28,24},{1,5},{5... | collective-permute-start | bytes 245768 | tf_op jit(solution)/shard_map/ppermute | solution.py:521
  91.2 5.2 %collective-permute-start.33 = (bf16[1024,512]{1,0:T(8,128)(2,1)S(1)}, bf16[1024,512]{1,0:T(8,128)(2,1)S(1)}, u32[]{:S(2)}, u32[]{:S(2)}) collective-permute-start(bf16[1024,512]{1,0:T(8,128)(2,1)S(1)} %get-tuple-element.249.refs_8_), channel_id=1, source_target_pairs={{0,1},{1,0},{2,3},{3,2},{4,5},{5,4},{6,7},{7,6},{8,9},{9,8},{10,11... | collective-permute-start | bytes 3145736 | tf_op jit(solution)/shard_map/ppermute | solution.py:521
  91.3 8.6 %collective-permute-start.34 = (bf16[160,512]{1,0:T(8,128)(2,1)S(1)}, bf16[160,512]{1,0:T(8,128)(2,1)S(1)}, u32[]{:S(2)}, u32[]{:S(2)}) collective-permute-start(bf16[160,512]{1,0:T(8,128)(2,1)S(1)} %get-tuple-element.253.refs_13_.refs_0_), channel_id=1, source_target_pairs={{0,4},{4,0},{8,12},{12,8},{16,20},{20,16},{24,28},{28,24},{1,5},{5... | collective-permute-start | bytes 491528 | tf_op jit(solution)/shard_map/ppermute | solution.py:521
  92.5 7.4 %collective-permute-start.35 = (bf16[160,512]{1,0:T(8,128)(2,1)S(1)}, bf16[160,512]{1,0:T(8,128)(2,1)S(1)}, u32[]{:S(2)}, u32[]{:S(2)}) collective-permute-start(bf16[160,512]{1,0:T(8,128)(2,1)S(1)} %get-tuple-element.256.refs_2_), channel_id=1, source_target_pairs={{0,8},{4,12},{8,0},{12,4},{16,24},{20,28},{24,16},{28,20},{1,9},{5... | collective-permute-start | bytes 491528 | tf_op jit(solution)/shard_map/ppermute | solution.py:521
  94.3 5.6 %collective-permute-start.36 = (f32[16,512]{1,0:T(8,128)S(1)}, f32[16,512]{1,0:T(8,128)S(1)}, u32[]{:S(2)}, u32[]{:S(2)}) collective-permute-start(f32[16,512]{1,0:T(8,128)S(1)} %get-tuple-element.257.refs_5_), channel_id=1, source_target_pairs={{0,2},{1,3},{2,0},{3,1},{4,6},{5,7},{6,4},{7,5},{8,10},{9,11},{10,... | collective-permute-start | bytes 98312 | tf_op jit(solution)/shard_map/ppermute | solution.py:521
